TPU v7x, 32 devices: a whole 2x2x4 slice. The times are simulated.
32 devices in a mesh: gy: 8 (over y, x, core), gz: 4 (over z).
Axes of the slice: x: 2, y: 2, z: 4, core: 2. Of those that a mesh axis runs over, the one named last changes fastest.
Arguments:
- reference_image: bfloat16 [64, 512, 2048], P(None, 'gy', 'gz'), may hold values from -6 to 6
- deformed: bfloat16 [64, 512, 2048], P(None, 'gy', 'gz'), may hold values from -12 to 12
- displacement: bfloat16 [3, 64, 512, 2048], P(None, None, 'gy', 'gz'), may hold values from -1 to 1
- plane_factors: float32 [2, 32, 8, 64], P(None, None, None, 'gy'), may hold values from -2.5 to 2.5
- depth_factors: float32 [2, 32, 2048], P(None, None, 'gz'), may hold values from -6 to 6
Outputs:
- residual: bfloat16 [64, 512, 2048], P(None, 'gy', 'gz')
- step_plane: float32 [2, 32, 8, 64], P(None, None, None, 'gy')
- step_depth: float32 [2, 32, 2048], P(None, None, 'gz')
All inputs are finite; a program needn't handle non-finite values.
Results may differ from a plain program's by a relative error of at most 0.0004.
Values may be sent and summed in bfloat16 or wider, within the bound.
No kernel may reach another device: no remote copies, remote signals or barrier semaphores. Data moves between devices by JAX's collectives and lax.ppermute only.
A program may use at most 256 MiB of HBM per device.

v0:
```python
import jax
import jax.numpy as jnp
from jax import lax
from jax.sharding import PartitionSpec as P

RANK = 32
KNOT = 8


epsilon = 1e-06
damping = 0.01
highest = lax.Precision.HIGHEST


def extended(cells, sides, width):
    for axis, dim in sides:
        count = lax.axis_size(axis)
        ends = count - 1
        head = lax.slice_in_dim(cells, 0, width, axis=dim)
        tail = lax.slice_in_dim(cells, cells.shape[dim] - width, cells.shape[dim], axis=dim)
        cells = jnp.concatenate(
            [
                lax.ppermute(tail, axis, [(i, (i + 1) % count) for i in range(ends)]),
                cells,
                lax.ppermute(head, axis, [((i + 1) % count, i) for i in range(ends)]),
            ],
            axis=dim,
        )
    return cells


def tent_weights(shift):
    moved = shift.astype(jnp.float32)
    return [jnp.maximum(0.0, 1.0 - jnp.abs(moved - offset)) for offset in (-1.0, 0.0, 1.0)]


def warp_image(padded, displacement):
    depth_x, width_y, width_z = displacement.shape[1:]
    weight_x = tent_weights(displacement[0])
    weight_y = tent_weights(displacement[1])
    weight_z = tent_weights(displacement[2])
    summed = jnp.zeros((depth_x, width_y, width_z), jnp.float32)
    for along_x in range(3):
        for along_y in range(3):
            partial_z = jnp.zeros((depth_x, width_y, width_z), jnp.float32)
            for along_z in range(3):
                window = padded[
                    along_x : along_x + depth_x,
                    along_y : along_y + width_y,
                    along_z : along_z + width_z,
                ]
                partial_z = partial_z + weight_z[along_z] * window.astype(jnp.float32)
            summed = summed + weight_x[along_x] * weight_y[along_y] * partial_z
    return summed


def expand_nodes(nodes):
    return jnp.repeat(jnp.repeat(nodes, KNOT, axis=2), KNOT, axis=3)


def reduce_nodes(field):
    leading = field.shape[:-2]
    depth_x, width_y = field.shape[-2:]
    shaped = field.reshape(leading + (depth_x // KNOT, KNOT, width_y // KNOT, KNOT))
    return jnp.sum(shaped, axis=(-3, -1))


def contract_rank(left, right):
    return lax.dot_general(left, right, (((0,), (0,)), ((), ())), precision=highest)


def contract_cells(left, right):
    return jnp.dot(left, right, precision=highest)


def contract_depth(left, right):
    return lax.dot_general(left, right, (((1,), (1,)), ((), ())), precision=highest)


def strip_terms(image, padded, displacement, plane_voxels, depth_factors):
    depth_x, width_y, width_z = image.shape
    cells = depth_x * width_y
    warped = warp_image(padded, displacement).reshape(cells, width_z)
    values = image.astype(jnp.float32).reshape(cells, width_z)
    flat_plane = plane_voxels.reshape(2, plane_voxels.shape[1], cells)
    contrast = contract_rank(flat_plane[0], depth_factors[0])
    brightness = contract_rank(flat_plane[1], depth_factors[1])
    misfit = warped - contrast * values - brightness
    product = misfit * values
    squares = values * values
    grad_depth = -jnp.stack(
        [contract_cells(flat_plane[0], product), contract_cells(flat_plane[1], misfit)]
    )
    level_sum = jnp.sum(flat_plane[1] * flat_plane[1], axis=1)
    first_depth = contract_cells(flat_plane[0] * flat_plane[0], squares)
    grad_voxels = -jnp.stack(
        [contract_depth(depth_factors[0], product), contract_depth(depth_factors[1], misfit)]
    )
    diag_voxels = contract_depth(depth_factors[0] * depth_factors[0], squares)
    grad_plane = reduce_nodes(grad_voxels.reshape(2, -1, depth_x, width_y))
    first_diag = reduce_nodes(diag_voxels.reshape(-1, depth_x, width_y))
    depth_level = KNOT * KNOT * jnp.sum(depth_factors[1] * depth_factors[1], axis=1)
    squared_sum = jnp.sum(misfit * misfit)
    residual = misfit.reshape(depth_x, width_y, width_z).astype(jnp.bfloat16)
    return (
        residual,
        squared_sum,
        grad_plane,
        first_diag,
        depth_level,
        grad_depth,
        first_depth,
        level_sum,
    )


def local(reference_image, deformed, displacement, plane_factors, depth_factors):
    rimmed = extended(deformed, (("gy", 1), ("gz", 2)), 1)
    padded = jnp.pad(rimmed, ((1, 1), (0, 0), (0, 0)))
    plane_voxels = expand_nodes(plane_factors)
    (
        residual,
        local_energy,
        grad_plane,
        first_diag,
        depth_level,
        grad_depth,
        first_depth,
        level_sum,
    ) = strip_terms(reference_image, padded, displacement, plane_voxels, depth_factors)
    nodes_x = plane_factors.shape[2]
    nodes_y = plane_factors.shape[3] * lax.axis_size("gy")
    full_z = depth_factors.shape[2] * lax.axis_size("gz")
    energy = lax.psum(local_energy, ("gy", "gz"))
    grad_plane, first_diag, depth_level = lax.psum((grad_plane, first_diag, depth_level), "gz")
    diag_plane = jnp.stack(
        [first_diag, jnp.broadcast_to(depth_level[:, None, None], first_diag.shape)]
    )
    lam_plane = damping * RANK * energy / (nodes_x * nodes_y)
    lam_depth = damping * energy / full_z
    step_plane = -grad_plane / (diag_plane + lam_plane + epsilon)
    grad_depth, first_depth, level_sum = lax.psum((grad_depth, first_depth, level_sum), "gy")
    diag_depth = jnp.stack([first_depth, jnp.broadcast_to(level_sum[:, None], first_depth.shape)])
    step_depth = -grad_depth / (diag_depth + lam_depth + epsilon)
    return (residual, step_plane, step_depth)


def solution(mesh):
    placed = (
        P(None, "gy", "gz"),
        P(None, "gy", "gz"),
        P(None, None, "gy", "gz"),
        P(None, None, None, "gy"),
        P(None, None, "gz"),
    )
    return jax.shard_map(
        local,
        mesh=mesh,
        in_specs=placed,
        out_specs=(P(None, "gy", "gz"), P(None, None, None, "gy"), P(None, None, "gz")),
        check_vma=False,
    )
```

profile of v0, /device:TPU:0, one launch (start us, length us, event | category | flops | bytes accessed | tf_op | source)
XLA Modules:
  0.0 486.1 jit_solution(957538562960458121)
XLA Ops:
  7.2 0.0 all-reduce.5.cloned.1.call-start
  7.2 1.4 fusion.133
  8.7 2.4 collective-permute-start
  11.1 0.0 copy-start.4
  11.1 1.6 collective-permute-start.1
  12.7 9.0 %fusion.132 = (bf16[1,64,64,512]{3,2,1,0:T(8,128)(2,1)}, bf16[1,64,64,512]{3,2,1,0:T(8,128)(2,1)}, bf16[1,64,64,512]{3,2,1,0:T(8,128)(2,1)}) fusion(bf16[3,64,64,512]{3,2,1,0:T(8,128)(2,1)} %param.7), kind=kLoop, calls=%fused_computation.173 | loop fusion | bytes 25165824 | tf_op jit(solution)/shard_map/slice | solution.py:41
  21.7 0.1 fusion.122
  21.8 0.3 broadcast_in_dim.28
  22.1 8.8 %fusion.124 = f32[4096,512]{1,0:T(8,128)} fusion(f32[32,4096]{0,1:T(8,128)S(1)} %bitcast.293, f32[2,32,512]{2,1,0:T(8,128)S(1)} %copy-done.5), kind=kOutput, calls=%fused_computation.159 | convolution fusion | flops 805306368 | bytes 10551296 | tf_op jit(solution)/shard_map/dot_general | solution.py:69
  30.9 1.2 convert_multiply_fusion
  32.2 7.5 %convolution_reduce_fusion = f32[32,8,8]{0,2,1:T(8,128)} fusion(f32[8,8,8,8,512]{4,3,2,1,0:T(8,128)S(1)} %bitcast.291, f32[2,32,512]{2,1,0:T(8,128)S(1)} %copy-done.5), kind=kOutput, calls=%fused_computation.139 | convolution fusion | flops 805451776 | bytes 8462336 | tf_op jit(solution)/shard_map/dot_general | solution.py:77
  39.6 0.3 broadcast_in_dim.34
  39.9 5.7 %convolution_bitcast_fusion.2 = f32[1,32,512]{2,1,0:T(8,128)} fusion(f32[32,4096]{0,1:T(8,128)S(1)} %bitcast.297, f32[4096,512]{1,0:T(8,128)S(1)} %bitcast.292), kind=kOutput, calls=%fused_computation.140 | convolution fusion | flops 805306368 | bytes 8978432 | tf_op jit(solution)/shard_map/dot_general | solution.py:73
  45.6 0.5 broadcast_multiply_fusion
  46.1 13.0 %copy.49 = bf16[64,64,512]{1,0,2:T(8,128)(2,1)} copy(bf16[64,64,512]{2,1,0:T(8,128)(2,1)} %param.6) | data formatting | bytes 8388608 | tf_op args[1]
  59.1 0.2 copy.59
  59.3 12.7 %copy.48 = bf16[64,1,512]{1,0,2:T(8,128)(2,1)} copy(bf16[64,1,512]{2,0,1:T(8,128)(2,1)S(1)} %collective-permute-done) | data formatting | bytes 131072 | tf_op jit(solution)/shard_map/ppermute | solution.py:23
  71.9 12.7 %copy.50 = bf16[64,1,512]{1,0,2:T(8,128)(2,1)} copy(bf16[64,1,512]{2,0,1:T(8,128)(2,1)S(1)} %collective-permute-done.1) | data formatting | bytes 131072 | tf_op jit(solution)/shard_map/ppermute | solution.py:25
  84.6 0.9 pad_maximum_fusion.5
  85.5 4.3 collective-permute-start.2
  89.8 1.3 collective-permute-start.3
  91.1 0.3 broadcast_reduce_fusion
  91.5 13.4 %copy.61 = bf16[1,64,64,512]{2,1,3,0:T(8,128)(2,1)} copy(bf16[1,64,64,512]{3,2,1,0:T(8,128)(2,1)} %get-tuple-element.14) | data formatting | bytes 8388608
  104.9 13.0 %copy.62 = bf16[1,64,64,512]{2,1,3,0:T(8,128)(2,1)} copy(bf16[1,64,64,512]{3,2,1,0:T(8,128)(2,1)} %get-tuple-element.13) | data formatting | bytes 8388608
  117.8 12.9 %copy.63 = bf16[1,64,64,512]{2,1,3,0:T(8,128)(2,1)} copy(bf16[1,64,64,512]{3,2,1,0:T(8,128)(2,1)} %get-tuple-element.12) | data formatting | bytes 8388608
  130.7 14.8 %psum.55 = f32[32]{0:T(128)S(1)} all-reduce(f32[32]{0:T(128)S(1)} %broadcast_reduce_fusion), channel_id=1, replica_groups=mesh['gy'=8,'gz'=4] {'gy'}, use_global_device_ids=true, to_apply=%region_11.12 | all-reduce | flops 32 | bytes 256 | tf_op jit(solution)/shard_map/psum | solution.py:142
  145.6 24.1 %maximum_maximum_fusion = (bf16[64,66,513]{1,0,2:T(8,128)(2,1)S(1)}, bf16[64,66,513]{1,0,2:T(8,128)(2,1)}) fusion(bf16[64,1,512]{1,0,2:T(8,128)(2,1)} %copy.50, bf16[64,64,512]{1,0,2:T(8,128)(2,1)} %copy.49, bf16[64,1,512]{1,0,2:T(8,128)(2,1)} %copy.48, bf16[64,66,1]{1,0,2:T(8,128)(2,1)S(1)} %collective-permute-done.2, ...), kind=kLoop, calls=%fused_computation.126 | loop fusion | flops 34670592 | bytes 13009920 | tf_op jit(solution)/shard_map/concatenate | solution.py:21
  169.6 24.0 %select_maximum_fusion = bf16[66,66,514]{1,0,2:T(8,128)(2,1)S(1)} fusion(bf16[64,66,1]{1,0,2:T(8,128)(2,1)S(1)} %collective-permute-done.3, bf16[64,66,1]{1,0,2:T(8,128)(2,1)S(1)} %collective-permute-done.2, bf16[64,1,512]{1,0,2:T(8,128)(2,1)} %copy.50, bf16[64,64,512]{1,0,2:T(8,128)(2,1)} %copy.49, bf16[64,1,512]{1,0,2:T(8,128)(2,1)} %copy.48), kind=kLoop, calls=%fused_computation.119 | loop fusion | flops 40301712 | bytes 8820240 | tf_op jit(solution)/shard_map/concatenate | solution.py:21
  193.7 119.0 %fusion.15 = f32[64,64,512]{1,0,2:T(8,128)} fusion(bf16[1,64,64,512]{2,1,3,0:T(8,128)(2,1)} %copy.61, bf16[1,64,64,512]{2,1,3,0:T(8,128)(2,1)} %copy.62, bf16[1,64,64,512]{2,1,3,0:T(8,128)(2,1)} %copy.63, bf16[64,64,512]{1,0,2:T(8,128)(2,1)} %copy.49, bf16[66,66,514]{1,0,2:T(8,128)(2,1)S(1)} %select_maximum_fusion, ...), kind=kLoop, calls=%fused_computation.26 | loop fusion | flops 293601280 | bytes 125960192 | tf_op jit(solution)/shard_map/add | solution.py:53
  312.7 12.7 %copy.56 = f32[64,64,512]{2,1,0:T(8,128)} copy(f32[64,64,512]{1,0,2:T(8,128)} %fusion.15) | data formatting | bytes 16777216 | tf_op jit(solution)/shard_map/add | solution.py:53
  325.5 1.6 broadcast_in_dim.32
  327.1 17.3 %multiply_reduce_fusion = (f32[]{:T(128)}, f32[4096,512]{1,0:T(8,128)}, bf16[4096,512]{1,0:T(8,128)(2,1)}, f32[4096,512]{1,0:T(8,128)S(1)}) fusion(bf16[64,64,512]{2,1,0:T(8,128)(2,1)} %param.5, f32[32,4096]{0,1:T(8,128)} %bitcast.295, f32[2,32,512]{2,1,0:T(8,128)S(1)} %copy-done.5, f32[4096,512]{1,0:T(8,128)} %fusion.124, f32[64,64,512]{2,1,0:T(8,128)} %copy.56), kind=kOutput, calls=%fused_computation.135 | convolution fusion | flops 822083584 | bytes 42532868 | tf_op jit(solution)/shard_map/dot_general | solution.py:69
  344.4 10.2 %convolution_bitcast_fusion.4 = f32[1,32,512]{2,1,0:T(8,128)S(1)} fusion(f32[4096,512]{1,0:T(8,128)} %get-tuple-element.16, f32[32,4096]{0,1:T(8,128)S(1)} %bitcast.294), kind=kOutput, calls=%fused_computation.142 | convolution fusion | flops 805306368 | bytes 8978432 | tf_op jit(solution)/shard_map/dot_general | solution.py:73
  354.6 7.7 %convolution_bitcast_fusion.1 = f32[32,4096]{1,0:T(8,128)S(1)} fusion(f32[4096,512]{1,0:T(8,128)S(1)} %copy-done, f32[2,32,512]{2,1,0:T(8,128)S(1)} %copy-done.5), kind=kOutput, calls=%fused_computation.137 | convolution fusion | flops 805306368 | bytes 8978432 | tf_op jit(solution)/shard_map/dot_general | solution.py:77
  362.3 0.0 copy-start.6
  362.4 5.3 %convolution_bitcast_fusion.3 = f32[1,32,512]{2,1,0:T(8,128)S(1)} fusion(f32[4096,512]{1,0:T(8,128)S(1)} %get-tuple-element.22, f32[32,4096]{0,1:T(8,128)S(1)} %bitcast.296), kind=kOutput, calls=%fused_computation.141 | convolution fusion | flops 805306368 | bytes 8978432 | tf_op jit(solution)/shard_map/dot_general | solution.py:73
  367.6 8.0 %convolution_bitcast_fusion = f32[32,4096]{1,0:T(8,128)S(1)} fusion(f32[4096,512]{1,0:T(8,128)S(1)} %get-tuple-element.22, f32[2,32,512]{2,1,0:T(8,128)S(1)} %copy-done.5), kind=kOutput, calls=%fused_computation.136 | convolution fusion | flops 805306368 | bytes 8978432 | tf_op jit(solution)/shard_map/dot_general | solution.py:77
  375.6 40.8 %psum.52 = f32[]{:T(128)} all-reduce(f32[]{:T(128)} %get-tuple-element.15), channel_id=1, replica_groups=mesh['gy'=8,'gz'=4] {'gy','gz'}, use_global_device_ids=true, to_apply=%region_7.8 | all-reduce | flops 1 | bytes 8 | tf_op jit(solution)/shard_map/psum | solution.py:134
  416.5 0.6 copy.57
  417.1 2.0 copy.58
  419.1 2.2 maximum_reduce_fusion
  421.3 0.7 maximum_negate_fusion
  422.0 0.0 all-reduce.5.cloned.1.call-update
  422.6 19.5 %all-reduce.2 = (f32[32]{0:T(128)S(1)}, f32[1,32,8,8]{1,3,2,0:T(8,128)S(1)}, f32[2,32,8,8]{1,3,2,0:T(8,128)S(1)}) all-reduce(f32[32]{0:T(128)S(1)} %copy-done.8, f32[1,32,8,8]{1,3,2,0:T(8,128)S(1)} %bitcast.303, f32[2,32,8,8]{1,3,2,0:T(8,128)S(1)} %neg.13), channel_id=1, replica_groups=mesh['gy'=8,'gz'=4] {'gz'}, use_global_device_ids=true, to_apply=%region_5.6 | all-reduce | flops 6176 | bytes 49408 | tf_op jit(solution)/shard_map/psum | solution.py:135
  442.1 0.7 fusion.118
  443.4 33.7 %all-reduce.5.cloned.1.call-done = (f32[1,32,512]{2,1,0:T(8,128)}, f32[2,32,512]{2,1,0:T(8,128)}) async-done(((f32[1,32,512]{2,1,0:T(8,128)}, f32[2,32,512]{2,1,0:T(8,128)}), (f32[1,32,512]{2,1,0:T(8,128)}, f32[2,32,512]{2,1,0:T(8,128)})) %all-reduce.5.cloned.1.call-update) | async-done | bytes 196624 | tf_op jit(solution)/shard_map/psum | solution.py:142
  477.1 0.1 stack_broadcast_in_dim.5
  477.2 1.6 fusion.116
  (28 shorter events, 0.2 us)
Async XLA Ops:
  7.2 14.5 %copy-start.7 = (f32[2,32,8,8]{1,3,2,0:T(8,128)S(1)}, f32[2,32,8,8]{1,3,2,0:T(8,128)}, u32[]{:S(2)}) copy-start(f32[2,32,8,8]{1,3,2,0:T(8,128)} %param.8) | copy-start | bytes 49156
  7.2 14.5 %copy-start.5 = (f32[2,32,512]{2,1,0:T(8,128)S(1)}, f32[2,32,512]{2,1,0:T(8,128)}, u32[]{:S(2)}) copy-start(f32[2,32,512]{2,1,0:T(8,128)} %param.9) | copy-start | bytes 393220
  7.2 469.9 %all-reduce.5.cloned.1.call-start = ((), (), s32[]{:S(2)}) async-start(), calls=%async_computation | async-start | bytes 393216 | tf_op jit(solution)/shard_map/psum | solution.py:142
  8.7 50.6 %collective-permute-start = (bf16[64,1,512]{2,0,1:T(8,128)(2,1)S(1)}, bf16[64,1,512]{2,0,1:T(8,128)(2,1)S(1)}, u32[]{:S(2)}, u32[]{:S(2)}) collective-permute-start(bf16[64,1,512]{2,0,1:T(8,128)(2,1)S(1)} %copy.64), channel_id=1, source_target_pairs={{0,4},{4,8},{8,12},{12,16},{16,20},{20,24},{24,28},{1,5},{5,9},{9,... | collective-permute-start | bytes 196616 | tf_op jit(solution)/shard_map/ppermute | solution.py:23
  11.1 19.8 %copy-start.4 = (bf16[64,64,512]{2,1,0:T(8,128)(2,1)S(1)}, bf16[64,64,512]{2,1,0:T(8,128)(2,1)}, u32[]{:S(2)}) copy-start(bf16[64,64,512]{2,1,0:T(8,128)(2,1)} %param.5) | copy-start | bytes 12582916
  11.1 60.8 %collective-permute-start.1 = (bf16[64,1,512]{2,0,1:T(8,128)(2,1)S(1)}, bf16[64,1,512]{2,0,1:T(8,128)(2,1)S(1)}, u32[]{:S(2)}, u32[]{:S(2)}) collective-permute-start(bf16[64,1,512]{2,0,1:T(8,128)(2,1)S(1)} %copy.65), channel_id=1, source_target_pairs={{4,0},{8,4},{12,8},{16,12},{20,16},{24,20},{28,24},{5,1},{9,5},{13... | collective-permute-start | bytes 196616 | tf_op jit(solution)/shard_map/ppermute | solution.py:25
  22.1 8.8 %copy-start.1 = (f32[32,64,8,8]{0,3,2,1:T(8,128)}, f32[32,64,8,8]{0,3,2,1:T(8,128)S(1)}, u32[]{:S(2)}) copy-start(f32[32,64,8,8]{0,3,2,1:T(8,128)S(1)} %broadcast_in_dim.28) | copy-start | bytes 1572868
  85.5 60.1 %collective-permute-start.2 = (bf16[64,66,1]{1,0,2:T(8,128)(2,1)S(1)}, bf16[64,66,1]{1,0,2:T(8,128)(2,1)S(1)}, u32[]{:S(2)}, u32[]{:S(2)}) collective-permute-start(bf16[64,66,1]{1,0,2:T(8,128)(2,1)S(1)} %get-tuple-element.10), channel_id=1, source_target_pairs={{0,1},{1,2},{2,3},{4,5},{5,6},{6,7},{8,9},{9,10},{10,11},{12,13},{... | collective-permute-start | bytes 25352 | tf_op jit(solution)/shard_map/ppermute | solution.py:23
  89.8 55.7 %collective-permute-start.3 = (bf16[64,66,1]{1,0,2:T(8,128)(2,1)S(1)}, bf16[64,66,1]{1,0,2:T(8,128)(2,1)S(1)}, u32[]{:S(2)}, u32[]{:S(2)}) collective-permute-start(bf16[64,66,1]{1,0,2:T(8,128)(2,1)S(1)} %get-tuple-element.11), channel_id=1, source_target_pairs={{1,0},{2,1},{3,2},{5,4},{6,5},{7,6},{9,8},{10,9},{11,10},{13,12},{... | collective-permute-start | bytes 25352 | tf_op jit(solution)/shard_map/ppermute | solution.py:25
  327.1 17.3 %copy-start.2 = (f32[32,64,8,8]{0,3,2,1:T(8,128)S(1)}, f32[32,64,8,8]{0,3,2,1:T(8,128)}, u32[]{:S(2)}) copy-start(f32[32,64,8,8]{0,3,2,1:T(8,128)} %copy-done.1) | copy-start | bytes 1572868
  344.4 10.2 %copy-start = (f32[4096,512]{1,0:T(8,128)S(1)}, f32[4096,512]{1,0:T(8,128)}, u32[]{:S(2)}) copy-start(f32[4096,512]{1,0:T(8,128)} %get-tuple-element.16) | copy-start | bytes 25165828
  344.4 18.0 %copy-start.3 = (f32[32,64,8,8]{0,3,2,1:T(8,128)S(1)}, f32[32,64,8,8]{0,3,2,1:T(8,128)}, u32[]{:S(2)}) copy-start(f32[32,64,8,8]{0,3,2,1:T(8,128)} %broadcast_in_dim.32) | copy-start | bytes 1572868
  362.3 60.3 %copy-start.6 = (f32[32,8,8]{0,2,1:T(8,128)S(1)}, f32[32,8,8]{0,2,1:T(8,128)}, u32[]{:S(2)}) copy-start(f32[32,8,8]{0,2,1:T(8,128)} %convolution_reduce_fusion) | copy-start | bytes 24580
  362.4 60.2 %copy-start.8 = (f32[32]{0:T(128)S(1)}, f32[32]{0:T(128)}, u32[]{:S(2)}) copy-start(f32[32]{0:T(128)} %broadcast_multiply_fusion) | copy-start | bytes 388
Sparse Core Ops, SparseCore 0:
  422.1 54.9 all-reduce.4
where the time goes:
time: 494 us; the launch traced here: 486 us
  other arithmetic  175 us (35%)
  local copies, waits for them, and re-layouts  106 us (21%)
  blocking collectives  75.1 us (15%)
  matrix products  70.4 us (14%)
  waiting for transfers between devices  33.8 us (7%)
  between operations  16 us (3%)
  starting transfers between devices  9.56 us (2%)
    add x1, other arithmetic, warp_image(): summed = summed + weight_x[along_x] * weight_y[along_y] * partial_z  119 us
    unnamed x24, local copies, waits for them, and re-layouts  52.3 us
    concatenate x2, other arithmetic, extended(): jnp.concatenate([lax.ppermute(tail, axis, [(i, (i + 1) % count) for i in...  48.1 us
    psum x1, blocking collectives, local(): energy = lax.psum(local_energy, ('gy', 'gz'))  40.8 us
    psum x1, waiting for transfers between devices, local(): lax.psum((grad_depth, first_depth, level_sum), 'gy')  33.7 us
    dot_general x2, matrix products, contract_rank(): lax.dot_general(left, right, (((0,), (0,)), ((), ())), precision=highest)  26.1 us
    dot_general x3, matrix products, contract_depth(): lax.dot_general(left, right, (((1,), (1,)), ((), ())), precision=highest)  23.2 us
    dot_general x3, matrix products, contract_cells(): return jnp.dot(left, right, precision=highest)  21.1 us
  transfers between devices with their start and end apart: 5, of which 1 were waited for; matrix products, arithmetic and copies ran while one was open for 20% of the time, Pallas kernels for 0%

commit v1 on v0

v1 whole, which is shorter than its diff:
```python
import functools

import jax
import jax.numpy as jnp
from jax import lax
from jax.experimental import pallas as pl
from jax.experimental.pallas import tpu as pltpu
from jax.sharding import PartitionSpec as P

RANK = 32
KNOT = 8
LANES = 128
TOP = 8

epsilon = 1e-06
damping = 0.01
highest = lax.Precision.HIGHEST
f32 = jnp.float32
bf16 = jnp.bfloat16


def dot(left, right, dims):
    return lax.dot_general(left, right, ((dims[0], dims[1]), ((), ())), precision=highest, preferred_element_type=f32)


def joined(ref):
    return jnp.concatenate([ref[tile] for tile in range(ref.shape[0])], axis=1)


def grid_params():
    return pltpu.CompilerParams(dimension_semantics=("arbitrary",), vmem_limit_bytes=60000000)


def plain_params():
    return pltpu.CompilerParams(vmem_limit_bytes=32000000)


def edges_kernel(cells_ref, first_ref, last_ref, low_ref, high_ref, cols):
    step = pl.program_id(0)
    planes, rows, width = cells_ref.shape
    lane = lax.broadcasted_iota(jnp.int32, (rows, LANES), 1)

    @pl.when(step == 0)
    def _():
        cols[...] = jnp.zeros_like(cols)

    first, last = cols[0], cols[1]
    for k in range(planes):
        x = step * planes + k
        left = cells_ref[k, :, 0:LANES].astype(f32)
        right = cells_ref[k, :, width - LANES : width].astype(f32)
        first = jnp.where(lane == x, pltpu.roll(left, x, 1), first)
        last = jnp.where(lane == x, pltpu.roll(right, x + 1, 1), last)
    cols[0] = first
    cols[1] = last
    low = [cells_ref[k, 0:16, :].astype(f32)[0:1] for k in range(planes)]
    high = [cells_ref[k, rows - 16 : rows, :].astype(f32)[15:16] for k in range(planes)]
    low_ref[...] = jnp.concatenate(low, axis=0)
    high_ref[...] = jnp.concatenate(high, axis=0)

    @pl.when(step == pl.num_programs(0) - 1)
    def _():
        first_ref[...] = first.astype(bf16)
        last_ref[...] = last.astype(bf16)


def edges(cells):
    depth, rows, width = cells.shape
    whole = lambda i: (0, 0)
    return pl.pallas_call(
        edges_kernel,
        grid=(depth // KNOT,),
        in_specs=[pl.BlockSpec((KNOT, rows, width), lambda i: (i, 0, 0))],
        out_specs=[
            pl.BlockSpec((rows, LANES), whole),
            pl.BlockSpec((rows, LANES), whole),
            pl.BlockSpec((KNOT, width), lambda i: (i, 0)),
            pl.BlockSpec((KNOT, width), lambda i: (i, 0)),
        ],
        out_shape=[
            jax.ShapeDtypeStruct((rows, LANES), bf16),
            jax.ShapeDtypeStruct((rows, LANES), bf16),
            jax.ShapeDtypeStruct((depth, width), f32),
            jax.ShapeDtypeStruct((depth, width), f32),
        ],
        scratch_shapes=[pltpu.VMEM((2, rows, LANES), f32)],
        compiler_params=grid_params(),
        name="edges",
    )(cells)


def rows_kernel(left_ref, right_ref, low_ref, high_ref, low_out, high_out):
    depth, width = low_ref.shape
    rows = left_ref.shape[0]
    lane = lax.broadcasted_iota(jnp.int32, (depth, LANES), 1)
    pad = jnp.zeros((LANES - rows, LANES), f32)
    left = jnp.transpose(jnp.concatenate([left_ref[...].astype(f32), pad], axis=0))[0:depth]
    right = jnp.transpose(jnp.concatenate([right_ref[...].astype(f32), pad], axis=0))[0:depth]
    for row, body, out in ((0, low_ref, low_out), (rows - 1, high_ref, high_out)):
        after = pltpu.roll(right, (LANES - row) % LANES, 1)
        before = pltpu.roll(left, LANES - 1 - row, 1)
        out[:, 0:width] = body[...].astype(bf16)
        out[:, width : width + LANES] = jnp.where(lane == 0, after, before).astype(bf16)


def packed_rows(left, right, low, high):
    depth, width = low.shape
    return pl.pallas_call(
        rows_kernel,
        out_shape=[jax.ShapeDtypeStruct((depth, width + LANES), bf16)] * 2,
        compiler_params=plain_params(),
        name="rows",
    )(left, right, low, high)


def shifted(part, axis, back):
    count = lax.axis_size(axis)
    if back:
        return lax.ppermute(part, axis, [(i + 1, i) for i in range(count - 1)])
    return lax.ppermute(part, axis, [(i, i + 1) for i in range(count - 1)])


def squares_kernel(image_ref, plane_ref, depth_ref, field_ref, diag_depth_ref, diag_plane_ref, sums):
    step = pl.program_id(0)
    planes, rows, width = image_ref.shape
    nodes = rows // KNOT
    tiles = width // LANES

    def one(t, carry):
        at = pl.multiple_of((t % tiles) * LANES, LANES)
        top = pl.multiple_of((t // tiles) * 16, 16)
        total = jnp.zeros((16, LANES), f32)
        for k in range(planes):
            values = image_ref[k, pl.ds(top, 16), pl.ds(at, LANES)].astype(f32)
            total = total + values * values
        for half in range(2):
            row = step * nodes + (t // tiles) * 2 + half
            sums[t % tiles, pl.ds(row, 1), :] = jnp.sum(total[8 * half : 8 * half + 8], axis=0, keepdims=True)
        return carry

    lax.fori_loop(0, (rows // 16) * tiles, one, 0)

    @pl.when(step == pl.num_programs(0) - 1)
    def _():
        for k in range(2):
            field = dot(plane_ref[k], depth_ref[k], ((1,), (0,)))
            for tile in range(tiles):
                field_ref[k, tile] = field[:, tile * LANES : (tile + 1) * LANES]
        squared = joined(sums)
        cells = jnp.full(squared.shape, float(KNOT * KNOT), f32)
        first, second = plane_ref[0], plane_ref[1]
        diag_depth_ref[0] = dot(first * first, squared, ((0,), (0,)))
        diag_depth_ref[1] = dot(second * second, cells, ((0,), (0,)))
        first, second = depth_ref[0], depth_ref[1]
        diag_plane_ref[0] = dot(squared, first * first, ((1,), (1,)))
        diag_plane_ref[1] = dot(cells, second * second, ((1,), (1,)))


def squares(image, plane, depth_factors):
    depth, rows, width = image.shape
    nodes = plane.shape[1]
    whole = lambda i: (0, 0, 0)
    return pl.pallas_call(
        squares_kernel,
        grid=(depth // KNOT,),
        in_specs=[
            pl.BlockSpec((KNOT, rows, width), lambda i: (i, 0, 0)),
            pl.BlockSpec(plane.shape, whole),
            pl.BlockSpec(depth_factors.shape, whole),
        ],
        out_specs=[
            pl.BlockSpec((2, width // LANES, nodes, LANES), lambda i: (0, 0, 0, 0)),
            pl.BlockSpec((2, RANK, width), whole),
            pl.BlockSpec((2, nodes, RANK), whole),
        ],
        out_shape=[
            jax.ShapeDtypeStruct((2, width // LANES, nodes, LANES), f32),
            jax.ShapeDtypeStruct((2, RANK, width), f32),
            jax.ShapeDtypeStruct((2, nodes, RANK), f32),
        ],
        scratch_shapes=[pltpu.VMEM((width // LANES, nodes, LANES), f32)],
        compiler_params=grid_params(),
        cost_estimate=pl.CostEstimate(flops=3 * image.size, bytes_accessed=2 * image.size, transcendentals=0),
        name="squares",
    )(image, plane, depth_factors)


def warp_kernel(
    cells_ref, image_ref, shift_ref, left_ref, right_ref, low_ref, high_ref, field_ref, plane_ref, depth_ref,
    diag_depth_ref, diag_plane_ref,
    residual_ref, depth_out, plane_out,
    window, columns, blocks, energy,
):
    step = pl.program_id(0)
    last = pl.num_programs(0) - 1
    planes, rows, width = cells_ref.shape
    nodes = rows // KNOT
    tiles = width // LANES
    depth = planes * last

    @pl.when(step == 0)
    def _():
        columns[0] = left_ref[...].astype(f32)
        columns[1] = right_ref[...].astype(f32)
        energy[...] = jnp.zeros_like(energy)
        nothing = jnp.zeros((rows + 2 * TOP, LANES), f32)
        for c in range(3):
            for tile in range(tiles):
                window[c, 0, tile] = nothing
                window[c, depth + 1, tile] = nothing

    @pl.when(step < last)
    def _():
        lane = lax.broadcasted_iota(jnp.int32, (rows, LANES), 1)

        def one(k, carry):
            x = step * planes + k
            middle = cells_ref[k].astype(f32)
            after = pltpu.roll(columns[1], (LANES - x) % LANES, 1)
            before = pltpu.roll(columns[0], LANES - 1 - x, 1)
            wide = jnp.concatenate([middle, jnp.where(lane == 0, after, before)], axis=1)
            moved = (pltpu.roll(wide, 1, 1), wide, pltpu.roll(wide, width + LANES - 1, 1))
            for c in range(3):
                for tile in range(tiles):
                    window[c, x + 1, tile, TOP : TOP + rows, :] = moved[c][:, tile * LANES : (tile + 1) * LANES]
            return carry

        lax.fori_loop(0, planes, one, 0)
        start = pl.multiple_of(step * planes, planes)
        for source, row in ((low_ref, TOP - 1), (high_ref, TOP + rows)):
            wide = source[...].astype(f32)
            moved = (pltpu.roll(wide, 1, 1), wide, pltpu.roll(wide, width + LANES - 1, 1))
            for c in range(3):
                for tile in range(tiles):
                    for k in range(planes):
                        window[c, start + k + 1, tile, row : row + 1, :] = moved[c][
                            k : k + 1, tile * LANES : (tile + 1) * LANES
                        ]

    @pl.when(step > 0)
    def _():
        base = (step - 1) * planes

        def one(t, total):
            tile = t % tiles
            pair = t // tiles
            at = pl.multiple_of(tile * LANES, LANES)
            top = pl.multiple_of(pair * 16, 16)

            def taps(x):
                return [[window[c, base + x, tile, pl.ds(TOP + top + b, 16), :] for c in range(3)] for b in (-1, 0, 1)]

            def node_rows(k):
                start = (step - 1) * nodes + pair * 2
                parts = [
                    jnp.broadcast_to(field_ref[k, tile, pl.ds(start + half, 1), :], (8, LANES))
                    for half in range(2)
                ]
                return jnp.concatenate(parts, axis=0)

            contrast, brightness = node_rows(0), node_rows(1)
            by_image = jnp.zeros((16, LANES), f32)
            plain = jnp.zeros((16, LANES), f32)
            before, here = taps(0), taps(1)
            for k in range(planes):
                after = taps(k + 2)
                place = (k, pl.ds(top, 16), pl.ds(at, LANES))
                sx, sy, sz = (shift_ref[(axis,) + place].astype(f32) for axis in range(3))
                image = image_ref[place].astype(f32)
                px, py, pz = sx > 0, sy > 0, sz > 0
                ax, ay, az = jnp.abs(sx), jnp.abs(sy), jnp.abs(sz)
                side = [[jnp.where(px, after[b][c], before[b][c]) for c in range(3)] for b in range(3)]

                def corners(values):
                    line = [jnp.where(py, values[2][c], values[0][c]) for c in range(3)]
                    return [[row[1], jnp.where(pz, row[2], row[0])] for row in (values[1], line)]

                near, far = corners(here), corners(side)
                flat = [[near[b][c] + ax * (far[b][c] - near[b][c]) for c in range(2)] for b in range(2)]
                line = [flat[0][c] + ay * (flat[1][c] - flat[0][c]) for c in range(2)]
                warped = line[0] + az * (line[1] - line[0])
                misfit = warped - contrast * image - brightness
                residual_ref[place] = misfit.astype(bf16)
                by_image = by_image + misfit * image
                plain = plain + misfit
                total = total + misfit * misfit
                before, here = here, after
            for k, value in ((0, by_image), (1, plain)):
                for half in range(2):
                    row = (step - 1) * nodes + pair * 2 + half
                    blocks[k, tile, pl.ds(row, 1), :] = jnp.sum(value[8 * half : 8 * half + 8], axis=0, keepdims=True)
            return total

        energy[...] = lax.fori_loop(0, (rows // 16) * tiles, one, energy[...])

    @pl.when(step == last)
    def _():
        parts = depth_out.shape[0]
        share = RANK // parts
        sums = [joined(blocks.at[k]) for k in range(2)]
        kinds = [dot(plane_ref[k], sums[k], ((0,), (0,))) for k in range(2)]
        kinds = kinds + [diag_depth_ref[0], diag_depth_ref[1]]
        for p in range(parts):
            for k in range(4):
                depth_out[p, k * share : (k + 1) * share, :] = kinds[k][p * share : (p + 1) * share]
        local = jnp.sum(energy[...])
        kinds = [dot(sums[k], depth_ref[k], ((1,), (1,))) for k in range(2)]
        kinds = kinds + [diag_plane_ref[0], diag_plane_ref[1]]
        for k in range(4):
            plane_out[:, k * RANK : (k + 1) * RANK] = kinds[k]
        cells = plane_out.shape[0]
        plane_out[cells // 2 :, 3 * RANK :] = jnp.full((cells // 2, RANK), local, f32)


def warp(cells, image, shift, left, right, low, high, field, plane, depth_factors, diag_depth, diag_plane, parts):
    depth, rows, width = cells.shape
    nodes = plane.shape[1]
    count = depth // KNOT
    behind = lambda i: (jnp.maximum(i - 1, 0), 0, 0)
    ahead = lambda i: (jnp.minimum(i, count - 1), 0, 0)
    flat = lambda i: (0, 0)
    whole = lambda i: (0, 0, 0)
    return pl.pallas_call(
        warp_kernel,
        grid=(count + 1,),
        in_specs=[
            pl.BlockSpec((KNOT, rows, width), ahead),
            pl.BlockSpec((KNOT, rows, width), behind),
            pl.BlockSpec((3, KNOT, rows, width), lambda i: (0, jnp.maximum(i - 1, 0), 0, 0)),
            pl.BlockSpec(left.shape, flat),
            pl.BlockSpec(right.shape, flat),
            pl.BlockSpec((KNOT, low.shape[1]), lambda i: (jnp.minimum(i, count - 1), 0)),
            pl.BlockSpec((KNOT, high.shape[1]), lambda i: (jnp.minimum(i, count - 1), 0)),
            pl.BlockSpec(field.shape, lambda i: (0, 0, 0, 0)),
            pl.BlockSpec(plane.shape, whole),
            pl.BlockSpec(depth_factors.shape, whole),
            pl.BlockSpec(diag_depth.shape, whole),
            pl.BlockSpec(diag_plane.shape, whole),
        ],
        out_specs=[
            pl.BlockSpec((KNOT, rows, width), behind),
            pl.BlockSpec((parts, 4 * RANK // parts, width), whole),
            pl.BlockSpec((nodes, 4 * RANK), flat),
        ],
        out_shape=[
            jax.ShapeDtypeStruct(cells.shape, bf16),
            jax.ShapeDtypeStruct((parts, 4 * RANK // parts, width), f32),
            jax.ShapeDtypeStruct((nodes, 4 * RANK), f32),
        ],
        scratch_shapes=[
            pltpu.VMEM((3, depth + 2, width // LANES, rows + 2 * TOP, LANES), f32),
            pltpu.VMEM((2, rows, LANES), f32),
            pltpu.VMEM((2, width // LANES, nodes, LANES), f32),
            pltpu.VMEM((16, LANES), f32),
        ],
        compiler_params=grid_params(),
        cost_estimate=pl.CostEstimate(flops=60 * cells.size, bytes_accessed=12 * cells.size, transcendentals=0),
        name="warp",
    )(cells, image, shift, left, right, low, high, field, plane, depth_factors, diag_depth, diag_plane)


def gather_kernel(depth_ref, plane_ref, depth_out, plane_out):
    total = jnp.sum(depth_ref[...], axis=0)
    planes = jnp.sum(plane_ref[...], axis=0)
    plane_out[...] = planes
    cells = planes.shape[0]
    share, width = total.shape[0] // 4, total.shape[1]
    row = lax.broadcasted_iota(jnp.int32, total.shape, 0)
    lane = lax.broadcasted_iota(jnp.int32, total.shape, 1)
    partial = planes[cells - 1, 4 * RANK - 1]
    total = jnp.where((row >= 3 * share) & (lane >= width // 2), partial, total)
    for p in range(depth_out.shape[0]):
        depth_out[p] = total


def step_kernel(full_z, node_count, depth_ref, plane_ref, depth_out, plane_out):
    parts, share, width = depth_ref.shape[0], depth_ref.shape[1] // 4, depth_ref.shape[2]
    energy = depth_ref[0, 3 * share, width - 1]
    for p in range(1, parts):
        energy = energy + depth_ref[p, 3 * share, width - 1]
    lam_depth = damping * energy / full_z
    lam_plane = damping * RANK * energy / node_count
    for p in range(parts):
        got = depth_ref[p]
        levels = got[3 * share :, 0 : width // 2]
        levels = jnp.concatenate([levels, levels], axis=1)
        rows = slice(p * share, (p + 1) * share)
        depth_out[0, rows, :] = got[0:share] / (got[2 * share : 3 * share] + lam_depth + epsilon)
        depth_out[1, rows, :] = got[share : 2 * share] / (levels + lam_depth + epsilon)
    planes = plane_ref[...]
    plane_out[0] = planes[:, 0:RANK] / (planes[:, 2 * RANK : 3 * RANK] + lam_plane + epsilon)
    plane_out[1] = planes[:, RANK : 2 * RANK] / (planes[0:1, 3 * RANK :] + lam_plane + epsilon)


def local(image, deformed, displacement, plane_factors, depth_factors):
    n_gy, n_gz = lax.axis_size("gy"), lax.axis_size("gz")
    nodes_x, nodes_y = plane_factors.shape[2:]
    plane = jnp.transpose(plane_factors, (0, 2, 3, 1)).reshape(2, nodes_x * nodes_y, RANK)
    first, last, low, high = edges(deformed)
    right = shifted(first, "gz", True)
    left = shifted(last, "gz", False)
    field, diag_depth, diag_plane = squares(image, plane, depth_factors)
    low, high = packed_rows(left, right, low, high)
    above = shifted(low, "gy", True)
    below = shifted(high, "gy", False)
    residual, depth_terms, plane_terms = warp(
        deformed, image, displacement, left, right, below, above, field, plane, depth_factors, diag_depth, diag_plane,
        n_gy,
    )
    depth_terms = lax.all_to_all(depth_terms, "gy", 0, 0)
    plane_terms = lax.all_to_all(jnp.broadcast_to(plane_terms[None], (n_gz,) + plane_terms.shape), "gz", 0, 0)
    depth_terms, plane_terms = pl.pallas_call(
        gather_kernel,
        out_shape=[
            jax.ShapeDtypeStruct(depth_terms.shape, f32),
            jax.ShapeDtypeStruct(plane_terms.shape[1:], f32),
        ],
        compiler_params=plain_params(),
        name="gather",
    )(depth_terms, plane_terms)
    depth_terms = lax.all_to_all(depth_terms, "gy", 0, 0)
    width = depth_factors.shape[2]
    step_depth, step_plane = pl.pallas_call(
        functools.partial(step_kernel, width * n_gz, nodes_x * nodes_y * n_gy),
        out_shape=[
            jax.ShapeDtypeStruct(depth_factors.shape, f32),
            jax.ShapeDtypeStruct(plane.shape, f32),
        ],
        compiler_params=plain_params(),
        name="steps",
    )(depth_terms, plane_terms)
    step_plane = jnp.transpose(step_plane.reshape(2, nodes_x, nodes_y, RANK), (0, 3, 1, 2))
    return residual, step_plane, step_depth


def solution(mesh):
    placed = (
        P(None, "gy", "gz"),
        P(None, "gy", "gz"),
        P(None, None, "gy", "gz"),
        P(None, None, None, "gy"),
        P(None, None, "gz"),
    )
    return jax.shard_map(
        local,
        mesh=mesh,
        in_specs=placed,
        out_specs=(P(None, "gy", "gz"), P(None, None, None, "gy"), P(None, None, "gz")),
        check_vma=False,
    )
```

time: 494 us -> 104 us (0.21); the launches traced: 486 us -> 103 us
  other arithmetic: 175 us -> 0 us
  local copies, waits for them, and re-layouts: 106 us -> 3.22 us
  matrix products: 70.4 us -> 0 us
  Pallas kernels: 0 us -> 53.2 us
  blocking collectives: 75.1 us -> 32.6 us
  waiting for transfers between devices: 33.8 us -> 4.55 us
  between operations: 16 us -> 0.72 us
    add x1 -> x0, other arithmetic: 119 us -> none  [warp_image(): summed = summed + weight_x[along_x] * weight_y[along_y] * partial_z]
    psum x3 -> x0, blocking collectives: 75.1 us -> none  [the longest x1 40.8 us: local(): energy = lax.psum(local_energy, ('gy', 'gz'))]
    dot_general x8 -> x0, matrix products: 70.4 us -> none  [the longest x2 26.1 us: contract_rank(): lax.dot_general(left, right, (((0,), (0,)), ((), ())), precision=highest)]
    pallas_call x0 -> x6, Pallas kernels: none -> 53.2 us  [the longest x1 38.1 us: warp(): pl.pallas_call(warp_kernel, grid=(count + 1,), in_specs=[pl.BlockSpec((KN...]
    unnamed x24 -> x12, local copies, waits for them, and re-layouts: 52.3 us -> 2.46 us
    concatenate x2 -> x0, other arithmetic: 48.1 us -> none  [extended(): jnp.concatenate([lax.ppermute(tail, axis, [(i, (i + 1) % count) for i in...]
    psum x1 -> x0, waiting for transfers between devices: 33.7 us -> none  [local(): lax.psum((grad_depth, first_depth, level_sum), 'gy')]
    all_to_all x0 -> x3, blocking collectives: none -> 32.6 us  [the longest x2 22.9 us: local(): depth_terms = lax.all_to_all(depth_terms, 'gy', 0, 0)]
  transfers between devices with their start and end apart: 5 -> 4, of which waited for: 1 -> 2; matrix products, arithmetic and copies ran while one was open for 20% -> 0% of each run, Pallas kernels for 0% -> 7%
where the time goes in v1:
time: 104 us; the launch traced here: 103 us
  Pallas kernels  53.2 us (51%)
  blocking collectives  32.6 us (31%)
  starting transfers between devices  8.81 us (8%)
  waiting for transfers between devices  4.55 us (4%)
  local copies, waits for them, and re-layouts  3.22 us (3%)
    pallas_call x1, Pallas kernels, warp(): pl.pallas_call(warp_kernel, grid=(count + 1,), in_specs=[pl.BlockSpec((KN...  38.1 us
    all_to_all x2, blocking collectives, local(): depth_terms = lax.all_to_all(depth_terms, 'gy', 0, 0)  22.9 us
    all_to_all x1, blocking collectives, local(): lax.all_to_all(jnp.broadcast_to(plane_terms[None], (n_gz,) + plane_terms....  9.69 us
    pallas_call x1, Pallas kernels, squares(): pl.pallas_call(squares_kernel, grid=(depth // KNOT,), in_specs=[pl.BlockS...  7.69 us
    ppermute x2, starting transfers between devices, shifted(): return lax.ppermute(part, axis, [(i, i + 1) for i in range(count - 1)])  6.22 us
    pallas_call x1, Pallas kernels, edges(): pl.pallas_call(edges_kernel, grid=(depth // KNOT,), in_specs=[pl.BlockSpe...  6.15 us
    ppermute x2, waiting for transfers between devices, shifted(): return lax.ppermute(part, axis, [(i + 1, i) for i in range(count - 1)])  4.21 us
    ppermute x2, starting transfers between devices, shifted(): return lax.ppermute(part, axis, [(i + 1, i) for i in range(count - 1)])  2.58 us
  transfers between devices with their start and end apart: 4, of which 2 were waited for; matrix products, arithmetic and copies ran while one was open for 0% of the time, Pallas kernels for 7%

profile of v1, /device:TPU:0, one launch (start us, length us, event | category | flops | bytes accessed | tf_op | source)
XLA Modules:
  0.0 103.0 jit_solution(17109982807706542034)
XLA Ops:
  0.6 6.2 %edges.1 = (bf16[64,128]{1,0:T(8,128)(2,1)}, bf16[64,128]{1,0:T(8,128)(2,1)}, f32[64,512]{1,0:T(8,128)}, f32[64,512]{1,0:T(8,128)}) custom-call(bf16[64,64,512]{2,1,0:T(8,128)(2,1)} %cells_ref.3), custom_call_target="tpu_custom_call" | custom-call | tf_op jit(solution)/shard_map/edges/pallas_call | solution.py:70
  6.8 4.9 %collective-permute-start = (bf16[64,128]{1,0:T(8,128)(2,1)}, bf16[64,128]{1,0:T(8,128)(2,1)S(1)}, u32[]{:S(2)}, u32[]{:S(2)}) collective-permute-start(bf16[64,128]{1,0:T(8,128)(2,1)} %get-tuple-element.19), channel_id=1, source_target_pairs={{0,1},{1,2},{2,3},{4,5},{5,6},{6,7},{8,9},{9,10},{10,11},{12,13},{... | collective-permute-start | bytes 49160 | tf_op jit(solution)/shard_map/ppermute | solution.py:120
  11.7 1.3 %collective-permute-start.1 = (bf16[64,128]{1,0:T(8,128)(2,1)}, bf16[64,128]{1,0:T(8,128)(2,1)S(1)}, u32[]{:S(2)}, u32[]{:S(2)}) collective-permute-start(bf16[64,128]{1,0:T(8,128)(2,1)} %get-tuple-element.20), channel_id=1, source_target_pairs={{1,0},{2,1},{3,2},{5,4},{6,5},{7,6},{9,8},{10,9},{11,10},{13,12},{... | collective-permute-start | bytes 49160 | tf_op jit(solution)/shard_map/ppermute | solution.py:119
  13.0 0.3 collective-permute-done.left_ref
  13.4 0.0 copy-start.2
  13.4 4.2 %collective-permute-done.1.right_ref = bf16[64,128]{1,0:T(8,128)(2,1)S(1)} collective-permute-done((bf16[64,128]{1,0:T(8,128)(2,1)}, bf16[64,128]{1,0:T(8,128)(2,1)S(1)}, u32[]{:S(2)}, u32[]{:S(2)}) %collective-permute-start.1) | collective-permute-done | bytes 16416 | tf_op jit(solution)/shard_map/ppermute | solution.py:119
  17.6 0.0 copy-start.3
  17.6 0.0 copy-start
  17.6 0.9 copy-done
  18.5 0.0 copy-start.1
  18.5 0.9 copy-done.1
  19.4 0.2 rows.1
  19.5 1.3 %collective-permute-start.2 = (bf16[64,640]{1,0:T(8,128)(2,1)S(1)}, bf16[64,640]{1,0:T(8,128)(2,1)S(1)}, u32[]{:S(2)}, u32[]{:S(2)}) collective-permute-start(bf16[64,640]{1,0:T(8,128)(2,1)S(1)} %get-tuple-element.23), channel_id=1, source_target_pairs={{0,4},{4,8},{8,12},{12,16},{16,20},{20,24},{24,28},{1,5},{5,9},{9,... | collective-permute-start | bytes 245768 | tf_op jit(solution)/shard_map/ppermute | solution.py:120
  20.9 1.3 %collective-permute-start.3 = (bf16[64,640]{1,0:T(8,128)(2,1)S(1)}, bf16[64,640]{1,0:T(8,128)(2,1)S(1)}, u32[]{:S(2)}, u32[]{:S(2)}) collective-permute-start(bf16[64,640]{1,0:T(8,128)(2,1)S(1)} %get-tuple-element.24), channel_id=1, source_target_pairs={{4,0},{8,4},{12,8},{16,12},{20,16},{24,20},{28,24},{5,1},{9,5},{13... | collective-permute-start | bytes 245768 | tf_op jit(solution)/shard_map/ppermute | solution.py:119
  22.2 7.7 %squares.1 = (f32[2,4,64,128]{3,2,1,0:T(8,128)}, f32[2,32,512]{2,1,0:T(8,128)}, f32[2,64,32]{2,1,0:T(8,128)}) custom-call(bf16[64,64,512]{2,1,0:T(8,128)(2,1)} %image_ref.3, f32[2,64,32]{2,1,0:T(8,128)} %bitcast.6, f32[2,32,512]{2,1,0:T(8,128)} %depth_ref.3), custom_call_target="tpu_custom_call" | custom-call | flops 6291456 | bytes 4194304 | tf_op jit(solution)/shard_map/squares/pallas_call | solution.py:163
  29.8 0.0 collective-permute-done.2.low_ref
  29.8 0.0 copy-start.4
  29.8 0.0 collective-permute-done.3.high_ref
  29.8 0.0 copy-start.5
  29.9 0.0 copy-done.2
  29.9 0.0 copy-done.3
  29.9 0.6 copy-done.4
  30.5 0.0 copy-done.5
  30.5 38.1 %warp.1 = (bf16[64,64,512]{2,1,0:T(8,128)(2,1)}, f32[8,16,512]{2,1,0:T(8,128)}, f32[64,128]{1,0:T(8,128)}) custom-call(bf16[64,64,512]{2,1,0:T(8,128)(2,1)} %cells_ref.3, bf16[64,64,512]{2,1,0:T(8,128)(2,1)} %image_ref.3, bf16[3,64,64,512]{3,2,1,0:T(8,128)(2,1)} %shift_ref.1, bf16[64,128]{1,0:T(8,128)(2,1)} %copy-done.2, bf16[64,128]{1,0:T(8,128)(2,1)} %copy-done.3, ...), custom_call_target="tpu_custom_call" | custom-call | flops 125829120 | bytes 25165824 | tf_op jit(solution)/shard_map/warp/pallas_call | solution.py:323
  68.7 0.8 broadcast_in_dim.2
  69.4 9.7 %all_to_all.15.plane_ref = f32[4,64,128]{2,1,0:T(8,128)S(1)} all-to-all(f32[4,64,128]{2,1,0:T(8,128)S(1)} %broadcast_in_dim.2), channel_id=1, replica_groups=mesh['gy'=8,'gz'=4] {'gz'}, dimensions={0} | all-to-all | bytes 262144 | tf_op jit(solution)/shard_map/all_to_all | solution.py:411
  79.1 13.5 %all_to_all.16.depth_ref = f32[8,16,512]{2,1,0:T(8,128)S(1)} all-to-all(f32[8,16,512]{2,1,0:T(8,128)} %get-tuple-element.29), channel_id=1, replica_groups=mesh['gy'=8,'gz'=4] {'gy'}, dimensions={0} | all-to-all | bytes 524288 | tf_op jit(solution)/shard_map/all_to_all | solution.py:410
  92.6 0.1 gather.1
  92.8 9.3 %all_to_all.17.depth_ref = f32[8,16,512]{2,1,0:T(8,128)S(1)} all-to-all(f32[8,16,512]{2,1,0:T(8,128)S(1)} %get-tuple-element.31), channel_id=1, replica_groups=mesh['gy'=8,'gz'=4] {'gy'}, dimensions={0} | all-to-all | bytes 524288 | tf_op jit(solution)/shard_map/all_to_all | solution.py:421
  102.1 0.9 steps.1
Async XLA Ops:
  6.8 6.6 %collective-permute-start = (bf16[64,128]{1,0:T(8,128)(2,1)}, bf16[64,128]{1,0:T(8,128)(2,1)S(1)}, u32[]{:S(2)}, u32[]{:S(2)}) collective-permute-start(bf16[64,128]{1,0:T(8,128)(2,1)} %get-tuple-element.19), channel_id=1, source_target_pairs={{0,1},{1,2},{2,3},{4,5},{5,6},{6,7},{8,9},{9,10},{10,11},{12,13},{... | collective-permute-start | bytes 49160 | tf_op jit(solution)/shard_map/ppermute | solution.py:120
  11.7 5.8 %collective-permute-start.1 = (bf16[64,128]{1,0:T(8,128)(2,1)}, bf16[64,128]{1,0:T(8,128)(2,1)S(1)}, u32[]{:S(2)}, u32[]{:S(2)}) collective-permute-start(bf16[64,128]{1,0:T(8,128)(2,1)} %get-tuple-element.20), channel_id=1, source_target_pairs={{1,0},{2,1},{3,2},{5,4},{6,5},{7,6},{9,8},{10,9},{11,10},{13,12},{... | collective-permute-start | bytes 49160 | tf_op jit(solution)/shard_map/ppermute | solution.py:119
  13.4 16.5 %copy-start.2 = (bf16[64,128]{1,0:T(8,128)(2,1)}, bf16[64,128]{1,0:T(8,128)(2,1)S(1)}, u32[]{:S(2)}) copy-start(bf16[64,128]{1,0:T(8,128)(2,1)S(1)} %collective-permute-done.left_ref) | copy-start | bytes 49156
  17.6 12.3 %copy-start.3 = (bf16[64,128]{1,0:T(8,128)(2,1)}, bf16[64,128]{1,0:T(8,128)(2,1)S(1)}, u32[]{:S(2)}) copy-start(bf16[64,128]{1,0:T(8,128)(2,1)S(1)} %collective-permute-done.1.right_ref) | copy-start | bytes 49156
  17.6 0.9 copy-start
  18.5 0.9 copy-start.1
  19.5 10.3 %collective-permute-start.2 = (bf16[64,640]{1,0:T(8,128)(2,1)S(1)}, bf16[64,640]{1,0:T(8,128)(2,1)S(1)}, u32[]{:S(2)}, u32[]{:S(2)}) collective-permute-start(bf16[64,640]{1,0:T(8,128)(2,1)S(1)} %get-tuple-element.23), channel_id=1, source_target_pairs={{0,4},{4,8},{8,12},{12,16},{16,20},{20,24},{24,28},{1,5},{5,9},{9,... | collective-permute-start | bytes 245768 | tf_op jit(solution)/shard_map/ppermute | solution.py:120
  20.9 9.0 %collective-permute-start.3 = (bf16[64,640]{1,0:T(8,128)(2,1)S(1)}, bf16[64,640]{1,0:T(8,128)(2,1)S(1)}, u32[]{:S(2)}, u32[]{:S(2)}) collective-permute-start(bf16[64,640]{1,0:T(8,128)(2,1)S(1)} %get-tuple-element.24), channel_id=1, source_target_pairs={{4,0},{8,4},{12,8},{16,12},{20,16},{24,20},{28,24},{5,1},{9,5},{13... | collective-permute-start | bytes 245768 | tf_op jit(solution)/shard_map/ppermute | solution.py:119
  29.8 0.6 copy-start.4
  29.8 0.7 copy-start.5

commit v2 on v1

--- a/solution.py
+++ b/solution.py
@@ -23,6 +23,15 @@
     return lax.dot_general(left, right, ((dims[0], dims[1]), ((), ())), precision=highest, preferred_element_type=f32)
 
 
+def split_dot(left, right, dim):
+    left_high, right_high = left.astype(bf16), right.astype(bf16)
+    left_low = (left - left_high.astype(f32)).astype(bf16)
+    right_low = (right - right_high.astype(f32)).astype(bf16)
+    left = jnp.concatenate([left_high, left_high, left_low], axis=dim)
+    right = jnp.concatenate([right_high, right_low, right_high], axis=dim)
+    return lax.dot_general(left, right, (((dim,), (dim,)), ((), ())), preferred_element_type=f32)
+
+
 def joined(ref):
     return jnp.concatenate([ref[tile] for tile in range(ref.shape[0])], axis=1)
 
@@ -35,58 +44,33 @@
     return pltpu.CompilerParams(vmem_limit_bytes=32000000)
 
 
-def edges_kernel(cells_ref, first_ref, last_ref, low_ref, high_ref, cols):
-    step = pl.program_id(0)
-    planes, rows, width = cells_ref.shape
+def columns_kernel(near_ref, far_ref, first_ref, last_ref):
+    depth, rows = near_ref.shape[0:2]
     lane = lax.broadcasted_iota(jnp.int32, (rows, LANES), 1)
-
-    @pl.when(step == 0)
-    def _():
-        cols[...] = jnp.zeros_like(cols)
-
-    first, last = cols[0], cols[1]
-    for k in range(planes):
-        x = step * planes + k
-        left = cells_ref[k, :, 0:LANES].astype(f32)
-        right = cells_ref[k, :, width - LANES : width].astype(f32)
-        first = jnp.where(lane == x, pltpu.roll(left, x, 1), first)
-        last = jnp.where(lane == x, pltpu.roll(right, x + 1, 1), last)
-    cols[0] = first
-    cols[1] = last
-    low = [cells_ref[k, 0:16, :].astype(f32)[0:1] for k in range(planes)]
-    high = [cells_ref[k, rows - 16 : rows, :].astype(f32)[15:16] for k in range(planes)]
-    low_ref[...] = jnp.concatenate(low, axis=0)
-    high_ref[...] = jnp.concatenate(high, axis=0)
-
-    @pl.when(step == pl.num_programs(0) - 1)
-    def _():
-        first_ref[...] = first.astype(bf16)
-        last_ref[...] = last.astype(bf16)
-
-
-def edges(cells):
+    first = jnp.zeros((rows, LANES), f32)
+    last = jnp.zeros((rows, LANES), f32)
+    for x in range(depth):
+        first = jnp.where(lane == x, pltpu.roll(near_ref[x].astype(f32), x, 1), first)
+        last = jnp.where(lane == x, pltpu.roll(far_ref[x].astype(f32), (x + 1) % LANES, 1), last)
+    first_ref[...] = first.astype(bf16)
+    last_ref[...] = last.astype(bf16)
+
+
+def end_columns(cells):
     depth, rows, width = cells.shape
-    whole = lambda i: (0, 0)
+    tiles = width // LANES
     return pl.pallas_call(
-        edges_kernel,
-        grid=(depth // KNOT,),
-        in_specs=[pl.BlockSpec((KNOT, rows, width), lambda i: (i, 0, 0))],
-        out_specs=[
-            pl.BlockSpec((rows, LANES), whole),
-            pl.BlockSpec((rows, LANES), whole),
-            pl.BlockSpec((KNOT, width), lambda i: (i, 0)),
-            pl.BlockSpec((KNOT, width), lambda i: (i, 0)),
-        ],
-        out_shape=[
-            jax.ShapeDtypeStruct((rows, LANES), bf16),
-            jax.ShapeDtypeStruct((rows, LANES), bf16),
-            jax.ShapeDtypeStruct((depth, width), f32),
-            jax.ShapeDtypeStruct((depth, width), f32),
-        ],
-        scratch_shapes=[pltpu.VMEM((2, rows, LANES), f32)],
+        columns_kernel,
+        grid=(1,),
+        in_specs=[
+            pl.BlockSpec((depth, rows, LANES), lambda i: (0, 0, 0)),
+            pl.BlockSpec((depth, rows, LANES), lambda i: (0, 0, tiles - 1)),
+        ],
+        out_specs=[pl.BlockSpec((rows, LANES), lambda i: (0, 0))] * 2,
+        out_shape=[jax.ShapeDtypeStruct((rows, LANES), bf16)] * 2,
         compiler_params=grid_params(),
-        name="edges",
-    )(cells)
+        name="columns",
+    )(cells, cells)
 
 
 def rows_kernel(left_ref, right_ref, low_ref, high_ref, low_out, high_out):
@@ -120,7 +104,7 @@
     return lax.ppermute(part, axis, [(i, i + 1) for i in range(count - 1)])
 
 
-def squares_kernel(image_ref, plane_ref, depth_ref, field_ref, diag_depth_ref, diag_plane_ref, sums):
+def squares_kernel(image_ref, top_ref, bottom_ref, sums, low_ref, high_ref):
     step = pl.program_id(0)
     planes, rows, width = image_ref.shape
     nodes = rows // KNOT
@@ -139,57 +123,72 @@
         return carry
 
     lax.fori_loop(0, (rows // 16) * tiles, one, 0)
-
-    @pl.when(step == pl.num_programs(0) - 1)
-    def _():
-        for k in range(2):
-            field = dot(plane_ref[k], depth_ref[k], ((1,), (0,)))
-            for tile in range(tiles):
-                field_ref[k, tile] = field[:, tile * LANES : (tile + 1) * LANES]
-        squared = joined(sums)
-        cells = jnp.full(squared.shape, float(KNOT * KNOT), f32)
-        first, second = plane_ref[0], plane_ref[1]
-        diag_depth_ref[0] = dot(first * first, squared, ((0,), (0,)))
-        diag_depth_ref[1] = dot(second * second, cells, ((0,), (0,)))
-        first, second = depth_ref[0], depth_ref[1]
-        diag_plane_ref[0] = dot(squared, first * first, ((1,), (1,)))
-        diag_plane_ref[1] = dot(cells, second * second, ((1,), (1,)))
-
-
-def squares(image, plane, depth_factors):
+    low_ref[...] = jnp.concatenate([top_ref[k].astype(f32)[0:1] for k in range(planes)], axis=0)
+    high_ref[...] = jnp.concatenate([bottom_ref[k].astype(f32)[15:16] for k in range(planes)], axis=0)
+
+
+def squares(image, cells, nodes):
     depth, rows, width = image.shape
-    nodes = plane.shape[1]
-    whole = lambda i: (0, 0, 0)
     return pl.pallas_call(
         squares_kernel,
         grid=(depth // KNOT,),
         in_specs=[
             pl.BlockSpec((KNOT, rows, width), lambda i: (i, 0, 0)),
-            pl.BlockSpec(plane.shape, whole),
-            pl.BlockSpec(depth_factors.shape, whole),
+            pl.BlockSpec((KNOT, 16, width), lambda i: (i, 0, 0)),
+            pl.BlockSpec((KNOT, 16, width), lambda i: (i, rows // 16 - 1, 0)),
         ],
         out_specs=[
-            pl.BlockSpec((2, width // LANES, nodes, LANES), lambda i: (0, 0, 0, 0)),
-            pl.BlockSpec((2, RANK, width), whole),
-            pl.BlockSpec((2, nodes, RANK), whole),
-        ],
+            pl.BlockSpec((width // LANES, nodes, LANES), lambda i: (0, 0, 0)),
+            pl.BlockSpec((KNOT, width), lambda i: (i, 0)),
+            pl.BlockSpec((KNOT, width), lambda i: (i, 0)),
+        ],
+        out_shape=[
+            jax.ShapeDtypeStruct((width // LANES, nodes, LANES), f32),
+            jax.ShapeDtypeStruct((depth, width), f32),
+            jax.ShapeDtypeStruct((depth, width), f32),
+        ],
+        compiler_params=grid_params(),
+        cost_estimate=pl.CostEstimate(flops=3 * image.size, bytes_accessed=2 * image.size, transcendentals=0),
+        name="squares",
+    )(image, cells, cells)
+
+
+def terms_kernel(sums, plane_ref, depth_ref, field_ref, diag_depth_ref, diag_plane_ref):
+    tiles = sums.shape[0]
+    for k in range(2):
+        field = dot(plane_ref[k], depth_ref[k], ((1,), (0,)))
+        for tile in range(tiles):
+            field_ref[k, tile] = field[:, tile * LANES : (tile + 1) * LANES]
+    squared = joined(sums)
+    cells = jnp.full(squared.shape, float(KNOT * KNOT), f32)
+    first, second = plane_ref[0], plane_ref[1]
+    diag_depth_ref[0] = dot(first * first, squared, ((0,), (0,)))
+    diag_depth_ref[1] = dot(second * second, cells, ((0,), (0,)))
+    first, second = depth_ref[0], depth_ref[1]
+    diag_plane_ref[0] = dot(squared, first * first, ((1,), (1,)))
+    diag_plane_ref[1] = dot(cells, second * second, ((1,), (1,)))
+
+
+def terms(sums, plane, depth_factors):
+    nodes, width = plane.shape[1], depth_factors.shape[2]
+    return pl.pallas_call(
+        terms_kernel,
         out_shape=[
             jax.ShapeDtypeStruct((2, width // LANES, nodes, LANES), f32),
             jax.ShapeDtypeStruct((2, RANK, width), f32),
             jax.ShapeDtypeStruct((2, nodes, RANK), f32),
         ],
-        scratch_shapes=[pltpu.VMEM((width // LANES, nodes, LANES), f32)],
-        compiler_params=grid_params(),
-        cost_estimate=pl.CostEstimate(flops=3 * image.size, bytes_accessed=2 * image.size, transcendentals=0),
-        name="squares",
-    )(image, plane, depth_factors)
+        compiler_params=plain_params(),
+        cost_estimate=pl.CostEstimate(flops=40 * nodes * RANK * width, bytes_accessed=1 << 20, transcendentals=0),
+        name="terms",
+    )(sums, plane, depth_factors)
 
 
 def warp_kernel(
     cells_ref, image_ref, shift_ref, left_ref, right_ref, low_ref, high_ref, field_ref, plane_ref, depth_ref,
     diag_depth_ref, diag_plane_ref,
     residual_ref, depth_out, plane_out,
-    window, columns, blocks, energy,
+    window, columns, blocks, energy, held,
 ):
     step = pl.program_id(0)
     last = pl.num_programs(0) - 1
@@ -246,49 +245,53 @@
             pair = t // tiles
             at = pl.multiple_of(tile * LANES, LANES)
             top = pl.multiple_of(pair * 16, 16)
-
-            def taps(x):
-                return [[window[c, base + x, tile, pl.ds(TOP + top + b, 16), :] for c in range(3)] for b in (-1, 0, 1)]
-
-            def node_rows(k):
-                start = (step - 1) * nodes + pair * 2
-                parts = [
-                    jnp.broadcast_to(field_ref[k, tile, pl.ds(start + half, 1), :], (8, LANES))
-                    for half in range(2)
-                ]
-                return jnp.concatenate(parts, axis=0)
-
-            contrast, brightness = node_rows(0), node_rows(1)
-            by_image = jnp.zeros((16, LANES), f32)
-            plain = jnp.zeros((16, LANES), f32)
-            before, here = taps(0), taps(1)
-            for k in range(planes):
-                after = taps(k + 2)
-                place = (k, pl.ds(top, 16), pl.ds(at, LANES))
-                sx, sy, sz = (shift_ref[(axis,) + place].astype(f32) for axis in range(3))
-                image = image_ref[place].astype(f32)
-                px, py, pz = sx > 0, sy > 0, sz > 0
-                ax, ay, az = jnp.abs(sx), jnp.abs(sy), jnp.abs(sz)
-                side = [[jnp.where(px, after[b][c], before[b][c]) for c in range(3)] for b in range(3)]
-
-                def corners(values):
-                    line = [jnp.where(py, values[2][c], values[0][c]) for c in range(3)]
-                    return [[row[1], jnp.where(pz, row[2], row[0])] for row in (values[1], line)]
-
-                near, far = corners(here), corners(side)
-                flat = [[near[b][c] + ax * (far[b][c] - near[b][c]) for c in range(2)] for b in range(2)]
-                line = [flat[0][c] + ay * (flat[1][c] - flat[0][c]) for c in range(2)]
-                warped = line[0] + az * (line[1] - line[0])
-                misfit = warped - contrast * image - brightness
-                residual_ref[place] = misfit.astype(bf16)
-                by_image = by_image + misfit * image
-                plain = plain + misfit
-                total = total + misfit * misfit
-                before, here = here, after
-            for k, value in ((0, by_image), (1, plain)):
-                for half in range(2):
-                    row = (step - 1) * nodes + pair * 2 + half
-                    blocks[k, tile, pl.ds(row, 1), :] = jnp.sum(value[8 * half : 8 * half + 8], axis=0, keepdims=True)
+            for half in range(2):
+                start = TOP + top + 8 * half
+                node = (step - 1) * nodes + pair * 2 + half
+                mine = slice(8 * half, 8 * half + 8)
+
+                def taps(x):
+                    return [[window[c, base + x, tile, pl.ds(start + b, 8), :] for c in range(3)] for b in (-1, 0, 1)]
+
+                contrast = jnp.broadcast_to(field_ref[0, tile, pl.ds(node, 1), :], (8, LANES))
+                brightness = jnp.broadcast_to(field_ref[1, tile, pl.ds(node, 1), :], (8, LANES))
+                by_image = jnp.zeros((8, LANES), f32)
+                plain = jnp.zeros((8, LANES), f32)
+                before, here = taps(0), taps(1)
+                for k in range(planes):
+                    after = taps(k + 2)
+                    place = (k, pl.ds(top, 16), pl.ds(at, LANES))
+                    sx, sy, sz = (shift_ref[(axis,) + place].astype(f32)[mine] for axis in range(3))
+                    image = image_ref[place].astype(f32)[mine]
+                    px, py, pz = sx > 0, sy > 0, sz > 0
+                    ax, ay, az = jnp.abs(sx), jnp.abs(sy), jnp.abs(sz)
+
+                    def sides(c):
+                        far = [jnp.where(px, after[b][c], before[b][c]) for b in range(3)]
+                        near = [here[b][c] for b in range(3)]
+                        return [(v[1], jnp.where(py, v[2], v[0])) for v in (near, far)]
+
+                    below, middle, above = sides(0), sides(1), sides(2)
+                    lines = []
+                    for b in range(2):
+                        ends = []
+                        for v in range(2):
+                            ends.append((middle[v][b], jnp.where(pz, above[v][b], below[v][b])))
+                        near, far = ends
+                        lines.append([near[c] + ax * (far[c] - near[c]) for c in range(2)])
+                    flat = [lines[0][c] + ay * (lines[1][c] - lines[0][c]) for c in range(2)]
+                    warped = flat[0] + az * (flat[1] - flat[0])
+                    misfit = warped - contrast * image - brightness
+                    if half == 0:
+                        held[k] = misfit
+                    else:
+                        residual_ref[place] = jnp.concatenate([held[k], misfit], axis=0).astype(bf16)
+                    by_image = by_image + misfit * image
+                    plain = plain + misfit
+                    total = total + misfit * misfit
+                    before, here = here, after
+                for k, value in ((0, by_image), (1, plain)):
+                    blocks[k, tile, pl.ds(node, 1), :] = jnp.sum(value, axis=0, keepdims=True)
             return total
 
         energy[...] = lax.fori_loop(0, (rows // 16) * tiles, one, energy[...])
@@ -298,13 +301,13 @@
         parts = depth_out.shape[0]
         share = RANK // parts
         sums = [joined(blocks.at[k]) for k in range(2)]
-        kinds = [dot(plane_ref[k], sums[k], ((0,), (0,))) for k in range(2)]
+        kinds = [split_dot(plane_ref[k], sums[k], 0) for k in range(2)]
         kinds = kinds + [diag_depth_ref[0], diag_depth_ref[1]]
         for p in range(parts):
             for k in range(4):
                 depth_out[p, k * share : (k + 1) * share, :] = kinds[k][p * share : (p + 1) * share]
         local = jnp.sum(energy[...])
-        kinds = [dot(sums[k], depth_ref[k], ((1,), (1,))) for k in range(2)]
+        kinds = [split_dot(sums[k], depth_ref[k], 1) for k in range(2)]
         kinds = kinds + [diag_plane_ref[0], diag_plane_ref[1]]
         for k in range(4):
             plane_out[:, k * RANK : (k + 1) * RANK] = kinds[k]
@@ -351,7 +354,8 @@
             pltpu.VMEM((3, depth + 2, width // LANES, rows + 2 * TOP, LANES), f32),
             pltpu.VMEM((2, rows, LANES), f32),
             pltpu.VMEM((2, width // LANES, nodes, LANES), f32),
-            pltpu.VMEM((16, LANES), f32),
+            pltpu.VMEM((8, LANES), f32),
+            pltpu.VMEM((KNOT, 8, LANES), f32),
         ],
         compiler_params=grid_params(),
         cost_estimate=pl.CostEstimate(flops=60 * cells.size, bytes_accessed=12 * cells.size, transcendentals=0),
@@ -359,9 +363,14 @@
     )(cells, image, shift, left, right, low, high, field, plane, depth_factors, diag_depth, diag_plane)
 
 
-def gather_kernel(depth_ref, plane_ref, depth_out, plane_out):
+def gather_kernel(depth_ref, *refs):
+    depth_out, plane_out = refs[-2:]
     total = jnp.sum(depth_ref[...], axis=0)
-    planes = jnp.sum(plane_ref[...], axis=0)
+    found = [ref[...] for ref in refs[:-2]]
+    while len(found) > 1:
+        half = len(found) // 2
+        found = [found[k] + found[k + half] for k in range(half)]
+    planes = found[0]
     plane_out[...] = planes
     cells = planes.shape[0]
     share, width = total.shape[0] // 4, total.shape[1]
@@ -396,28 +405,31 @@
     n_gy, n_gz = lax.axis_size("gy"), lax.axis_size("gz")
     nodes_x, nodes_y = plane_factors.shape[2:]
     plane = jnp.transpose(plane_factors, (0, 2, 3, 1)).reshape(2, nodes_x * nodes_y, RANK)
-    first, last, low, high = edges(deformed)
+    first, last = end_columns(deformed)
     right = shifted(first, "gz", True)
     left = shifted(last, "gz", False)
-    field, diag_depth, diag_plane = squares(image, plane, depth_factors)
+    sums, low, high = squares(image, deformed, nodes_x * nodes_y)
     low, high = packed_rows(left, right, low, high)
     above = shifted(low, "gy", True)
     below = shifted(high, "gy", False)
+    field, diag_depth, diag_plane = terms(sums, plane, depth_factors)
     residual, depth_terms, plane_terms = warp(
         deformed, image, displacement, left, right, below, above, field, plane, depth_factors, diag_depth, diag_plane,
         n_gy,
     )
+    others = [
+        lax.ppermute(plane_terms, "gz", [(i, (i + hop) % n_gz) for i in range(n_gz)]) for hop in range(1, n_gz)
+    ]
     depth_terms = lax.all_to_all(depth_terms, "gy", 0, 0)
-    plane_terms = lax.all_to_all(jnp.broadcast_to(plane_terms[None], (n_gz,) + plane_terms.shape), "gz", 0, 0)
     depth_terms, plane_terms = pl.pallas_call(
         gather_kernel,
         out_shape=[
             jax.ShapeDtypeStruct(depth_terms.shape, f32),
-            jax.ShapeDtypeStruct(plane_terms.shape[1:], f32),
+            jax.ShapeDtypeStruct(plane_terms.shape, f32),
         ],
         compiler_params=plain_params(),
         name="gather",
-    )(depth_terms, plane_terms)
+    )(depth_terms, plane_terms, *others)
     depth_terms = lax.all_to_all(depth_terms, "gy", 0, 0)
     width = depth_factors.shape[2]
     step_depth, step_plane = pl.pallas_call(

time: 104 us -> 93.2 us (0.90)
  blocking collectives: 32.6 us -> 10.9 us
  starting transfers between devices: 8.81 us -> 21.3 us
  Pallas kernels: 53.2 us -> 48.4 us
  local copies, waits for them, and re-layouts: 3.22 us -> 6.1 us
    all_to_all x2 -> x1, blocking collectives: 22.9 us -> 10.9 us  [local(): depth_terms = lax.all_to_all(depth_terms, 'gy', 0, 0)]
    all_to_all x1 -> x0, blocking collectives: 9.69 us -> none  [local(): lax.all_to_all(jnp.broadcast_to(plane_terms[None], (n_gz,) + plane_terms....]
    all_to_all x0 -> x1, starting transfers between devices: none -> 6.54 us  [local(): depth_terms = lax.all_to_all(depth_terms, 'gy', 0, 0)]
    ppermute x0 -> x3, starting transfers between devices: none -> 5.68 us  [local(): lax.ppermute(plane_terms, 'gz', [(i, (i + hop) % n_gz) for i in range(n_g...]
    ppermute x0 -> x3, waiting for transfers between devices: none -> 4.91 us  [local(): lax.ppermute(plane_terms, 'gz', [(i, (i + hop) % n_gz) for i in range(n_g...]
    ppermute x2, waiting for transfers between devices: 4.21 us -> 0.01 us  [shifted(): return lax.ppermute(part, axis, [(i + 1, i) for i in range(count - 1)])]
    unnamed x12 -> x26, local copies, waits for them, and re-layouts: 2.46 us -> 6.1 us
    pallas_call x1 -> x2, Pallas kernels: 6.15 us -> 3.4 us  [the longest x1 2.77 us: end_columns(): pl.pallas_call(columns_kernel, grid=(1,), in_specs=[pl.BlockSpec((depth,...]
  transfers between devices with their start and end apart: 4 -> 8, of which waited for: 2 -> 3; matrix products, arithmetic and copies ran while one was open for 0% -> 0% of each run, Pallas kernels for 7% -> 9%
where the time goes in v2:
time: 93.2 us; the launch traced here: 92.5 us
  Pallas kernels  48.4 us (52%)
  starting transfers between devices  21.3 us (23%)
  blocking collectives  10.9 us (12%)
  local copies, waits for them, and re-layouts  6.1 us (7%)
  waiting for transfers between devices  4.93 us (5%)
    pallas_call x1, Pallas kernels, warp(): pl.pallas_call(warp_kernel, grid=(count + 1,), in_specs=[pl.BlockSpec((KN...  36.2 us
    all_to_all x1, blocking collectives, local(): depth_terms = lax.all_to_all(depth_terms, 'gy', 0, 0)  10.9 us
    pallas_call x1, Pallas kernels, squares(): pl.pallas_call(squares_kernel, grid=(depth // KNOT,), in_specs=[pl.BlockS...  7.63 us
    all_to_all x1, starting transfers between devices, local(): depth_terms = lax.all_to_all(depth_terms, 'gy', 0, 0)  6.54 us
    ppermute x2, starting transfers between devices, shifted(): return lax.ppermute(part, axis, [(i, i + 1) for i in range(count - 1)])  6.38 us
    unnamed x26, local copies, waits for them, and re-layouts  6.1 us
    ppermute x3, starting transfers between devices, local(): lax.ppermute(plane_terms, 'gz', [(i, (i + hop) % n_gz) for i in range(n_g...  5.68 us
    ppermute x3, waiting for transfers between devices, local(): lax.ppermute(plane_terms, 'gz', [(i, (i + hop) % n_gz) for i in range(n_g...  4.91 us
  transfers between devices with their start and end apart: 8, of which 3 were waited for; matrix products, arithmetic and copies ran while one was open for 0% of the time, Pallas kernels for 9%

profile of v2, /device:TPU:0, one launch (start us, length us, event | category | flops | bytes accessed | tf_op | source)
XLA Modules:
  0.0 92.5 jit_solution(15693091116377957215)
XLA Ops:
  0.6 2.8 %columns.1 = (bf16[64,128]{1,0:T(8,128)(2,1)}, bf16[64,128]{1,0:T(8,128)(2,1)}) custom-call(bf16[64,64,512]{2,1,0:T(8,128)(2,1)} %cells_ref.1, bf16[64,64,512]{2,1,0:T(8,128)(2,1)} %cells_ref.1), custom_call_target="tpu_custom_call" | custom-call | tf_op jit(solution)/shard_map/columns/pallas_call | solution.py:62
  3.4 4.9 %collective-permute-start = (bf16[64,128]{1,0:T(8,128)(2,1)}, bf16[64,128]{1,0:T(8,128)(2,1)S(1)}, u32[]{:S(2)}, u32[]{:S(2)}) collective-permute-start(bf16[64,128]{1,0:T(8,128)(2,1)} %get-tuple-element.20), channel_id=1, source_target_pairs={{0,1},{1,2},{2,3},{4,5},{5,6},{6,7},{8,9},{9,10},{10,11},{12,13},{... | collective-permute-start | bytes 49160 | tf_op jit(solution)/shard_map/ppermute | solution.py:104
  8.3 0.0 copy-start
  8.3 0.0 copy-start.2
  8.3 1.4 %collective-permute-start.1 = (bf16[64,128]{1,0:T(8,128)(2,1)}, bf16[64,128]{1,0:T(8,128)(2,1)S(1)}, u32[]{:S(2)}, u32[]{:S(2)}) collective-permute-start(bf16[64,128]{1,0:T(8,128)(2,1)} %get-tuple-element.21), channel_id=1, source_target_pairs={{1,0},{2,1},{3,2},{5,4},{6,5},{7,6},{9,8},{10,9},{11,10},{13,12},{... | collective-permute-start | bytes 49160 | tf_op jit(solution)/shard_map/ppermute | solution.py:103
  9.8 7.6 %squares.1 = (f32[4,64,128]{2,1,0:T(8,128)}, f32[64,512]{1,0:T(8,128)}, f32[64,512]{1,0:T(8,128)}) custom-call(bf16[64,64,512]{2,1,0:T(8,128)(2,1)} %image_ref.3, bf16[64,64,512]{2,1,0:T(8,128)(2,1)} %cells_ref.1, bf16[64,64,512]{2,1,0:T(8,128)(2,1)} %cells_ref.1), custom_call_target="tpu_custom_call" | custom-call | flops 6291456 | bytes 4194304 | tf_op jit(solution)/shard_map/squares/pallas_call | solution.py:132
  17.4 0.0 collective-permute-done.left_ref
  17.4 0.0 copy-start.8
  17.4 0.0 collective-permute-done.1.right_ref
  17.4 0.0 copy-start.9
  17.5 0.0 copy-start.5
  17.5 0.9 copy-done.5
  18.4 0.0 copy-start.6
  18.4 0.9 copy-done.6
  19.3 0.2 rows.1
  19.4 1.5 %collective-permute-start.2 = (bf16[64,640]{1,0:T(8,128)(2,1)S(1)}, bf16[64,640]{1,0:T(8,128)(2,1)S(1)}, u32[]{:S(2)}, u32[]{:S(2)}) collective-permute-start(bf16[64,640]{1,0:T(8,128)(2,1)S(1)} %get-tuple-element.24), channel_id=1, source_target_pairs={{0,4},{4,8},{8,12},{12,16},{16,20},{20,24},{24,28},{1,5},{5,9},{9,... | collective-permute-start | bytes 245768 | tf_op jit(solution)/shard_map/ppermute | solution.py:104
  20.9 1.3 %collective-permute-start.3 = (bf16[64,640]{1,0:T(8,128)(2,1)S(1)}, bf16[64,640]{1,0:T(8,128)(2,1)S(1)}, u32[]{:S(2)}, u32[]{:S(2)}) collective-permute-start(bf16[64,640]{1,0:T(8,128)(2,1)S(1)} %get-tuple-element.25), channel_id=1, source_target_pairs={{4,0},{8,4},{12,8},{16,12},{20,16},{24,20},{28,24},{5,1},{9,5},{13... | collective-permute-start | bytes 245768 | tf_op jit(solution)/shard_map/ppermute | solution.py:103
  22.2 0.0 copy-done
  22.2 0.0 copy-done.2
  22.2 0.0 copy-start.4
  22.2 0.9 copy-done.4
  23.1 0.6 terms.1
  23.8 0.0 copy-start.1
  23.8 0.7 copy-done.1
  24.5 0.0 copy-start.3
  24.5 0.7 copy-done.3
  25.1 0.0 copy-start.7
  25.1 0.6 copy-done.7
  25.8 0.0 collective-permute-done.2.low_ref
  25.8 0.0 collective-permute-done.3.high_ref
  25.8 0.0 copy-start.12
  25.8 0.0 copy-done.8
  25.8 0.0 copy-done.9
  25.8 0.6 copy-done.11
  26.4 0.0 copy-done.12
  26.4 36.2 %warp.1 = (bf16[64,64,512]{2,1,0:T(8,128)(2,1)}, f32[8,16,512]{2,1,0:T(8,128)}, f32[64,128]{1,0:T(8,128)}) custom-call(bf16[64,64,512]{2,1,0:T(8,128)(2,1)} %cells_ref.1, bf16[64,64,512]{2,1,0:T(8,128)(2,1)} %image_ref.3, bf16[3,64,64,512]{3,2,1,0:T(8,128)(2,1)} %shift_ref.1, bf16[64,128]{1,0:T(8,128)(2,1)} %copy-done.8, bf16[64,128]{1,0:T(8,128)(2,1)} %copy-done.9, ...), custom_call_target="tpu_custom_call" | custom-call | flops 125829120 | bytes 25165824 | tf_op jit(solution)/shard_map/warp/pallas_call | solution.py:326
  62.7 6.5 %all-to-all-start = ((f32[8,16,512]{2,1,0:T(8,128)}), f32[8,16,512]{2,1,0:T(8,128)S(1)}, u32[]{:S(2)}, u32[]{:S(2)}) async-start(f32[8,16,512]{2,1,0:T(8,128)} %get-tuple-element.31), calls=%async_computation | async-start | bytes 524288 | tf_op jit(solution)/shard_map/all_to_all | solution.py:423
  69.2 4.7 %collective-permute-start.6 = (f32[64,128]{1,0:T(8,128)}, f32[64,128]{1,0:T(8,128)S(1)}, u32[]{:S(2)}, u32[]{:S(2)}) collective-permute-start(f32[64,128]{1,0:T(8,128)} %get-tuple-element.32.refs_0_), channel_id=1, source_target_pairs={{0,3},{1,0},{2,1},{3,2},{4,7},{5,4},{6,5},{7,6},{8,11},{9,8},{10,9... | collective-permute-start | bytes 98312 | tf_op jit(solution)/shard_map/ppermute | solution.py:421
  73.9 0.0 collective-permute-start.5
  73.9 1.0 %collective-permute-start.4 = (f32[64,128]{1,0:T(8,128)}, f32[64,128]{1,0:T(8,128)S(1)}, u32[]{:S(2)}, u32[]{:S(2)}) collective-permute-start(f32[64,128]{1,0:T(8,128)} %get-tuple-element.32.refs_0_), channel_id=1, source_target_pairs={{0,1},{1,2},{2,3},{3,0},{4,5},{5,6},{6,7},{7,4},{8,9},{9,10},{10,1... | collective-permute-start | bytes 98312 | tf_op jit(solution)/shard_map/ppermute | solution.py:421
  74.9 1.0 %collective-permute-done.6.refs_3_ = f32[64,128]{1,0:T(8,128)S(1)} collective-permute-done((f32[64,128]{1,0:T(8,128)}, f32[64,128]{1,0:T(8,128)S(1)}, u32[]{:S(2)}, u32[]{:S(2)}) %collective-permute-start.6) | collective-permute-done | bytes 32800 | tf_op jit(solution)/shard_map/ppermute | solution.py:421
  75.9 3.4 %collective-permute-done.5.refs_2_ = f32[64,128]{1,0:T(8,128)S(1)} collective-permute-done((f32[64,128]{1,0:T(8,128)}, f32[64,128]{1,0:T(8,128)S(1)}, u32[]{:S(2)}, u32[]{:S(2)}) %collective-permute-start.5) | collective-permute-done | bytes 32800 | tf_op jit(solution)/shard_map/ppermute | solution.py:421
  79.2 0.6 collective-permute-done.4.refs_1_
  79.8 0.0 all-to-all-done.depth_ref
  79.8 0.8 copy-done.10
  80.6 0.1 gather.1
  80.7 10.9 %all_to_all.10.depth_ref = f32[8,16,512]{2,1,0:T(8,128)S(1)} all-to-all(f32[8,16,512]{2,1,0:T(8,128)S(1)} %get-tuple-element.33), channel_id=1, replica_groups=mesh['gy'=8,'gz'=4] {'gy'}, dimensions={0} | all-to-all | bytes 524288 | tf_op jit(solution)/shard_map/all_to_all | solution.py:433
  91.6 0.9 steps.1
  (2 shorter events, 0.0 us)
Async XLA Ops:
  3.4 14.0 %collective-permute-start = (bf16[64,128]{1,0:T(8,128)(2,1)}, bf16[64,128]{1,0:T(8,128)(2,1)S(1)}, u32[]{:S(2)}, u32[]{:S(2)}) collective-permute-start(bf16[64,128]{1,0:T(8,128)(2,1)} %get-tuple-element.20), channel_id=1, source_target_pairs={{0,1},{1,2},{2,3},{4,5},{5,6},{6,7},{8,9},{9,10},{10,11},{12,13},{... | collective-permute-start | bytes 49160 | tf_op jit(solution)/shard_map/ppermute | solution.py:104
  8.3 13.9 %copy-start = (f32[2,32,512]{2,1,0:T(8,128)S(1)}, f32[2,32,512]{2,1,0:T(8,128)}, u32[]{:S(2)}) copy-start(f32[2,32,512]{2,1,0:T(8,128)} %depth_ref.3) | copy-start | bytes 393220
  8.3 13.9 %copy-start.2 = (f32[2,32,8,8]{1,3,2,0:T(8,128)S(1)}, f32[2,32,8,8]{1,3,2,0:T(8,128)}, u32[]{:S(2)}) copy-start(f32[2,32,8,8]{1,3,2,0:T(8,128)} %param.8) | copy-start | bytes 49156
  8.3 9.1 %collective-permute-start.1 = (bf16[64,128]{1,0:T(8,128)(2,1)}, bf16[64,128]{1,0:T(8,128)(2,1)S(1)}, u32[]{:S(2)}, u32[]{:S(2)}) collective-permute-start(bf16[64,128]{1,0:T(8,128)(2,1)} %get-tuple-element.21), channel_id=1, source_target_pairs={{1,0},{2,1},{3,2},{5,4},{6,5},{7,6},{9,8},{10,9},{11,10},{13,12},{... | collective-permute-start | bytes 49160 | tf_op jit(solution)/shard_map/ppermute | solution.py:103
  17.4 8.4 %copy-start.8 = (bf16[64,128]{1,0:T(8,128)(2,1)}, bf16[64,128]{1,0:T(8,128)(2,1)S(1)}, u32[]{:S(2)}) copy-start(bf16[64,128]{1,0:T(8,128)(2,1)S(1)} %collective-permute-done.left_ref) | copy-start | bytes 49156
  17.4 8.4 %copy-start.9 = (bf16[64,128]{1,0:T(8,128)(2,1)}, bf16[64,128]{1,0:T(8,128)(2,1)S(1)}, u32[]{:S(2)}) copy-start(bf16[64,128]{1,0:T(8,128)(2,1)S(1)} %collective-permute-done.1.right_ref) | copy-start | bytes 49156
  17.5 0.9 copy-start.5
  18.4 0.9 copy-start.6
  19.4 6.3 %collective-permute-start.2 = (bf16[64,640]{1,0:T(8,128)(2,1)S(1)}, bf16[64,640]{1,0:T(8,128)(2,1)S(1)}, u32[]{:S(2)}, u32[]{:S(2)}) collective-permute-start(bf16[64,640]{1,0:T(8,128)(2,1)S(1)} %get-tuple-element.24), channel_id=1, source_target_pairs={{0,4},{4,8},{8,12},{12,16},{16,20},{20,24},{24,28},{1,5},{5,9},{9,... | collective-permute-start | bytes 245768 | tf_op jit(solution)/shard_map/ppermute | solution.py:104
  20.9 4.9 %collective-permute-start.3 = (bf16[64,640]{1,0:T(8,128)(2,1)S(1)}, bf16[64,640]{1,0:T(8,128)(2,1)S(1)}, u32[]{:S(2)}, u32[]{:S(2)}) collective-permute-start(bf16[64,640]{1,0:T(8,128)(2,1)S(1)} %get-tuple-element.25), channel_id=1, source_target_pairs={{4,0},{8,4},{12,8},{16,12},{20,16},{24,20},{28,24},{5,1},{9,5},{13... | collective-permute-start | bytes 245768 | tf_op jit(solution)/shard_map/ppermute | solution.py:103
  22.2 0.9 copy-start.4
  23.8 0.7 copy-start.1
  24.5 0.7 copy-start.3
  25.1 0.6 copy-start.7
  25.8 0.6 copy-start.11
  25.8 0.7 copy-start.12
  62.7 17.1 %all-to-all-start = ((f32[8,16,512]{2,1,0:T(8,128)}), f32[8,16,512]{2,1,0:T(8,128)S(1)}, u32[]{:S(2)}, u32[]{:S(2)}) async-start(f32[8,16,512]{2,1,0:T(8,128)} %get-tuple-element.31), calls=%async_computation | async-start | bytes 524288 | tf_op jit(solution)/shard_map/all_to_all | solution.py:423
  69.2 6.7 %collective-permute-start.6 = (f32[64,128]{1,0:T(8,128)}, f32[64,128]{1,0:T(8,128)S(1)}, u32[]{:S(2)}, u32[]{:S(2)}) collective-permute-start(f32[64,128]{1,0:T(8,128)} %get-tuple-element.32.refs_0_), channel_id=1, source_target_pairs={{0,3},{1,0},{2,1},{3,2},{4,7},{5,4},{6,5},{7,6},{8,11},{9,8},{10,9... | collective-permute-start | bytes 98312 | tf_op jit(solution)/shard_map/ppermute | solution.py:421
  73.9 5.4 %collective-permute-start.5 = (f32[64,128]{1,0:T(8,128)}, f32[64,128]{1,0:T(8,128)S(1)}, u32[]{:S(2)}, u32[]{:S(2)}) collective-permute-start(f32[64,128]{1,0:T(8,128)} %get-tuple-element.32.refs_0_), channel_id=1, source_target_pairs={{0,2},{1,3},{2,0},{3,1},{4,6},{5,7},{6,4},{7,5},{8,10},{9,11},{10,... | collective-permute-start | bytes 98312 | tf_op jit(solution)/shard_map/ppermute | solution.py:421
  73.9 5.9 %collective-permute-start.4 = (f32[64,128]{1,0:T(8,128)}, f32[64,128]{1,0:T(8,128)S(1)}, u32[]{:S(2)}, u32[]{:S(2)}) collective-permute-start(f32[64,128]{1,0:T(8,128)} %get-tuple-element.32.refs_0_), channel_id=1, source_target_pairs={{0,1},{1,2},{2,3},{3,0},{4,5},{5,6},{6,7},{7,4},{8,9},{9,10},{10,1... | collective-permute-start | bytes 98312 | tf_op jit(solution)/shard_map/ppermute | solution.py:421
  79.8 0.8 copy-start.10

commit v3 on v2

--- a/solution.py
+++ b/solution.py
@@ -33,11 +33,12 @@
 
 
 def joined(ref):
-    return jnp.concatenate([ref[tile] for tile in range(ref.shape[0])], axis=1)
+    tiles, rows = ref.shape[0:2]
+    return jnp.concatenate([jnp.sum(ref[t].reshape(rows // 8, 8, LANES), axis=1) for t in range(tiles)], axis=1)
 
 
 def grid_params():
-    return pltpu.CompilerParams(dimension_semantics=("arbitrary",), vmem_limit_bytes=60000000)
+    return pltpu.CompilerParams(dimension_semantics=("arbitrary",), vmem_limit_bytes=40000000)
 
 
 def plain_params():
@@ -107,27 +108,24 @@
 def squares_kernel(image_ref, top_ref, bottom_ref, sums, low_ref, high_ref):
     step = pl.program_id(0)
     planes, rows, width = image_ref.shape
-    nodes = rows // KNOT
     tiles = width // LANES
 
-    def one(t, carry):
-        at = pl.multiple_of((t % tiles) * LANES, LANES)
-        top = pl.multiple_of((t // tiles) * 16, 16)
-        total = jnp.zeros((16, LANES), f32)
-        for k in range(planes):
-            values = image_ref[k, pl.ds(top, 16), pl.ds(at, LANES)].astype(f32)
-            total = total + values * values
-        for half in range(2):
-            row = step * nodes + (t // tiles) * 2 + half
-            sums[t % tiles, pl.ds(row, 1), :] = jnp.sum(total[8 * half : 8 * half + 8], axis=0, keepdims=True)
+    def one(tile, carry):
+        at = pl.multiple_of(tile * LANES, LANES)
+        for pair in range(rows // 16):
+            total = jnp.zeros((16, LANES), f32)
+            for k in range(planes):
+                values = image_ref[k, 16 * pair : 16 * pair + 16, pl.ds(at, LANES)].astype(f32)
+                total = total + values * values
+            sums[tile, pl.ds(step * rows + 16 * pair, 16), :] = total
         return carry
 
-    lax.fori_loop(0, (rows // 16) * tiles, one, 0)
+    lax.fori_loop(0, tiles, one, 0)
     low_ref[...] = jnp.concatenate([top_ref[k].astype(f32)[0:1] for k in range(planes)], axis=0)
     high_ref[...] = jnp.concatenate([bottom_ref[k].astype(f32)[15:16] for k in range(planes)], axis=0)
 
 
-def squares(image, cells, nodes):
+def squares(image, cells):
     depth, rows, width = image.shape
     return pl.pallas_call(
         squares_kernel,
@@ -138,12 +136,12 @@
             pl.BlockSpec((KNOT, 16, width), lambda i: (i, rows // 16 - 1, 0)),
         ],
         out_specs=[
-            pl.BlockSpec((width // LANES, nodes, LANES), lambda i: (0, 0, 0)),
+            pl.BlockSpec((width // LANES, depth * rows // KNOT, LANES), lambda i: (0, 0, 0)),
             pl.BlockSpec((KNOT, width), lambda i: (i, 0)),
             pl.BlockSpec((KNOT, width), lambda i: (i, 0)),
         ],
         out_shape=[
-            jax.ShapeDtypeStruct((width // LANES, nodes, LANES), f32),
+            jax.ShapeDtypeStruct((width // LANES, depth * rows // KNOT, LANES), f32),
             jax.ShapeDtypeStruct((depth, width), f32),
             jax.ShapeDtypeStruct((depth, width), f32),
         ],
@@ -153,49 +151,26 @@
     )(image, cells, cells)
 
 
-def terms_kernel(sums, plane_ref, depth_ref, field_ref, diag_depth_ref, diag_plane_ref):
-    tiles = sums.shape[0]
-    for k in range(2):
-        field = dot(plane_ref[k], depth_ref[k], ((1,), (0,)))
-        for tile in range(tiles):
-            field_ref[k, tile] = field[:, tile * LANES : (tile + 1) * LANES]
-    squared = joined(sums)
-    cells = jnp.full(squared.shape, float(KNOT * KNOT), f32)
-    first, second = plane_ref[0], plane_ref[1]
-    diag_depth_ref[0] = dot(first * first, squared, ((0,), (0,)))
-    diag_depth_ref[1] = dot(second * second, cells, ((0,), (0,)))
-    first, second = depth_ref[0], depth_ref[1]
-    diag_plane_ref[0] = dot(squared, first * first, ((1,), (1,)))
-    diag_plane_ref[1] = dot(cells, second * second, ((1,), (1,)))
-
-
-def terms(sums, plane, depth_factors):
-    nodes, width = plane.shape[1], depth_factors.shape[2]
-    return pl.pallas_call(
-        terms_kernel,
-        out_shape=[
-            jax.ShapeDtypeStruct((2, width // LANES, nodes, LANES), f32),
-            jax.ShapeDtypeStruct((2, RANK, width), f32),
-            jax.ShapeDtypeStruct((2, nodes, RANK), f32),
-        ],
-        compiler_params=plain_params(),
-        cost_estimate=pl.CostEstimate(flops=40 * nodes * RANK * width, bytes_accessed=1 << 20, transcendentals=0),
-        name="terms",
-    )(sums, plane, depth_factors)
-
-
 def warp_kernel(
-    cells_ref, image_ref, shift_ref, left_ref, right_ref, low_ref, high_ref, field_ref, plane_ref, depth_ref,
-    diag_depth_ref, diag_plane_ref,
+    cells_ref, image_ref, shift_ref, left_ref, right_ref, low_ref, high_ref, squares_ref, plane_ref, depth_ref,
     residual_ref, depth_out, plane_out,
-    window, columns, blocks, energy, held,
+    window, columns, field, blocks, energy, held,
 ):
     step = pl.program_id(0)
     last = pl.num_programs(0) - 1
     planes, rows, width = cells_ref.shape
     nodes = rows // KNOT
     tiles = width // LANES
-    depth = planes * last
+    slots = window.shape[1]
+
+    def store_row(plane, moved, k, row):
+        for c in range(3):
+            for tile in range(tiles):
+                window[c, plane, tile, row : row + 1, :] = moved[c][k : k + 1, tile * LANES : (tile + 1) * LANES]
+
+    def differences(wide):
+        ahead = pltpu.roll(wide, wide.shape[1] - 1, 1) - wide
+        return ahead, wide, pltpu.roll(ahead, 1, 1)
 
     @pl.when(step == 0)
     def _():
@@ -205,40 +180,45 @@
         nothing = jnp.zeros((rows + 2 * TOP, LANES), f32)
         for c in range(3):
             for tile in range(tiles):
-                window[c, 0, tile] = nothing
-                window[c, depth + 1, tile] = nothing
+                window[c, slots - 1, tile] = nothing
+        for k in range(2):
+            values = dot(plane_ref[k], depth_ref[k], ((1,), (0,)))
+            for tile in range(tiles):
+                field[k, tile] = values[:, tile * LANES : (tile + 1) * LANES]
 
     @pl.when(step < last)
     def _():
         lane = lax.broadcasted_iota(jnp.int32, (rows, LANES), 1)
+        slot = (step % 3) * planes
 
         def one(k, carry):
             x = step * planes + k
             middle = cells_ref[k].astype(f32)
             after = pltpu.roll(columns[1], (LANES - x) % LANES, 1)
             before = pltpu.roll(columns[0], LANES - 1 - x, 1)
-            wide = jnp.concatenate([middle, jnp.where(lane == 0, after, before)], axis=1)
-            moved = (pltpu.roll(wide, 1, 1), wide, pltpu.roll(wide, width + LANES - 1, 1))
+            moved = differences(jnp.concatenate([middle, jnp.where(lane == 0, after, before)], axis=1))
             for c in range(3):
                 for tile in range(tiles):
-                    window[c, x + 1, tile, TOP : TOP + rows, :] = moved[c][:, tile * LANES : (tile + 1) * LANES]
+                    window[c, slot + k, tile, TOP : TOP + rows, :] = moved[c][:, tile * LANES : (tile + 1) * LANES]
             return carry
 
         lax.fori_loop(0, planes, one, 0)
-        start = pl.multiple_of(step * planes, planes)
         for source, row in ((low_ref, TOP - 1), (high_ref, TOP + rows)):
-            wide = source[...].astype(f32)
-            moved = (pltpu.roll(wide, 1, 1), wide, pltpu.roll(wide, width + LANES - 1, 1))
-            for c in range(3):
-                for tile in range(tiles):
-                    for k in range(planes):
-                        window[c, start + k + 1, tile, row : row + 1, :] = moved[c][
-                            k : k + 1, tile * LANES : (tile + 1) * LANES
-                        ]
+            moved = differences(source[...].astype(f32))
+            for k in range(planes):
+                store_row(slot + k, moved, k, row)
+
+    @pl.when(step == last)
+    def _():
+        nothing = jnp.zeros((rows + 2 * TOP, LANES), f32)
+        for c in range(3):
+            for tile in range(tiles):
+                window[c, (step % 3) * planes, tile] = nothing
 
     @pl.when(step > 0)
     def _():
-        base = (step - 1) * planes
+        base = ((step + 2) % 3) * planes
+        places = [(base + slots - 1) % slots] + [base + k for k in range(planes)] + [(base + planes) % slots]
 
         def one(t, total):
             tile = t % tiles
@@ -251,47 +231,49 @@
                 mine = slice(8 * half, 8 * half + 8)
 
                 def taps(x):
-                    return [[window[c, base + x, tile, pl.ds(start + b, 8), :] for c in range(3)] for b in (-1, 0, 1)]
-
-                contrast = jnp.broadcast_to(field_ref[0, tile, pl.ds(node, 1), :], (8, LANES))
-                brightness = jnp.broadcast_to(field_ref[1, tile, pl.ds(node, 1), :], (8, LANES))
+                    return [
+                        [window[c, places[x], tile, pl.ds(start + b, 8), :] for c in range(3)] for b in (-1, 0, 1)
+                    ]
+
+                contrast = jnp.broadcast_to(field[0, tile, pl.ds(node, 1), :], (8, LANES))
+                brightness = jnp.broadcast_to(field[1, tile, pl.ds(node, 1), :], (8, LANES))
                 by_image = jnp.zeros((8, LANES), f32)
                 plain = jnp.zeros((8, LANES), f32)
                 before, here = taps(0), taps(1)
+                results = []
                 for k in range(planes):
                     after = taps(k + 2)
                     place = (k, pl.ds(top, 16), pl.ds(at, LANES))
                     sx, sy, sz = (shift_ref[(axis,) + place].astype(f32)[mine] for axis in range(3))
                     image = image_ref[place].astype(f32)[mine]
                     px, py, pz = sx > 0, sy > 0, sz > 0
-                    ax, ay, az = jnp.abs(sx), jnp.abs(sy), jnp.abs(sz)
+                    ax, ay = jnp.abs(sx), jnp.abs(sy)
 
                     def sides(c):
                         far = [jnp.where(px, after[b][c], before[b][c]) for b in range(3)]
                         near = [here[b][c] for b in range(3)]
                         return [(v[1], jnp.where(py, v[2], v[0])) for v in (near, far)]
 
-                    below, middle, above = sides(0), sides(1), sides(2)
+                    ahead, middle, behind = sides(0), sides(1), sides(2)
                     lines = []
                     for b in range(2):
-                        ends = []
-                        for v in range(2):
-                            ends.append((middle[v][b], jnp.where(pz, above[v][b], below[v][b])))
-                        near, far = ends
-                        lines.append([near[c] + ax * (far[c] - near[c]) for c in range(2)])
-                    flat = [lines[0][c] + ay * (lines[1][c] - lines[0][c]) for c in range(2)]
-                    warped = flat[0] + az * (flat[1] - flat[0])
+                        near, far = (middle[v][b] + sz * jnp.where(pz, ahead[v][b], behind[v][b]) for v in range(2))
+                        lines.append(near + ax * (far - near))
+                    warped = lines[0] + ay * (lines[1] - lines[0])
                     misfit = warped - contrast * image - brightness
-                    if half == 0:
-                        held[k] = misfit
-                    else:
-                        residual_ref[place] = jnp.concatenate([held[k], misfit], axis=0).astype(bf16)
+                    results.append(misfit)
                     by_image = by_image + misfit * image
                     plain = plain + misfit
                     total = total + misfit * misfit
                     before, here = here, after
+                for k in range(planes):
+                    if half == 0:
+                        held[k] = results[k]
+                    else:
+                        place = (k, pl.ds(top, 16), pl.ds(at, LANES))
+                        residual_ref[place] = jnp.concatenate([held[k], results[k]], axis=0).astype(bf16)
                 for k, value in ((0, by_image), (1, plain)):
-                    blocks[k, tile, pl.ds(node, 1), :] = jnp.sum(value, axis=0, keepdims=True)
+                    blocks[k, tile, pl.ds(pl.multiple_of(node * 8, 8), 8), :] = value
             return total
 
         energy[...] = lax.fori_loop(0, (rows // 16) * tiles, one, energy[...])
@@ -302,22 +284,27 @@
         share = RANK // parts
         sums = [joined(blocks.at[k]) for k in range(2)]
         kinds = [split_dot(plane_ref[k], sums[k], 0) for k in range(2)]
-        kinds = kinds + [diag_depth_ref[0], diag_depth_ref[1]]
+        squared = joined(squares_ref)
+        cells = jnp.full(squared.shape, float(KNOT * KNOT), f32)
+        second = plane_ref[1]
+        kinds = kinds + [split_dot(plane_ref[0] * plane_ref[0], squared, 0), split_dot(second * second, cells, 0)]
         for p in range(parts):
             for k in range(4):
                 depth_out[p, k * share : (k + 1) * share, :] = kinds[k][p * share : (p + 1) * share]
         local = jnp.sum(energy[...])
         kinds = [split_dot(sums[k], depth_ref[k], 1) for k in range(2)]
-        kinds = kinds + [diag_plane_ref[0], diag_plane_ref[1]]
+        second = depth_ref[1]
+        kinds = kinds + [split_dot(squared, depth_ref[0] * depth_ref[0], 1), split_dot(cells, second * second, 1)]
         for k in range(4):
             plane_out[:, k * RANK : (k + 1) * RANK] = kinds[k]
-        cells = plane_out.shape[0]
-        plane_out[cells // 2 :, 3 * RANK :] = jnp.full((cells // 2, RANK), local, f32)
-
-
-def warp(cells, image, shift, left, right, low, high, field, plane, depth_factors, diag_depth, diag_plane, parts):
+        count = plane_out.shape[0]
+        plane_out[count // 2 :, 3 * RANK :] = jnp.full((count // 2, RANK), local, f32)
+
+
+def warp(cells, image, shift, left, right, low, high, squared, plane, depth_factors, parts):
     depth, rows, width = cells.shape
     nodes = plane.shape[1]
+    tiles = width // LANES
     count = depth // KNOT
     behind = lambda i: (jnp.maximum(i - 1, 0), 0, 0)
     ahead = lambda i: (jnp.minimum(i, count - 1), 0, 0)
@@ -334,11 +321,9 @@
             pl.BlockSpec(right.shape, flat),
             pl.BlockSpec((KNOT, low.shape[1]), lambda i: (jnp.minimum(i, count - 1), 0)),
             pl.BlockSpec((KNOT, high.shape[1]), lambda i: (jnp.minimum(i, count - 1), 0)),
-            pl.BlockSpec(field.shape, lambda i: (0, 0, 0, 0)),
+            pl.BlockSpec(squared.shape, whole),
             pl.BlockSpec(plane.shape, whole),
             pl.BlockSpec(depth_factors.shape, whole),
-            pl.BlockSpec(diag_depth.shape, whole),
-            pl.BlockSpec(diag_plane.shape, whole),
         ],
         out_specs=[
             pl.BlockSpec((KNOT, rows, width), behind),
@@ -351,16 +336,17 @@
             jax.ShapeDtypeStruct((nodes, 4 * RANK), f32),
         ],
         scratch_shapes=[
-            pltpu.VMEM((3, depth + 2, width // LANES, rows + 2 * TOP, LANES), f32),
+            pltpu.VMEM((3, 3 * KNOT, tiles, rows + 2 * TOP, LANES), f32),
             pltpu.VMEM((2, rows, LANES), f32),
-            pltpu.VMEM((2, width // LANES, nodes, LANES), f32),
+            pltpu.VMEM((2, tiles, nodes, LANES), f32),
+            pltpu.VMEM((2, tiles, 8 * nodes, LANES), f32),
             pltpu.VMEM((8, LANES), f32),
             pltpu.VMEM((KNOT, 8, LANES), f32),
         ],
         compiler_params=grid_params(),
         cost_estimate=pl.CostEstimate(flops=60 * cells.size, bytes_accessed=12 * cells.size, transcendentals=0),
         name="warp",
-    )(cells, image, shift, left, right, low, high, field, plane, depth_factors, diag_depth, diag_plane)
+    )(cells, image, shift, left, right, low, high, squared, plane, depth_factors)
 
 
 def gather_kernel(depth_ref, *refs):
@@ -408,14 +394,12 @@
     first, last = end_columns(deformed)
     right = shifted(first, "gz", True)
     left = shifted(last, "gz", False)
-    sums, low, high = squares(image, deformed, nodes_x * nodes_y)
+    sums, low, high = squares(image, deformed)
     low, high = packed_rows(left, right, low, high)
     above = shifted(low, "gy", True)
     below = shifted(high, "gy", False)
-    field, diag_depth, diag_plane = terms(sums, plane, depth_factors)
     residual, depth_terms, plane_terms = warp(
-        deformed, image, displacement, left, right, below, above, field, plane, depth_factors, diag_depth, diag_plane,
-        n_gy,
+        deformed, image, displacement, left, right, below, above, sums, plane, depth_factors, n_gy
     )
     others = [
         lax.ppermute(plane_terms, "gz", [(i, (i + hop) % n_gz) for i in range(n_gz)]) for hop in range(1, n_gz)

time: 93.2 us -> 89.4 us (0.959)
  waiting for transfers between devices: 4.93 us -> 10.5 us
  local copies, waits for them, and re-layouts: 6.1 us -> 2.2 us
  Pallas kernels: 48.4 us -> 44.6 us
  starting transfers between devices: 21.3 us -> 20 us
    ppermute x2, waiting for transfers between devices: 0.01 us -> 6.33 us  [shifted(): return lax.ppermute(part, axis, [(i + 1, i) for i in range(count - 1)])]
    pallas_call x1, Pallas kernels: 7.63 us -> 1.55 us  [squares(): pl.pallas_call(squares_kernel, grid=(depth // KNOT,), in_specs=[pl.BlockS...]
    pallas_call x1, Pallas kernels: 36.2 us -> 41.2 us  [warp(): pl.pallas_call(warp_kernel, grid=(count + 1,), in_specs=[pl.BlockSpec((KN...]
    unnamed x26 -> x8, local copies, waits for them, and re-layouts: 6.1 us -> 2.2 us
    pallas_call x1, Pallas kernels: 2.77 us -> 0.72 us  [end_columns(): pl.pallas_call(columns_kernel, grid=(1,), in_specs=[pl.BlockSpec((depth,...]
    ppermute x3, starting transfers between devices: 5.68 us -> 4.62 us  [local(): lax.ppermute(plane_terms, 'gz', [(i, (i + hop) % n_gz) for i in range(n_g...]
  transfers between devices with their start and end apart: 8 -> 8, of which waited for: 3 -> 4; matrix products, arithmetic and copies ran while one was open for 0% -> 0% of each run, Pallas kernels for 9% -> 2%
where the time goes in v3:
time: 89.4 us; the launch traced here: 89 us
  Pallas kernels  44.6 us (50%)
  starting transfers between devices  20 us (22%)
  blocking collectives  10.9 us (12%)
  waiting for transfers between devices  10.5 us (12%)
  local copies, waits for them, and re-layouts  2.2 us (2%)
    pallas_call x1, Pallas kernels, warp(): pl.pallas_call(warp_kernel, grid=(count + 1,), in_specs=[pl.BlockSpec((KN...  41.2 us
    all_to_all x1, blocking collectives, local(): depth_terms = lax.all_to_all(depth_terms, 'gy', 0, 0)  10.9 us
    ppermute x2, starting transfers between devices, shifted(): return lax.ppermute(part, axis, [(i, i + 1) for i in range(count - 1)])  6.35 us
    all_to_all x1, starting transfers between devices, local(): depth_terms = lax.all_to_all(depth_terms, 'gy', 0, 0)  6.35 us
    ppermute x2, waiting for transfers between devices, shifted(): return lax.ppermute(part, axis, [(i + 1, i) for i in range(count - 1)])  6.33 us
    ppermute x3, starting transfers between devices, local(): lax.ppermute(plane_terms, 'gz', [(i, (i + hop) % n_gz) for i in range(n_g...  4.62 us
    ppermute x3, waiting for transfers between devices, local(): lax.ppermute(plane_terms, 'gz', [(i, (i + hop) % n_gz) for i in range(n_g...  4.13 us
    ppermute x2, starting transfers between devices, shifted(): return lax.ppermute(part, axis, [(i + 1, i) for i in range(count - 1)])  2.72 us
  transfers between devices with their start and end apart: 8, of which 4 were waited for; matrix products, arithmetic and copies ran while one was open for 0% of the time, Pallas kernels for 2%

profile of v3, /device:TPU:0, one launch (start us, length us, event | category | flops | bytes accessed | tf_op | source)
XLA Modules:
  0.0 89.0 jit_solution(569945220993086965)
XLA Ops:
  0.6 0.0 copy-start
  0.6 2.2 %copy-done = bf16[64,64,512]{2,1,0:T(8,128)(2,1)S(1)} copy-done((bf16[64,64,512]{2,1,0:T(8,128)(2,1)S(1)}, bf16[64,64,512]{2,1,0:T(8,128)(2,1)}, u32[]{:S(2)}) %copy-start) | copy-done | bytes 4194328
  2.8 0.0 copy-start.1
  2.8 0.7 columns.1
  3.5 5.1 %collective-permute-start = (bf16[64,128]{1,0:T(8,128)(2,1)S(1)}, bf16[64,128]{1,0:T(8,128)(2,1)S(1)}, u32[]{:S(2)}, u32[]{:S(2)}) collective-permute-start(bf16[64,128]{1,0:T(8,128)(2,1)S(1)} %get-tuple-element.17), channel_id=1, source_target_pairs={{0,1},{1,2},{2,3},{4,5},{5,6},{6,7},{8,9},{9,10},{10,11},{12,13},{... | collective-permute-start | bytes 49160 | tf_op jit(solution)/shard_map/ppermute | solution.py:105
  8.6 0.0 copy-start.2
  8.6 0.0 copy-start.3
  8.6 1.4 %collective-permute-start.1 = (bf16[64,128]{1,0:T(8,128)(2,1)S(1)}, bf16[64,128]{1,0:T(8,128)(2,1)S(1)}, u32[]{:S(2)}, u32[]{:S(2)}) collective-permute-start(bf16[64,128]{1,0:T(8,128)(2,1)S(1)} %get-tuple-element.18), channel_id=1, source_target_pairs={{1,0},{2,1},{3,2},{5,4},{6,5},{7,6},{9,8},{10,9},{11,10},{13,12},{... | collective-permute-start | bytes 49160 | tf_op jit(solution)/shard_map/ppermute | solution.py:104
  10.1 0.0 copy-done.1
  10.1 1.6 %squares.1 = (f32[4,512,128]{2,1,0:T(8,128)S(1)}, f32[64,512]{1,0:T(8,128)S(1)}, f32[64,512]{1,0:T(8,128)S(1)}) custom-call(bf16[64,64,512]{2,1,0:T(8,128)(2,1)S(1)} %copy-done.1, bf16[64,64,512]{2,1,0:T(8,128)(2,1)S(1)} %copy-done, bf16[64,64,512]{2,1,0:T(8,128)(2,1)S(1)} %copy-done), custom_call_target="tpu_custom_call" | custom-call | flops 6291456 | bytes 4194304 | tf_op jit(solution)/shard_map/squares/pallas_call | solution.py:130
  11.6 0.0 collective-permute-done.left_ref
  11.6 2.8 %collective-permute-done.1.right_ref = bf16[64,128]{1,0:T(8,128)(2,1)S(1)} collective-permute-done((bf16[64,128]{1,0:T(8,128)(2,1)S(1)}, bf16[64,128]{1,0:T(8,128)(2,1)S(1)}, u32[]{:S(2)}, u32[]{:S(2)}) %collective-permute-start.1) | collective-permute-done | bytes 16416 | tf_op jit(solution)/shard_map/ppermute | solution.py:104
  14.4 0.2 rows.1
  14.6 1.3 %collective-permute-start.2 = (bf16[64,640]{1,0:T(8,128)(2,1)S(1)}, bf16[64,640]{1,0:T(8,128)(2,1)S(1)}, u32[]{:S(2)}, u32[]{:S(2)}) collective-permute-start(bf16[64,640]{1,0:T(8,128)(2,1)S(1)} %get-tuple-element.21), channel_id=1, source_target_pairs={{0,4},{4,8},{8,12},{12,16},{16,20},{20,24},{24,28},{1,5},{5,9},{9,... | collective-permute-start | bytes 245768 | tf_op jit(solution)/shard_map/ppermute | solution.py:105
  15.9 1.3 %collective-permute-start.3 = (bf16[64,640]{1,0:T(8,128)(2,1)S(1)}, bf16[64,640]{1,0:T(8,128)(2,1)S(1)}, u32[]{:S(2)}, u32[]{:S(2)}) collective-permute-start(bf16[64,640]{1,0:T(8,128)(2,1)S(1)} %get-tuple-element.22), channel_id=1, source_target_pairs={{4,0},{8,4},{12,8},{16,12},{20,16},{24,20},{28,24},{5,1},{9,5},{13... | collective-permute-start | bytes 245768 | tf_op jit(solution)/shard_map/ppermute | solution.py:104
  17.2 0.0 collective-permute-done.2.low_ref
  17.2 3.6 %collective-permute-done.3.high_ref = bf16[64,640]{1,0:T(8,128)(2,1)S(1)} collective-permute-done((bf16[64,640]{1,0:T(8,128)(2,1)S(1)}, bf16[64,640]{1,0:T(8,128)(2,1)S(1)}, u32[]{:S(2)}, u32[]{:S(2)}) %collective-permute-start.3) | collective-permute-done | bytes 81952 | tf_op jit(solution)/shard_map/ppermute | solution.py:104
  20.8 0.0 copy-done.2
  20.8 0.0 copy-done.3
  20.8 41.2 %warp.1 = (bf16[64,64,512]{2,1,0:T(8,128)(2,1)}, f32[8,16,512]{2,1,0:T(8,128)}, f32[64,128]{1,0:T(8,128)S(1)}) custom-call(bf16[64,64,512]{2,1,0:T(8,128)(2,1)S(1)} %copy-done, bf16[64,64,512]{2,1,0:T(8,128)(2,1)S(1)} %copy-done.1, bf16[3,64,64,512]{3,2,1,0:T(8,128)(2,1)} %shift_ref.1, bf16[64,128]{1,0:T(8,128)(2,1)S(1)} %collective-permute-done.left_ref, ...), custom_call_target="tpu_custom_call" | custom-call | flops 125829120 | bytes 25165824 | tf_op jit(solution)/shard_map/warp/pallas_call | solution.py:313
  61.9 6.4 %all-to-all-start = ((f32[8,16,512]{2,1,0:T(8,128)}), f32[8,16,512]{2,1,0:T(8,128)S(1)}, u32[]{:S(2)}, u32[]{:S(2)}) async-start(f32[8,16,512]{2,1,0:T(8,128)} %get-tuple-element.25), calls=%async_computation | async-start | bytes 524288 | tf_op jit(solution)/shard_map/all_to_all | solution.py:407
  68.3 1.9 %collective-permute-start.6 = (f32[64,128]{1,0:T(8,128)S(1)}, f32[64,128]{1,0:T(8,128)S(1)}, u32[]{:S(2)}, u32[]{:S(2)}) collective-permute-start(f32[64,128]{1,0:T(8,128)S(1)} %get-tuple-element.26.refs_0_), channel_id=1, source_target_pairs={{0,3},{1,0},{2,1},{3,2},{4,7},{5,4},{6,5},{7,6},{8,11},{9,8},{10,9... | collective-permute-start | bytes 98312 | tf_op jit(solution)/shard_map/ppermute | solution.py:405
  70.2 1.1 %collective-permute-start.5 = (f32[64,128]{1,0:T(8,128)S(1)}, f32[64,128]{1,0:T(8,128)S(1)}, u32[]{:S(2)}, u32[]{:S(2)}) collective-permute-start(f32[64,128]{1,0:T(8,128)S(1)} %get-tuple-element.26.refs_0_), channel_id=1, source_target_pairs={{0,2},{1,3},{2,0},{3,1},{4,6},{5,7},{6,4},{7,5},{8,10},{9,11},{10,... | collective-permute-start | bytes 98312 | tf_op jit(solution)/shard_map/ppermute | solution.py:405
  71.3 1.6 %collective-permute-start.4 = (f32[64,128]{1,0:T(8,128)S(1)}, f32[64,128]{1,0:T(8,128)S(1)}, u32[]{:S(2)}, u32[]{:S(2)}) collective-permute-start(f32[64,128]{1,0:T(8,128)S(1)} %get-tuple-element.26.refs_0_), channel_id=1, source_target_pairs={{0,1},{1,2},{2,3},{3,0},{4,5},{5,6},{6,7},{7,4},{8,9},{9,10},{10,1... | collective-permute-start | bytes 98312 | tf_op jit(solution)/shard_map/ppermute | solution.py:405
  72.9 0.0 collective-permute-done.6.refs_3_
  72.9 2.3 %collective-permute-done.5.refs_2_ = f32[64,128]{1,0:T(8,128)S(1)} collective-permute-done((f32[64,128]{1,0:T(8,128)S(1)}, f32[64,128]{1,0:T(8,128)S(1)}, u32[]{:S(2)}, u32[]{:S(2)}) %collective-permute-start.5) | collective-permute-done | bytes 32800 | tf_op jit(solution)/shard_map/ppermute | solution.py:405
  75.2 1.8 %collective-permute-done.4.refs_1_ = f32[64,128]{1,0:T(8,128)S(1)} collective-permute-done((f32[64,128]{1,0:T(8,128)S(1)}, f32[64,128]{1,0:T(8,128)S(1)}, u32[]{:S(2)}, u32[]{:S(2)}) %collective-permute-start.4) | collective-permute-done | bytes 32800 | tf_op jit(solution)/shard_map/ppermute | solution.py:405
  77.0 0.0 all-to-all-done.depth_ref
  77.1 0.1 gather.1
  77.2 10.9 %all_to_all.10.depth_ref = f32[8,16,512]{2,1,0:T(8,128)S(1)} all-to-all(f32[8,16,512]{2,1,0:T(8,128)S(1)} %get-tuple-element.27), channel_id=1, replica_groups=mesh['gy'=8,'gz'=4] {'gy'}, dimensions={0} | all-to-all | bytes 524288 | tf_op jit(solution)/shard_map/all_to_all | solution.py:417
  88.1 0.9 %steps.1 = (f32[2,32,512]{2,1,0:T(8,128)}, f32[2,64,32]{2,1,0:T(8,128)}) custom-call(f32[8,16,512]{2,1,0:T(8,128)S(1)} %all_to_all.10.depth_ref, f32[64,128]{1,0:T(8,128)S(1)} %get-tuple-element.28.plane_ref), custom_call_target="tpu_custom_call" | custom-call | tf_op jit(solution)/shard_map/steps/pallas_call | solution.py:419
Async XLA Ops:
  0.6 2.2 %copy-start = (bf16[64,64,512]{2,1,0:T(8,128)(2,1)S(1)}, bf16[64,64,512]{2,1,0:T(8,128)(2,1)}, u32[]{:S(2)}) copy-start(bf16[64,64,512]{2,1,0:T(8,128)(2,1)} %cells_ref.1) | copy-start | bytes 12582916
  2.8 7.2 %copy-start.1 = (bf16[64,64,512]{2,1,0:T(8,128)(2,1)S(1)}, bf16[64,64,512]{2,1,0:T(8,128)(2,1)}, u32[]{:S(2)}) copy-start(bf16[64,64,512]{2,1,0:T(8,128)(2,1)} %image_ref.3) | copy-start | bytes 12582916
  3.5 8.1 %collective-permute-start = (bf16[64,128]{1,0:T(8,128)(2,1)S(1)}, bf16[64,128]{1,0:T(8,128)(2,1)S(1)}, u32[]{:S(2)}, u32[]{:S(2)}) collective-permute-start(bf16[64,128]{1,0:T(8,128)(2,1)S(1)} %get-tuple-element.17), channel_id=1, source_target_pairs={{0,1},{1,2},{2,3},{4,5},{5,6},{6,7},{8,9},{9,10},{10,11},{12,13},{... | collective-permute-start | bytes 49160 | tf_op jit(solution)/shard_map/ppermute | solution.py:105
  8.6 12.2 %copy-start.2 = (f32[2,32,512]{2,1,0:T(8,128)S(1)}, f32[2,32,512]{2,1,0:T(8,128)}, u32[]{:S(2)}) copy-start(f32[2,32,512]{2,1,0:T(8,128)} %depth_ref.1) | copy-start | bytes 393220
  8.6 12.1 %copy-start.3 = (f32[2,32,8,8]{1,3,2,0:T(8,128)S(1)}, f32[2,32,8,8]{1,3,2,0:T(8,128)}, u32[]{:S(2)}) copy-start(f32[2,32,8,8]{1,3,2,0:T(8,128)} %param.8) | copy-start | bytes 49156
  8.6 5.8 %collective-permute-start.1 = (bf16[64,128]{1,0:T(8,128)(2,1)S(1)}, bf16[64,128]{1,0:T(8,128)(2,1)S(1)}, u32[]{:S(2)}, u32[]{:S(2)}) collective-permute-start(bf16[64,128]{1,0:T(8,128)(2,1)S(1)} %get-tuple-element.18), channel_id=1, source_target_pairs={{1,0},{2,1},{3,2},{5,4},{6,5},{7,6},{9,8},{10,9},{11,10},{13,12},{... | collective-permute-start | bytes 49160 | tf_op jit(solution)/shard_map/ppermute | solution.py:104
  14.6 2.6 %collective-permute-start.2 = (bf16[64,640]{1,0:T(8,128)(2,1)S(1)}, bf16[64,640]{1,0:T(8,128)(2,1)S(1)}, u32[]{:S(2)}, u32[]{:S(2)}) collective-permute-start(bf16[64,640]{1,0:T(8,128)(2,1)S(1)} %get-tuple-element.21), channel_id=1, source_target_pairs={{0,4},{4,8},{8,12},{12,16},{16,20},{20,24},{24,28},{1,5},{5,9},{9,... | collective-permute-start | bytes 245768 | tf_op jit(solution)/shard_map/ppermute | solution.py:105
  15.9 4.9 %collective-permute-start.3 = (bf16[64,640]{1,0:T(8,128)(2,1)S(1)}, bf16[64,640]{1,0:T(8,128)(2,1)S(1)}, u32[]{:S(2)}, u32[]{:S(2)}) collective-permute-start(bf16[64,640]{1,0:T(8,128)(2,1)S(1)} %get-tuple-element.22), channel_id=1, source_target_pairs={{4,0},{8,4},{12,8},{16,12},{20,16},{24,20},{28,24},{5,1},{9,5},{13... | collective-permute-start | bytes 245768 | tf_op jit(solution)/shard_map/ppermute | solution.py:104
  61.9 15.1 %all-to-all-start = ((f32[8,16,512]{2,1,0:T(8,128)}), f32[8,16,512]{2,1,0:T(8,128)S(1)}, u32[]{:S(2)}, u32[]{:S(2)}) async-start(f32[8,16,512]{2,1,0:T(8,128)} %get-tuple-element.25), calls=%async_computation | async-start | bytes 524288 | tf_op jit(solution)/shard_map/all_to_all | solution.py:407
  68.3 4.6 %collective-permute-start.6 = (f32[64,128]{1,0:T(8,128)S(1)}, f32[64,128]{1,0:T(8,128)S(1)}, u32[]{:S(2)}, u32[]{:S(2)}) collective-permute-start(f32[64,128]{1,0:T(8,128)S(1)} %get-tuple-element.26.refs_0_), channel_id=1, source_target_pairs={{0,3},{1,0},{2,1},{3,2},{4,7},{5,4},{6,5},{7,6},{8,11},{9,8},{10,9... | collective-permute-start | bytes 98312 | tf_op jit(solution)/shard_map/ppermute | solution.py:405
  70.2 5.0 %collective-permute-start.5 = (f32[64,128]{1,0:T(8,128)S(1)}, f32[64,128]{1,0:T(8,128)S(1)}, u32[]{:S(2)}, u32[]{:S(2)}) collective-permute-start(f32[64,128]{1,0:T(8,128)S(1)} %get-tuple-element.26.refs_0_), channel_id=1, source_target_pairs={{0,2},{1,3},{2,0},{3,1},{4,6},{5,7},{6,4},{7,5},{8,10},{9,11},{10,... | collective-permute-start | bytes 98312 | tf_op jit(solution)/shard_map/ppermute | solution.py:405
  71.3 5.7 %collective-permute-start.4 = (f32[64,128]{1,0:T(8,128)S(1)}, f32[64,128]{1,0:T(8,128)S(1)}, u32[]{:S(2)}, u32[]{:S(2)}) collective-permute-start(f32[64,128]{1,0:T(8,128)S(1)} %get-tuple-element.26.refs_0_), channel_id=1, source_target_pairs={{0,1},{1,2},{2,3},{3,0},{4,5},{5,6},{6,7},{7,4},{8,9},{9,10},{10,1... | collective-permute-start | bytes 98312 | tf_op jit(solution)/shard_map/ppermute | solution.py:405

commit v4 on v3

--- a/solution.py
+++ b/solution.py
@@ -154,7 +154,7 @@
 def warp_kernel(
     cells_ref, image_ref, shift_ref, left_ref, right_ref, low_ref, high_ref, squares_ref, plane_ref, depth_ref,
     residual_ref, depth_out, plane_out,
-    window, columns, field, blocks, energy, held,
+    window, columns, field, blocks, energy,
 ):
     step = pl.program_id(0)
     last = pl.num_programs(0) - 1
@@ -188,18 +188,24 @@
 
     @pl.when(step < last)
     def _():
-        lane = lax.broadcasted_iota(jnp.int32, (rows, LANES), 1)
+        lane = lax.broadcasted_iota(jnp.int32, (16, LANES), 1)
         slot = (step % 3) * planes
 
         def one(k, carry):
             x = step * planes + k
-            middle = cells_ref[k].astype(f32)
-            after = pltpu.roll(columns[1], (LANES - x) % LANES, 1)
-            before = pltpu.roll(columns[0], LANES - 1 - x, 1)
-            moved = differences(jnp.concatenate([middle, jnp.where(lane == 0, after, before)], axis=1))
-            for c in range(3):
-                for tile in range(tiles):
-                    window[c, slot + k, tile, TOP : TOP + rows, :] = moved[c][:, tile * LANES : (tile + 1) * LANES]
+            raw = cells_ref[k]
+            right, left = columns[1], columns[0]
+            for group in range(rows // 16):
+                mine = slice(16 * group, 16 * group + 16)
+                after = pltpu.roll(right[mine], (LANES - x) % LANES, 1)
+                before = pltpu.roll(left[mine], LANES - 1 - x, 1)
+                beyond = jnp.where(lane == 0, after, before)
+                moved = differences(jnp.concatenate([raw[mine].astype(f32), beyond], axis=1))
+                for c in range(3):
+                    for tile in range(tiles):
+                        window[c, slot + k, tile, TOP + 16 * group : TOP + 16 * group + 16, :] = moved[c][
+                            :, tile * LANES : (tile + 1) * LANES
+                        ]
             return carry
 
         lax.fori_loop(0, planes, one, 0)
@@ -218,65 +224,63 @@
     @pl.when(step > 0)
     def _():
         base = ((step + 2) % 3) * planes
-        places = [(base + slots - 1) % slots] + [base + k for k in range(planes)] + [(base + planes) % slots]
-
-        def one(t, total):
-            tile = t % tiles
-            pair = t // tiles
-            at = pl.multiple_of(tile * LANES, LANES)
+
+        def row_pair(pair, total):
             top = pl.multiple_of(pair * 16, 16)
-            for half in range(2):
-                start = TOP + top + 8 * half
-                node = (step - 1) * nodes + pair * 2 + half
-                mine = slice(8 * half, 8 * half + 8)
-
-                def taps(x):
-                    return [
-                        [window[c, places[x], tile, pl.ds(start + b, 8), :] for c in range(3)] for b in (-1, 0, 1)
-                    ]
-
-                contrast = jnp.broadcast_to(field[0, tile, pl.ds(node, 1), :], (8, LANES))
-                brightness = jnp.broadcast_to(field[1, tile, pl.ds(node, 1), :], (8, LANES))
-                by_image = jnp.zeros((8, LANES), f32)
-                plain = jnp.zeros((8, LANES), f32)
-                before, here = taps(0), taps(1)
-                results = []
-                for k in range(planes):
-                    after = taps(k + 2)
-                    place = (k, pl.ds(top, 16), pl.ds(at, LANES))
-                    sx, sy, sz = (shift_ref[(axis,) + place].astype(f32)[mine] for axis in range(3))
-                    image = image_ref[place].astype(f32)[mine]
+            outputs = [(tile, half) for tile in range(tiles) for half in range(2)]
+
+            def plane(k, carry):
+                total, by_image, plain = carry[0], list(carry[1]), list(carry[2])
+                here = base + k
+                before = jnp.where(here == 0, slots - 1, here - 1)
+                after = jnp.where(here == slots - 1, 0, here + 1)
+                inputs, results = [], []
+                for tile in range(tiles):
+                    place = (k, pl.ds(top, 16), slice(tile * LANES, (tile + 1) * LANES))
+                    loaded = [shift_ref[(axis,) + place].astype(f32) for axis in range(3)]
+                    inputs.append(loaded + [image_ref[place].astype(f32)])
+                for n, (tile, half) in enumerate(outputs):
+                    sx, sy, sz, image = (v[8 * half : 8 * half + 8] for v in inputs[tile])
                     px, py, pz = sx > 0, sy > 0, sz > 0
-                    ax, ay = jnp.abs(sx), jnp.abs(sy)
+                    start = TOP + top + 8 * half
+                    node = (step - 1) * nodes + pair * 2 + half
+
+                    def tap(x, b, c):
+                        return window[c, x, tile, pl.ds(start + b, 8), :]
 
                     def sides(c):
-                        far = [jnp.where(px, after[b][c], before[b][c]) for b in range(3)]
-                        near = [here[b][c] for b in range(3)]
+                        near = [tap(here, b, c) for b in (-1, 0, 1)]
+                        far = [jnp.where(px, tap(after, b, c), tap(before, b, c)) for b in (-1, 0, 1)]
                         return [(v[1], jnp.where(py, v[2], v[0])) for v in (near, far)]
 
                     ahead, middle, behind = sides(0), sides(1), sides(2)
                     lines = []
                     for b in range(2):
                         near, far = (middle[v][b] + sz * jnp.where(pz, ahead[v][b], behind[v][b]) for v in range(2))
-                        lines.append(near + ax * (far - near))
-                    warped = lines[0] + ay * (lines[1] - lines[0])
+                        lines.append(near + jnp.abs(sx) * (far - near))
+                    warped = lines[0] + jnp.abs(sy) * (lines[1] - lines[0])
+                    contrast = jnp.broadcast_to(field[0, tile, pl.ds(node, 1), :], (8, LANES))
+                    brightness = jnp.broadcast_to(field[1, tile, pl.ds(node, 1), :], (8, LANES))
                     misfit = warped - contrast * image - brightness
                     results.append(misfit)
-                    by_image = by_image + misfit * image
-                    plain = plain + misfit
+                    by_image[n] = by_image[n] + misfit * image
+                    plain[n] = plain[n] + misfit
                     total = total + misfit * misfit
-                    before, here = here, after
-                for k in range(planes):
-                    if half == 0:
-                        held[k] = results[k]
-                    else:
-                        place = (k, pl.ds(top, 16), pl.ds(at, LANES))
-                        residual_ref[place] = jnp.concatenate([held[k], results[k]], axis=0).astype(bf16)
-                for k, value in ((0, by_image), (1, plain)):
-                    blocks[k, tile, pl.ds(pl.multiple_of(node * 8, 8), 8), :] = value
+                for tile in range(tiles):
+                    place = (k, pl.ds(top, 16), slice(tile * LANES, (tile + 1) * LANES))
+                    residual_ref[place] = jnp.concatenate(results[2 * tile : 2 * tile + 2], axis=0).astype(bf16)
+                return total, tuple(by_image), tuple(plain)
+
+            none = tuple(jnp.zeros((8, LANES), f32) for _ in outputs)
+            total, by_image, plain = lax.fori_loop(0, planes, plane, (total, none, none))
+            for n, (tile, half) in enumerate(outputs):
+                node = (step - 1) * nodes + pair * 2 + half
+                place = pl.ds(pl.multiple_of(node * 8, 8), 8)
+                blocks[0, tile, place, :] = by_image[n]
+                blocks[1, tile, place, :] = plain[n]
             return total
 
-        energy[...] = lax.fori_loop(0, (rows // 16) * tiles, one, energy[...])
+        energy[...] = lax.fori_loop(0, rows // 16, row_pair, energy[...])
 
     @pl.when(step == last)
     def _():
@@ -341,7 +345,6 @@
             pltpu.VMEM((2, tiles, nodes, LANES), f32),
             pltpu.VMEM((2, tiles, 8 * nodes, LANES), f32),
             pltpu.VMEM((8, LANES), f32),
-            pltpu.VMEM((KNOT, 8, LANES), f32),
         ],
         compiler_params=grid_params(),
         cost_estimate=pl.CostEstimate(flops=60 * cells.size, bytes_accessed=12 * cells.size, transcendentals=0),

time: 89.4 us -> 96.8 us (1.083)
  Pallas kernels: 44.6 us -> 52 us
    pallas_call x1, Pallas kernels: 41.2 us -> 48.5 us  [warp(): pl.pallas_call(warp_kernel, grid=(count + 1,), in_specs=[pl.BlockSpec((KN...]
where the time goes in v4:
time: 96.8 us; the launch traced here: 96.4 us
  Pallas kernels  52 us (54%)
  starting transfers between devices  20 us (21%)
  blocking collectives  10.9 us (11%)
  waiting for transfers between devices  10.5 us (11%)
  local copies, waits for them, and re-layouts  2.2 us (2%)
    pallas_call x1, Pallas kernels, warp(): pl.pallas_call(warp_kernel, grid=(count + 1,), in_specs=[pl.BlockSpec((KN...  48.5 us
    all_to_all x1, blocking collectives, local(): depth_terms = lax.all_to_all(depth_terms, 'gy', 0, 0)  10.9 us
    all_to_all x1, starting transfers between devices, local(): depth_terms = lax.all_to_all(depth_terms, 'gy', 0, 0)  6.36 us
    ppermute x2, starting transfers between devices, shifted(): return lax.ppermute(part, axis, [(i, i + 1) for i in range(count - 1)])  6.35 us
    ppermute x2, waiting for transfers between devices, shifted(): return lax.ppermute(part, axis, [(i + 1, i) for i in range(count - 1)])  6.33 us
    ppermute x3, starting transfers between devices, local(): lax.ppermute(plane_terms, 'gz', [(i, (i + hop) % n_gz) for i in range(n_g...  4.62 us
    ppermute x3, waiting for transfers between devices, local(): lax.ppermute(plane_terms, 'gz', [(i, (i + hop) % n_gz) for i in range(n_g...  4.14 us
    ppermute x2, starting transfers between devices, shifted(): return lax.ppermute(part, axis, [(i + 1, i) for i in range(count - 1)])  2.72 us
  transfers between devices with their start and end apart: 8, of which 4 were waited for; matrix products, arithmetic and copies ran while one was open for 0% of the time, Pallas kernels for 2%

profile of v4, /device:TPU:0, one launch (start us, length us, event | category | flops | bytes accessed | tf_op | source)
XLA Modules:
  0.0 96.4 jit_solution(5354687395697844290)
XLA Ops:
  0.6 0.0 copy-start
  0.6 2.2 %copy-done = bf16[64,64,512]{2,1,0:T(8,128)(2,1)S(1)} copy-done((bf16[64,64,512]{2,1,0:T(8,128)(2,1)S(1)}, bf16[64,64,512]{2,1,0:T(8,128)(2,1)}, u32[]{:S(2)}) %copy-start) | copy-done | bytes 4194328
  2.8 0.0 copy-start.1
  2.8 0.7 columns.1
  3.5 5.1 %collective-permute-start = (bf16[64,128]{1,0:T(8,128)(2,1)S(1)}, bf16[64,128]{1,0:T(8,128)(2,1)S(1)}, u32[]{:S(2)}, u32[]{:S(2)}) collective-permute-start(bf16[64,128]{1,0:T(8,128)(2,1)S(1)} %get-tuple-element.17), channel_id=1, source_target_pairs={{0,1},{1,2},{2,3},{4,5},{5,6},{6,7},{8,9},{9,10},{10,11},{12,13},{... | collective-permute-start | bytes 49160 | tf_op jit(solution)/shard_map/ppermute | solution.py:105
  8.6 0.0 copy-start.2
  8.6 0.0 copy-start.3
  8.6 1.4 %collective-permute-start.1 = (bf16[64,128]{1,0:T(8,128)(2,1)S(1)}, bf16[64,128]{1,0:T(8,128)(2,1)S(1)}, u32[]{:S(2)}, u32[]{:S(2)}) collective-permute-start(bf16[64,128]{1,0:T(8,128)(2,1)S(1)} %get-tuple-element.18), channel_id=1, source_target_pairs={{1,0},{2,1},{3,2},{5,4},{6,5},{7,6},{9,8},{10,9},{11,10},{13,12},{... | collective-permute-start | bytes 49160 | tf_op jit(solution)/shard_map/ppermute | solution.py:104
  10.1 0.0 copy-done.1
  10.1 1.6 %squares.1 = (f32[4,512,128]{2,1,0:T(8,128)S(1)}, f32[64,512]{1,0:T(8,128)S(1)}, f32[64,512]{1,0:T(8,128)S(1)}) custom-call(bf16[64,64,512]{2,1,0:T(8,128)(2,1)S(1)} %copy-done.1, bf16[64,64,512]{2,1,0:T(8,128)(2,1)S(1)} %copy-done, bf16[64,64,512]{2,1,0:T(8,128)(2,1)S(1)} %copy-done), custom_call_target="tpu_custom_call" | custom-call | flops 6291456 | bytes 4194304 | tf_op jit(solution)/shard_map/squares/pallas_call | solution.py:130
  11.6 0.0 collective-permute-done.left_ref
  11.6 2.8 %collective-permute-done.1.right_ref = bf16[64,128]{1,0:T(8,128)(2,1)S(1)} collective-permute-done((bf16[64,128]{1,0:T(8,128)(2,1)S(1)}, bf16[64,128]{1,0:T(8,128)(2,1)S(1)}, u32[]{:S(2)}, u32[]{:S(2)}) %collective-permute-start.1) | collective-permute-done | bytes 16416 | tf_op jit(solution)/shard_map/ppermute | solution.py:104
  14.4 0.2 rows.1
  14.6 1.3 %collective-permute-start.2 = (bf16[64,640]{1,0:T(8,128)(2,1)S(1)}, bf16[64,640]{1,0:T(8,128)(2,1)S(1)}, u32[]{:S(2)}, u32[]{:S(2)}) collective-permute-start(bf16[64,640]{1,0:T(8,128)(2,1)S(1)} %get-tuple-element.21), channel_id=1, source_target_pairs={{0,4},{4,8},{8,12},{12,16},{16,20},{20,24},{24,28},{1,5},{5,9},{9,... | collective-permute-start | bytes 245768 | tf_op jit(solution)/shard_map/ppermute | solution.py:105
  15.9 1.3 %collective-permute-start.3 = (bf16[64,640]{1,0:T(8,128)(2,1)S(1)}, bf16[64,640]{1,0:T(8,128)(2,1)S(1)}, u32[]{:S(2)}, u32[]{:S(2)}) collective-permute-start(bf16[64,640]{1,0:T(8,128)(2,1)S(1)} %get-tuple-element.22), channel_id=1, source_target_pairs={{4,0},{8,4},{12,8},{16,12},{20,16},{24,20},{28,24},{5,1},{9,5},{13... | collective-permute-start | bytes 245768 | tf_op jit(solution)/shard_map/ppermute | solution.py:104
  17.2 0.0 collective-permute-done.2.low_ref
  17.2 3.6 %collective-permute-done.3.high_ref = bf16[64,640]{1,0:T(8,128)(2,1)S(1)} collective-permute-done((bf16[64,640]{1,0:T(8,128)(2,1)S(1)}, bf16[64,640]{1,0:T(8,128)(2,1)S(1)}, u32[]{:S(2)}, u32[]{:S(2)}) %collective-permute-start.3) | collective-permute-done | bytes 81952 | tf_op jit(solution)/shard_map/ppermute | solution.py:104
  20.8 0.0 copy-done.2
  20.8 0.0 copy-done.3
  20.8 48.5 %warp.1 = (bf16[64,64,512]{2,1,0:T(8,128)(2,1)}, f32[8,16,512]{2,1,0:T(8,128)}, f32[64,128]{1,0:T(8,128)S(1)}) custom-call(bf16[64,64,512]{2,1,0:T(8,128)(2,1)S(1)} %copy-done, bf16[64,64,512]{2,1,0:T(8,128)(2,1)S(1)} %copy-done.1, bf16[3,64,64,512]{3,2,1,0:T(8,128)(2,1)} %shift_ref.1, bf16[64,128]{1,0:T(8,128)(2,1)S(1)} %collective-permute-done.left_ref, ...), custom_call_target="tpu_custom_call" | custom-call | flops 125829120 | bytes 25165824 | tf_op jit(solution)/shard_map/warp/pallas_call | solution.py:317
  69.3 6.4 %all-to-all-start = ((f32[8,16,512]{2,1,0:T(8,128)}), f32[8,16,512]{2,1,0:T(8,128)S(1)}, u32[]{:S(2)}, u32[]{:S(2)}) async-start(f32[8,16,512]{2,1,0:T(8,128)} %get-tuple-element.25), calls=%async_computation | async-start | bytes 524288 | tf_op jit(solution)/shard_map/all_to_all | solution.py:410
  75.7 1.9 %collective-permute-start.6 = (f32[64,128]{1,0:T(8,128)S(1)}, f32[64,128]{1,0:T(8,128)S(1)}, u32[]{:S(2)}, u32[]{:S(2)}) collective-permute-start(f32[64,128]{1,0:T(8,128)S(1)} %get-tuple-element.26.refs_0_), channel_id=1, source_target_pairs={{0,3},{1,0},{2,1},{3,2},{4,7},{5,4},{6,5},{7,6},{8,11},{9,8},{10,9... | collective-permute-start | bytes 98312 | tf_op jit(solution)/shard_map/ppermute | solution.py:408
  77.6 1.1 %collective-permute-start.5 = (f32[64,128]{1,0:T(8,128)S(1)}, f32[64,128]{1,0:T(8,128)S(1)}, u32[]{:S(2)}, u32[]{:S(2)}) collective-permute-start(f32[64,128]{1,0:T(8,128)S(1)} %get-tuple-element.26.refs_0_), channel_id=1, source_target_pairs={{0,2},{1,3},{2,0},{3,1},{4,6},{5,7},{6,4},{7,5},{8,10},{9,11},{10,... | collective-permute-start | bytes 98312 | tf_op jit(solution)/shard_map/ppermute | solution.py:408
  78.7 1.6 %collective-permute-start.4 = (f32[64,128]{1,0:T(8,128)S(1)}, f32[64,128]{1,0:T(8,128)S(1)}, u32[]{:S(2)}, u32[]{:S(2)}) collective-permute-start(f32[64,128]{1,0:T(8,128)S(1)} %get-tuple-element.26.refs_0_), channel_id=1, source_target_pairs={{0,1},{1,2},{2,3},{3,0},{4,5},{5,6},{6,7},{7,4},{8,9},{9,10},{10,1... | collective-permute-start | bytes 98312 | tf_op jit(solution)/shard_map/ppermute | solution.py:408
  80.3 0.0 collective-permute-done.6.refs_3_
  80.3 2.3 %collective-permute-done.5.refs_2_ = f32[64,128]{1,0:T(8,128)S(1)} collective-permute-done((f32[64,128]{1,0:T(8,128)S(1)}, f32[64,128]{1,0:T(8,128)S(1)}, u32[]{:S(2)}, u32[]{:S(2)}) %collective-permute-start.5) | collective-permute-done | bytes 32800 | tf_op jit(solution)/shard_map/ppermute | solution.py:408
  82.6 1.8 %collective-permute-done.4.refs_1_ = f32[64,128]{1,0:T(8,128)S(1)} collective-permute-done((f32[64,128]{1,0:T(8,128)S(1)}, f32[64,128]{1,0:T(8,128)S(1)}, u32[]{:S(2)}, u32[]{:S(2)}) %collective-permute-start.4) | collective-permute-done | bytes 32800 | tf_op jit(solution)/shard_map/ppermute | solution.py:408
  84.4 0.0 all-to-all-done.depth_ref
  84.4 0.1 gather.1
  84.6 10.9 %all_to_all.10.depth_ref = f32[8,16,512]{2,1,0:T(8,128)S(1)} all-to-all(f32[8,16,512]{2,1,0:T(8,128)S(1)} %get-tuple-element.27), channel_id=1, replica_groups=mesh['gy'=8,'gz'=4] {'gy'}, dimensions={0} | all-to-all | bytes 524288 | tf_op jit(solution)/shard_map/all_to_all | solution.py:420
  95.5 0.9 steps.1
Async XLA Ops:
  0.6 2.2 %copy-start = (bf16[64,64,512]{2,1,0:T(8,128)(2,1)S(1)}, bf16[64,64,512]{2,1,0:T(8,128)(2,1)}, u32[]{:S(2)}) copy-start(bf16[64,64,512]{2,1,0:T(8,128)(2,1)} %cells_ref.1) | copy-start | bytes 12582916
  2.8 7.2 %copy-start.1 = (bf16[64,64,512]{2,1,0:T(8,128)(2,1)S(1)}, bf16[64,64,512]{2,1,0:T(8,128)(2,1)}, u32[]{:S(2)}) copy-start(bf16[64,64,512]{2,1,0:T(8,128)(2,1)} %image_ref.3) | copy-start | bytes 12582916
  3.5 8.1 %collective-permute-start = (bf16[64,128]{1,0:T(8,128)(2,1)S(1)}, bf16[64,128]{1,0:T(8,128)(2,1)S(1)}, u32[]{:S(2)}, u32[]{:S(2)}) collective-permute-start(bf16[64,128]{1,0:T(8,128)(2,1)S(1)} %get-tuple-element.17), channel_id=1, source_target_pairs={{0,1},{1,2},{2,3},{4,5},{5,6},{6,7},{8,9},{9,10},{10,11},{12,13},{... | collective-permute-start | bytes 49160 | tf_op jit(solution)/shard_map/ppermute | solution.py:105
  8.6 12.2 %copy-start.2 = (f32[2,32,512]{2,1,0:T(8,128)S(1)}, f32[2,32,512]{2,1,0:T(8,128)}, u32[]{:S(2)}) copy-start(f32[2,32,512]{2,1,0:T(8,128)} %depth_ref.1) | copy-start | bytes 393220
  8.6 12.1 %copy-start.3 = (f32[2,32,8,8]{1,3,2,0:T(8,128)S(1)}, f32[2,32,8,8]{1,3,2,0:T(8,128)}, u32[]{:S(2)}) copy-start(f32[2,32,8,8]{1,3,2,0:T(8,128)} %param.8) | copy-start | bytes 49156
  8.6 5.8 %collective-permute-start.1 = (bf16[64,128]{1,0:T(8,128)(2,1)S(1)}, bf16[64,128]{1,0:T(8,128)(2,1)S(1)}, u32[]{:S(2)}, u32[]{:S(2)}) collective-permute-start(bf16[64,128]{1,0:T(8,128)(2,1)S(1)} %get-tuple-element.18), channel_id=1, source_target_pairs={{1,0},{2,1},{3,2},{5,4},{6,5},{7,6},{9,8},{10,9},{11,10},{13,12},{... | collective-permute-start | bytes 49160 | tf_op jit(solution)/shard_map/ppermute | solution.py:104
  14.6 2.6 %collective-permute-start.2 = (bf16[64,640]{1,0:T(8,128)(2,1)S(1)}, bf16[64,640]{1,0:T(8,128)(2,1)S(1)}, u32[]{:S(2)}, u32[]{:S(2)}) collective-permute-start(bf16[64,640]{1,0:T(8,128)(2,1)S(1)} %get-tuple-element.21), channel_id=1, source_target_pairs={{0,4},{4,8},{8,12},{12,16},{16,20},{20,24},{24,28},{1,5},{5,9},{9,... | collective-permute-start | bytes 245768 | tf_op jit(solution)/shard_map/ppermute | solution.py:105
  15.9 4.9 %collective-permute-start.3 = (bf16[64,640]{1,0:T(8,128)(2,1)S(1)}, bf16[64,640]{1,0:T(8,128)(2,1)S(1)}, u32[]{:S(2)}, u32[]{:S(2)}) collective-permute-start(bf16[64,640]{1,0:T(8,128)(2,1)S(1)} %get-tuple-element.22), channel_id=1, source_target_pairs={{4,0},{8,4},{12,8},{16,12},{20,16},{24,20},{28,24},{5,1},{9,5},{13... | collective-permute-start | bytes 245768 | tf_op jit(solution)/shard_map/ppermute | solution.py:104
  69.3 15.1 %all-to-all-start = ((f32[8,16,512]{2,1,0:T(8,128)}), f32[8,16,512]{2,1,0:T(8,128)S(1)}, u32[]{:S(2)}, u32[]{:S(2)}) async-start(f32[8,16,512]{2,1,0:T(8,128)} %get-tuple-element.25), calls=%async_computation | async-start | bytes 524288 | tf_op jit(solution)/shard_map/all_to_all | solution.py:410
  75.7 4.6 %collective-permute-start.6 = (f32[64,128]{1,0:T(8,128)S(1)}, f32[64,128]{1,0:T(8,128)S(1)}, u32[]{:S(2)}, u32[]{:S(2)}) collective-permute-start(f32[64,128]{1,0:T(8,128)S(1)} %get-tuple-element.26.refs_0_), channel_id=1, source_target_pairs={{0,3},{1,0},{2,1},{3,2},{4,7},{5,4},{6,5},{7,6},{8,11},{9,8},{10,9... | collective-permute-start | bytes 98312 | tf_op jit(solution)/shard_map/ppermute | solution.py:408
  77.6 5.0 %collective-permute-start.5 = (f32[64,128]{1,0:T(8,128)S(1)}, f32[64,128]{1,0:T(8,128)S(1)}, u32[]{:S(2)}, u32[]{:S(2)}) collective-permute-start(f32[64,128]{1,0:T(8,128)S(1)} %get-tuple-element.26.refs_0_), channel_id=1, source_target_pairs={{0,2},{1,3},{2,0},{3,1},{4,6},{5,7},{6,4},{7,5},{8,10},{9,11},{10,... | collective-permute-start | bytes 98312 | tf_op jit(solution)/shard_map/ppermute | solution.py:408
  78.7 5.7 %collective-permute-start.4 = (f32[64,128]{1,0:T(8,128)S(1)}, f32[64,128]{1,0:T(8,128)S(1)}, u32[]{:S(2)}, u32[]{:S(2)}) collective-permute-start(f32[64,128]{1,0:T(8,128)S(1)} %get-tuple-element.26.refs_0_), channel_id=1, source_target_pairs={{0,1},{1,2},{2,3},{3,0},{4,5},{5,6},{6,7},{7,4},{8,9},{9,10},{10,1... | collective-permute-start | bytes 98312 | tf_op jit(solution)/shard_map/ppermute | solution.py:408

commit v5 on v3

--- a/solution.py
+++ b/solution.py
@@ -154,19 +154,23 @@
 def warp_kernel(
     cells_ref, image_ref, shift_ref, left_ref, right_ref, low_ref, high_ref, squares_ref, plane_ref, depth_ref,
     residual_ref, depth_out, plane_out,
-    window, columns, field, blocks, energy, held,
+    ahead_ref, here_ref, behind_ref, columns, field, blocks, energy, held,
 ):
     step = pl.program_id(0)
     last = pl.num_programs(0) - 1
     planes, rows, width = cells_ref.shape
     nodes = rows // KNOT
     tiles = width // LANES
-    slots = window.shape[1]
+    window = (ahead_ref, here_ref, behind_ref)
+    pitch = rows + 2 * TOP
+    plane_rows = tiles * pitch
+    block_rows = planes * plane_rows
 
     def store_row(plane, moved, k, row):
         for c in range(3):
             for tile in range(tiles):
-                window[c, plane, tile, row : row + 1, :] = moved[c][k : k + 1, tile * LANES : (tile + 1) * LANES]
+                piece = moved[c][k : k + 1, tile * LANES : (tile + 1) * LANES]
+                window[c][pl.ds(plane + tile * pitch + row, 1), :] = piece
 
     def differences(wide):
         ahead = pltpu.roll(wide, wide.shape[1] - 1, 1) - wide
@@ -177,10 +181,8 @@
         columns[0] = left_ref[...].astype(f32)
         columns[1] = right_ref[...].astype(f32)
         energy[...] = jnp.zeros_like(energy)
-        nothing = jnp.zeros((rows + 2 * TOP, LANES), f32)
         for c in range(3):
-            for tile in range(tiles):
-                window[c, slots - 1, tile] = nothing
+            window[c][3 * block_rows - plane_rows : 3 * block_rows, :] = jnp.zeros((plane_rows, LANES), f32)
         for k in range(2):
             values = dot(plane_ref[k], depth_ref[k], ((1,), (0,)))
             for tile in range(tiles):
@@ -188,51 +190,63 @@
 
     @pl.when(step < last)
     def _():
-        lane = lax.broadcasted_iota(jnp.int32, (rows, LANES), 1)
-        slot = (step % 3) * planes
+        lane = lax.broadcasted_iota(jnp.int32, (16, LANES), 1)
+        slot = (step % 3) * block_rows
 
         def one(k, carry):
             x = step * planes + k
-            middle = cells_ref[k].astype(f32)
-            after = pltpu.roll(columns[1], (LANES - x) % LANES, 1)
-            before = pltpu.roll(columns[0], LANES - 1 - x, 1)
-            moved = differences(jnp.concatenate([middle, jnp.where(lane == 0, after, before)], axis=1))
-            for c in range(3):
-                for tile in range(tiles):
-                    window[c, slot + k, tile, TOP : TOP + rows, :] = moved[c][:, tile * LANES : (tile + 1) * LANES]
+            first = pl.multiple_of(slot + k * plane_rows, 8)
+            raw = cells_ref[k]
+            right, left = columns[1], columns[0]
+            for group in range(rows // 16):
+                mine = slice(16 * group, 16 * group + 16)
+                after = pltpu.roll(right[mine], (LANES - x) % LANES, 1)
+                before = pltpu.roll(left[mine], LANES - 1 - x, 1)
+                beyond = jnp.where(lane == 0, after, before)
+                moved = differences(jnp.concatenate([raw[mine].astype(f32), beyond], axis=1))
+                for c in range(3):
+                    for tile in range(tiles):
+                        window[c][pl.ds(first + tile * pitch + TOP + 16 * group, 16), :] = moved[c][
+                            :, tile * LANES : (tile + 1) * LANES
+                        ]
             return carry
 
         lax.fori_loop(0, planes, one, 0)
         for source, row in ((low_ref, TOP - 1), (high_ref, TOP + rows)):
             moved = differences(source[...].astype(f32))
             for k in range(planes):
-                store_row(slot + k, moved, k, row)
+                store_row(slot + k * plane_rows, moved, k, row)
 
     @pl.when(step == last)
     def _():
-        nothing = jnp.zeros((rows + 2 * TOP, LANES), f32)
+        first = pl.multiple_of((step % 3) * block_rows, 8)
         for c in range(3):
-            for tile in range(tiles):
-                window[c, (step % 3) * planes, tile] = nothing
+            window[c][pl.ds(first, plane_rows), :] = jnp.zeros((plane_rows, LANES), f32)
 
     @pl.when(step > 0)
     def _():
-        base = ((step + 2) % 3) * planes
-        places = [(base + slots - 1) % slots] + [base + k for k in range(planes)] + [(base + planes) % slots]
+        mid = (step + 2) % 3
+        first_rows = (
+            jnp.where(mid == 0, 3, mid) * block_rows - plane_rows,
+            mid * block_rows,
+            jnp.where(mid == 2, 0, mid + 1) * block_rows,
+        )
 
         def one(t, total):
             tile = t % tiles
             pair = t // tiles
             at = pl.multiple_of(tile * LANES, LANES)
             top = pl.multiple_of(pair * 16, 16)
+            origins = [first + tile * pitch + top + TOP for first in first_rows]
             for half in range(2):
-                start = TOP + top + 8 * half
                 node = (step - 1) * nodes + pair * 2 + half
                 mine = slice(8 * half, 8 * half + 8)
 
                 def taps(x):
+                    part = 0 if x == 0 else 2 if x == planes + 1 else 1
+                    plus = (x - 1) * plane_rows + 8 * half if part == 1 else 8 * half
                     return [
-                        [window[c, places[x], tile, pl.ds(start + b, 8), :] for c in range(3)] for b in (-1, 0, 1)
+                        [window[c][pl.ds(origins[part] + (plus + b), 8), :] for c in range(3)] for b in (-1, 0, 1)
                     ]
 
                 contrast = jnp.broadcast_to(field[0, tile, pl.ds(node, 1), :], (8, LANES))
@@ -336,7 +350,7 @@
             jax.ShapeDtypeStruct((nodes, 4 * RANK), f32),
         ],
         scratch_shapes=[
-            pltpu.VMEM((3, 3 * KNOT, tiles, rows + 2 * TOP, LANES), f32),
+            *[pltpu.VMEM((3 * KNOT * tiles * (rows + 2 * TOP), LANES), f32)] * 3,
             pltpu.VMEM((2, rows, LANES), f32),
             pltpu.VMEM((2, tiles, nodes, LANES), f32),
             pltpu.VMEM((2, tiles, 8 * nodes, LANES), f32),

time: 89.4 us -> 89 us (level)
  no operation moved by 1% of the time
where the time goes in v5:
time: 89 us; the launch traced here: 88.6 us
  Pallas kernels  44.2 us (50%)
  starting transfers between devices  20 us (22%)
  blocking collectives  10.9 us (12%)
  waiting for transfers between devices  10.5 us (12%)
  local copies, waits for them, and re-layouts  2.2 us (2%)
    pallas_call x1, Pallas kernels, warp(): pl.pallas_call(warp_kernel, grid=(count + 1,), in_specs=[pl.BlockSpec((KN...  40.8 us
    all_to_all x1, blocking collectives, local(): depth_terms = lax.all_to_all(depth_terms, 'gy', 0, 0)  10.9 us
    all_to_all x1, starting transfers between devices, local(): depth_terms = lax.all_to_all(depth_terms, 'gy', 0, 0)  6.36 us
    ppermute x2, starting transfers between devices, shifted(): return lax.ppermute(part, axis, [(i, i + 1) for i in range(count - 1)])  6.35 us
    ppermute x2, waiting for transfers between devices, shifted(): return lax.ppermute(part, axis, [(i + 1, i) for i in range(count - 1)])  6.33 us
    ppermute x3, starting transfers between devices, local(): lax.ppermute(plane_terms, 'gz', [(i, (i + hop) % n_gz) for i in range(n_g...  4.62 us
    ppermute x3, waiting for transfers between devices, local(): lax.ppermute(plane_terms, 'gz', [(i, (i + hop) % n_gz) for i in range(n_g...  4.13 us
    ppermute x2, starting transfers between devices, shifted(): return lax.ppermute(part, axis, [(i + 1, i) for i in range(count - 1)])  2.72 us
  transfers between devices with their start and end apart: 8, of which 4 were waited for; matrix products, arithmetic and copies ran while one was open for 0% of the time, Pallas kernels for 2%

profile of v5, /device:TPU:0, one launch (start us, length us, event | category | flops | bytes accessed | tf_op | source)
XLA Modules:
  0.0 88.6 jit_solution(5693136028770417274)
XLA Ops:
  0.6 0.0 copy-start
  0.6 2.2 %copy-done = bf16[64,64,512]{2,1,0:T(8,128)(2,1)S(1)} copy-done((bf16[64,64,512]{2,1,0:T(8,128)(2,1)S(1)}, bf16[64,64,512]{2,1,0:T(8,128)(2,1)}, u32[]{:S(2)}) %copy-start) | copy-done | bytes 4194328
  2.8 0.0 copy-start.1
  2.8 0.7 columns.1
  3.5 5.1 %collective-permute-start = (bf16[64,128]{1,0:T(8,128)(2,1)S(1)}, bf16[64,128]{1,0:T(8,128)(2,1)S(1)}, u32[]{:S(2)}, u32[]{:S(2)}) collective-permute-start(bf16[64,128]{1,0:T(8,128)(2,1)S(1)} %get-tuple-element.17), channel_id=1, source_target_pairs={{0,1},{1,2},{2,3},{4,5},{5,6},{6,7},{8,9},{9,10},{10,11},{12,13},{... | collective-permute-start | bytes 49160 | tf_op jit(solution)/shard_map/ppermute | solution.py:105
  8.6 0.0 copy-start.2
  8.6 0.0 copy-start.3
  8.6 1.4 %collective-permute-start.1 = (bf16[64,128]{1,0:T(8,128)(2,1)S(1)}, bf16[64,128]{1,0:T(8,128)(2,1)S(1)}, u32[]{:S(2)}, u32[]{:S(2)}) collective-permute-start(bf16[64,128]{1,0:T(8,128)(2,1)S(1)} %get-tuple-element.18), channel_id=1, source_target_pairs={{1,0},{2,1},{3,2},{5,4},{6,5},{7,6},{9,8},{10,9},{11,10},{13,12},{... | collective-permute-start | bytes 49160 | tf_op jit(solution)/shard_map/ppermute | solution.py:104
  10.1 0.0 copy-done.1
  10.1 1.6 %squares.1 = (f32[4,512,128]{2,1,0:T(8,128)S(1)}, f32[64,512]{1,0:T(8,128)S(1)}, f32[64,512]{1,0:T(8,128)S(1)}) custom-call(bf16[64,64,512]{2,1,0:T(8,128)(2,1)S(1)} %copy-done.1, bf16[64,64,512]{2,1,0:T(8,128)(2,1)S(1)} %copy-done, bf16[64,64,512]{2,1,0:T(8,128)(2,1)S(1)} %copy-done), custom_call_target="tpu_custom_call" | custom-call | flops 6291456 | bytes 4194304 | tf_op jit(solution)/shard_map/squares/pallas_call | solution.py:130
  11.6 0.0 collective-permute-done.left_ref
  11.6 2.8 %collective-permute-done.1.right_ref = bf16[64,128]{1,0:T(8,128)(2,1)S(1)} collective-permute-done((bf16[64,128]{1,0:T(8,128)(2,1)S(1)}, bf16[64,128]{1,0:T(8,128)(2,1)S(1)}, u32[]{:S(2)}, u32[]{:S(2)}) %collective-permute-start.1) | collective-permute-done | bytes 16416 | tf_op jit(solution)/shard_map/ppermute | solution.py:104
  14.4 0.2 rows.1
  14.6 1.3 %collective-permute-start.2 = (bf16[64,640]{1,0:T(8,128)(2,1)S(1)}, bf16[64,640]{1,0:T(8,128)(2,1)S(1)}, u32[]{:S(2)}, u32[]{:S(2)}) collective-permute-start(bf16[64,640]{1,0:T(8,128)(2,1)S(1)} %get-tuple-element.21), channel_id=1, source_target_pairs={{0,4},{4,8},{8,12},{12,16},{16,20},{20,24},{24,28},{1,5},{5,9},{9,... | collective-permute-start | bytes 245768 | tf_op jit(solution)/shard_map/ppermute | solution.py:105
  15.9 1.3 %collective-permute-start.3 = (bf16[64,640]{1,0:T(8,128)(2,1)S(1)}, bf16[64,640]{1,0:T(8,128)(2,1)S(1)}, u32[]{:S(2)}, u32[]{:S(2)}) collective-permute-start(bf16[64,640]{1,0:T(8,128)(2,1)S(1)} %get-tuple-element.22), channel_id=1, source_target_pairs={{4,0},{8,4},{12,8},{16,12},{20,16},{24,20},{28,24},{5,1},{9,5},{13... | collective-permute-start | bytes 245768 | tf_op jit(solution)/shard_map/ppermute | solution.py:104
  17.2 0.0 collective-permute-done.2.low_ref
  17.2 3.6 %collective-permute-done.3.high_ref = bf16[64,640]{1,0:T(8,128)(2,1)S(1)} collective-permute-done((bf16[64,640]{1,0:T(8,128)(2,1)S(1)}, bf16[64,640]{1,0:T(8,128)(2,1)S(1)}, u32[]{:S(2)}, u32[]{:S(2)}) %collective-permute-start.3) | collective-permute-done | bytes 81952 | tf_op jit(solution)/shard_map/ppermute | solution.py:104
  20.8 0.0 copy-done.2
  20.8 0.0 copy-done.3
  20.8 40.8 %warp.1 = (bf16[64,64,512]{2,1,0:T(8,128)(2,1)}, f32[8,16,512]{2,1,0:T(8,128)}, f32[64,128]{1,0:T(8,128)S(1)}) custom-call(bf16[64,64,512]{2,1,0:T(8,128)(2,1)S(1)} %copy-done, bf16[64,64,512]{2,1,0:T(8,128)(2,1)S(1)} %copy-done.1, bf16[3,64,64,512]{3,2,1,0:T(8,128)(2,1)} %shift_ref.1, bf16[64,128]{1,0:T(8,128)(2,1)S(1)} %collective-permute-done.left_ref, ...), custom_call_target="tpu_custom_call" | custom-call | flops 125829120 | bytes 25165824 | tf_op jit(solution)/shard_map/warp/pallas_call | solution.py:327
  61.5 6.4 %all-to-all-start = ((f32[8,16,512]{2,1,0:T(8,128)}), f32[8,16,512]{2,1,0:T(8,128)S(1)}, u32[]{:S(2)}, u32[]{:S(2)}) async-start(f32[8,16,512]{2,1,0:T(8,128)} %get-tuple-element.25), calls=%async_computation | async-start | bytes 524288 | tf_op jit(solution)/shard_map/all_to_all | solution.py:421
  67.9 1.9 %collective-permute-start.6 = (f32[64,128]{1,0:T(8,128)S(1)}, f32[64,128]{1,0:T(8,128)S(1)}, u32[]{:S(2)}, u32[]{:S(2)}) collective-permute-start(f32[64,128]{1,0:T(8,128)S(1)} %get-tuple-element.26.refs_0_), channel_id=1, source_target_pairs={{0,3},{1,0},{2,1},{3,2},{4,7},{5,4},{6,5},{7,6},{8,11},{9,8},{10,9... | collective-permute-start | bytes 98312 | tf_op jit(solution)/shard_map/ppermute | solution.py:419
  69.8 1.1 %collective-permute-start.5 = (f32[64,128]{1,0:T(8,128)S(1)}, f32[64,128]{1,0:T(8,128)S(1)}, u32[]{:S(2)}, u32[]{:S(2)}) collective-permute-start(f32[64,128]{1,0:T(8,128)S(1)} %get-tuple-element.26.refs_0_), channel_id=1, source_target_pairs={{0,2},{1,3},{2,0},{3,1},{4,6},{5,7},{6,4},{7,5},{8,10},{9,11},{10,... | collective-permute-start | bytes 98312 | tf_op jit(solution)/shard_map/ppermute | solution.py:419
  70.9 1.6 %collective-permute-start.4 = (f32[64,128]{1,0:T(8,128)S(1)}, f32[64,128]{1,0:T(8,128)S(1)}, u32[]{:S(2)}, u32[]{:S(2)}) collective-permute-start(f32[64,128]{1,0:T(8,128)S(1)} %get-tuple-element.26.refs_0_), channel_id=1, source_target_pairs={{0,1},{1,2},{2,3},{3,0},{4,5},{5,6},{6,7},{7,4},{8,9},{9,10},{10,1... | collective-permute-start | bytes 98312 | tf_op jit(solution)/shard_map/ppermute | solution.py:419
  72.5 0.0 collective-permute-done.6.refs_3_
  72.5 2.3 %collective-permute-done.5.refs_2_ = f32[64,128]{1,0:T(8,128)S(1)} collective-permute-done((f32[64,128]{1,0:T(8,128)S(1)}, f32[64,128]{1,0:T(8,128)S(1)}, u32[]{:S(2)}, u32[]{:S(2)}) %collective-permute-start.5) | collective-permute-done | bytes 32800 | tf_op jit(solution)/shard_map/ppermute | solution.py:419
  74.8 1.8 %collective-permute-done.4.refs_1_ = f32[64,128]{1,0:T(8,128)S(1)} collective-permute-done((f32[64,128]{1,0:T(8,128)S(1)}, f32[64,128]{1,0:T(8,128)S(1)}, u32[]{:S(2)}, u32[]{:S(2)}) %collective-permute-start.4) | collective-permute-done | bytes 32800 | tf_op jit(solution)/shard_map/ppermute | solution.py:419
  76.7 0.0 all-to-all-done.depth_ref
  76.7 0.1 gather.1
  76.8 10.9 %all_to_all.10.depth_ref = f32[8,16,512]{2,1,0:T(8,128)S(1)} all-to-all(f32[8,16,512]{2,1,0:T(8,128)S(1)} %get-tuple-element.27), channel_id=1, replica_groups=mesh['gy'=8,'gz'=4] {'gy'}, dimensions={0} | all-to-all | bytes 524288 | tf_op jit(solution)/shard_map/all_to_all | solution.py:431
  87.7 0.9 %steps.1 = (f32[2,32,512]{2,1,0:T(8,128)}, f32[2,64,32]{2,1,0:T(8,128)}) custom-call(f32[8,16,512]{2,1,0:T(8,128)S(1)} %all_to_all.10.depth_ref, f32[64,128]{1,0:T(8,128)S(1)} %get-tuple-element.28.plane_ref), custom_call_target="tpu_custom_call" | custom-call | tf_op jit(solution)/shard_map/steps/pallas_call | solution.py:433
Async XLA Ops:
  0.6 2.2 %copy-start = (bf16[64,64,512]{2,1,0:T(8,128)(2,1)S(1)}, bf16[64,64,512]{2,1,0:T(8,128)(2,1)}, u32[]{:S(2)}) copy-start(bf16[64,64,512]{2,1,0:T(8,128)(2,1)} %cells_ref.1) | copy-start | bytes 12582916
  2.8 7.2 %copy-start.1 = (bf16[64,64,512]{2,1,0:T(8,128)(2,1)S(1)}, bf16[64,64,512]{2,1,0:T(8,128)(2,1)}, u32[]{:S(2)}) copy-start(bf16[64,64,512]{2,1,0:T(8,128)(2,1)} %image_ref.3) | copy-start | bytes 12582916
  3.5 8.1 %collective-permute-start = (bf16[64,128]{1,0:T(8,128)(2,1)S(1)}, bf16[64,128]{1,0:T(8,128)(2,1)S(1)}, u32[]{:S(2)}, u32[]{:S(2)}) collective-permute-start(bf16[64,128]{1,0:T(8,128)(2,1)S(1)} %get-tuple-element.17), channel_id=1, source_target_pairs={{0,1},{1,2},{2,3},{4,5},{5,6},{6,7},{8,9},{9,10},{10,11},{12,13},{... | collective-permute-start | bytes 49160 | tf_op jit(solution)/shard_map/ppermute | solution.py:105
  8.6 12.2 %copy-start.2 = (f32[2,32,512]{2,1,0:T(8,128)S(1)}, f32[2,32,512]{2,1,0:T(8,128)}, u32[]{:S(2)}) copy-start(f32[2,32,512]{2,1,0:T(8,128)} %depth_ref.1) | copy-start | bytes 393220
  8.6 12.1 %copy-start.3 = (f32[2,32,8,8]{1,3,2,0:T(8,128)S(1)}, f32[2,32,8,8]{1,3,2,0:T(8,128)}, u32[]{:S(2)}) copy-start(f32[2,32,8,8]{1,3,2,0:T(8,128)} %param.8) | copy-start | bytes 49156
  8.6 5.8 %collective-permute-start.1 = (bf16[64,128]{1,0:T(8,128)(2,1)S(1)}, bf16[64,128]{1,0:T(8,128)(2,1)S(1)}, u32[]{:S(2)}, u32[]{:S(2)}) collective-permute-start(bf16[64,128]{1,0:T(8,128)(2,1)S(1)} %get-tuple-element.18), channel_id=1, source_target_pairs={{1,0},{2,1},{3,2},{5,4},{6,5},{7,6},{9,8},{10,9},{11,10},{13,12},{... | collective-permute-start | bytes 49160 | tf_op jit(solution)/shard_map/ppermute | solution.py:104
  14.6 2.6 %collective-permute-start.2 = (bf16[64,640]{1,0:T(8,128)(2,1)S(1)}, bf16[64,640]{1,0:T(8,128)(2,1)S(1)}, u32[]{:S(2)}, u32[]{:S(2)}) collective-permute-start(bf16[64,640]{1,0:T(8,128)(2,1)S(1)} %get-tuple-element.21), channel_id=1, source_target_pairs={{0,4},{4,8},{8,12},{12,16},{16,20},{20,24},{24,28},{1,5},{5,9},{9,... | collective-permute-start | bytes 245768 | tf_op jit(solution)/shard_map/ppermute | solution.py:105
  15.9 4.9 %collective-permute-start.3 = (bf16[64,640]{1,0:T(8,128)(2,1)S(1)}, bf16[64,640]{1,0:T(8,128)(2,1)S(1)}, u32[]{:S(2)}, u32[]{:S(2)}) collective-permute-start(bf16[64,640]{1,0:T(8,128)(2,1)S(1)} %get-tuple-element.22), channel_id=1, source_target_pairs={{4,0},{8,4},{12,8},{16,12},{20,16},{24,20},{28,24},{5,1},{9,5},{13... | collective-permute-start | bytes 245768 | tf_op jit(solution)/shard_map/ppermute | solution.py:104
  61.5 15.1 %all-to-all-start = ((f32[8,16,512]{2,1,0:T(8,128)}), f32[8,16,512]{2,1,0:T(8,128)S(1)}, u32[]{:S(2)}, u32[]{:S(2)}) async-start(f32[8,16,512]{2,1,0:T(8,128)} %get-tuple-element.25), calls=%async_computation | async-start | bytes 524288 | tf_op jit(solution)/shard_map/all_to_all | solution.py:421
  67.9 4.6 %collective-permute-start.6 = (f32[64,128]{1,0:T(8,128)S(1)}, f32[64,128]{1,0:T(8,128)S(1)}, u32[]{:S(2)}, u32[]{:S(2)}) collective-permute-start(f32[64,128]{1,0:T(8,128)S(1)} %get-tuple-element.26.refs_0_), channel_id=1, source_target_pairs={{0,3},{1,0},{2,1},{3,2},{4,7},{5,4},{6,5},{7,6},{8,11},{9,8},{10,9... | collective-permute-start | bytes 98312 | tf_op jit(solution)/shard_map/ppermute | solution.py:419
  69.8 5.0 %collective-permute-start.5 = (f32[64,128]{1,0:T(8,128)S(1)}, f32[64,128]{1,0:T(8,128)S(1)}, u32[]{:S(2)}, u32[]{:S(2)}) collective-permute-start(f32[64,128]{1,0:T(8,128)S(1)} %get-tuple-element.26.refs_0_), channel_id=1, source_target_pairs={{0,2},{1,3},{2,0},{3,1},{4,6},{5,7},{6,4},{7,5},{8,10},{9,11},{10,... | collective-permute-start | bytes 98312 | tf_op jit(solution)/shard_map/ppermute | solution.py:419
  70.9 5.7 %collective-permute-start.4 = (f32[64,128]{1,0:T(8,128)S(1)}, f32[64,128]{1,0:T(8,128)S(1)}, u32[]{:S(2)}, u32[]{:S(2)}) collective-permute-start(f32[64,128]{1,0:T(8,128)S(1)} %get-tuple-element.26.refs_0_), channel_id=1, source_target_pairs={{0,1},{1,2},{2,3},{3,0},{4,5},{5,6},{6,7},{7,4},{8,9},{9,10},{10,1... | collective-permute-start | bytes 98312 | tf_op jit(solution)/shard_map/ppermute | solution.py:419

commit v6 on v5

--- a/solution.py
+++ b/solution.py
@@ -254,7 +254,6 @@
                 by_image = jnp.zeros((8, LANES), f32)
                 plain = jnp.zeros((8, LANES), f32)
                 before, here = taps(0), taps(1)
-                results = []
                 for k in range(planes):
                     after = taps(k + 2)
                     place = (k, pl.ds(top, 16), pl.ds(at, LANES))
@@ -275,17 +274,14 @@
                         lines.append(near + ax * (far - near))
                     warped = lines[0] + ay * (lines[1] - lines[0])
                     misfit = warped - contrast * image - brightness
-                    results.append(misfit)
+                    if half == 0:
+                        held[k] = misfit
+                    else:
+                        residual_ref[place] = jnp.concatenate([held[k], misfit], axis=0).astype(bf16)
                     by_image = by_image + misfit * image
                     plain = plain + misfit
                     total = total + misfit * misfit
                     before, here = here, after
-                for k in range(planes):
-                    if half == 0:
-                        held[k] = results[k]
-                    else:
-                        place = (k, pl.ds(top, 16), pl.ds(at, LANES))
-                        residual_ref[place] = jnp.concatenate([held[k], results[k]], axis=0).astype(bf16)
                 for k, value in ((0, by_image), (1, plain)):
                     blocks[k, tile, pl.ds(pl.multiple_of(node * 8, 8), 8), :] = value
             return total

time: 89 us -> 89 us (level)
  no operation moved by 1% of the time
where the time goes in v6:
time: 89 us; the launch traced here: 88.6 us
  Pallas kernels  44.2 us (50%)
  starting transfers between devices  20 us (22%)
  blocking collectives  10.9 us (12%)
  waiting for transfers between devices  10.5 us (12%)
  local copies, waits for them, and re-layouts  2.2 us (2%)
    pallas_call x1, Pallas kernels, warp(): pl.pallas_call(warp_kernel, grid=(count + 1,), in_specs=[pl.BlockSpec((KN...  40.8 us
    all_to_all x1, blocking collectives, local(): depth_terms = lax.all_to_all(depth_terms, 'gy', 0, 0)  10.9 us
    all_to_all x1, starting transfers between devices, local(): depth_terms = lax.all_to_all(depth_terms, 'gy', 0, 0)  6.36 us
    ppermute x2, starting transfers between devices, shifted(): return lax.ppermute(part, axis, [(i, i + 1) for i in range(count - 1)])  6.35 us
    ppermute x2, waiting for transfers between devices, shifted(): return lax.ppermute(part, axis, [(i + 1, i) for i in range(count - 1)])  6.33 us
    ppermute x3, starting transfers between devices, local(): lax.ppermute(plane_terms, 'gz', [(i, (i + hop) % n_gz) for i in range(n_g...  4.62 us
    ppermute x3, waiting for transfers between devices, local(): lax.ppermute(plane_terms, 'gz', [(i, (i + hop) % n_gz) for i in range(n_g...  4.13 us
    ppermute x2, starting transfers between devices, shifted(): return lax.ppermute(part, axis, [(i + 1, i) for i in range(count - 1)])  2.72 us
  transfers between devices with their start and end apart: 8, of which 4 were waited for; matrix products, arithmetic and copies ran while one was open for 0% of the time, Pallas kernels for 2%

profile of v6, /device:TPU:0, one launch (start us, length us, event | category | flops | bytes accessed | tf_op | source)
XLA Modules:
  0.0 88.6 jit_solution(14336233343996372790)
XLA Ops:
  0.6 0.0 copy-start
  0.6 2.2 %copy-done = bf16[64,64,512]{2,1,0:T(8,128)(2,1)S(1)} copy-done((bf16[64,64,512]{2,1,0:T(8,128)(2,1)S(1)}, bf16[64,64,512]{2,1,0:T(8,128)(2,1)}, u32[]{:S(2)}) %copy-start) | copy-done | bytes 4194328
  2.8 0.0 copy-start.1
  2.8 0.7 columns.1
  3.5 5.1 %collective-permute-start = (bf16[64,128]{1,0:T(8,128)(2,1)S(1)}, bf16[64,128]{1,0:T(8,128)(2,1)S(1)}, u32[]{:S(2)}, u32[]{:S(2)}) collective-permute-start(bf16[64,128]{1,0:T(8,128)(2,1)S(1)} %get-tuple-element.17), channel_id=1, source_target_pairs={{0,1},{1,2},{2,3},{4,5},{5,6},{6,7},{8,9},{9,10},{10,11},{12,13},{... | collective-permute-start | bytes 49160 | tf_op jit(solution)/shard_map/ppermute | solution.py:105
  8.6 0.0 copy-start.2
  8.6 0.0 copy-start.3
  8.6 1.4 %collective-permute-start.1 = (bf16[64,128]{1,0:T(8,128)(2,1)S(1)}, bf16[64,128]{1,0:T(8,128)(2,1)S(1)}, u32[]{:S(2)}, u32[]{:S(2)}) collective-permute-start(bf16[64,128]{1,0:T(8,128)(2,1)S(1)} %get-tuple-element.18), channel_id=1, source_target_pairs={{1,0},{2,1},{3,2},{5,4},{6,5},{7,6},{9,8},{10,9},{11,10},{13,12},{... | collective-permute-start | bytes 49160 | tf_op jit(solution)/shard_map/ppermute | solution.py:104
  10.1 0.0 copy-done.1
  10.1 1.6 %squares.1 = (f32[4,512,128]{2,1,0:T(8,128)S(1)}, f32[64,512]{1,0:T(8,128)S(1)}, f32[64,512]{1,0:T(8,128)S(1)}) custom-call(bf16[64,64,512]{2,1,0:T(8,128)(2,1)S(1)} %copy-done.1, bf16[64,64,512]{2,1,0:T(8,128)(2,1)S(1)} %copy-done, bf16[64,64,512]{2,1,0:T(8,128)(2,1)S(1)} %copy-done), custom_call_target="tpu_custom_call" | custom-call | flops 6291456 | bytes 4194304 | tf_op jit(solution)/shard_map/squares/pallas_call | solution.py:130
  11.6 0.0 collective-permute-done.left_ref
  11.6 2.8 %collective-permute-done.1.right_ref = bf16[64,128]{1,0:T(8,128)(2,1)S(1)} collective-permute-done((bf16[64,128]{1,0:T(8,128)(2,1)S(1)}, bf16[64,128]{1,0:T(8,128)(2,1)S(1)}, u32[]{:S(2)}, u32[]{:S(2)}) %collective-permute-start.1) | collective-permute-done | bytes 16416 | tf_op jit(solution)/shard_map/ppermute | solution.py:104
  14.4 0.2 rows.1
  14.6 1.3 %collective-permute-start.2 = (bf16[64,640]{1,0:T(8,128)(2,1)S(1)}, bf16[64,640]{1,0:T(8,128)(2,1)S(1)}, u32[]{:S(2)}, u32[]{:S(2)}) collective-permute-start(bf16[64,640]{1,0:T(8,128)(2,1)S(1)} %get-tuple-element.21), channel_id=1, source_target_pairs={{0,4},{4,8},{8,12},{12,16},{16,20},{20,24},{24,28},{1,5},{5,9},{9,... | collective-permute-start | bytes 245768 | tf_op jit(solution)/shard_map/ppermute | solution.py:105
  15.9 1.3 %collective-permute-start.3 = (bf16[64,640]{1,0:T(8,128)(2,1)S(1)}, bf16[64,640]{1,0:T(8,128)(2,1)S(1)}, u32[]{:S(2)}, u32[]{:S(2)}) collective-permute-start(bf16[64,640]{1,0:T(8,128)(2,1)S(1)} %get-tuple-element.22), channel_id=1, source_target_pairs={{4,0},{8,4},{12,8},{16,12},{20,16},{24,20},{28,24},{5,1},{9,5},{13... | collective-permute-start | bytes 245768 | tf_op jit(solution)/shard_map/ppermute | solution.py:104
  17.2 0.0 collective-permute-done.2.low_ref
  17.2 3.6 %collective-permute-done.3.high_ref = bf16[64,640]{1,0:T(8,128)(2,1)S(1)} collective-permute-done((bf16[64,640]{1,0:T(8,128)(2,1)S(1)}, bf16[64,640]{1,0:T(8,128)(2,1)S(1)}, u32[]{:S(2)}, u32[]{:S(2)}) %collective-permute-start.3) | collective-permute-done | bytes 81952 | tf_op jit(solution)/shard_map/ppermute | solution.py:104
  20.8 0.0 copy-done.2
  20.8 0.0 copy-done.3
  20.8 40.8 %warp.1 = (bf16[64,64,512]{2,1,0:T(8,128)(2,1)}, f32[8,16,512]{2,1,0:T(8,128)}, f32[64,128]{1,0:T(8,128)S(1)}) custom-call(bf16[64,64,512]{2,1,0:T(8,128)(2,1)S(1)} %copy-done, bf16[64,64,512]{2,1,0:T(8,128)(2,1)S(1)} %copy-done.1, bf16[3,64,64,512]{3,2,1,0:T(8,128)(2,1)} %shift_ref.1, bf16[64,128]{1,0:T(8,128)(2,1)S(1)} %collective-permute-done.left_ref, ...), custom_call_target="tpu_custom_call" | custom-call | flops 125829120 | bytes 25165824 | tf_op jit(solution)/shard_map/warp/pallas_call | solution.py:323
  61.5 6.4 %all-to-all-start = ((f32[8,16,512]{2,1,0:T(8,128)}), f32[8,16,512]{2,1,0:T(8,128)S(1)}, u32[]{:S(2)}, u32[]{:S(2)}) async-start(f32[8,16,512]{2,1,0:T(8,128)} %get-tuple-element.25), calls=%async_computation | async-start | bytes 524288 | tf_op jit(solution)/shard_map/all_to_all | solution.py:417
  67.9 1.9 %collective-permute-start.6 = (f32[64,128]{1,0:T(8,128)S(1)}, f32[64,128]{1,0:T(8,128)S(1)}, u32[]{:S(2)}, u32[]{:S(2)}) collective-permute-start(f32[64,128]{1,0:T(8,128)S(1)} %get-tuple-element.26.refs_0_), channel_id=1, source_target_pairs={{0,3},{1,0},{2,1},{3,2},{4,7},{5,4},{6,5},{7,6},{8,11},{9,8},{10,9... | collective-permute-start | bytes 98312 | tf_op jit(solution)/shard_map/ppermute | solution.py:415
  69.8 1.1 %collective-permute-start.5 = (f32[64,128]{1,0:T(8,128)S(1)}, f32[64,128]{1,0:T(8,128)S(1)}, u32[]{:S(2)}, u32[]{:S(2)}) collective-permute-start(f32[64,128]{1,0:T(8,128)S(1)} %get-tuple-element.26.refs_0_), channel_id=1, source_target_pairs={{0,2},{1,3},{2,0},{3,1},{4,6},{5,7},{6,4},{7,5},{8,10},{9,11},{10,... | collective-permute-start | bytes 98312 | tf_op jit(solution)/shard_map/ppermute | solution.py:415
  70.9 1.6 %collective-permute-start.4 = (f32[64,128]{1,0:T(8,128)S(1)}, f32[64,128]{1,0:T(8,128)S(1)}, u32[]{:S(2)}, u32[]{:S(2)}) collective-permute-start(f32[64,128]{1,0:T(8,128)S(1)} %get-tuple-element.26.refs_0_), channel_id=1, source_target_pairs={{0,1},{1,2},{2,3},{3,0},{4,5},{5,6},{6,7},{7,4},{8,9},{9,10},{10,1... | collective-permute-start | bytes 98312 | tf_op jit(solution)/shard_map/ppermute | solution.py:415
  72.5 0.0 collective-permute-done.6.refs_3_
  72.5 2.3 %collective-permute-done.5.refs_2_ = f32[64,128]{1,0:T(8,128)S(1)} collective-permute-done((f32[64,128]{1,0:T(8,128)S(1)}, f32[64,128]{1,0:T(8,128)S(1)}, u32[]{:S(2)}, u32[]{:S(2)}) %collective-permute-start.5) | collective-permute-done | bytes 32800 | tf_op jit(solution)/shard_map/ppermute | solution.py:415
  74.8 1.8 %collective-permute-done.4.refs_1_ = f32[64,128]{1,0:T(8,128)S(1)} collective-permute-done((f32[64,128]{1,0:T(8,128)S(1)}, f32[64,128]{1,0:T(8,128)S(1)}, u32[]{:S(2)}, u32[]{:S(2)}) %collective-permute-start.4) | collective-permute-done | bytes 32800 | tf_op jit(solution)/shard_map/ppermute | solution.py:415
  76.7 0.0 all-to-all-done.depth_ref
  76.7 0.1 gather.1
  76.8 10.9 %all_to_all.10.depth_ref = f32[8,16,512]{2,1,0:T(8,128)S(1)} all-to-all(f32[8,16,512]{2,1,0:T(8,128)S(1)} %get-tuple-element.27), channel_id=1, replica_groups=mesh['gy'=8,'gz'=4] {'gy'}, dimensions={0} | all-to-all | bytes 524288 | tf_op jit(solution)/shard_map/all_to_all | solution.py:427
  87.7 0.9 %steps.1 = (f32[2,32,512]{2,1,0:T(8,128)}, f32[2,64,32]{2,1,0:T(8,128)}) custom-call(f32[8,16,512]{2,1,0:T(8,128)S(1)} %all_to_all.10.depth_ref, f32[64,128]{1,0:T(8,128)S(1)} %get-tuple-element.28.plane_ref), custom_call_target="tpu_custom_call" | custom-call | tf_op jit(solution)/shard_map/steps/pallas_call | solution.py:429
Async XLA Ops:
  0.6 2.2 %copy-start = (bf16[64,64,512]{2,1,0:T(8,128)(2,1)S(1)}, bf16[64,64,512]{2,1,0:T(8,128)(2,1)}, u32[]{:S(2)}) copy-start(bf16[64,64,512]{2,1,0:T(8,128)(2,1)} %cells_ref.1) | copy-start | bytes 12582916
  2.8 7.2 %copy-start.1 = (bf16[64,64,512]{2,1,0:T(8,128)(2,1)S(1)}, bf16[64,64,512]{2,1,0:T(8,128)(2,1)}, u32[]{:S(2)}) copy-start(bf16[64,64,512]{2,1,0:T(8,128)(2,1)} %image_ref.3) | copy-start | bytes 12582916
  3.5 8.1 %collective-permute-start = (bf16[64,128]{1,0:T(8,128)(2,1)S(1)}, bf16[64,128]{1,0:T(8,128)(2,1)S(1)}, u32[]{:S(2)}, u32[]{:S(2)}) collective-permute-start(bf16[64,128]{1,0:T(8,128)(2,1)S(1)} %get-tuple-element.17), channel_id=1, source_target_pairs={{0,1},{1,2},{2,3},{4,5},{5,6},{6,7},{8,9},{9,10},{10,11},{12,13},{... | collective-permute-start | bytes 49160 | tf_op jit(solution)/shard_map/ppermute | solution.py:105
  8.6 12.2 %copy-start.2 = (f32[2,32,512]{2,1,0:T(8,128)S(1)}, f32[2,32,512]{2,1,0:T(8,128)}, u32[]{:S(2)}) copy-start(f32[2,32,512]{2,1,0:T(8,128)} %depth_ref.1) | copy-start | bytes 393220
  8.6 12.1 %copy-start.3 = (f32[2,32,8,8]{1,3,2,0:T(8,128)S(1)}, f32[2,32,8,8]{1,3,2,0:T(8,128)}, u32[]{:S(2)}) copy-start(f32[2,32,8,8]{1,3,2,0:T(8,128)} %param.8) | copy-start | bytes 49156
  8.6 5.8 %collective-permute-start.1 = (bf16[64,128]{1,0:T(8,128)(2,1)S(1)}, bf16[64,128]{1,0:T(8,128)(2,1)S(1)}, u32[]{:S(2)}, u32[]{:S(2)}) collective-permute-start(bf16[64,128]{1,0:T(8,128)(2,1)S(1)} %get-tuple-element.18), channel_id=1, source_target_pairs={{1,0},{2,1},{3,2},{5,4},{6,5},{7,6},{9,8},{10,9},{11,10},{13,12},{... | collective-permute-start | bytes 49160 | tf_op jit(solution)/shard_map/ppermute | solution.py:104
  14.6 2.6 %collective-permute-start.2 = (bf16[64,640]{1,0:T(8,128)(2,1)S(1)}, bf16[64,640]{1,0:T(8,128)(2,1)S(1)}, u32[]{:S(2)}, u32[]{:S(2)}) collective-permute-start(bf16[64,640]{1,0:T(8,128)(2,1)S(1)} %get-tuple-element.21), channel_id=1, source_target_pairs={{0,4},{4,8},{8,12},{12,16},{16,20},{20,24},{24,28},{1,5},{5,9},{9,... | collective-permute-start | bytes 245768 | tf_op jit(solution)/shard_map/ppermute | solution.py:105
  15.9 4.9 %collective-permute-start.3 = (bf16[64,640]{1,0:T(8,128)(2,1)S(1)}, bf16[64,640]{1,0:T(8,128)(2,1)S(1)}, u32[]{:S(2)}, u32[]{:S(2)}) collective-permute-start(bf16[64,640]{1,0:T(8,128)(2,1)S(1)} %get-tuple-element.22), channel_id=1, source_target_pairs={{4,0},{8,4},{12,8},{16,12},{20,16},{24,20},{28,24},{5,1},{9,5},{13... | collective-permute-start | bytes 245768 | tf_op jit(solution)/shard_map/ppermute | solution.py:104
  61.5 15.1 %all-to-all-start = ((f32[8,16,512]{2,1,0:T(8,128)}), f32[8,16,512]{2,1,0:T(8,128)S(1)}, u32[]{:S(2)}, u32[]{:S(2)}) async-start(f32[8,16,512]{2,1,0:T(8,128)} %get-tuple-element.25), calls=%async_computation | async-start | bytes 524288 | tf_op jit(solution)/shard_map/all_to_all | solution.py:417
  67.9 4.6 %collective-permute-start.6 = (f32[64,128]{1,0:T(8,128)S(1)}, f32[64,128]{1,0:T(8,128)S(1)}, u32[]{:S(2)}, u32[]{:S(2)}) collective-permute-start(f32[64,128]{1,0:T(8,128)S(1)} %get-tuple-element.26.refs_0_), channel_id=1, source_target_pairs={{0,3},{1,0},{2,1},{3,2},{4,7},{5,4},{6,5},{7,6},{8,11},{9,8},{10,9... | collective-permute-start | bytes 98312 | tf_op jit(solution)/shard_map/ppermute | solution.py:415
  69.8 5.0 %collective-permute-start.5 = (f32[64,128]{1,0:T(8,128)S(1)}, f32[64,128]{1,0:T(8,128)S(1)}, u32[]{:S(2)}, u32[]{:S(2)}) collective-permute-start(f32[64,128]{1,0:T(8,128)S(1)} %get-tuple-element.26.refs_0_), channel_id=1, source_target_pairs={{0,2},{1,3},{2,0},{3,1},{4,6},{5,7},{6,4},{7,5},{8,10},{9,11},{10,... | collective-permute-start | bytes 98312 | tf_op jit(solution)/shard_map/ppermute | solution.py:415
  70.9 5.7 %collective-permute-start.4 = (f32[64,128]{1,0:T(8,128)S(1)}, f32[64,128]{1,0:T(8,128)S(1)}, u32[]{:S(2)}, u32[]{:S(2)}) collective-permute-start(f32[64,128]{1,0:T(8,128)S(1)} %get-tuple-element.26.refs_0_), channel_id=1, source_target_pairs={{0,1},{1,2},{2,3},{3,0},{4,5},{5,6},{6,7},{7,4},{8,9},{9,10},{10,1... | collective-permute-start | bytes 98312 | tf_op jit(solution)/shard_map/ppermute | solution.py:415

commit v7 on v6

--- a/solution.py
+++ b/solution.py
@@ -37,41 +37,32 @@
     return jnp.concatenate([jnp.sum(ref[t].reshape(rows // 8, 8, LANES), axis=1) for t in range(tiles)], axis=1)
 
 
-def grid_params():
-    return pltpu.CompilerParams(dimension_semantics=("arbitrary",), vmem_limit_bytes=40000000)
-
-
 def plain_params():
     return pltpu.CompilerParams(vmem_limit_bytes=32000000)
 
 
-def columns_kernel(near_ref, far_ref, first_ref, last_ref):
-    depth, rows = near_ref.shape[0:2]
+def columns_kernel(cells_ref, first_ref, last_ref):
+    depth, rows, width = cells_ref.shape
     lane = lax.broadcasted_iota(jnp.int32, (rows, LANES), 1)
     first = jnp.zeros((rows, LANES), f32)
     last = jnp.zeros((rows, LANES), f32)
     for x in range(depth):
-        first = jnp.where(lane == x, pltpu.roll(near_ref[x].astype(f32), x, 1), first)
-        last = jnp.where(lane == x, pltpu.roll(far_ref[x].astype(f32), (x + 1) % LANES, 1), last)
+        near = cells_ref[x, :, 0:LANES].astype(f32)
+        far = cells_ref[x, :, width - LANES : width].astype(f32)
+        first = jnp.where(lane == x, pltpu.roll(near, x, 1), first)
+        last = jnp.where(lane == x, pltpu.roll(far, (x + 1) % LANES, 1), last)
     first_ref[...] = first.astype(bf16)
     last_ref[...] = last.astype(bf16)
 
 
 def end_columns(cells):
-    depth, rows, width = cells.shape
-    tiles = width // LANES
+    rows = cells.shape[1]
     return pl.pallas_call(
         columns_kernel,
-        grid=(1,),
-        in_specs=[
-            pl.BlockSpec((depth, rows, LANES), lambda i: (0, 0, 0)),
-            pl.BlockSpec((depth, rows, LANES), lambda i: (0, 0, tiles - 1)),
-        ],
-        out_specs=[pl.BlockSpec((rows, LANES), lambda i: (0, 0))] * 2,
         out_shape=[jax.ShapeDtypeStruct((rows, LANES), bf16)] * 2,
-        compiler_params=grid_params(),
+        compiler_params=plain_params(),
         name="columns",
-    )(cells, cells)
+    )(cells)
 
 
 def rows_kernel(left_ref, right_ref, low_ref, high_ref, low_out, high_out):
@@ -105,60 +96,57 @@
     return lax.ppermute(part, axis, [(i, i + 1) for i in range(count - 1)])
 
 
-def squares_kernel(image_ref, top_ref, bottom_ref, sums, low_ref, high_ref):
-    step = pl.program_id(0)
-    planes, rows, width = image_ref.shape
+def squares_kernel(image_ref, cells_ref, sums, low_ref, high_ref):
+    depth, rows, width = image_ref.shape
     tiles = width // LANES
 
-    def one(tile, carry):
+    def one(t, carry):
+        block, tile = t // tiles, t % tiles
         at = pl.multiple_of(tile * LANES, LANES)
         for pair in range(rows // 16):
             total = jnp.zeros((16, LANES), f32)
-            for k in range(planes):
-                values = image_ref[k, 16 * pair : 16 * pair + 16, pl.ds(at, LANES)].astype(f32)
+            for k in range(KNOT):
+                values = image_ref[block * KNOT + k, 16 * pair : 16 * pair + 16, pl.ds(at, LANES)].astype(f32)
                 total = total + values * values
-            sums[tile, pl.ds(step * rows + 16 * pair, 16), :] = total
+            sums[tile, pl.ds(pl.multiple_of(block * rows + 16 * pair, 16), 16), :] = total
         return carry
 
-    lax.fori_loop(0, tiles, one, 0)
-    low_ref[...] = jnp.concatenate([top_ref[k].astype(f32)[0:1] for k in range(planes)], axis=0)
-    high_ref[...] = jnp.concatenate([bottom_ref[k].astype(f32)[15:16] for k in range(planes)], axis=0)
+    lax.fori_loop(0, depth // KNOT * tiles, one, 0)
+
+    def ends(block, carry):
+        x = pl.multiple_of(block * KNOT, KNOT)
+        low = [cells_ref[x + k, 0:16, :].astype(f32)[0:1] for k in range(KNOT)]
+        high = [cells_ref[x + k, rows - 16 : rows, :].astype(f32)[15:16] for k in range(KNOT)]
+        low_ref[pl.ds(x, KNOT), :] = jnp.concatenate(low, axis=0)
+        high_ref[pl.ds(x, KNOT), :] = jnp.concatenate(high, axis=0)
+        return carry
+
+    lax.fori_loop(0, depth // KNOT, ends, 0)
 
 
 def squares(image, cells):
     depth, rows, width = image.shape
     return pl.pallas_call(
         squares_kernel,
-        grid=(depth // KNOT,),
-        in_specs=[
-            pl.BlockSpec((KNOT, rows, width), lambda i: (i, 0, 0)),
-            pl.BlockSpec((KNOT, 16, width), lambda i: (i, 0, 0)),
-            pl.BlockSpec((KNOT, 16, width), lambda i: (i, rows // 16 - 1, 0)),
-        ],
-        out_specs=[
-            pl.BlockSpec((width // LANES, depth * rows // KNOT, LANES), lambda i: (0, 0, 0)),
-            pl.BlockSpec((KNOT, width), lambda i: (i, 0)),
-            pl.BlockSpec((KNOT, width), lambda i: (i, 0)),
-        ],
         out_shape=[
             jax.ShapeDtypeStruct((width // LANES, depth * rows // KNOT, LANES), f32),
             jax.ShapeDtypeStruct((depth, width), f32),
             jax.ShapeDtypeStruct((depth, width), f32),
         ],
-        compiler_params=grid_params(),
+        compiler_params=plain_params(),
         cost_estimate=pl.CostEstimate(flops=3 * image.size, bytes_accessed=2 * image.size, transcendentals=0),
         name="squares",
-    )(image, cells, cells)
+    )(image, cells)
 
 
 def warp_kernel(
-    cells_ref, image_ref, shift_ref, left_ref, right_ref, low_ref, high_ref, squares_ref, plane_ref, depth_ref,
-    residual_ref, depth_out, plane_out,
-    ahead_ref, here_ref, behind_ref, columns, field, blocks, energy, held,
+    cells_ref, image_ref, shift_hbm, left_ref, right_ref, low_ref, high_ref, squares_ref, plane_ref, depth_ref,
+    residual_hbm, depth_out, plane_out,
+    ahead_ref, here_ref, behind_ref, shift_ref, residual_ref, columns, field, blocks, energy, held, got, sent,
 ):
-    step = pl.program_id(0)
-    last = pl.num_programs(0) - 1
-    planes, rows, width = cells_ref.shape
+    depth, rows, width = cells_ref.shape
+    planes = KNOT
+    count = depth // planes
     nodes = rows // KNOT
     tiles = width // LANES
     window = (ahead_ref, here_ref, behind_ref)
@@ -166,6 +154,18 @@
     plane_rows = tiles * pitch
     block_rows = planes * plane_rows
 
+    def fetch(axis, n):
+        part = (axis, pl.ds(n * planes, planes))
+        return pltpu.make_async_copy(shift_hbm.at[part], shift_ref.at[part], got.at[axis, n])
+
+    def send(n):
+        part = pl.ds(n * planes, planes)
+        return pltpu.make_async_copy(residual_ref.at[part], residual_hbm.at[part], sent.at[n])
+
+    for n in range(count):
+        for axis in range(3):
+            fetch(axis, n).start()
+
     def store_row(plane, moved, k, row):
         for c in range(3):
             for tile in range(tiles):
@@ -176,27 +176,24 @@
         ahead = pltpu.roll(wide, wide.shape[1] - 1, 1) - wide
         return ahead, wide, pltpu.roll(ahead, 1, 1)
 
-    @pl.when(step == 0)
-    def _():
-        columns[0] = left_ref[...].astype(f32)
-        columns[1] = right_ref[...].astype(f32)
-        energy[...] = jnp.zeros_like(energy)
-        for c in range(3):
-            window[c][3 * block_rows - plane_rows : 3 * block_rows, :] = jnp.zeros((plane_rows, LANES), f32)
-        for k in range(2):
-            values = dot(plane_ref[k], depth_ref[k], ((1,), (0,)))
-            for tile in range(tiles):
-                field[k, tile] = values[:, tile * LANES : (tile + 1) * LANES]
-
-    @pl.when(step < last)
-    def _():
+    columns[0] = left_ref[...].astype(f32)
+    columns[1] = right_ref[...].astype(f32)
+    energy[...] = jnp.zeros_like(energy)
+    for c in range(3):
+        window[c][3 * block_rows - plane_rows : 3 * block_rows, :] = jnp.zeros((plane_rows, LANES), f32)
+    for k in range(2):
+        values = dot(plane_ref[k], depth_ref[k], ((1,), (0,)))
+        for tile in range(tiles):
+            field[k, tile] = values[:, tile * LANES : (tile + 1) * LANES]
+
+    def build(step):
         lane = lax.broadcasted_iota(jnp.int32, (16, LANES), 1)
         slot = (step % 3) * block_rows
 
         def one(k, carry):
             x = step * planes + k
             first = pl.multiple_of(slot + k * plane_rows, 8)
-            raw = cells_ref[k]
+            raw = cells_ref[x]
             right, left = columns[1], columns[0]
             for group in range(rows // 16):
                 mine = slice(16 * group, 16 * group + 16)
@@ -213,18 +210,27 @@
 
         lax.fori_loop(0, planes, one, 0)
         for source, row in ((low_ref, TOP - 1), (high_ref, TOP + rows)):
-            moved = differences(source[...].astype(f32))
+            some = source[pl.ds(pl.multiple_of(step * planes // 16 * 16, 16), 16), :].astype(f32)
+            moved = differences(jnp.where(step % 2 == 0, some[0:8], some[8:16]))
             for k in range(planes):
                 store_row(slot + k * plane_rows, moved, k, row)
 
-    @pl.when(step == last)
-    def _():
-        first = pl.multiple_of((step % 3) * block_rows, 8)
-        for c in range(3):
-            window[c][pl.ds(first, plane_rows), :] = jnp.zeros((plane_rows, LANES), f32)
-
-    @pl.when(step > 0)
-    def _():
+    build(0)
+
+    def block(step, carry):
+        @pl.when(step < count)
+        def _():
+            build(step)
+
+        @pl.when(step == count)
+        def _():
+            first = pl.multiple_of((step % 3) * block_rows, 8)
+            for c in range(3):
+                window[c][pl.ds(first, plane_rows), :] = jnp.zeros((plane_rows, LANES), f32)
+
+        for axis in range(3):
+            fetch(axis, step - 1).wait()
+
         mid = (step + 2) % 3
         first_rows = (
             jnp.where(mid == 0, 3, mid) * block_rows - plane_rows,
@@ -256,7 +262,7 @@
                 before, here = taps(0), taps(1)
                 for k in range(planes):
                     after = taps(k + 2)
-                    place = (k, pl.ds(top, 16), pl.ds(at, LANES))
+                    place = ((step - 1) * planes + k, pl.ds(top, 16), pl.ds(at, LANES))
                     sx, sy, sz = (shift_ref[(axis,) + place].astype(f32)[mine] for axis in range(3))
                     image = image_ref[place].astype(f32)[mine]
                     px, py, pz = sx > 0, sy > 0, sz > 0
@@ -288,58 +294,41 @@
 
         energy[...] = lax.fori_loop(0, (rows // 16) * tiles, one, energy[...])
 
-    @pl.when(step == last)
-    def _():
-        parts = depth_out.shape[0]
-        share = RANK // parts
-        sums = [joined(blocks.at[k]) for k in range(2)]
-        kinds = [split_dot(plane_ref[k], sums[k], 0) for k in range(2)]
-        squared = joined(squares_ref)
-        cells = jnp.full(squared.shape, float(KNOT * KNOT), f32)
-        second = plane_ref[1]
-        kinds = kinds + [split_dot(plane_ref[0] * plane_ref[0], squared, 0), split_dot(second * second, cells, 0)]
-        for p in range(parts):
-            for k in range(4):
-                depth_out[p, k * share : (k + 1) * share, :] = kinds[k][p * share : (p + 1) * share]
-        local = jnp.sum(energy[...])
-        kinds = [split_dot(sums[k], depth_ref[k], 1) for k in range(2)]
-        second = depth_ref[1]
-        kinds = kinds + [split_dot(squared, depth_ref[0] * depth_ref[0], 1), split_dot(cells, second * second, 1)]
+        send(step - 1).start()
+        return carry
+
+    lax.fori_loop(1, count + 1, block, 0)
+    for n in range(count):
+        send(n).wait()
+    parts = depth_out.shape[0]
+    share = RANK // parts
+    sums = [joined(blocks.at[k]) for k in range(2)]
+    kinds = [split_dot(plane_ref[k], sums[k], 0) for k in range(2)]
+    squared = joined(squares_ref)
+    cells = jnp.full(squared.shape, float(KNOT * KNOT), f32)
+    second = plane_ref[1]
+    kinds = kinds + [split_dot(plane_ref[0] * plane_ref[0], squared, 0), split_dot(second * second, cells, 0)]
+    for p in range(parts):
         for k in range(4):
-            plane_out[:, k * RANK : (k + 1) * RANK] = kinds[k]
-        count = plane_out.shape[0]
-        plane_out[count // 2 :, 3 * RANK :] = jnp.full((count // 2, RANK), local, f32)
+            depth_out[p, k * share : (k + 1) * share, :] = kinds[k][p * share : (p + 1) * share]
+    local = jnp.sum(energy[...])
+    kinds = [split_dot(sums[k], depth_ref[k], 1) for k in range(2)]
+    second = depth_ref[1]
+    kinds = kinds + [split_dot(squared, depth_ref[0] * depth_ref[0], 1), split_dot(cells, second * second, 1)]
+    for k in range(4):
+        plane_out[:, k * RANK : (k + 1) * RANK] = kinds[k]
+    count = plane_out.shape[0]
+    plane_out[count // 2 :, 3 * RANK :] = jnp.full((count // 2, RANK), local, f32)
 
 
 def warp(cells, image, shift, left, right, low, high, squared, plane, depth_factors, parts):
     depth, rows, width = cells.shape
     nodes = plane.shape[1]
     tiles = width // LANES
-    count = depth // KNOT
-    behind = lambda i: (jnp.maximum(i - 1, 0), 0, 0)
-    ahead = lambda i: (jnp.minimum(i, count - 1), 0, 0)
-    flat = lambda i: (0, 0)
-    whole = lambda i: (0, 0, 0)
     return pl.pallas_call(
         warp_kernel,
-        grid=(count + 1,),
-        in_specs=[
-            pl.BlockSpec((KNOT, rows, width), ahead),
-            pl.BlockSpec((KNOT, rows, width), behind),
-            pl.BlockSpec((3, KNOT, rows, width), lambda i: (0, jnp.maximum(i - 1, 0), 0, 0)),
-            pl.BlockSpec(left.shape, flat),
-            pl.BlockSpec(right.shape, flat),
-            pl.BlockSpec((KNOT, low.shape[1]), lambda i: (jnp.minimum(i, count - 1), 0)),
-            pl.BlockSpec((KNOT, high.shape[1]), lambda i: (jnp.minimum(i, count - 1), 0)),
-            pl.BlockSpec(squared.shape, whole),
-            pl.BlockSpec(plane.shape, whole),
-            pl.BlockSpec(depth_factors.shape, whole),
-        ],
-        out_specs=[
-            pl.BlockSpec((KNOT, rows, width), behind),
-            pl.BlockSpec((parts, 4 * RANK // parts, width), whole),
-            pl.BlockSpec((nodes, 4 * RANK), flat),
-        ],
+        in_specs=[pl.BlockSpec(memory_space=pltpu.HBM if n == 2 else pltpu.VMEM) for n in range(10)],
+        out_specs=[pl.BlockSpec(memory_space=pltpu.HBM if n == 0 else pltpu.VMEM) for n in range(3)],
         out_shape=[
             jax.ShapeDtypeStruct(cells.shape, bf16),
             jax.ShapeDtypeStruct((parts, 4 * RANK // parts, width), f32),
@@ -347,13 +336,17 @@
         ],
         scratch_shapes=[
             *[pltpu.VMEM((3 * KNOT * tiles * (rows + 2 * TOP), LANES), f32)] * 3,
+            pltpu.VMEM(shift.shape, bf16),
+            pltpu.VMEM(cells.shape, bf16),
             pltpu.VMEM((2, rows, LANES), f32),
             pltpu.VMEM((2, tiles, nodes, LANES), f32),
             pltpu.VMEM((2, tiles, 8 * nodes, LANES), f32),
             pltpu.VMEM((8, LANES), f32),
             pltpu.VMEM((KNOT, 8, LANES), f32),
+            pltpu.SemaphoreType.DMA((3, depth // KNOT)),
+            pltpu.SemaphoreType.DMA((depth // KNOT,)),
         ],
-        compiler_params=grid_params(),
+        compiler_params=plain_params(),
         cost_estimate=pl.CostEstimate(flops=60 * cells.size, bytes_accessed=12 * cells.size, transcendentals=0),
         name="warp",
     )(cells, image, shift, left, right, low, high, squared, plane, depth_factors)

time: 89 us -> 93.6 us (1.052)
  local copies, waits for them, and re-layouts: 2.2 us -> 6.78 us
    unnamed x8 -> x12, local copies, waits for them, and re-layouts: 2.2 us -> 6.78 us
where the time goes in v7:
time: 93.6 us; the launch traced here: 93.2 us
  Pallas kernels  43.9 us (47%)
  starting transfers between devices  20.2 us (22%)
  blocking collectives  10.9 us (12%)
  waiting for transfers between devices  10.6 us (11%)
  local copies, waits for them, and re-layouts  6.78 us (7%)
    pallas_call x1, Pallas kernels, warp(): pl.pallas_call(warp_kernel, in_specs=[pl.BlockSpec(memory_space=pltpu.HBM...  40.7 us
    all_to_all x1, blocking collectives, local(): depth_terms = lax.all_to_all(depth_terms, 'gy', 0, 0)  10.9 us
    unnamed x12, local copies, waits for them, and re-layouts  6.78 us
    ppermute x2, waiting for transfers between devices, shifted(): return lax.ppermute(part, axis, [(i + 1, i) for i in range(count - 1)])  6.45 us
    all_to_all x1, starting transfers between devices, local(): depth_terms = lax.all_to_all(depth_terms, 'gy', 0, 0)  6.37 us
    ppermute x2, starting transfers between devices, shifted(): return lax.ppermute(part, axis, [(i, i + 1) for i in range(count - 1)])  6.35 us
    ppermute x3, starting transfers between devices, local(): lax.ppermute(plane_terms, 'gz', [(i, (i + hop) % n_gz) for i in range(n_g...  4.62 us
    ppermute x3, waiting for transfers between devices, local(): lax.ppermute(plane_terms, 'gz', [(i, (i + hop) % n_gz) for i in range(n_g...  4.13 us
  transfers between devices with their start and end apart: 8, of which 4 were waited for; matrix products, arithmetic and copies ran while one was open for 0% of the time, Pallas kernels for 2%

profile of v7, /device:TPU:0, one launch (start us, length us, event | category | flops | bytes accessed | tf_op | source)
XLA Modules:
  0.0 93.2 jit_solution(13036592819332810323)
XLA Ops:
  0.6 0.0 copy-start
  0.6 2.2 %copy-done = bf16[64,64,512]{2,1,0:T(8,128)(2,1)S(1)} copy-done((bf16[64,64,512]{2,1,0:T(8,128)(2,1)S(1)}, bf16[64,64,512]{2,1,0:T(8,128)(2,1)}, u32[]{:S(2)}) %copy-start) | copy-done | bytes 4194328
  2.8 0.0 copy-start.2
  2.8 0.6 columns.1
  3.5 5.1 %collective-permute-start = (bf16[64,128]{1,0:T(8,128)(2,1)S(1)}, bf16[64,128]{1,0:T(8,128)(2,1)S(1)}, u32[]{:S(2)}, u32[]{:S(2)}) collective-permute-start(bf16[64,128]{1,0:T(8,128)(2,1)S(1)} %get-tuple-element.17), channel_id=1, source_target_pairs={{0,1},{1,2},{2,3},{4,5},{5,6},{6,7},{8,9},{9,10},{10,11},{12,13},{... | collective-permute-start | bytes 49160 | tf_op jit(solution)/shard_map/ppermute | solution.py:96
  8.5 0.0 copy-start.1
  8.5 0.0 copy-start.4
  8.5 0.0 copy-start.5
  8.6 1.6 %collective-permute-start.1 = (bf16[64,128]{1,0:T(8,128)(2,1)S(1)}, bf16[64,128]{1,0:T(8,128)(2,1)S(1)}, u32[]{:S(2)}, u32[]{:S(2)}) collective-permute-start(bf16[64,128]{1,0:T(8,128)(2,1)S(1)} %get-tuple-element.18), channel_id=1, source_target_pairs={{1,0},{2,1},{3,2},{5,4},{6,5},{7,6},{9,8},{10,9},{11,10},{13,12},{... | collective-permute-start | bytes 49160 | tf_op jit(solution)/shard_map/ppermute | solution.py:95
  10.1 0.0 copy-done.2
  10.1 1.4 %squares.1 = (f32[4,512,128]{2,1,0:T(8,128)S(1)}, f32[64,512]{1,0:T(8,128)S(1)}, f32[64,512]{1,0:T(8,128)S(1)}) custom-call(bf16[64,64,512]{2,1,0:T(8,128)(2,1)S(1)} %copy-done.2, bf16[64,64,512]{2,1,0:T(8,128)(2,1)S(1)} %copy-done), custom_call_target="tpu_custom_call" | custom-call | flops 6291456 | bytes 4194304 | tf_op jit(solution)/shard_map/squares/pallas_call | solution.py:129
  11.6 0.0 collective-permute-done.left_ref
  11.6 2.9 %collective-permute-done.1.right_ref = bf16[64,128]{1,0:T(8,128)(2,1)S(1)} collective-permute-done((bf16[64,128]{1,0:T(8,128)(2,1)S(1)}, bf16[64,128]{1,0:T(8,128)(2,1)S(1)}, u32[]{:S(2)}, u32[]{:S(2)}) %collective-permute-start.1) | collective-permute-done | bytes 16416 | tf_op jit(solution)/shard_map/ppermute | solution.py:95
  14.5 0.2 rows.1
  14.6 1.3 %collective-permute-start.2 = (bf16[64,640]{1,0:T(8,128)(2,1)S(1)}, bf16[64,640]{1,0:T(8,128)(2,1)S(1)}, u32[]{:S(2)}, u32[]{:S(2)}) collective-permute-start(bf16[64,640]{1,0:T(8,128)(2,1)S(1)} %get-tuple-element.21), channel_id=1, source_target_pairs={{0,4},{4,8},{8,12},{12,16},{16,20},{20,24},{24,28},{1,5},{5,9},{9,... | collective-permute-start | bytes 245768 | tf_op jit(solution)/shard_map/ppermute | solution.py:96
  15.9 1.3 %collective-permute-start.3 = (bf16[64,640]{1,0:T(8,128)(2,1)S(1)}, bf16[64,640]{1,0:T(8,128)(2,1)S(1)}, u32[]{:S(2)}, u32[]{:S(2)}) collective-permute-start(bf16[64,640]{1,0:T(8,128)(2,1)S(1)} %get-tuple-element.22), channel_id=1, source_target_pairs={{4,0},{8,4},{12,8},{16,12},{20,16},{24,20},{28,24},{5,1},{9,5},{13... | collective-permute-start | bytes 245768 | tf_op jit(solution)/shard_map/ppermute | solution.py:95
  17.2 0.0 collective-permute-done.2.low_ref
  17.2 3.6 %collective-permute-done.3.high_ref = bf16[64,640]{1,0:T(8,128)(2,1)S(1)} collective-permute-done((bf16[64,640]{1,0:T(8,128)(2,1)S(1)}, bf16[64,640]{1,0:T(8,128)(2,1)S(1)}, u32[]{:S(2)}, u32[]{:S(2)}) %collective-permute-start.3) | collective-permute-done | bytes 81952 | tf_op jit(solution)/shard_map/ppermute | solution.py:95
  20.8 0.0 copy-done.1
  20.8 0.0 copy-done.4
  20.8 0.0 copy-done.5
  20.8 0.0 copy-start.3
  20.8 4.6 %copy-done.3 = bf16[3,64,64,512]{3,2,1,0:T(8,128)(2,1)S(1)} copy-done((bf16[3,64,64,512]{3,2,1,0:T(8,128)(2,1)S(1)}, bf16[3,64,64,512]{3,2,1,0:T(8,128)(2,1)}, u32[]{:S(2)}) %copy-start.3) | copy-done | bytes 12582936
  25.4 40.7 %warp.1 = (bf16[64,64,512]{2,1,0:T(8,128)(2,1)}, f32[8,16,512]{2,1,0:T(8,128)}, f32[64,128]{1,0:T(8,128)S(1)}) custom-call(bf16[64,64,512]{2,1,0:T(8,128)(2,1)S(1)} %copy-done.1, bf16[64,64,512]{2,1,0:T(8,128)(2,1)S(1)} %copy-done.2, bf16[3,64,64,512]{3,2,1,0:T(8,128)(2,1)S(1)} %copy-done.3, bf16[64,128]{1,0:T(8,128)(2,1)S(1)} %collective-permute-done.left_ref, ...), custom_call_target="tpu_custom_call" | custom-call | flops 125829120 | bytes 25165824 | tf_op jit(solution)/shard_map/warp/pallas_call | solution.py:328
  66.1 6.4 %all-to-all-start = ((f32[8,16,512]{2,1,0:T(8,128)}), f32[8,16,512]{2,1,0:T(8,128)S(1)}, u32[]{:S(2)}, u32[]{:S(2)}) async-start(f32[8,16,512]{2,1,0:T(8,128)} %get-tuple-element.25), calls=%async_computation | async-start | bytes 524288 | tf_op jit(solution)/shard_map/all_to_all | solution.py:410
  72.5 1.8 %collective-permute-start.6 = (f32[64,128]{1,0:T(8,128)S(1)}, f32[64,128]{1,0:T(8,128)S(1)}, u32[]{:S(2)}, u32[]{:S(2)}) collective-permute-start(f32[64,128]{1,0:T(8,128)S(1)} %get-tuple-element.26.refs_0_), channel_id=1, source_target_pairs={{0,3},{1,0},{2,1},{3,2},{4,7},{5,4},{6,5},{7,6},{8,11},{9,8},{10,9... | collective-permute-start | bytes 98312 | tf_op jit(solution)/shard_map/ppermute | solution.py:408
  74.3 1.2 %collective-permute-start.5 = (f32[64,128]{1,0:T(8,128)S(1)}, f32[64,128]{1,0:T(8,128)S(1)}, u32[]{:S(2)}, u32[]{:S(2)}) collective-permute-start(f32[64,128]{1,0:T(8,128)S(1)} %get-tuple-element.26.refs_0_), channel_id=1, source_target_pairs={{0,2},{1,3},{2,0},{3,1},{4,6},{5,7},{6,4},{7,5},{8,10},{9,11},{10,... | collective-permute-start | bytes 98312 | tf_op jit(solution)/shard_map/ppermute | solution.py:408
  75.5 1.6 %collective-permute-start.4 = (f32[64,128]{1,0:T(8,128)S(1)}, f32[64,128]{1,0:T(8,128)S(1)}, u32[]{:S(2)}, u32[]{:S(2)}) collective-permute-start(f32[64,128]{1,0:T(8,128)S(1)} %get-tuple-element.26.refs_0_), channel_id=1, source_target_pairs={{0,1},{1,2},{2,3},{3,0},{4,5},{5,6},{6,7},{7,4},{8,9},{9,10},{10,1... | collective-permute-start | bytes 98312 | tf_op jit(solution)/shard_map/ppermute | solution.py:408
  77.1 0.0 collective-permute-done.6.refs_3_
  77.1 2.3 %collective-permute-done.5.refs_2_ = f32[64,128]{1,0:T(8,128)S(1)} collective-permute-done((f32[64,128]{1,0:T(8,128)S(1)}, f32[64,128]{1,0:T(8,128)S(1)}, u32[]{:S(2)}, u32[]{:S(2)}) %collective-permute-start.5) | collective-permute-done | bytes 32800 | tf_op jit(solution)/shard_map/ppermute | solution.py:408
  79.3 1.9 %collective-permute-done.4.refs_1_ = f32[64,128]{1,0:T(8,128)S(1)} collective-permute-done((f32[64,128]{1,0:T(8,128)S(1)}, f32[64,128]{1,0:T(8,128)S(1)}, u32[]{:S(2)}, u32[]{:S(2)}) %collective-permute-start.4) | collective-permute-done | bytes 32800 | tf_op jit(solution)/shard_map/ppermute | solution.py:408
  81.2 0.0 all-to-all-done.depth_ref
  81.2 0.1 gather.1
  81.4 10.9 %all_to_all.10.depth_ref = f32[8,16,512]{2,1,0:T(8,128)S(1)} all-to-all(f32[8,16,512]{2,1,0:T(8,128)S(1)} %get-tuple-element.27), channel_id=1, replica_groups=mesh['gy'=8,'gz'=4] {'gy'}, dimensions={0} | all-to-all | bytes 524288 | tf_op jit(solution)/shard_map/all_to_all | solution.py:420
  92.3 0.9 steps.1
Async XLA Ops:
  0.6 2.2 %copy-start = (bf16[64,64,512]{2,1,0:T(8,128)(2,1)S(1)}, bf16[64,64,512]{2,1,0:T(8,128)(2,1)}, u32[]{:S(2)}) copy-start(bf16[64,64,512]{2,1,0:T(8,128)(2,1)} %cells_ref.5) | copy-start | bytes 12582916
  2.8 7.3 %copy-start.2 = (bf16[64,64,512]{2,1,0:T(8,128)(2,1)S(1)}, bf16[64,64,512]{2,1,0:T(8,128)(2,1)}, u32[]{:S(2)}) copy-start(bf16[64,64,512]{2,1,0:T(8,128)(2,1)} %image_ref.3) | copy-start | bytes 12582916
  3.5 8.1 %collective-permute-start = (bf16[64,128]{1,0:T(8,128)(2,1)S(1)}, bf16[64,128]{1,0:T(8,128)(2,1)S(1)}, u32[]{:S(2)}, u32[]{:S(2)}) collective-permute-start(bf16[64,128]{1,0:T(8,128)(2,1)S(1)} %get-tuple-element.17), channel_id=1, source_target_pairs={{0,1},{1,2},{2,3},{4,5},{5,6},{6,7},{8,9},{9,10},{10,11},{12,13},{... | collective-permute-start | bytes 49160 | tf_op jit(solution)/shard_map/ppermute | solution.py:96
  8.5 12.3 %copy-start.1 = (bf16[64,64,512]{2,1,0:T(8,128)(2,1)S(1)}, bf16[64,64,512]{2,1,0:T(8,128)(2,1)}, u32[]{:S(2)}) copy-start(bf16[64,64,512]{2,1,0:T(8,128)(2,1)} %cells_ref.5) | copy-start | bytes 12582916
  8.5 12.3 %copy-start.4 = (f32[2,32,512]{2,1,0:T(8,128)S(1)}, f32[2,32,512]{2,1,0:T(8,128)}, u32[]{:S(2)}) copy-start(f32[2,32,512]{2,1,0:T(8,128)} %depth_ref.1) | copy-start | bytes 393220
  8.5 12.3 %copy-start.5 = (f32[2,32,8,8]{1,3,2,0:T(8,128)S(1)}, f32[2,32,8,8]{1,3,2,0:T(8,128)}, u32[]{:S(2)}) copy-start(f32[2,32,8,8]{1,3,2,0:T(8,128)} %param.8) | copy-start | bytes 49156
  8.6 5.9 %collective-permute-start.1 = (bf16[64,128]{1,0:T(8,128)(2,1)S(1)}, bf16[64,128]{1,0:T(8,128)(2,1)S(1)}, u32[]{:S(2)}, u32[]{:S(2)}) collective-permute-start(bf16[64,128]{1,0:T(8,128)(2,1)S(1)} %get-tuple-element.18), channel_id=1, source_target_pairs={{1,0},{2,1},{3,2},{5,4},{6,5},{7,6},{9,8},{10,9},{11,10},{13,12},{... | collective-permute-start | bytes 49160 | tf_op jit(solution)/shard_map/ppermute | solution.py:95
  14.6 2.6 %collective-permute-start.2 = (bf16[64,640]{1,0:T(8,128)(2,1)S(1)}, bf16[64,640]{1,0:T(8,128)(2,1)S(1)}, u32[]{:S(2)}, u32[]{:S(2)}) collective-permute-start(bf16[64,640]{1,0:T(8,128)(2,1)S(1)} %get-tuple-element.21), channel_id=1, source_target_pairs={{0,4},{4,8},{8,12},{12,16},{16,20},{20,24},{24,28},{1,5},{5,9},{9,... | collective-permute-start | bytes 245768 | tf_op jit(solution)/shard_map/ppermute | solution.py:96
  15.9 4.9 %collective-permute-start.3 = (bf16[64,640]{1,0:T(8,128)(2,1)S(1)}, bf16[64,640]{1,0:T(8,128)(2,1)S(1)}, u32[]{:S(2)}, u32[]{:S(2)}) collective-permute-start(bf16[64,640]{1,0:T(8,128)(2,1)S(1)} %get-tuple-element.22), channel_id=1, source_target_pairs={{4,0},{8,4},{12,8},{16,12},{20,16},{24,20},{28,24},{5,1},{9,5},{13... | collective-permute-start | bytes 245768 | tf_op jit(solution)/shard_map/ppermute | solution.py:95
  20.8 4.6 %copy-start.3 = (bf16[3,64,64,512]{3,2,1,0:T(8,128)(2,1)S(1)}, bf16[3,64,64,512]{3,2,1,0:T(8,128)(2,1)}, u32[]{:S(2)}) copy-start(bf16[3,64,64,512]{3,2,1,0:T(8,128)(2,1)} %shift_hbm.1) | copy-start | bytes 37748740
  66.1 15.1 %all-to-all-start = ((f32[8,16,512]{2,1,0:T(8,128)}), f32[8,16,512]{2,1,0:T(8,128)S(1)}, u32[]{:S(2)}, u32[]{:S(2)}) async-start(f32[8,16,512]{2,1,0:T(8,128)} %get-tuple-element.25), calls=%async_computation | async-start | bytes 524288 | tf_op jit(solution)/shard_map/all_to_all | solution.py:410
  72.5 4.6 %collective-permute-start.6 = (f32[64,128]{1,0:T(8,128)S(1)}, f32[64,128]{1,0:T(8,128)S(1)}, u32[]{:S(2)}, u32[]{:S(2)}) collective-permute-start(f32[64,128]{1,0:T(8,128)S(1)} %get-tuple-element.26.refs_0_), channel_id=1, source_target_pairs={{0,3},{1,0},{2,1},{3,2},{4,7},{5,4},{6,5},{7,6},{8,11},{9,8},{10,9... | collective-permute-start | bytes 98312 | tf_op jit(solution)/shard_map/ppermute | solution.py:408
  74.3 5.1 %collective-permute-start.5 = (f32[64,128]{1,0:T(8,128)S(1)}, f32[64,128]{1,0:T(8,128)S(1)}, u32[]{:S(2)}, u32[]{:S(2)}) collective-permute-start(f32[64,128]{1,0:T(8,128)S(1)} %get-tuple-element.26.refs_0_), channel_id=1, source_target_pairs={{0,2},{1,3},{2,0},{3,1},{4,6},{5,7},{6,4},{7,5},{8,10},{9,11},{10,... | collective-permute-start | bytes 98312 | tf_op jit(solution)/shard_map/ppermute | solution.py:408
  75.5 5.7 %collective-permute-start.4 = (f32[64,128]{1,0:T(8,128)S(1)}, f32[64,128]{1,0:T(8,128)S(1)}, u32[]{:S(2)}, u32[]{:S(2)}) collective-permute-start(f32[64,128]{1,0:T(8,128)S(1)} %get-tuple-element.26.refs_0_), channel_id=1, source_target_pairs={{0,1},{1,2},{2,3},{3,0},{4,5},{5,6},{6,7},{7,4},{8,9},{9,10},{10,1... | collective-permute-start | bytes 98312 | tf_op jit(solution)/shard_map/ppermute | solution.py:408

commit v8 on v6

--- a/solution.py
+++ b/solution.py
@@ -33,8 +33,7 @@
 
 
 def joined(ref):
-    tiles, rows = ref.shape[0:2]
-    return jnp.concatenate([jnp.sum(ref[t].reshape(rows // 8, 8, LANES), axis=1) for t in range(tiles)], axis=1)
+    return jnp.concatenate([ref[tile] for tile in range(ref.shape[0])], axis=1)
 
 
 def grid_params():
@@ -45,33 +44,28 @@
     return pltpu.CompilerParams(vmem_limit_bytes=32000000)
 
 
-def columns_kernel(near_ref, far_ref, first_ref, last_ref):
-    depth, rows = near_ref.shape[0:2]
+def columns_kernel(cells_ref, first_ref, last_ref):
+    depth, rows, width = cells_ref.shape
     lane = lax.broadcasted_iota(jnp.int32, (rows, LANES), 1)
     first = jnp.zeros((rows, LANES), f32)
     last = jnp.zeros((rows, LANES), f32)
     for x in range(depth):
-        first = jnp.where(lane == x, pltpu.roll(near_ref[x].astype(f32), x, 1), first)
-        last = jnp.where(lane == x, pltpu.roll(far_ref[x].astype(f32), (x + 1) % LANES, 1), last)
+        near = cells_ref[x, :, 0:LANES].astype(f32)
+        far = cells_ref[x, :, width - LANES : width].astype(f32)
+        first = jnp.where(lane == x, pltpu.roll(near, x, 1), first)
+        last = jnp.where(lane == x, pltpu.roll(far, (x + 1) % LANES, 1), last)
     first_ref[...] = first.astype(bf16)
     last_ref[...] = last.astype(bf16)
 
 
 def end_columns(cells):
-    depth, rows, width = cells.shape
-    tiles = width // LANES
+    rows = cells.shape[1]
     return pl.pallas_call(
         columns_kernel,
-        grid=(1,),
-        in_specs=[
-            pl.BlockSpec((depth, rows, LANES), lambda i: (0, 0, 0)),
-            pl.BlockSpec((depth, rows, LANES), lambda i: (0, 0, tiles - 1)),
-        ],
-        out_specs=[pl.BlockSpec((rows, LANES), lambda i: (0, 0))] * 2,
         out_shape=[jax.ShapeDtypeStruct((rows, LANES), bf16)] * 2,
-        compiler_params=grid_params(),
+        compiler_params=plain_params(),
         name="columns",
-    )(cells, cells)
+    )(cells)
 
 
 def rows_kernel(left_ref, right_ref, low_ref, high_ref, low_out, high_out):
@@ -105,56 +99,87 @@
     return lax.ppermute(part, axis, [(i, i + 1) for i in range(count - 1)])
 
 
-def squares_kernel(image_ref, top_ref, bottom_ref, sums, low_ref, high_ref):
-    step = pl.program_id(0)
-    planes, rows, width = image_ref.shape
+def squares_kernel(image_ref, cells_ref, sums, low_ref, high_ref):
+    depth, rows, width = image_ref.shape
     tiles = width // LANES
 
-    def one(tile, carry):
+    def one(t, carry):
+        block, tile = t // tiles, t % tiles
         at = pl.multiple_of(tile * LANES, LANES)
         for pair in range(rows // 16):
             total = jnp.zeros((16, LANES), f32)
-            for k in range(planes):
-                values = image_ref[k, 16 * pair : 16 * pair + 16, pl.ds(at, LANES)].astype(f32)
+            for k in range(KNOT):
+                values = image_ref[block * KNOT + k, 16 * pair : 16 * pair + 16, pl.ds(at, LANES)].astype(f32)
                 total = total + values * values
-            sums[tile, pl.ds(step * rows + 16 * pair, 16), :] = total
+            for half in range(2):
+                row = block * (rows // KNOT) + 2 * pair + half
+                sums[tile, pl.ds(row, 1), :] = jnp.sum(total[8 * half : 8 * half + 8], axis=0, keepdims=True)
         return carry
 
-    lax.fori_loop(0, tiles, one, 0)
-    low_ref[...] = jnp.concatenate([top_ref[k].astype(f32)[0:1] for k in range(planes)], axis=0)
-    high_ref[...] = jnp.concatenate([bottom_ref[k].astype(f32)[15:16] for k in range(planes)], axis=0)
+    lax.fori_loop(0, depth // KNOT * tiles, one, 0)
+
+    def ends(block, carry):
+        x = pl.multiple_of(block * KNOT, KNOT)
+        low = [cells_ref[x + k, 0:16, :].astype(f32)[0:1] for k in range(KNOT)]
+        high = [cells_ref[x + k, rows - 16 : rows, :].astype(f32)[15:16] for k in range(KNOT)]
+        low_ref[pl.ds(x, KNOT), :] = jnp.concatenate(low, axis=0)
+        high_ref[pl.ds(x, KNOT), :] = jnp.concatenate(high, axis=0)
+        return carry
+
+    lax.fori_loop(0, depth // KNOT, ends, 0)
 
 
 def squares(image, cells):
     depth, rows, width = image.shape
     return pl.pallas_call(
         squares_kernel,
-        grid=(depth // KNOT,),
-        in_specs=[
-            pl.BlockSpec((KNOT, rows, width), lambda i: (i, 0, 0)),
-            pl.BlockSpec((KNOT, 16, width), lambda i: (i, 0, 0)),
-            pl.BlockSpec((KNOT, 16, width), lambda i: (i, rows // 16 - 1, 0)),
-        ],
-        out_specs=[
-            pl.BlockSpec((width // LANES, depth * rows // KNOT, LANES), lambda i: (0, 0, 0)),
-            pl.BlockSpec((KNOT, width), lambda i: (i, 0)),
-            pl.BlockSpec((KNOT, width), lambda i: (i, 0)),
-        ],
         out_shape=[
-            jax.ShapeDtypeStruct((width // LANES, depth * rows // KNOT, LANES), f32),
+            jax.ShapeDtypeStruct((width // LANES, depth * rows // KNOT**2, LANES), f32),
             jax.ShapeDtypeStruct((depth, width), f32),
             jax.ShapeDtypeStruct((depth, width), f32),
         ],
-        compiler_params=grid_params(),
+        compiler_params=plain_params(),
         cost_estimate=pl.CostEstimate(flops=3 * image.size, bytes_accessed=2 * image.size, transcendentals=0),
         name="squares",
-    )(image, cells, cells)
+    )(image, cells)
+
+
+def terms_kernel(sums, plane_ref, depth_ref, field_ref, diag_depth_ref, diag_plane_ref):
+    tiles = sums.shape[0]
+    for k in range(2):
+        field = dot(plane_ref[k], depth_ref[k], ((1,), (0,)))
+        for tile in range(tiles):
+            field_ref[k, tile] = field[:, tile * LANES : (tile + 1) * LANES]
+    squared = joined(sums)
+    cells = jnp.full(squared.shape, float(KNOT * KNOT), f32)
+    first, second = plane_ref[0], plane_ref[1]
+    diag_depth_ref[0] = dot(first * first, squared, ((0,), (0,)))
+    diag_depth_ref[1] = dot(second * second, cells, ((0,), (0,)))
+    first, second = depth_ref[0], depth_ref[1]
+    diag_plane_ref[0] = dot(squared, first * first, ((1,), (1,)))
+    diag_plane_ref[1] = dot(cells, second * second, ((1,), (1,)))
+
+
+def terms(sums, plane, depth_factors):
+    nodes, width = plane.shape[1], depth_factors.shape[2]
+    return pl.pallas_call(
+        terms_kernel,
+        out_shape=[
+            jax.ShapeDtypeStruct((2, width // LANES, nodes, LANES), f32),
+            jax.ShapeDtypeStruct((2, RANK, width), f32),
+            jax.ShapeDtypeStruct((2, nodes, RANK), f32),
+        ],
+        compiler_params=plain_params(),
+        cost_estimate=pl.CostEstimate(flops=40 * nodes * RANK * width, bytes_accessed=1 << 20, transcendentals=0),
+        name="terms",
+    )(sums, plane, depth_factors)
 
 
 def warp_kernel(
-    cells_ref, image_ref, shift_ref, left_ref, right_ref, low_ref, high_ref, squares_ref, plane_ref, depth_ref,
+    cells_ref, image_ref, shift_ref, left_ref, right_ref, low_ref, high_ref, field, plane_ref, depth_ref,
+    diag_depth_ref, diag_plane_ref,
     residual_ref, depth_out, plane_out,
-    ahead_ref, here_ref, behind_ref, columns, field, blocks, energy, held,
+    ahead_ref, here_ref, behind_ref, columns, rims, blocks, energy, held,
 ):
     step = pl.program_id(0)
     last = pl.num_programs(0) - 1
@@ -166,12 +191,6 @@
     plane_rows = tiles * pitch
     block_rows = planes * plane_rows
 
-    def store_row(plane, moved, k, row):
-        for c in range(3):
-            for tile in range(tiles):
-                piece = moved[c][k : k + 1, tile * LANES : (tile + 1) * LANES]
-                window[c][pl.ds(plane + tile * pitch + row, 1), :] = piece
-
     def differences(wide):
         ahead = pltpu.roll(wide, wide.shape[1] - 1, 1) - wide
         return ahead, wide, pltpu.roll(ahead, 1, 1)
@@ -183,15 +202,16 @@
         energy[...] = jnp.zeros_like(energy)
         for c in range(3):
             window[c][3 * block_rows - plane_rows : 3 * block_rows, :] = jnp.zeros((plane_rows, LANES), f32)
-        for k in range(2):
-            values = dot(plane_ref[k], depth_ref[k], ((1,), (0,)))
-            for tile in range(tiles):
-                field[k, tile] = values[:, tile * LANES : (tile + 1) * LANES]
 
     @pl.when(step < last)
     def _():
         lane = lax.broadcasted_iota(jnp.int32, (16, LANES), 1)
         slot = (step % 3) * block_rows
+        for side, source in enumerate((low_ref, high_ref)):
+            moved = differences(source[...].astype(f32))
+            for c in range(3):
+                for tile in range(tiles):
+                    rims[(side * 3 + c) * tiles + tile] = moved[c][:, tile * LANES : (tile + 1) * LANES]
 
         def one(k, carry):
             x = step * planes + k
@@ -209,14 +229,14 @@
                         window[c][pl.ds(first + tile * pitch + TOP + 16 * group, 16), :] = moved[c][
                             :, tile * LANES : (tile + 1) * LANES
                         ]
+            for side, row in enumerate((0, TOP + rows)):
+                for c in range(3):
+                    for tile in range(tiles):
+                        rim = rims[(side * 3 + c) * tiles + tile, pl.ds(k, 1), :]
+                        window[c][pl.ds(first + tile * pitch + row, 8), :] = jnp.broadcast_to(rim, (8, LANES))
             return carry
 
         lax.fori_loop(0, planes, one, 0)
-        for source, row in ((low_ref, TOP - 1), (high_ref, TOP + rows)):
-            moved = differences(source[...].astype(f32))
-            for k in range(planes):
-                store_row(slot + k * plane_rows, moved, k, row)
-
     @pl.when(step == last)
     def _():
         first = pl.multiple_of((step % 3) * block_rows, 8)
@@ -283,7 +303,7 @@
                     total = total + misfit * misfit
                     before, here = here, after
                 for k, value in ((0, by_image), (1, plain)):
-                    blocks[k, tile, pl.ds(pl.multiple_of(node * 8, 8), 8), :] = value
+                    blocks[k, tile, pl.ds(node, 1), :] = jnp.sum(value, axis=0, keepdims=True)
             return total
 
         energy[...] = lax.fori_loop(0, (rows // 16) * tiles, one, energy[...])
@@ -294,24 +314,20 @@
         share = RANK // parts
         sums = [joined(blocks.at[k]) for k in range(2)]
         kinds = [split_dot(plane_ref[k], sums[k], 0) for k in range(2)]
-        squared = joined(squares_ref)
-        cells = jnp.full(squared.shape, float(KNOT * KNOT), f32)
-        second = plane_ref[1]
-        kinds = kinds + [split_dot(plane_ref[0] * plane_ref[0], squared, 0), split_dot(second * second, cells, 0)]
+        kinds = kinds + [diag_depth_ref[0], diag_depth_ref[1]]
         for p in range(parts):
             for k in range(4):
                 depth_out[p, k * share : (k + 1) * share, :] = kinds[k][p * share : (p + 1) * share]
         local = jnp.sum(energy[...])
         kinds = [split_dot(sums[k], depth_ref[k], 1) for k in range(2)]
-        second = depth_ref[1]
-        kinds = kinds + [split_dot(squared, depth_ref[0] * depth_ref[0], 1), split_dot(cells, second * second, 1)]
+        kinds = kinds + [diag_plane_ref[0], diag_plane_ref[1]]
         for k in range(4):
             plane_out[:, k * RANK : (k + 1) * RANK] = kinds[k]
         count = plane_out.shape[0]
         plane_out[count // 2 :, 3 * RANK :] = jnp.full((count // 2, RANK), local, f32)
 
 
-def warp(cells, image, shift, left, right, low, high, squared, plane, depth_factors, parts):
+def warp(cells, image, shift, left, right, low, high, field, plane, depth_factors, diag_depth, diag_plane, parts):
     depth, rows, width = cells.shape
     nodes = plane.shape[1]
     tiles = width // LANES
@@ -331,9 +347,11 @@
             pl.BlockSpec(right.shape, flat),
             pl.BlockSpec((KNOT, low.shape[1]), lambda i: (jnp.minimum(i, count - 1), 0)),
             pl.BlockSpec((KNOT, high.shape[1]), lambda i: (jnp.minimum(i, count - 1), 0)),
-            pl.BlockSpec(squared.shape, whole),
+            pl.BlockSpec(field.shape, lambda i: (0, 0, 0, 0)),
             pl.BlockSpec(plane.shape, whole),
             pl.BlockSpec(depth_factors.shape, whole),
+            pl.BlockSpec(diag_depth.shape, whole),
+            pl.BlockSpec(diag_plane.shape, whole),
         ],
         out_specs=[
             pl.BlockSpec((KNOT, rows, width), behind),
@@ -348,15 +366,15 @@
         scratch_shapes=[
             *[pltpu.VMEM((3 * KNOT * tiles * (rows + 2 * TOP), LANES), f32)] * 3,
             pltpu.VMEM((2, rows, LANES), f32),
+            pltpu.VMEM((6 * tiles, KNOT, LANES), f32),
             pltpu.VMEM((2, tiles, nodes, LANES), f32),
-            pltpu.VMEM((2, tiles, 8 * nodes, LANES), f32),
             pltpu.VMEM((8, LANES), f32),
             pltpu.VMEM((KNOT, 8, LANES), f32),
         ],
         compiler_params=grid_params(),
         cost_estimate=pl.CostEstimate(flops=60 * cells.size, bytes_accessed=12 * cells.size, transcendentals=0),
         name="warp",
-    )(cells, image, shift, left, right, low, high, squared, plane, depth_factors)
+    )(cells, image, shift, left, right, low, high, field, plane, depth_factors, diag_depth, diag_plane)
 
 
 def gather_kernel(depth_ref, *refs):
@@ -408,8 +426,10 @@
     low, high = packed_rows(left, right, low, high)
     above = shifted(low, "gy", True)
     below = shifted(high, "gy", False)
+    field, diag_depth, diag_plane = terms(sums, plane, depth_factors)
     residual, depth_terms, plane_terms = warp(
-        deformed, image, displacement, left, right, below, above, sums, plane, depth_factors, n_gy
+        deformed, image, displacement, left, right, below, above, field, plane, depth_factors, diag_depth, diag_plane,
+        n_gy,
     )
     others = [
         lax.ppermute(plane_terms, "gz", [(i, (i + hop) % n_gz) for i in range(n_gz)]) for hop in range(1, n_gz)

time: 89 us -> 88.3 us (level)
    pallas_call x2 -> x3, Pallas kernels: 2.27 us -> 3 us  [the longest x1 1.74 us: squares(): pl.pallas_call(squares_kernel, out_shape=[jax.ShapeDtypeStruct((width //...]
    unnamed x8 -> x10, local copies, waits for them, and re-layouts: 2.2 us -> 2.21 us
  transfers between devices with their start and end apart: 8 -> 8, of which waited for: 4 -> 4; matrix products, arithmetic and copies ran while one was open for 0% -> 0% of each run, Pallas kernels for 2% -> 3%
where the time goes in v8:
time: 88.3 us; the launch traced here: 88 us
  Pallas kernels  44.3 us (50%)
  starting transfers between devices  20.2 us (23%)
  blocking collectives  10.9 us (12%)
  waiting for transfers between devices  9.62 us (11%)
  local copies, waits for them, and re-layouts  2.21 us (3%)
    pallas_call x1, Pallas kernels, warp(): pl.pallas_call(warp_kernel, grid=(count + 1,), in_specs=[pl.BlockSpec((KN...  40.1 us
    all_to_all x1, blocking collectives, local(): depth_terms = lax.all_to_all(depth_terms, 'gy', 0, 0)  10.9 us
    all_to_all x1, starting transfers between devices, local(): depth_terms = lax.all_to_all(depth_terms, 'gy', 0, 0)  6.36 us
    ppermute x2, starting transfers between devices, shifted(): return lax.ppermute(part, axis, [(i, i + 1) for i in range(count - 1)])  6.35 us
    ppermute x2, waiting for transfers between devices, shifted(): return lax.ppermute(part, axis, [(i + 1, i) for i in range(count - 1)])  5.49 us
    ppermute x3, starting transfers between devices, local(): lax.ppermute(plane_terms, 'gz', [(i, (i + hop) % n_gz) for i in range(n_g...  4.62 us
    ppermute x3, waiting for transfers between devices, local(): lax.ppermute(plane_terms, 'gz', [(i, (i + hop) % n_gz) for i in range(n_g...  4.13 us
    ppermute x2, starting transfers between devices, shifted(): return lax.ppermute(part, axis, [(i + 1, i) for i in range(count - 1)])  2.85 us
  transfers between devices with their start and end apart: 8, of which 4 were waited for; matrix products, arithmetic and copies ran while one was open for 0% of the time, Pallas kernels for 3%

profile of v8, /device:TPU:0, one launch (start us, length us, event | category | flops | bytes accessed | tf_op | source)
XLA Modules:
  0.0 88.0 jit_solution(7593108283711489119)
XLA Ops:
  0.6 0.0 copy-start
  0.6 2.2 %copy-done = bf16[64,64,512]{2,1,0:T(8,128)(2,1)S(1)} copy-done((bf16[64,64,512]{2,1,0:T(8,128)(2,1)S(1)}, bf16[64,64,512]{2,1,0:T(8,128)(2,1)}, u32[]{:S(2)}) %copy-start) | copy-done | bytes 4194328
  2.8 0.0 copy-start.2
  2.8 0.6 columns.1
  3.5 5.1 %collective-permute-start = (bf16[64,128]{1,0:T(8,128)(2,1)S(1)}, bf16[64,128]{1,0:T(8,128)(2,1)S(1)}, u32[]{:S(2)}, u32[]{:S(2)}) collective-permute-start(bf16[64,128]{1,0:T(8,128)(2,1)S(1)} %get-tuple-element.20), channel_id=1, source_target_pairs={{0,1},{1,2},{2,3},{4,5},{5,6},{6,7},{8,9},{9,10},{10,11},{12,13},{... | collective-permute-start | bytes 49160 | tf_op jit(solution)/shard_map/ppermute | solution.py:99
  8.5 0.0 copy-start.3
  8.5 0.0 copy-start.4
  8.5 0.0 copy-start.1
  8.6 1.6 %collective-permute-start.1 = (bf16[64,128]{1,0:T(8,128)(2,1)S(1)}, bf16[64,128]{1,0:T(8,128)(2,1)S(1)}, u32[]{:S(2)}, u32[]{:S(2)}) collective-permute-start(bf16[64,128]{1,0:T(8,128)(2,1)S(1)} %get-tuple-element.21), channel_id=1, source_target_pairs={{1,0},{2,1},{3,2},{5,4},{6,5},{7,6},{9,8},{10,9},{11,10},{13,12},{... | collective-permute-start | bytes 49160 | tf_op jit(solution)/shard_map/ppermute | solution.py:98
  10.1 0.0 copy-done.2
  10.1 1.7 %squares.1 = (f32[4,64,128]{2,1,0:T(8,128)S(1)}, f32[64,512]{1,0:T(8,128)S(1)}, f32[64,512]{1,0:T(8,128)S(1)}) custom-call(bf16[64,64,512]{2,1,0:T(8,128)(2,1)S(1)} %copy-done.2, bf16[64,64,512]{2,1,0:T(8,128)(2,1)S(1)} %copy-done), custom_call_target="tpu_custom_call" | custom-call | flops 6291456 | bytes 4194304 | tf_op jit(solution)/shard_map/squares/pallas_call | solution.py:134
  11.9 0.0 collective-permute-done.left_ref
  11.9 2.6 %collective-permute-done.1.right_ref = bf16[64,128]{1,0:T(8,128)(2,1)S(1)} collective-permute-done((bf16[64,128]{1,0:T(8,128)(2,1)S(1)}, bf16[64,128]{1,0:T(8,128)(2,1)S(1)}, u32[]{:S(2)}, u32[]{:S(2)}) %collective-permute-start.1) | collective-permute-done | bytes 16416 | tf_op jit(solution)/shard_map/ppermute | solution.py:98
  14.5 0.2 rows.1
  14.6 1.3 %collective-permute-start.2 = (bf16[64,640]{1,0:T(8,128)(2,1)S(1)}, bf16[64,640]{1,0:T(8,128)(2,1)S(1)}, u32[]{:S(2)}, u32[]{:S(2)}) collective-permute-start(bf16[64,640]{1,0:T(8,128)(2,1)S(1)} %get-tuple-element.24), channel_id=1, source_target_pairs={{0,4},{4,8},{8,12},{12,16},{16,20},{20,24},{24,28},{1,5},{5,9},{9,... | collective-permute-start | bytes 245768 | tf_op jit(solution)/shard_map/ppermute | solution.py:99
  15.9 1.3 %collective-permute-start.3 = (bf16[64,640]{1,0:T(8,128)(2,1)S(1)}, bf16[64,640]{1,0:T(8,128)(2,1)S(1)}, u32[]{:S(2)}, u32[]{:S(2)}) collective-permute-start(bf16[64,640]{1,0:T(8,128)(2,1)S(1)} %get-tuple-element.25), channel_id=1, source_target_pairs={{4,0},{8,4},{12,8},{16,12},{20,16},{24,20},{28,24},{5,1},{9,5},{13... | collective-permute-start | bytes 245768 | tf_op jit(solution)/shard_map/ppermute | solution.py:98
  17.2 0.0 copy-done.3
  17.2 0.0 copy-done.4
  17.2 0.6 terms.1
  17.9 0.0 collective-permute-done.2.low_ref
  17.9 2.9 %collective-permute-done.3.high_ref = bf16[64,640]{1,0:T(8,128)(2,1)S(1)} collective-permute-done((bf16[64,640]{1,0:T(8,128)(2,1)S(1)}, bf16[64,640]{1,0:T(8,128)(2,1)S(1)}, u32[]{:S(2)}, u32[]{:S(2)}) %collective-permute-start.3) | collective-permute-done | bytes 81952 | tf_op jit(solution)/shard_map/ppermute | solution.py:98
  20.8 0.0 copy-done.1
  20.8 40.1 %warp.1 = (bf16[64,64,512]{2,1,0:T(8,128)(2,1)}, f32[8,16,512]{2,1,0:T(8,128)}, f32[64,128]{1,0:T(8,128)S(1)}) custom-call(bf16[64,64,512]{2,1,0:T(8,128)(2,1)S(1)} %copy-done.1, bf16[64,64,512]{2,1,0:T(8,128)(2,1)S(1)} %copy-done.2, bf16[3,64,64,512]{3,2,1,0:T(8,128)(2,1)} %shift_ref.1, bf16[64,128]{1,0:T(8,128)(2,1)S(1)} %collective-permute-done.left_ref, ...), custom_call_target="tpu_custom_call" | custom-call | flops 125829120 | bytes 25165824 | tf_op jit(solution)/shard_map/warp/pallas_call | solution.py:339
  60.9 6.4 %all-to-all-start = ((f32[8,16,512]{2,1,0:T(8,128)}), f32[8,16,512]{2,1,0:T(8,128)S(1)}, u32[]{:S(2)}, u32[]{:S(2)}) async-start(f32[8,16,512]{2,1,0:T(8,128)} %get-tuple-element.31), calls=%async_computation | async-start | bytes 524288 | tf_op jit(solution)/shard_map/all_to_all | solution.py:437
  67.3 2.1 %collective-permute-start.6 = (f32[64,128]{1,0:T(8,128)S(1)}, f32[64,128]{1,0:T(8,128)S(1)}, u32[]{:S(2)}, u32[]{:S(2)}) collective-permute-start(f32[64,128]{1,0:T(8,128)S(1)} %get-tuple-element.32.refs_0_), channel_id=1, source_target_pairs={{0,3},{1,0},{2,1},{3,2},{4,7},{5,4},{6,5},{7,6},{8,11},{9,8},{10,9... | collective-permute-start | bytes 98312 | tf_op jit(solution)/shard_map/ppermute | solution.py:435
  69.4 0.9 %collective-permute-start.5 = (f32[64,128]{1,0:T(8,128)S(1)}, f32[64,128]{1,0:T(8,128)S(1)}, u32[]{:S(2)}, u32[]{:S(2)}) collective-permute-start(f32[64,128]{1,0:T(8,128)S(1)} %get-tuple-element.32.refs_0_), channel_id=1, source_target_pairs={{0,2},{1,3},{2,0},{3,1},{4,6},{5,7},{6,4},{7,5},{8,10},{9,11},{10,... | collective-permute-start | bytes 98312 | tf_op jit(solution)/shard_map/ppermute | solution.py:435
  70.3 1.6 %collective-permute-start.4 = (f32[64,128]{1,0:T(8,128)S(1)}, f32[64,128]{1,0:T(8,128)S(1)}, u32[]{:S(2)}, u32[]{:S(2)}) collective-permute-start(f32[64,128]{1,0:T(8,128)S(1)} %get-tuple-element.32.refs_0_), channel_id=1, source_target_pairs={{0,1},{1,2},{2,3},{3,0},{4,5},{5,6},{6,7},{7,4},{8,9},{9,10},{10,1... | collective-permute-start | bytes 98312 | tf_op jit(solution)/shard_map/ppermute | solution.py:435
  71.9 0.0 collective-permute-done.6.refs_3_
  71.9 2.4 %collective-permute-done.5.refs_2_ = f32[64,128]{1,0:T(8,128)S(1)} collective-permute-done((f32[64,128]{1,0:T(8,128)S(1)}, f32[64,128]{1,0:T(8,128)S(1)}, u32[]{:S(2)}, u32[]{:S(2)}) %collective-permute-start.5) | collective-permute-done | bytes 32800 | tf_op jit(solution)/shard_map/ppermute | solution.py:435
  74.3 1.7 %collective-permute-done.4.refs_1_ = f32[64,128]{1,0:T(8,128)S(1)} collective-permute-done((f32[64,128]{1,0:T(8,128)S(1)}, f32[64,128]{1,0:T(8,128)S(1)}, u32[]{:S(2)}, u32[]{:S(2)}) %collective-permute-start.4) | collective-permute-done | bytes 32800 | tf_op jit(solution)/shard_map/ppermute | solution.py:435
  76.0 0.0 all-to-all-done.depth_ref
  76.0 0.1 gather.1
  76.2 10.9 %all_to_all.10.depth_ref = f32[8,16,512]{2,1,0:T(8,128)S(1)} all-to-all(f32[8,16,512]{2,1,0:T(8,128)S(1)} %get-tuple-element.33), channel_id=1, replica_groups=mesh['gy'=8,'gz'=4] {'gy'}, dimensions={0} | all-to-all | bytes 524288 | tf_op jit(solution)/shard_map/all_to_all | solution.py:447
  87.1 0.9 %steps.1 = (f32[2,32,512]{2,1,0:T(8,128)}, f32[2,64,32]{2,1,0:T(8,128)}) custom-call(f32[8,16,512]{2,1,0:T(8,128)S(1)} %all_to_all.10.depth_ref, f32[64,128]{1,0:T(8,128)S(1)} %get-tuple-element.34.plane_ref), custom_call_target="tpu_custom_call" | custom-call | tf_op jit(solution)/shard_map/steps/pallas_call | solution.py:449
Async XLA Ops:
  0.6 2.2 %copy-start = (bf16[64,64,512]{2,1,0:T(8,128)(2,1)S(1)}, bf16[64,64,512]{2,1,0:T(8,128)(2,1)}, u32[]{:S(2)}) copy-start(bf16[64,64,512]{2,1,0:T(8,128)(2,1)} %cells_ref.5) | copy-start | bytes 12582916
  2.8 7.3 %copy-start.2 = (bf16[64,64,512]{2,1,0:T(8,128)(2,1)S(1)}, bf16[64,64,512]{2,1,0:T(8,128)(2,1)}, u32[]{:S(2)}) copy-start(bf16[64,64,512]{2,1,0:T(8,128)(2,1)} %image_ref.3) | copy-start | bytes 12582916
  3.5 8.4 %collective-permute-start = (bf16[64,128]{1,0:T(8,128)(2,1)S(1)}, bf16[64,128]{1,0:T(8,128)(2,1)S(1)}, u32[]{:S(2)}, u32[]{:S(2)}) collective-permute-start(bf16[64,128]{1,0:T(8,128)(2,1)S(1)} %get-tuple-element.20), channel_id=1, source_target_pairs={{0,1},{1,2},{2,3},{4,5},{5,6},{6,7},{8,9},{9,10},{10,11},{12,13},{... | collective-permute-start | bytes 49160 | tf_op jit(solution)/shard_map/ppermute | solution.py:99
  8.5 8.7 %copy-start.3 = (f32[2,32,512]{2,1,0:T(8,128)S(1)}, f32[2,32,512]{2,1,0:T(8,128)}, u32[]{:S(2)}) copy-start(f32[2,32,512]{2,1,0:T(8,128)} %depth_ref.3) | copy-start | bytes 393220
  8.5 8.7 %copy-start.4 = (f32[2,32,8,8]{1,3,2,0:T(8,128)S(1)}, f32[2,32,8,8]{1,3,2,0:T(8,128)}, u32[]{:S(2)}) copy-start(f32[2,32,8,8]{1,3,2,0:T(8,128)} %param.8) | copy-start | bytes 49156
  8.5 12.3 %copy-start.1 = (bf16[64,64,512]{2,1,0:T(8,128)(2,1)S(1)}, bf16[64,64,512]{2,1,0:T(8,128)(2,1)}, u32[]{:S(2)}) copy-start(bf16[64,64,512]{2,1,0:T(8,128)(2,1)} %cells_ref.5) | copy-start | bytes 12582916
  8.6 5.9 %collective-permute-start.1 = (bf16[64,128]{1,0:T(8,128)(2,1)S(1)}, bf16[64,128]{1,0:T(8,128)(2,1)S(1)}, u32[]{:S(2)}, u32[]{:S(2)}) collective-permute-start(bf16[64,128]{1,0:T(8,128)(2,1)S(1)} %get-tuple-element.21), channel_id=1, source_target_pairs={{1,0},{2,1},{3,2},{5,4},{6,5},{7,6},{9,8},{10,9},{11,10},{13,12},{... | collective-permute-start | bytes 49160 | tf_op jit(solution)/shard_map/ppermute | solution.py:98
  14.6 3.3 %collective-permute-start.2 = (bf16[64,640]{1,0:T(8,128)(2,1)S(1)}, bf16[64,640]{1,0:T(8,128)(2,1)S(1)}, u32[]{:S(2)}, u32[]{:S(2)}) collective-permute-start(bf16[64,640]{1,0:T(8,128)(2,1)S(1)} %get-tuple-element.24), channel_id=1, source_target_pairs={{0,4},{4,8},{8,12},{12,16},{16,20},{20,24},{24,28},{1,5},{5,9},{9,... | collective-permute-start | bytes 245768 | tf_op jit(solution)/shard_map/ppermute | solution.py:99
  15.9 4.9 %collective-permute-start.3 = (bf16[64,640]{1,0:T(8,128)(2,1)S(1)}, bf16[64,640]{1,0:T(8,128)(2,1)S(1)}, u32[]{:S(2)}, u32[]{:S(2)}) collective-permute-start(bf16[64,640]{1,0:T(8,128)(2,1)S(1)} %get-tuple-element.25), channel_id=1, source_target_pairs={{4,0},{8,4},{12,8},{16,12},{20,16},{24,20},{28,24},{5,1},{9,5},{13... | collective-permute-start | bytes 245768 | tf_op jit(solution)/shard_map/ppermute | solution.py:98
  60.9 15.1 %all-to-all-start = ((f32[8,16,512]{2,1,0:T(8,128)}), f32[8,16,512]{2,1,0:T(8,128)S(1)}, u32[]{:S(2)}, u32[]{:S(2)}) async-start(f32[8,16,512]{2,1,0:T(8,128)} %get-tuple-element.31), calls=%async_computation | async-start | bytes 524288 | tf_op jit(solution)/shard_map/all_to_all | solution.py:437
  67.3 4.6 %collective-permute-start.6 = (f32[64,128]{1,0:T(8,128)S(1)}, f32[64,128]{1,0:T(8,128)S(1)}, u32[]{:S(2)}, u32[]{:S(2)}) collective-permute-start(f32[64,128]{1,0:T(8,128)S(1)} %get-tuple-element.32.refs_0_), channel_id=1, source_target_pairs={{0,3},{1,0},{2,1},{3,2},{4,7},{5,4},{6,5},{7,6},{8,11},{9,8},{10,9... | collective-permute-start | bytes 98312 | tf_op jit(solution)/shard_map/ppermute | solution.py:435
  69.4 4.9 %collective-permute-start.5 = (f32[64,128]{1,0:T(8,128)S(1)}, f32[64,128]{1,0:T(8,128)S(1)}, u32[]{:S(2)}, u32[]{:S(2)}) collective-permute-start(f32[64,128]{1,0:T(8,128)S(1)} %get-tuple-element.32.refs_0_), channel_id=1, source_target_pairs={{0,2},{1,3},{2,0},{3,1},{4,6},{5,7},{6,4},{7,5},{8,10},{9,11},{10,... | collective-permute-start | bytes 98312 | tf_op jit(solution)/shard_map/ppermute | solution.py:435
  70.3 5.7 %collective-permute-start.4 = (f32[64,128]{1,0:T(8,128)S(1)}, f32[64,128]{1,0:T(8,128)S(1)}, u32[]{:S(2)}, u32[]{:S(2)}) collective-permute-start(f32[64,128]{1,0:T(8,128)S(1)} %get-tuple-element.32.refs_0_), channel_id=1, source_target_pairs={{0,1},{1,2},{2,3},{3,0},{4,5},{5,6},{6,7},{7,4},{8,9},{9,10},{10,1... | collective-permute-start | bytes 98312 | tf_op jit(solution)/shard_map/ppermute | solution.py:435

commit v9 on v8

--- a/solution.py
+++ b/solution.py
@@ -191,9 +191,8 @@
     plane_rows = tiles * pitch
     block_rows = planes * plane_rows
 
-    def differences(wide):
-        ahead = pltpu.roll(wide, wide.shape[1] - 1, 1) - wide
-        return ahead, wide, pltpu.roll(ahead, 1, 1)
+    def neighbours(wide):
+        return pltpu.roll(wide, wide.shape[1] - 1, 1), wide, pltpu.roll(wide, 1, 1)
 
     @pl.when(step == 0)
     def _():
@@ -208,7 +207,7 @@
         lane = lax.broadcasted_iota(jnp.int32, (16, LANES), 1)
         slot = (step % 3) * block_rows
         for side, source in enumerate((low_ref, high_ref)):
-            moved = differences(source[...].astype(f32))
+            moved = neighbours(source[...].astype(f32))
             for c in range(3):
                 for tile in range(tiles):
                     rims[(side * 3 + c) * tiles + tile] = moved[c][:, tile * LANES : (tile + 1) * LANES]
@@ -223,7 +222,7 @@
                 after = pltpu.roll(right[mine], (LANES - x) % LANES, 1)
                 before = pltpu.roll(left[mine], LANES - 1 - x, 1)
                 beyond = jnp.where(lane == 0, after, before)
-                moved = differences(jnp.concatenate([raw[mine].astype(f32), beyond], axis=1))
+                moved = neighbours(jnp.concatenate([raw[mine].astype(f32), beyond], axis=1))
                 for c in range(3):
                     for tile in range(tiles):
                         window[c][pl.ds(first + tile * pitch + TOP + 16 * group, 16), :] = moved[c][
@@ -290,9 +289,11 @@
                     ahead, middle, behind = sides(0), sides(1), sides(2)
                     lines = []
                     for b in range(2):
-                        near, far = (middle[v][b] + sz * jnp.where(pz, ahead[v][b], behind[v][b]) for v in range(2))
-                        lines.append(near + ax * (far - near))
-                    warped = lines[0] + ay * (lines[1] - lines[0])
+                        ends = [(middle[v][b], jnp.where(pz, ahead[v][b], behind[v][b])) for v in range(2)]
+                        near, far = ends
+                        lines.append([near[c] + ax * (far[c] - near[c]) for c in range(2)])
+                    flat = [lines[0][c] + ay * (lines[1][c] - lines[0][c]) for c in range(2)]
+                    warped = flat[0] + jnp.abs(sz) * (flat[1] - flat[0])
                     misfit = warped - contrast * image - brightness
                     if half == 0:
                         held[k] = misfit

time: 88.3 us -> 84 us (0.951)
  Pallas kernels: 44.3 us -> 39.9 us
    pallas_call x1, Pallas kernels: 40.1 us -> 35.7 us  [warp(): pl.pallas_call(warp_kernel, grid=(count + 1,), in_specs=[pl.BlockSpec((KN...]
where the time goes in v9:
time: 84 us; the launch traced here: 83.6 us
  Pallas kernels  39.9 us (48%)
  starting transfers between devices  20.2 us (24%)
  blocking collectives  10.9 us (13%)
  waiting for transfers between devices  9.64 us (11%)
  local copies, waits for them, and re-layouts  2.21 us (3%)
    pallas_call x1, Pallas kernels, warp(): pl.pallas_call(warp_kernel, grid=(count + 1,), in_specs=[pl.BlockSpec((KN...  35.7 us
    all_to_all x1, blocking collectives, local(): depth_terms = lax.all_to_all(depth_terms, 'gy', 0, 0)  10.9 us
    all_to_all x1, starting transfers between devices, local(): depth_terms = lax.all_to_all(depth_terms, 'gy', 0, 0)  6.36 us
    ppermute x2, starting transfers between devices, shifted(): return lax.ppermute(part, axis, [(i, i + 1) for i in range(count - 1)])  6.35 us
    ppermute x2, waiting for transfers between devices, shifted(): return lax.ppermute(part, axis, [(i + 1, i) for i in range(count - 1)])  5.49 us
    ppermute x3, starting transfers between devices, local(): lax.ppermute(plane_terms, 'gz', [(i, (i + hop) % n_gz) for i in range(n_g...  4.61 us
    ppermute x3, waiting for transfers between devices, local(): lax.ppermute(plane_terms, 'gz', [(i, (i + hop) % n_gz) for i in range(n_g...  4.14 us
    ppermute x2, starting transfers between devices, shifted(): return lax.ppermute(part, axis, [(i + 1, i) for i in range(count - 1)])  2.85 us
  transfers between devices with their start and end apart: 8, of which 4 were waited for; matrix products, arithmetic and copies ran while one was open for 0% of the time, Pallas kernels for 3%

profile of v9, /device:TPU:0, one launch (start us, length us, event | category | flops | bytes accessed | tf_op | source)
XLA Modules:
  0.0 83.6 jit_solution(9193474346811696735)
XLA Ops:
  0.6 0.0 copy-start
  0.6 2.2 %copy-done = bf16[64,64,512]{2,1,0:T(8,128)(2,1)S(1)} copy-done((bf16[64,64,512]{2,1,0:T(8,128)(2,1)S(1)}, bf16[64,64,512]{2,1,0:T(8,128)(2,1)}, u32[]{:S(2)}) %copy-start) | copy-done | bytes 4194328
  2.8 0.0 copy-start.2
  2.8 0.6 columns.1
  3.5 5.1 %collective-permute-start = (bf16[64,128]{1,0:T(8,128)(2,1)S(1)}, bf16[64,128]{1,0:T(8,128)(2,1)S(1)}, u32[]{:S(2)}, u32[]{:S(2)}) collective-permute-start(bf16[64,128]{1,0:T(8,128)(2,1)S(1)} %get-tuple-element.20), channel_id=1, source_target_pairs={{0,1},{1,2},{2,3},{4,5},{5,6},{6,7},{8,9},{9,10},{10,11},{12,13},{... | collective-permute-start | bytes 49160 | tf_op jit(solution)/shard_map/ppermute | solution.py:99
  8.5 0.0 copy-start.3
  8.5 0.0 copy-start.4
  8.5 0.0 copy-start.1
  8.6 1.6 %collective-permute-start.1 = (bf16[64,128]{1,0:T(8,128)(2,1)S(1)}, bf16[64,128]{1,0:T(8,128)(2,1)S(1)}, u32[]{:S(2)}, u32[]{:S(2)}) collective-permute-start(bf16[64,128]{1,0:T(8,128)(2,1)S(1)} %get-tuple-element.21), channel_id=1, source_target_pairs={{1,0},{2,1},{3,2},{5,4},{6,5},{7,6},{9,8},{10,9},{11,10},{13,12},{... | collective-permute-start | bytes 49160 | tf_op jit(solution)/shard_map/ppermute | solution.py:98
  10.1 0.0 copy-done.2
  10.1 1.7 %squares.1 = (f32[4,64,128]{2,1,0:T(8,128)S(1)}, f32[64,512]{1,0:T(8,128)S(1)}, f32[64,512]{1,0:T(8,128)S(1)}) custom-call(bf16[64,64,512]{2,1,0:T(8,128)(2,1)S(1)} %copy-done.2, bf16[64,64,512]{2,1,0:T(8,128)(2,1)S(1)} %copy-done), custom_call_target="tpu_custom_call" | custom-call | flops 6291456 | bytes 4194304 | tf_op jit(solution)/shard_map/squares/pallas_call | solution.py:134
  11.9 0.0 collective-permute-done.left_ref
  11.9 2.6 %collective-permute-done.1.right_ref = bf16[64,128]{1,0:T(8,128)(2,1)S(1)} collective-permute-done((bf16[64,128]{1,0:T(8,128)(2,1)S(1)}, bf16[64,128]{1,0:T(8,128)(2,1)S(1)}, u32[]{:S(2)}, u32[]{:S(2)}) %collective-permute-start.1) | collective-permute-done | bytes 16416 | tf_op jit(solution)/shard_map/ppermute | solution.py:98
  14.5 0.2 rows.1
  14.6 1.3 %collective-permute-start.2 = (bf16[64,640]{1,0:T(8,128)(2,1)S(1)}, bf16[64,640]{1,0:T(8,128)(2,1)S(1)}, u32[]{:S(2)}, u32[]{:S(2)}) collective-permute-start(bf16[64,640]{1,0:T(8,128)(2,1)S(1)} %get-tuple-element.24), channel_id=1, source_target_pairs={{0,4},{4,8},{8,12},{12,16},{16,20},{20,24},{24,28},{1,5},{5,9},{9,... | collective-permute-start | bytes 245768 | tf_op jit(solution)/shard_map/ppermute | solution.py:99
  15.9 1.3 %collective-permute-start.3 = (bf16[64,640]{1,0:T(8,128)(2,1)S(1)}, bf16[64,640]{1,0:T(8,128)(2,1)S(1)}, u32[]{:S(2)}, u32[]{:S(2)}) collective-permute-start(bf16[64,640]{1,0:T(8,128)(2,1)S(1)} %get-tuple-element.25), channel_id=1, source_target_pairs={{4,0},{8,4},{12,8},{16,12},{20,16},{24,20},{28,24},{5,1},{9,5},{13... | collective-permute-start | bytes 245768 | tf_op jit(solution)/shard_map/ppermute | solution.py:98
  17.2 0.0 copy-done.3
  17.2 0.0 copy-done.4
  17.2 0.6 terms.1
  17.9 0.0 collective-permute-done.2.low_ref
  17.9 2.9 %collective-permute-done.3.high_ref = bf16[64,640]{1,0:T(8,128)(2,1)S(1)} collective-permute-done((bf16[64,640]{1,0:T(8,128)(2,1)S(1)}, bf16[64,640]{1,0:T(8,128)(2,1)S(1)}, u32[]{:S(2)}, u32[]{:S(2)}) %collective-permute-start.3) | collective-permute-done | bytes 81952 | tf_op jit(solution)/shard_map/ppermute | solution.py:98
  20.8 0.0 copy-done.1
  20.8 35.7 %warp.1 = (bf16[64,64,512]{2,1,0:T(8,128)(2,1)}, f32[8,16,512]{2,1,0:T(8,128)}, f32[64,128]{1,0:T(8,128)S(1)}) custom-call(bf16[64,64,512]{2,1,0:T(8,128)(2,1)S(1)} %copy-done.1, bf16[64,64,512]{2,1,0:T(8,128)(2,1)S(1)} %copy-done.2, bf16[3,64,64,512]{3,2,1,0:T(8,128)(2,1)} %shift_ref.1, bf16[64,128]{1,0:T(8,128)(2,1)S(1)} %collective-permute-done.left_ref, ...), custom_call_target="tpu_custom_call" | custom-call | flops 125829120 | bytes 25165824 | tf_op jit(solution)/shard_map/warp/pallas_call | solution.py:340
  56.5 6.4 %all-to-all-start = ((f32[8,16,512]{2,1,0:T(8,128)}), f32[8,16,512]{2,1,0:T(8,128)S(1)}, u32[]{:S(2)}, u32[]{:S(2)}) async-start(f32[8,16,512]{2,1,0:T(8,128)} %get-tuple-element.31), calls=%async_computation | async-start | bytes 524288 | tf_op jit(solution)/shard_map/all_to_all | solution.py:438
  62.9 2.1 %collective-permute-start.6 = (f32[64,128]{1,0:T(8,128)S(1)}, f32[64,128]{1,0:T(8,128)S(1)}, u32[]{:S(2)}, u32[]{:S(2)}) collective-permute-start(f32[64,128]{1,0:T(8,128)S(1)} %get-tuple-element.32.refs_0_), channel_id=1, source_target_pairs={{0,3},{1,0},{2,1},{3,2},{4,7},{5,4},{6,5},{7,6},{8,11},{9,8},{10,9... | collective-permute-start | bytes 98312 | tf_op jit(solution)/shard_map/ppermute | solution.py:436
  65.0 0.9 %collective-permute-start.5 = (f32[64,128]{1,0:T(8,128)S(1)}, f32[64,128]{1,0:T(8,128)S(1)}, u32[]{:S(2)}, u32[]{:S(2)}) collective-permute-start(f32[64,128]{1,0:T(8,128)S(1)} %get-tuple-element.32.refs_0_), channel_id=1, source_target_pairs={{0,2},{1,3},{2,0},{3,1},{4,6},{5,7},{6,4},{7,5},{8,10},{9,11},{10,... | collective-permute-start | bytes 98312 | tf_op jit(solution)/shard_map/ppermute | solution.py:436
  65.9 1.6 %collective-permute-start.4 = (f32[64,128]{1,0:T(8,128)S(1)}, f32[64,128]{1,0:T(8,128)S(1)}, u32[]{:S(2)}, u32[]{:S(2)}) collective-permute-start(f32[64,128]{1,0:T(8,128)S(1)} %get-tuple-element.32.refs_0_), channel_id=1, source_target_pairs={{0,1},{1,2},{2,3},{3,0},{4,5},{5,6},{6,7},{7,4},{8,9},{9,10},{10,1... | collective-permute-start | bytes 98312 | tf_op jit(solution)/shard_map/ppermute | solution.py:436
  67.5 0.0 collective-permute-done.6.refs_3_
  67.5 2.4 %collective-permute-done.5.refs_2_ = f32[64,128]{1,0:T(8,128)S(1)} collective-permute-done((f32[64,128]{1,0:T(8,128)S(1)}, f32[64,128]{1,0:T(8,128)S(1)}, u32[]{:S(2)}, u32[]{:S(2)}) %collective-permute-start.5) | collective-permute-done | bytes 32800 | tf_op jit(solution)/shard_map/ppermute | solution.py:436
  69.9 1.7 %collective-permute-done.4.refs_1_ = f32[64,128]{1,0:T(8,128)S(1)} collective-permute-done((f32[64,128]{1,0:T(8,128)S(1)}, f32[64,128]{1,0:T(8,128)S(1)}, u32[]{:S(2)}, u32[]{:S(2)}) %collective-permute-start.4) | collective-permute-done | bytes 32800 | tf_op jit(solution)/shard_map/ppermute | solution.py:436
  71.6 0.0 all-to-all-done.depth_ref
  71.6 0.1 gather.1
  71.8 10.9 %all_to_all.10.depth_ref = f32[8,16,512]{2,1,0:T(8,128)S(1)} all-to-all(f32[8,16,512]{2,1,0:T(8,128)S(1)} %get-tuple-element.33), channel_id=1, replica_groups=mesh['gy'=8,'gz'=4] {'gy'}, dimensions={0} | all-to-all | bytes 524288 | tf_op jit(solution)/shard_map/all_to_all | solution.py:448
  82.7 0.9 %steps.1 = (f32[2,32,512]{2,1,0:T(8,128)}, f32[2,64,32]{2,1,0:T(8,128)}) custom-call(f32[8,16,512]{2,1,0:T(8,128)S(1)} %all_to_all.10.depth_ref, f32[64,128]{1,0:T(8,128)S(1)} %get-tuple-element.34.plane_ref), custom_call_target="tpu_custom_call" | custom-call | tf_op jit(solution)/shard_map/steps/pallas_call | solution.py:450
Async XLA Ops:
  0.6 2.2 %copy-start = (bf16[64,64,512]{2,1,0:T(8,128)(2,1)S(1)}, bf16[64,64,512]{2,1,0:T(8,128)(2,1)}, u32[]{:S(2)}) copy-start(bf16[64,64,512]{2,1,0:T(8,128)(2,1)} %cells_ref.5) | copy-start | bytes 12582916
  2.8 7.3 %copy-start.2 = (bf16[64,64,512]{2,1,0:T(8,128)(2,1)S(1)}, bf16[64,64,512]{2,1,0:T(8,128)(2,1)}, u32[]{:S(2)}) copy-start(bf16[64,64,512]{2,1,0:T(8,128)(2,1)} %image_ref.3) | copy-start | bytes 12582916
  3.5 8.4 %collective-permute-start = (bf16[64,128]{1,0:T(8,128)(2,1)S(1)}, bf16[64,128]{1,0:T(8,128)(2,1)S(1)}, u32[]{:S(2)}, u32[]{:S(2)}) collective-permute-start(bf16[64,128]{1,0:T(8,128)(2,1)S(1)} %get-tuple-element.20), channel_id=1, source_target_pairs={{0,1},{1,2},{2,3},{4,5},{5,6},{6,7},{8,9},{9,10},{10,11},{12,13},{... | collective-permute-start | bytes 49160 | tf_op jit(solution)/shard_map/ppermute | solution.py:99
  8.5 8.7 %copy-start.3 = (f32[2,32,512]{2,1,0:T(8,128)S(1)}, f32[2,32,512]{2,1,0:T(8,128)}, u32[]{:S(2)}) copy-start(f32[2,32,512]{2,1,0:T(8,128)} %depth_ref.3) | copy-start | bytes 393220
  8.5 8.7 %copy-start.4 = (f32[2,32,8,8]{1,3,2,0:T(8,128)S(1)}, f32[2,32,8,8]{1,3,2,0:T(8,128)}, u32[]{:S(2)}) copy-start(f32[2,32,8,8]{1,3,2,0:T(8,128)} %param.8) | copy-start | bytes 49156
  8.5 12.3 %copy-start.1 = (bf16[64,64,512]{2,1,0:T(8,128)(2,1)S(1)}, bf16[64,64,512]{2,1,0:T(8,128)(2,1)}, u32[]{:S(2)}) copy-start(bf16[64,64,512]{2,1,0:T(8,128)(2,1)} %cells_ref.5) | copy-start | bytes 12582916
  8.6 5.9 %collective-permute-start.1 = (bf16[64,128]{1,0:T(8,128)(2,1)S(1)}, bf16[64,128]{1,0:T(8,128)(2,1)S(1)}, u32[]{:S(2)}, u32[]{:S(2)}) collective-permute-start(bf16[64,128]{1,0:T(8,128)(2,1)S(1)} %get-tuple-element.21), channel_id=1, source_target_pairs={{1,0},{2,1},{3,2},{5,4},{6,5},{7,6},{9,8},{10,9},{11,10},{13,12},{... | collective-permute-start | bytes 49160 | tf_op jit(solution)/shard_map/ppermute | solution.py:98
  14.6 3.3 %collective-permute-start.2 = (bf16[64,640]{1,0:T(8,128)(2,1)S(1)}, bf16[64,640]{1,0:T(8,128)(2,1)S(1)}, u32[]{:S(2)}, u32[]{:S(2)}) collective-permute-start(bf16[64,640]{1,0:T(8,128)(2,1)S(1)} %get-tuple-element.24), channel_id=1, source_target_pairs={{0,4},{4,8},{8,12},{12,16},{16,20},{20,24},{24,28},{1,5},{5,9},{9,... | collective-permute-start | bytes 245768 | tf_op jit(solution)/shard_map/ppermute | solution.py:99
  15.9 4.9 %collective-permute-start.3 = (bf16[64,640]{1,0:T(8,128)(2,1)S(1)}, bf16[64,640]{1,0:T(8,128)(2,1)S(1)}, u32[]{:S(2)}, u32[]{:S(2)}) collective-permute-start(bf16[64,640]{1,0:T(8,128)(2,1)S(1)} %get-tuple-element.25), channel_id=1, source_target_pairs={{4,0},{8,4},{12,8},{16,12},{20,16},{24,20},{28,24},{5,1},{9,5},{13... | collective-permute-start | bytes 245768 | tf_op jit(solution)/shard_map/ppermute | solution.py:98
  56.5 15.1 %all-to-all-start = ((f32[8,16,512]{2,1,0:T(8,128)}), f32[8,16,512]{2,1,0:T(8,128)S(1)}, u32[]{:S(2)}, u32[]{:S(2)}) async-start(f32[8,16,512]{2,1,0:T(8,128)} %get-tuple-element.31), calls=%async_computation | async-start | bytes 524288 | tf_op jit(solution)/shard_map/all_to_all | solution.py:438
  62.9 4.6 %collective-permute-start.6 = (f32[64,128]{1,0:T(8,128)S(1)}, f32[64,128]{1,0:T(8,128)S(1)}, u32[]{:S(2)}, u32[]{:S(2)}) collective-permute-start(f32[64,128]{1,0:T(8,128)S(1)} %get-tuple-element.32.refs_0_), channel_id=1, source_target_pairs={{0,3},{1,0},{2,1},{3,2},{4,7},{5,4},{6,5},{7,6},{8,11},{9,8},{10,9... | collective-permute-start | bytes 98312 | tf_op jit(solution)/shard_map/ppermute | solution.py:436
  65.0 4.9 %collective-permute-start.5 = (f32[64,128]{1,0:T(8,128)S(1)}, f32[64,128]{1,0:T(8,128)S(1)}, u32[]{:S(2)}, u32[]{:S(2)}) collective-permute-start(f32[64,128]{1,0:T(8,128)S(1)} %get-tuple-element.32.refs_0_), channel_id=1, source_target_pairs={{0,2},{1,3},{2,0},{3,1},{4,6},{5,7},{6,4},{7,5},{8,10},{9,11},{10,... | collective-permute-start | bytes 98312 | tf_op jit(solution)/shard_map/ppermute | solution.py:436
  65.9 5.7 %collective-permute-start.4 = (f32[64,128]{1,0:T(8,128)S(1)}, f32[64,128]{1,0:T(8,128)S(1)}, u32[]{:S(2)}, u32[]{:S(2)}) collective-permute-start(f32[64,128]{1,0:T(8,128)S(1)} %get-tuple-element.32.refs_0_), channel_id=1, source_target_pairs={{0,1},{1,2},{2,3},{3,0},{4,5},{5,6},{6,7},{7,4},{8,9},{9,10},{10,1... | collective-permute-start | bytes 98312 | tf_op jit(solution)/shard_map/ppermute | solution.py:436

commit v10 on v8

--- a/solution.py
+++ b/solution.py
@@ -213,7 +213,7 @@
                 for tile in range(tiles):
                     rims[(side * 3 + c) * tiles + tile] = moved[c][:, tile * LANES : (tile + 1) * LANES]
 
-        def one(k, carry):
+        for k in range(planes):
             x = step * planes + k
             first = pl.multiple_of(slot + k * plane_rows, 8)
             raw = cells_ref[k]
@@ -234,9 +234,6 @@
                     for tile in range(tiles):
                         rim = rims[(side * 3 + c) * tiles + tile, pl.ds(k, 1), :]
                         window[c][pl.ds(first + tile * pitch + row, 8), :] = jnp.broadcast_to(rim, (8, LANES))
-            return carry
-
-        lax.fori_loop(0, planes, one, 0)
     @pl.when(step == last)
     def _():
         first = pl.multiple_of((step % 3) * block_rows, 8)

time: 88.3 us -> 101 us (1.14)
  Pallas kernels: 44.3 us -> 56.8 us
    pallas_call x1, Pallas kernels: 40.1 us -> 52.6 us  [warp(): pl.pallas_call(warp_kernel, grid=(count + 1,), in_specs=[pl.BlockSpec((KN...]
  transfers between devices with their start and end apart: 8 -> 8, of which waited for: 4 -> 4; matrix products, arithmetic and copies ran while one was open for 0% -> 0% of each run, Pallas kernels for 3% -> 2%
where the time goes in v10:
time: 101 us; the launch traced here: 100 us
  Pallas kernels  56.8 us (56%)
  starting transfers between devices  20.2 us (20%)
  blocking collectives  10.9 us (11%)
  waiting for transfers between devices  9.63 us (10%)
  local copies, waits for them, and re-layouts  2.21 us (2%)
    pallas_call x1, Pallas kernels, warp(): pl.pallas_call(warp_kernel, grid=(count + 1,), in_specs=[pl.BlockSpec((KN...  52.6 us
    all_to_all x1, blocking collectives, local(): depth_terms = lax.all_to_all(depth_terms, 'gy', 0, 0)  10.9 us
    all_to_all x1, starting transfers between devices, local(): depth_terms = lax.all_to_all(depth_terms, 'gy', 0, 0)  6.36 us
    ppermute x2, starting transfers between devices, shifted(): return lax.ppermute(part, axis, [(i, i + 1) for i in range(count - 1)])  6.35 us
    ppermute x2, waiting for transfers between devices, shifted(): return lax.ppermute(part, axis, [(i + 1, i) for i in range(count - 1)])  5.49 us
    ppermute x3, starting transfers between devices, local(): lax.ppermute(plane_terms, 'gz', [(i, (i + hop) % n_gz) for i in range(n_g...  4.63 us
    ppermute x3, waiting for transfers between devices, local(): lax.ppermute(plane_terms, 'gz', [(i, (i + hop) % n_gz) for i in range(n_g...  4.13 us
    ppermute x2, starting transfers between devices, shifted(): return lax.ppermute(part, axis, [(i + 1, i) for i in range(count - 1)])  2.85 us
  transfers between devices with their start and end apart: 8, of which 4 were waited for; matrix products, arithmetic and copies ran while one was open for 0% of the time, Pallas kernels for 2%

profile of v10, /device:TPU:0, one launch (start us, length us, event | category | flops | bytes accessed | tf_op | source)
XLA Modules:
  0.0 100.5 jit_solution(3944201906693086594)
XLA Ops:
  0.6 0.0 copy-start
  0.6 2.2 %copy-done = bf16[64,64,512]{2,1,0:T(8,128)(2,1)S(1)} copy-done((bf16[64,64,512]{2,1,0:T(8,128)(2,1)S(1)}, bf16[64,64,512]{2,1,0:T(8,128)(2,1)}, u32[]{:S(2)}) %copy-start) | copy-done | bytes 4194328
  2.8 0.0 copy-start.2
  2.8 0.6 columns.1
  3.5 5.1 %collective-permute-start = (bf16[64,128]{1,0:T(8,128)(2,1)S(1)}, bf16[64,128]{1,0:T(8,128)(2,1)S(1)}, u32[]{:S(2)}, u32[]{:S(2)}) collective-permute-start(bf16[64,128]{1,0:T(8,128)(2,1)S(1)} %get-tuple-element.20), channel_id=1, source_target_pairs={{0,1},{1,2},{2,3},{4,5},{5,6},{6,7},{8,9},{9,10},{10,11},{12,13},{... | collective-permute-start | bytes 49160 | tf_op jit(solution)/shard_map/ppermute | solution.py:99
  8.5 0.0 copy-start.3
  8.5 0.0 copy-start.4
  8.5 0.0 copy-start.1
  8.6 1.6 %collective-permute-start.1 = (bf16[64,128]{1,0:T(8,128)(2,1)S(1)}, bf16[64,128]{1,0:T(8,128)(2,1)S(1)}, u32[]{:S(2)}, u32[]{:S(2)}) collective-permute-start(bf16[64,128]{1,0:T(8,128)(2,1)S(1)} %get-tuple-element.21), channel_id=1, source_target_pairs={{1,0},{2,1},{3,2},{5,4},{6,5},{7,6},{9,8},{10,9},{11,10},{13,12},{... | collective-permute-start | bytes 49160 | tf_op jit(solution)/shard_map/ppermute | solution.py:98
  10.1 0.0 copy-done.2
  10.1 1.7 %squares.1 = (f32[4,64,128]{2,1,0:T(8,128)S(1)}, f32[64,512]{1,0:T(8,128)S(1)}, f32[64,512]{1,0:T(8,128)S(1)}) custom-call(bf16[64,64,512]{2,1,0:T(8,128)(2,1)S(1)} %copy-done.2, bf16[64,64,512]{2,1,0:T(8,128)(2,1)S(1)} %copy-done), custom_call_target="tpu_custom_call" | custom-call | flops 6291456 | bytes 4194304 | tf_op jit(solution)/shard_map/squares/pallas_call | solution.py:134
  11.9 0.0 collective-permute-done.left_ref
  11.9 2.6 %collective-permute-done.1.right_ref = bf16[64,128]{1,0:T(8,128)(2,1)S(1)} collective-permute-done((bf16[64,128]{1,0:T(8,128)(2,1)S(1)}, bf16[64,128]{1,0:T(8,128)(2,1)S(1)}, u32[]{:S(2)}, u32[]{:S(2)}) %collective-permute-start.1) | collective-permute-done | bytes 16416 | tf_op jit(solution)/shard_map/ppermute | solution.py:98
  14.5 0.2 rows.1
  14.6 1.3 %collective-permute-start.2 = (bf16[64,640]{1,0:T(8,128)(2,1)S(1)}, bf16[64,640]{1,0:T(8,128)(2,1)S(1)}, u32[]{:S(2)}, u32[]{:S(2)}) collective-permute-start(bf16[64,640]{1,0:T(8,128)(2,1)S(1)} %get-tuple-element.24), channel_id=1, source_target_pairs={{0,4},{4,8},{8,12},{12,16},{16,20},{20,24},{24,28},{1,5},{5,9},{9,... | collective-permute-start | bytes 245768 | tf_op jit(solution)/shard_map/ppermute | solution.py:99
  15.9 1.3 %collective-permute-start.3 = (bf16[64,640]{1,0:T(8,128)(2,1)S(1)}, bf16[64,640]{1,0:T(8,128)(2,1)S(1)}, u32[]{:S(2)}, u32[]{:S(2)}) collective-permute-start(bf16[64,640]{1,0:T(8,128)(2,1)S(1)} %get-tuple-element.25), channel_id=1, source_target_pairs={{4,0},{8,4},{12,8},{16,12},{20,16},{24,20},{28,24},{5,1},{9,5},{13... | collective-permute-start | bytes 245768 | tf_op jit(solution)/shard_map/ppermute | solution.py:98
  17.2 0.0 copy-done.3
  17.2 0.0 copy-done.4
  17.2 0.6 terms.1
  17.9 0.0 collective-permute-done.2.low_ref
  17.9 2.9 %collective-permute-done.3.high_ref = bf16[64,640]{1,0:T(8,128)(2,1)S(1)} collective-permute-done((bf16[64,640]{1,0:T(8,128)(2,1)S(1)}, bf16[64,640]{1,0:T(8,128)(2,1)S(1)}, u32[]{:S(2)}, u32[]{:S(2)}) %collective-permute-start.3) | collective-permute-done | bytes 81952 | tf_op jit(solution)/shard_map/ppermute | solution.py:98
  20.8 0.0 copy-done.1
  20.8 52.6 %warp.1 = (bf16[64,64,512]{2,1,0:T(8,128)(2,1)}, f32[8,16,512]{2,1,0:T(8,128)}, f32[64,128]{1,0:T(8,128)S(1)}) custom-call(bf16[64,64,512]{2,1,0:T(8,128)(2,1)S(1)} %copy-done.1, bf16[64,64,512]{2,1,0:T(8,128)(2,1)S(1)} %copy-done.2, bf16[3,64,64,512]{3,2,1,0:T(8,128)(2,1)} %shift_ref.1, bf16[64,128]{1,0:T(8,128)(2,1)S(1)} %collective-permute-done.left_ref, ...), custom_call_target="tpu_custom_call" | custom-call | flops 125829120 | bytes 25165824 | tf_op jit(solution)/shard_map/warp/pallas_call | solution.py:336
  73.4 6.4 %all-to-all-start = ((f32[8,16,512]{2,1,0:T(8,128)}), f32[8,16,512]{2,1,0:T(8,128)S(1)}, u32[]{:S(2)}, u32[]{:S(2)}) async-start(f32[8,16,512]{2,1,0:T(8,128)} %get-tuple-element.31), calls=%async_computation | async-start | bytes 524288 | tf_op jit(solution)/shard_map/all_to_all | solution.py:434
  79.8 2.1 %collective-permute-start.6 = (f32[64,128]{1,0:T(8,128)S(1)}, f32[64,128]{1,0:T(8,128)S(1)}, u32[]{:S(2)}, u32[]{:S(2)}) collective-permute-start(f32[64,128]{1,0:T(8,128)S(1)} %get-tuple-element.32.refs_0_), channel_id=1, source_target_pairs={{0,3},{1,0},{2,1},{3,2},{4,7},{5,4},{6,5},{7,6},{8,11},{9,8},{10,9... | collective-permute-start | bytes 98312 | tf_op jit(solution)/shard_map/ppermute | solution.py:432
  81.9 0.9 collective-permute-start.5
  82.8 1.6 %collective-permute-start.4 = (f32[64,128]{1,0:T(8,128)S(1)}, f32[64,128]{1,0:T(8,128)S(1)}, u32[]{:S(2)}, u32[]{:S(2)}) collective-permute-start(f32[64,128]{1,0:T(8,128)S(1)} %get-tuple-element.32.refs_0_), channel_id=1, source_target_pairs={{0,1},{1,2},{2,3},{3,0},{4,5},{5,6},{6,7},{7,4},{8,9},{9,10},{10,1... | collective-permute-start | bytes 98312 | tf_op jit(solution)/shard_map/ppermute | solution.py:432
  84.4 0.0 collective-permute-done.6.refs_3_
  84.4 2.4 %collective-permute-done.5.refs_2_ = f32[64,128]{1,0:T(8,128)S(1)} collective-permute-done((f32[64,128]{1,0:T(8,128)S(1)}, f32[64,128]{1,0:T(8,128)S(1)}, u32[]{:S(2)}, u32[]{:S(2)}) %collective-permute-start.5) | collective-permute-done | bytes 32800 | tf_op jit(solution)/shard_map/ppermute | solution.py:432
  86.8 1.7 %collective-permute-done.4.refs_1_ = f32[64,128]{1,0:T(8,128)S(1)} collective-permute-done((f32[64,128]{1,0:T(8,128)S(1)}, f32[64,128]{1,0:T(8,128)S(1)}, u32[]{:S(2)}, u32[]{:S(2)}) %collective-permute-start.4) | collective-permute-done | bytes 32800 | tf_op jit(solution)/shard_map/ppermute | solution.py:432
  88.5 0.0 all-to-all-done.depth_ref
  88.5 0.1 gather.1
  88.7 10.9 %all_to_all.10.depth_ref = f32[8,16,512]{2,1,0:T(8,128)S(1)} all-to-all(f32[8,16,512]{2,1,0:T(8,128)S(1)} %get-tuple-element.33), channel_id=1, replica_groups=mesh['gy'=8,'gz'=4] {'gy'}, dimensions={0} | all-to-all | bytes 524288 | tf_op jit(solution)/shard_map/all_to_all | solution.py:444
  99.6 0.9 steps.1
Async XLA Ops:
  0.6 2.2 %copy-start = (bf16[64,64,512]{2,1,0:T(8,128)(2,1)S(1)}, bf16[64,64,512]{2,1,0:T(8,128)(2,1)}, u32[]{:S(2)}) copy-start(bf16[64,64,512]{2,1,0:T(8,128)(2,1)} %cells_ref.5) | copy-start | bytes 12582916
  2.8 7.3 %copy-start.2 = (bf16[64,64,512]{2,1,0:T(8,128)(2,1)S(1)}, bf16[64,64,512]{2,1,0:T(8,128)(2,1)}, u32[]{:S(2)}) copy-start(bf16[64,64,512]{2,1,0:T(8,128)(2,1)} %image_ref.3) | copy-start | bytes 12582916
  3.5 8.4 %collective-permute-start = (bf16[64,128]{1,0:T(8,128)(2,1)S(1)}, bf16[64,128]{1,0:T(8,128)(2,1)S(1)}, u32[]{:S(2)}, u32[]{:S(2)}) collective-permute-start(bf16[64,128]{1,0:T(8,128)(2,1)S(1)} %get-tuple-element.20), channel_id=1, source_target_pairs={{0,1},{1,2},{2,3},{4,5},{5,6},{6,7},{8,9},{9,10},{10,11},{12,13},{... | collective-permute-start | bytes 49160 | tf_op jit(solution)/shard_map/ppermute | solution.py:99
  8.5 8.7 %copy-start.3 = (f32[2,32,512]{2,1,0:T(8,128)S(1)}, f32[2,32,512]{2,1,0:T(8,128)}, u32[]{:S(2)}) copy-start(f32[2,32,512]{2,1,0:T(8,128)} %depth_ref.3) | copy-start | bytes 393220
  8.5 8.7 %copy-start.4 = (f32[2,32,8,8]{1,3,2,0:T(8,128)S(1)}, f32[2,32,8,8]{1,3,2,0:T(8,128)}, u32[]{:S(2)}) copy-start(f32[2,32,8,8]{1,3,2,0:T(8,128)} %param.8) | copy-start | bytes 49156
  8.5 12.3 %copy-start.1 = (bf16[64,64,512]{2,1,0:T(8,128)(2,1)S(1)}, bf16[64,64,512]{2,1,0:T(8,128)(2,1)}, u32[]{:S(2)}) copy-start(bf16[64,64,512]{2,1,0:T(8,128)(2,1)} %cells_ref.5) | copy-start | bytes 12582916
  8.6 5.9 %collective-permute-start.1 = (bf16[64,128]{1,0:T(8,128)(2,1)S(1)}, bf16[64,128]{1,0:T(8,128)(2,1)S(1)}, u32[]{:S(2)}, u32[]{:S(2)}) collective-permute-start(bf16[64,128]{1,0:T(8,128)(2,1)S(1)} %get-tuple-element.21), channel_id=1, source_target_pairs={{1,0},{2,1},{3,2},{5,4},{6,5},{7,6},{9,8},{10,9},{11,10},{13,12},{... | collective-permute-start | bytes 49160 | tf_op jit(solution)/shard_map/ppermute | solution.py:98
  14.6 3.3 %collective-permute-start.2 = (bf16[64,640]{1,0:T(8,128)(2,1)S(1)}, bf16[64,640]{1,0:T(8,128)(2,1)S(1)}, u32[]{:S(2)}, u32[]{:S(2)}) collective-permute-start(bf16[64,640]{1,0:T(8,128)(2,1)S(1)} %get-tuple-element.24), channel_id=1, source_target_pairs={{0,4},{4,8},{8,12},{12,16},{16,20},{20,24},{24,28},{1,5},{5,9},{9,... | collective-permute-start | bytes 245768 | tf_op jit(solution)/shard_map/ppermute | solution.py:99
  15.9 4.9 %collective-permute-start.3 = (bf16[64,640]{1,0:T(8,128)(2,1)S(1)}, bf16[64,640]{1,0:T(8,128)(2,1)S(1)}, u32[]{:S(2)}, u32[]{:S(2)}) collective-permute-start(bf16[64,640]{1,0:T(8,128)(2,1)S(1)} %get-tuple-element.25), channel_id=1, source_target_pairs={{4,0},{8,4},{12,8},{16,12},{20,16},{24,20},{28,24},{5,1},{9,5},{13... | collective-permute-start | bytes 245768 | tf_op jit(solution)/shard_map/ppermute | solution.py:98
  73.4 15.1 %all-to-all-start = ((f32[8,16,512]{2,1,0:T(8,128)}), f32[8,16,512]{2,1,0:T(8,128)S(1)}, u32[]{:S(2)}, u32[]{:S(2)}) async-start(f32[8,16,512]{2,1,0:T(8,128)} %get-tuple-element.31), calls=%async_computation | async-start | bytes 524288 | tf_op jit(solution)/shard_map/all_to_all | solution.py:434
  79.8 4.6 %collective-permute-start.6 = (f32[64,128]{1,0:T(8,128)S(1)}, f32[64,128]{1,0:T(8,128)S(1)}, u32[]{:S(2)}, u32[]{:S(2)}) collective-permute-start(f32[64,128]{1,0:T(8,128)S(1)} %get-tuple-element.32.refs_0_), channel_id=1, source_target_pairs={{0,3},{1,0},{2,1},{3,2},{4,7},{5,4},{6,5},{7,6},{8,11},{9,8},{10,9... | collective-permute-start | bytes 98312 | tf_op jit(solution)/shard_map/ppermute | solution.py:432
  81.9 4.9 %collective-permute-start.5 = (f32[64,128]{1,0:T(8,128)S(1)}, f32[64,128]{1,0:T(8,128)S(1)}, u32[]{:S(2)}, u32[]{:S(2)}) collective-permute-start(f32[64,128]{1,0:T(8,128)S(1)} %get-tuple-element.32.refs_0_), channel_id=1, source_target_pairs={{0,2},{1,3},{2,0},{3,1},{4,6},{5,7},{6,4},{7,5},{8,10},{9,11},{10,... | collective-permute-start | bytes 98312 | tf_op jit(solution)/shard_map/ppermute | solution.py:432
  82.8 5.7 %collective-permute-start.4 = (f32[64,128]{1,0:T(8,128)S(1)}, f32[64,128]{1,0:T(8,128)S(1)}, u32[]{:S(2)}, u32[]{:S(2)}) collective-permute-start(f32[64,128]{1,0:T(8,128)S(1)} %get-tuple-element.32.refs_0_), channel_id=1, source_target_pairs={{0,1},{1,2},{2,3},{3,0},{4,5},{5,6},{6,7},{7,4},{8,9},{9,10},{10,1... | collective-permute-start | bytes 98312 | tf_op jit(solution)/shard_map/ppermute | solution.py:432

commit v11 on v10

--- a/solution.py
+++ b/solution.py
@@ -144,8 +144,16 @@
     )(image, cells)
 
 
-def terms_kernel(sums, plane_ref, depth_ref, field_ref, diag_depth_ref, diag_plane_ref):
+def terms_kernel(
+    sums, plane_ref, depth_ref, left_ref, right_ref, field_ref, diag_depth_ref, diag_plane_ref, beyond_ref
+):
     tiles = sums.shape[0]
+    left, right = left_ref[...].astype(f32), right_ref[...].astype(f32)
+    lane = lax.broadcasted_iota(jnp.int32, left.shape, 1)
+    for x in range(beyond_ref.shape[0]):
+        after = pltpu.roll(right, (LANES - x) % LANES, 1)
+        before = pltpu.roll(left, LANES - 1 - x, 1)
+        beyond_ref[x] = jnp.where(lane == 0, after, before).astype(bf16)
     for k in range(2):
         field = dot(plane_ref[k], depth_ref[k], ((1,), (0,)))
         for tile in range(tiles):
@@ -160,7 +168,7 @@
     diag_plane_ref[1] = dot(cells, second * second, ((1,), (1,)))
 
 
-def terms(sums, plane, depth_factors):
+def terms(sums, plane, depth_factors, left, right, depth):
     nodes, width = plane.shape[1], depth_factors.shape[2]
     return pl.pallas_call(
         terms_kernel,
@@ -168,18 +176,19 @@
             jax.ShapeDtypeStruct((2, width // LANES, nodes, LANES), f32),
             jax.ShapeDtypeStruct((2, RANK, width), f32),
             jax.ShapeDtypeStruct((2, nodes, RANK), f32),
+            jax.ShapeDtypeStruct((depth,) + left.shape, bf16),
         ],
         compiler_params=plain_params(),
         cost_estimate=pl.CostEstimate(flops=40 * nodes * RANK * width, bytes_accessed=1 << 20, transcendentals=0),
         name="terms",
-    )(sums, plane, depth_factors)
+    )(sums, plane, depth_factors, left, right)
 
 
 def warp_kernel(
-    cells_ref, image_ref, shift_ref, left_ref, right_ref, low_ref, high_ref, field, plane_ref, depth_ref,
+    cells_ref, image_ref, shift_ref, beyond_ref, low_ref, high_ref, field, plane_ref, depth_ref,
     diag_depth_ref, diag_plane_ref,
     residual_ref, depth_out, plane_out,
-    ahead_ref, here_ref, behind_ref, columns, rims, blocks, energy, held,
+    ahead_ref, here_ref, behind_ref, wide, bands, rims, blocks, energy, held,
 ):
     step = pl.program_id(0)
     last = pl.num_programs(0) - 1
@@ -191,49 +200,55 @@
     plane_rows = tiles * pitch
     block_rows = planes * plane_rows
 
-    def differences(wide):
-        ahead = pltpu.roll(wide, wide.shape[1] - 1, 1) - wide
-        return ahead, wide, pltpu.roll(ahead, 1, 1)
-
     @pl.when(step == 0)
     def _():
-        columns[0] = left_ref[...].astype(f32)
-        columns[1] = right_ref[...].astype(f32)
+        row = lax.broadcasted_iota(jnp.int32, bands.shape[1:], 0)
+        column = lax.broadcasted_iota(jnp.int32, bands.shape[1:], 1)
+        one, none = jnp.ones(bands.shape[1:], f32), jnp.zeros(bands.shape[1:], f32)
+        up, down = jnp.where(row == column + 1, one, none), jnp.where(row == column, one, none)
+        bands[0] = (up - down).astype(bf16)
+        up = jnp.where(row == column + LANES, one, none)
+        down = jnp.where(row == column + LANES - 1, one, none)
+        bands[1] = (up - down).astype(bf16)
         energy[...] = jnp.zeros_like(energy)
         for c in range(3):
             window[c][3 * block_rows - plane_rows : 3 * block_rows, :] = jnp.zeros((plane_rows, LANES), f32)
 
     @pl.when(step < last)
     def _():
-        lane = lax.broadcasted_iota(jnp.int32, (16, LANES), 1)
         slot = (step % 3) * block_rows
-        for side, source in enumerate((low_ref, high_ref)):
-            moved = differences(source[...].astype(f32))
-            for c in range(3):
-                for tile in range(tiles):
-                    rims[(side * 3 + c) * tiles + tile] = moved[c][:, tile * LANES : (tile + 1) * LANES]
-
+        span = planes * rows
         for k in range(planes):
-            x = step * planes + k
-            first = pl.multiple_of(slot + k * plane_rows, 8)
-            raw = cells_ref[k]
-            right, left = columns[1], columns[0]
-            for group in range(rows // 16):
-                mine = slice(16 * group, 16 * group + 16)
-                after = pltpu.roll(right[mine], (LANES - x) % LANES, 1)
-                before = pltpu.roll(left[mine], LANES - 1 - x, 1)
-                beyond = jnp.where(lane == 0, after, before)
-                moved = differences(jnp.concatenate([raw[mine].astype(f32), beyond], axis=1))
-                for c in range(3):
-                    for tile in range(tiles):
-                        window[c][pl.ds(first + tile * pitch + TOP + 16 * group, 16), :] = moved[c][
-                            :, tile * LANES : (tile + 1) * LANES
-                        ]
+            wide[k * rows : (k + 1) * rows, 0:width] = cells_ref[k]
+            wide[k * rows : (k + 1) * rows, width:] = beyond_ref[k]
+        wide[span:, :] = jnp.concatenate([low_ref[...].astype(f32), high_ref[...].astype(f32)], axis=0).astype(bf16)
+
+        def put(c, tile, values):
+            for k in range(planes):
+                first = pl.multiple_of(slot + k * plane_rows + tile * pitch, 8)
+                window[c][pl.ds(first + TOP, rows), :] = values[k * rows : (k + 1) * rows]
             for side, row in enumerate((0, TOP + rows)):
-                for c in range(3):
-                    for tile in range(tiles):
-                        rim = rims[(side * 3 + c) * tiles + tile, pl.ds(k, 1), :]
-                        window[c][pl.ds(first + tile * pitch + row, 8), :] = jnp.broadcast_to(rim, (8, LANES))
+                rims[...] = values[span + side * planes : span + (side + 1) * planes]
+                for k in range(planes):
+                    first = pl.multiple_of(slot + k * plane_rows + tile * pitch, 8)
+                    window[c][pl.ds(first + row, 8), :] = jnp.broadcast_to(rims[k : k + 1], (8, LANES))
+
+        pieces = width // (2 * LANES)
+        for piece in range(pieces):
+            start = 2 * LANES * piece
+            after = wide[:, start : start + 3 * LANES]
+            if piece == 0:
+                before = jnp.concatenate([wide[:, width:], wide[:, 0 : 2 * LANES]], axis=1)
+            else:
+                before = wide[:, start - LANES : start + 2 * LANES]
+            ahead = jnp.dot(after, bands[0], preferred_element_type=f32)
+            behind = jnp.dot(before, bands[1], preferred_element_type=f32)
+            for half in range(2):
+                mine = slice(half * LANES, (half + 1) * LANES)
+                put(0, 2 * piece + half, ahead[:, mine])
+                put(1, 2 * piece + half, wide[:, start + half * LANES : start + (half + 1) * LANES].astype(f32))
+                put(2, 2 * piece + half, behind[:, mine])
+
     @pl.when(step == last)
     def _():
         first = pl.multiple_of((step % 3) * block_rows, 8)
@@ -324,7 +339,7 @@
         plane_out[count // 2 :, 3 * RANK :] = jnp.full((count // 2, RANK), local, f32)
 
 
-def warp(cells, image, shift, left, right, low, high, field, plane, depth_factors, diag_depth, diag_plane, parts):
+def warp(cells, image, shift, beyond, low, high, field, plane, depth_factors, diag_depth, diag_plane, parts):
     depth, rows, width = cells.shape
     nodes = plane.shape[1]
     tiles = width // LANES
@@ -340,8 +355,7 @@
             pl.BlockSpec((KNOT, rows, width), ahead),
             pl.BlockSpec((KNOT, rows, width), behind),
             pl.BlockSpec((3, KNOT, rows, width), lambda i: (0, jnp.maximum(i - 1, 0), 0, 0)),
-            pl.BlockSpec(left.shape, flat),
-            pl.BlockSpec(right.shape, flat),
+            pl.BlockSpec((KNOT, rows, LANES), ahead),
             pl.BlockSpec((KNOT, low.shape[1]), lambda i: (jnp.minimum(i, count - 1), 0)),
             pl.BlockSpec((KNOT, high.shape[1]), lambda i: (jnp.minimum(i, count - 1), 0)),
             pl.BlockSpec(field.shape, lambda i: (0, 0, 0, 0)),
@@ -362,8 +376,9 @@
         ],
         scratch_shapes=[
             *[pltpu.VMEM((3 * KNOT * tiles * (rows + 2 * TOP), LANES), f32)] * 3,
-            pltpu.VMEM((2, rows, LANES), f32),
-            pltpu.VMEM((6 * tiles, KNOT, LANES), f32),
+            pltpu.VMEM((KNOT * rows + 2 * KNOT, width + LANES), bf16),
+            pltpu.VMEM((2, 3 * LANES, 2 * LANES), bf16),
+            pltpu.VMEM((KNOT, LANES), f32),
             pltpu.VMEM((2, tiles, nodes, LANES), f32),
             pltpu.VMEM((8, LANES), f32),
             pltpu.VMEM((KNOT, 8, LANES), f32),
@@ -371,7 +386,7 @@
         compiler_params=grid_params(),
         cost_estimate=pl.CostEstimate(flops=60 * cells.size, bytes_accessed=12 * cells.size, transcendentals=0),
         name="warp",
-    )(cells, image, shift, left, right, low, high, field, plane, depth_factors, diag_depth, diag_plane)
+    )(cells, image, shift, beyond, low, high, field, plane, depth_factors, diag_depth, diag_plane)
 
 
 def gather_kernel(depth_ref, *refs):
@@ -423,9 +438,9 @@
     low, high = packed_rows(left, right, low, high)
     above = shifted(low, "gy", True)
     below = shifted(high, "gy", False)
-    field, diag_depth, diag_plane = terms(sums, plane, depth_factors)
+    field, diag_depth, diag_plane, beyond = terms(sums, plane, depth_factors, left, right, deformed.shape[0])
     residual, depth_terms, plane_terms = warp(
-        deformed, image, displacement, left, right, below, above, field, plane, depth_factors, diag_depth, diag_plane,
+        deformed, image, displacement, beyond, below, above, field, plane, depth_factors, diag_depth, diag_plane,
         n_gy,
     )
     others = [

time: 101 us -> 79.1 us (0.78)
  Pallas kernels: 56.8 us -> 34 us
  local copies, waits for them, and re-layouts: 2.21 us -> 4.38 us
  waiting for transfers between devices: 9.63 us -> 7.95 us
    pallas_call x1, Pallas kernels: 52.6 us -> 29.8 us  [warp(): pl.pallas_call(warp_kernel, grid=(count + 1,), in_specs=[pl.BlockSpec((KN...]
    ppermute x2, waiting for transfers between devices: 5.49 us -> 3.25 us  [shifted(): return lax.ppermute(part, axis, [(i + 1, i) for i in range(count - 1)])]
    unnamed x10 -> x12, local copies, waits for them, and re-layouts: 2.21 us -> 4.38 us
  transfers between devices with their start and end apart: 8 -> 8, of which waited for: 4 -> 5; matrix products, arithmetic and copies ran while one was open for 0% -> 0% of each run, Pallas kernels for 2% -> 3%
where the time goes in v11:
time: 79.1 us; the launch traced here: 78.6 us
  Pallas kernels  34 us (43%)
  starting transfers between devices  20.6 us (26%)
  blocking collectives  10.9 us (14%)
  waiting for transfers between devices  7.95 us (10%)
  local copies, waits for them, and re-layouts  4.38 us (6%)
    pallas_call x1, Pallas kernels, warp(): pl.pallas_call(warp_kernel, grid=(count + 1,), in_specs=[pl.BlockSpec((KN...  29.8 us
    all_to_all x1, blocking collectives, local(): depth_terms = lax.all_to_all(depth_terms, 'gy', 0, 0)  10.9 us
    ppermute x2, starting transfers between devices, shifted(): return lax.ppermute(part, axis, [(i, i + 1) for i in range(count - 1)])  6.35 us
    all_to_all x1, starting transfers between devices, local(): depth_terms = lax.all_to_all(depth_terms, 'gy', 0, 0)  6.35 us
    ppermute x3, starting transfers between devices, local(): lax.ppermute(plane_terms, 'gz', [(i, (i + hop) % n_gz) for i in range(n_g...  5.33 us
    ppermute x3, waiting for transfers between devices, local(): lax.ppermute(plane_terms, 'gz', [(i, (i + hop) % n_gz) for i in range(n_g...  4.69 us
    unnamed x12, local copies, waits for them, and re-layouts  4.38 us
    ppermute x2, waiting for transfers between devices, shifted(): return lax.ppermute(part, axis, [(i + 1, i) for i in range(count - 1)])  3.25 us
  transfers between devices with their start and end apart: 8, of which 5 were waited for; matrix products, arithmetic and copies ran while one was open for 0% of the time, Pallas kernels for 3%

profile of v11, /device:TPU:0, one launch (start us, length us, event | category | flops | bytes accessed | tf_op | source)
XLA Modules:
  0.0 78.6 jit_solution(18117256926312094679)
XLA Ops:
  0.6 0.0 copy-start
  0.6 2.2 %copy-done = bf16[64,64,512]{2,1,0:T(8,128)(2,1)S(1)} copy-done((bf16[64,64,512]{2,1,0:T(8,128)(2,1)S(1)}, bf16[64,64,512]{2,1,0:T(8,128)(2,1)}, u32[]{:S(2)}) %copy-start) | copy-done | bytes 4194328
  2.8 0.0 copy-start.1
  2.8 0.6 columns.1
  3.5 5.1 %collective-permute-start = (bf16[64,128]{1,0:T(8,128)(2,1)S(1)}, bf16[64,128]{1,0:T(8,128)(2,1)S(1)}, u32[]{:S(2)}, u32[]{:S(2)}) collective-permute-start(bf16[64,128]{1,0:T(8,128)(2,1)S(1)} %get-tuple-element.22), channel_id=1, source_target_pairs={{0,1},{1,2},{2,3},{4,5},{5,6},{6,7},{8,9},{9,10},{10,11},{12,13},{... | collective-permute-start | bytes 49160 | tf_op jit(solution)/shard_map/ppermute | solution.py:99
  8.5 1.3 %collective-permute-start.1 = (bf16[64,128]{1,0:T(8,128)(2,1)S(1)}, bf16[64,128]{1,0:T(8,128)(2,1)S(1)}, u32[]{:S(2)}, u32[]{:S(2)}) collective-permute-start(bf16[64,128]{1,0:T(8,128)(2,1)S(1)} %get-tuple-element.23), channel_id=1, source_target_pairs={{1,0},{2,1},{3,2},{5,4},{6,5},{7,6},{9,8},{10,9},{11,10},{13,12},{... | collective-permute-start | bytes 49160 | tf_op jit(solution)/shard_map/ppermute | solution.py:98
  9.8 0.0 copy-done.1
  9.8 0.0 copy-start.2
  9.8 2.2 %copy-done.2 = bf16[64,64,512]{2,1,0:T(8,128)(2,1)S(1)} copy-done((bf16[64,64,512]{2,1,0:T(8,128)(2,1)S(1)}, bf16[64,64,512]{2,1,0:T(8,128)(2,1)}, u32[]{:S(2)}) %copy-start.2) | copy-done | bytes 4194328
  12.0 0.0 copy-start.4
  12.0 0.0 copy-start.5
  12.0 0.0 copy-start.3
  12.0 1.7 %squares.1 = (f32[4,64,128]{2,1,0:T(8,128)S(1)}, f32[64,512]{1,0:T(8,128)S(1)}, f32[64,512]{1,0:T(8,128)S(1)}) custom-call(bf16[64,64,512]{2,1,0:T(8,128)(2,1)S(1)} %copy-done.2, bf16[64,64,512]{2,1,0:T(8,128)(2,1)S(1)} %copy-done.1), custom_call_target="tpu_custom_call" | custom-call | flops 6291456 | bytes 4194304 | tf_op jit(solution)/shard_map/squares/pallas_call | solution.py:134
  13.8 0.0 collective-permute-done.left_ref
  13.8 0.4 collective-permute-done.1.right_ref
  14.2 0.2 rows.1
  14.3 1.3 %collective-permute-start.2 = (bf16[64,640]{1,0:T(8,128)(2,1)S(1)}, bf16[64,640]{1,0:T(8,128)(2,1)S(1)}, u32[]{:S(2)}, u32[]{:S(2)}) collective-permute-start(bf16[64,640]{1,0:T(8,128)(2,1)S(1)} %get-tuple-element.27), channel_id=1, source_target_pairs={{0,4},{4,8},{8,12},{12,16},{16,20},{20,24},{24,28},{1,5},{5,9},{9,... | collective-permute-start | bytes 245768 | tf_op jit(solution)/shard_map/ppermute | solution.py:99
  15.6 1.3 %collective-permute-start.3 = (bf16[64,640]{1,0:T(8,128)(2,1)S(1)}, bf16[64,640]{1,0:T(8,128)(2,1)S(1)}, u32[]{:S(2)}, u32[]{:S(2)}) collective-permute-start(bf16[64,640]{1,0:T(8,128)(2,1)S(1)} %get-tuple-element.28), channel_id=1, source_target_pairs={{4,0},{8,4},{12,8},{16,12},{20,16},{24,20},{28,24},{5,1},{9,5},{13... | collective-permute-start | bytes 245768 | tf_op jit(solution)/shard_map/ppermute | solution.py:98
  16.9 0.0 copy-done.4
  16.9 0.0 copy-done.5
  16.9 0.7 terms.1
  17.6 0.0 collective-permute-done.2.low_ref
  17.6 2.9 %collective-permute-done.3.high_ref = bf16[64,640]{1,0:T(8,128)(2,1)S(1)} collective-permute-done((bf16[64,640]{1,0:T(8,128)(2,1)S(1)}, bf16[64,640]{1,0:T(8,128)(2,1)S(1)}, u32[]{:S(2)}, u32[]{:S(2)}) %collective-permute-start.3) | collective-permute-done | bytes 81952 | tf_op jit(solution)/shard_map/ppermute | solution.py:98
  20.5 0.0 copy-done.3
  20.5 29.8 %warp.1 = (bf16[64,64,512]{2,1,0:T(8,128)(2,1)}, f32[8,16,512]{2,1,0:T(8,128)}, f32[64,128]{1,0:T(8,128)S(1)}) custom-call(bf16[64,64,512]{2,1,0:T(8,128)(2,1)S(1)} %copy-done.1, bf16[64,64,512]{2,1,0:T(8,128)(2,1)S(1)} %copy-done.3, bf16[3,64,64,512]{3,2,1,0:T(8,128)(2,1)} %shift_ref.1, bf16[64,64,128]{2,1,0:T(8,128)(2,1)S(1)} %get-tuple-element.24.beyond_ref, ...), custom_call_target="tpu_custom_call" | custom-call | flops 125829120 | bytes 25165824 | tf_op jit(solution)/shard_map/warp/pallas_call | solution.py:351
  50.3 6.3 %all-to-all-start = ((f32[8,16,512]{2,1,0:T(8,128)}), f32[8,16,512]{2,1,0:T(8,128)S(1)}, u32[]{:S(2)}, u32[]{:S(2)}) async-start(f32[8,16,512]{2,1,0:T(8,128)} %get-tuple-element.33), calls=%async_computation | async-start | bytes 524288 | tf_op jit(solution)/shard_map/all_to_all | solution.py:449
  56.7 4.3 %collective-permute-start.6 = (f32[64,128]{1,0:T(8,128)S(1)}, f32[64,128]{1,0:T(8,128)S(1)}, u32[]{:S(2)}, u32[]{:S(2)}) collective-permute-start(f32[64,128]{1,0:T(8,128)S(1)} %get-tuple-element.34.refs_0_), channel_id=1, source_target_pairs={{0,3},{1,0},{2,1},{3,2},{4,7},{5,4},{6,5},{7,6},{8,11},{9,8},{10,9... | collective-permute-start | bytes 98312 | tf_op jit(solution)/shard_map/ppermute | solution.py:447
  61.0 0.0 collective-permute-start.5
  61.0 1.0 %collective-permute-start.4 = (f32[64,128]{1,0:T(8,128)S(1)}, f32[64,128]{1,0:T(8,128)S(1)}, u32[]{:S(2)}, u32[]{:S(2)}) collective-permute-start(f32[64,128]{1,0:T(8,128)S(1)} %get-tuple-element.34.refs_0_), channel_id=1, source_target_pairs={{0,1},{1,2},{2,3},{3,0},{4,5},{5,6},{6,7},{7,4},{8,9},{9,10},{10,1... | collective-permute-start | bytes 98312 | tf_op jit(solution)/shard_map/ppermute | solution.py:447
  62.0 0.7 collective-permute-done.6.refs_3_
  62.7 3.5 %collective-permute-done.5.refs_2_ = f32[64,128]{1,0:T(8,128)S(1)} collective-permute-done((f32[64,128]{1,0:T(8,128)S(1)}, f32[64,128]{1,0:T(8,128)S(1)}, u32[]{:S(2)}, u32[]{:S(2)}) %collective-permute-start.5) | collective-permute-done | bytes 32800 | tf_op jit(solution)/shard_map/ppermute | solution.py:447
  66.1 0.6 collective-permute-done.4.refs_1_
  66.7 0.0 all-to-all-done.depth_ref
  66.7 0.1 gather.1
  66.8 10.9 %all_to_all.10.depth_ref = f32[8,16,512]{2,1,0:T(8,128)S(1)} all-to-all(f32[8,16,512]{2,1,0:T(8,128)S(1)} %get-tuple-element.35), channel_id=1, replica_groups=mesh['gy'=8,'gz'=4] {'gy'}, dimensions={0} | all-to-all | bytes 524288 | tf_op jit(solution)/shard_map/all_to_all | solution.py:459
  77.8 0.9 %steps.1 = (f32[2,32,512]{2,1,0:T(8,128)}, f32[2,64,32]{2,1,0:T(8,128)}) custom-call(f32[8,16,512]{2,1,0:T(8,128)S(1)} %all_to_all.10.depth_ref, f32[64,128]{1,0:T(8,128)S(1)} %get-tuple-element.36.plane_ref), custom_call_target="tpu_custom_call" | custom-call | tf_op jit(solution)/shard_map/steps/pallas_call | solution.py:461
Async XLA Ops:
  0.6 2.2 %copy-start = (bf16[64,64,512]{2,1,0:T(8,128)(2,1)S(1)}, bf16[64,64,512]{2,1,0:T(8,128)(2,1)}, u32[]{:S(2)}) copy-start(bf16[64,64,512]{2,1,0:T(8,128)(2,1)} %cells_ref.5) | copy-start | bytes 12582916
  2.8 7.0 %copy-start.1 = (bf16[64,64,512]{2,1,0:T(8,128)(2,1)S(1)}, bf16[64,64,512]{2,1,0:T(8,128)(2,1)}, u32[]{:S(2)}) copy-start(bf16[64,64,512]{2,1,0:T(8,128)(2,1)} %cells_ref.5) | copy-start | bytes 12582916
  3.5 10.3 %collective-permute-start = (bf16[64,128]{1,0:T(8,128)(2,1)S(1)}, bf16[64,128]{1,0:T(8,128)(2,1)S(1)}, u32[]{:S(2)}, u32[]{:S(2)}) collective-permute-start(bf16[64,128]{1,0:T(8,128)(2,1)S(1)} %get-tuple-element.22), channel_id=1, source_target_pairs={{0,1},{1,2},{2,3},{4,5},{5,6},{6,7},{8,9},{9,10},{10,11},{12,13},{... | collective-permute-start | bytes 49160 | tf_op jit(solution)/shard_map/ppermute | solution.py:99
  8.5 5.6 %collective-permute-start.1 = (bf16[64,128]{1,0:T(8,128)(2,1)S(1)}, bf16[64,128]{1,0:T(8,128)(2,1)S(1)}, u32[]{:S(2)}, u32[]{:S(2)}) collective-permute-start(bf16[64,128]{1,0:T(8,128)(2,1)S(1)} %get-tuple-element.23), channel_id=1, source_target_pairs={{1,0},{2,1},{3,2},{5,4},{6,5},{7,6},{9,8},{10,9},{11,10},{13,12},{... | collective-permute-start | bytes 49160 | tf_op jit(solution)/shard_map/ppermute | solution.py:98
  9.8 2.2 %copy-start.2 = (bf16[64,64,512]{2,1,0:T(8,128)(2,1)S(1)}, bf16[64,64,512]{2,1,0:T(8,128)(2,1)}, u32[]{:S(2)}) copy-start(bf16[64,64,512]{2,1,0:T(8,128)(2,1)} %image_ref.3) | copy-start | bytes 12582916
  12.0 4.9 %copy-start.4 = (f32[2,32,512]{2,1,0:T(8,128)S(1)}, f32[2,32,512]{2,1,0:T(8,128)}, u32[]{:S(2)}) copy-start(f32[2,32,512]{2,1,0:T(8,128)} %depth_ref.3) | copy-start | bytes 393220
  12.0 4.9 %copy-start.5 = (f32[2,32,8,8]{1,3,2,0:T(8,128)S(1)}, f32[2,32,8,8]{1,3,2,0:T(8,128)}, u32[]{:S(2)}) copy-start(f32[2,32,8,8]{1,3,2,0:T(8,128)} %param.8) | copy-start | bytes 49156
  12.0 8.5 %copy-start.3 = (bf16[64,64,512]{2,1,0:T(8,128)(2,1)S(1)}, bf16[64,64,512]{2,1,0:T(8,128)(2,1)}, u32[]{:S(2)}) copy-start(bf16[64,64,512]{2,1,0:T(8,128)(2,1)} %image_ref.3) | copy-start | bytes 12582916
  14.3 3.3 %collective-permute-start.2 = (bf16[64,640]{1,0:T(8,128)(2,1)S(1)}, bf16[64,640]{1,0:T(8,128)(2,1)S(1)}, u32[]{:S(2)}, u32[]{:S(2)}) collective-permute-start(bf16[64,640]{1,0:T(8,128)(2,1)S(1)} %get-tuple-element.27), channel_id=1, source_target_pairs={{0,4},{4,8},{8,12},{12,16},{16,20},{20,24},{24,28},{1,5},{5,9},{9,... | collective-permute-start | bytes 245768 | tf_op jit(solution)/shard_map/ppermute | solution.py:99
  15.6 4.9 %collective-permute-start.3 = (bf16[64,640]{1,0:T(8,128)(2,1)S(1)}, bf16[64,640]{1,0:T(8,128)(2,1)S(1)}, u32[]{:S(2)}, u32[]{:S(2)}) collective-permute-start(bf16[64,640]{1,0:T(8,128)(2,1)S(1)} %get-tuple-element.28), channel_id=1, source_target_pairs={{4,0},{8,4},{12,8},{16,12},{20,16},{24,20},{28,24},{5,1},{9,5},{13... | collective-permute-start | bytes 245768 | tf_op jit(solution)/shard_map/ppermute | solution.py:98
  50.3 16.4 %all-to-all-start = ((f32[8,16,512]{2,1,0:T(8,128)}), f32[8,16,512]{2,1,0:T(8,128)S(1)}, u32[]{:S(2)}, u32[]{:S(2)}) async-start(f32[8,16,512]{2,1,0:T(8,128)} %get-tuple-element.33), calls=%async_computation | async-start | bytes 524288 | tf_op jit(solution)/shard_map/all_to_all | solution.py:449
  56.7 6.0 %collective-permute-start.6 = (f32[64,128]{1,0:T(8,128)S(1)}, f32[64,128]{1,0:T(8,128)S(1)}, u32[]{:S(2)}, u32[]{:S(2)}) collective-permute-start(f32[64,128]{1,0:T(8,128)S(1)} %get-tuple-element.34.refs_0_), channel_id=1, source_target_pairs={{0,3},{1,0},{2,1},{3,2},{4,7},{5,4},{6,5},{7,6},{8,11},{9,8},{10,9... | collective-permute-start | bytes 98312 | tf_op jit(solution)/shard_map/ppermute | solution.py:447
  61.0 5.2 %collective-permute-start.5 = (f32[64,128]{1,0:T(8,128)S(1)}, f32[64,128]{1,0:T(8,128)S(1)}, u32[]{:S(2)}, u32[]{:S(2)}) collective-permute-start(f32[64,128]{1,0:T(8,128)S(1)} %get-tuple-element.34.refs_0_), channel_id=1, source_target_pairs={{0,2},{1,3},{2,0},{3,1},{4,6},{5,7},{6,4},{7,5},{8,10},{9,11},{10,... | collective-permute-start | bytes 98312 | tf_op jit(solution)/shard_map/ppermute | solution.py:447
  61.0 5.7 %collective-permute-start.4 = (f32[64,128]{1,0:T(8,128)S(1)}, f32[64,128]{1,0:T(8,128)S(1)}, u32[]{:S(2)}, u32[]{:S(2)}) collective-permute-start(f32[64,128]{1,0:T(8,128)S(1)} %get-tuple-element.34.refs_0_), channel_id=1, source_target_pairs={{0,1},{1,2},{2,3},{3,0},{4,5},{5,6},{6,7},{7,4},{8,9},{9,10},{10,1... | collective-permute-start | bytes 98312 | tf_op jit(solution)/shard_map/ppermute | solution.py:447

commit v12 on v11

--- a/solution.py
+++ b/solution.py
@@ -44,7 +44,7 @@
     return pltpu.CompilerParams(vmem_limit_bytes=32000000)
 
 
-def columns_kernel(cells_ref, first_ref, last_ref):
+def ends_kernel(cells_ref, first_ref, last_ref, low_ref, high_ref):
     depth, rows, width = cells_ref.shape
     lane = lax.broadcasted_iota(jnp.int32, (rows, LANES), 1)
     first = jnp.zeros((rows, LANES), f32)
@@ -56,40 +56,37 @@
         last = jnp.where(lane == x, pltpu.roll(far, (x + 1) % LANES, 1), last)
     first_ref[...] = first.astype(bf16)
     last_ref[...] = last.astype(bf16)
-
-
-def end_columns(cells):
-    rows = cells.shape[1]
+    for x in range(0, depth, 16):
+        low = [cells_ref[x + k, 0:16, :].astype(f32)[0:1] for k in range(16)]
+        high = [cells_ref[x + k, rows - 16 : rows, :].astype(f32)[15:16] for k in range(16)]
+        low_ref[x : x + 16, :] = jnp.concatenate(low, axis=0).astype(bf16)
+        high_ref[x : x + 16, :] = jnp.concatenate(high, axis=0).astype(bf16)
+
+
+def ends(cells):
+    depth, rows, width = cells.shape
     return pl.pallas_call(
-        columns_kernel,
-        out_shape=[jax.ShapeDtypeStruct((rows, LANES), bf16)] * 2,
-        compiler_params=plain_params(),
-        name="columns",
+        ends_kernel,
+        out_shape=[jax.ShapeDtypeStruct((rows, LANES), bf16)] * 2 + [jax.ShapeDtypeStruct((depth, width), bf16)] * 2,
+        compiler_params=plain_params(),
+        name="ends",
     )(cells)
 
 
-def rows_kernel(left_ref, right_ref, low_ref, high_ref, low_out, high_out):
-    depth, width = low_ref.shape
-    rows = left_ref.shape[0]
-    lane = lax.broadcasted_iota(jnp.int32, (depth, LANES), 1)
-    pad = jnp.zeros((LANES - rows, LANES), f32)
-    left = jnp.transpose(jnp.concatenate([left_ref[...].astype(f32), pad], axis=0))[0:depth]
-    right = jnp.transpose(jnp.concatenate([right_ref[...].astype(f32), pad], axis=0))[0:depth]
-    for row, body, out in ((0, low_ref, low_out), (rows - 1, high_ref, high_out)):
-        after = pltpu.roll(right, (LANES - row) % LANES, 1)
-        before = pltpu.roll(left, LANES - 1 - row, 1)
-        out[:, 0:width] = body[...].astype(bf16)
-        out[:, width : width + LANES] = jnp.where(lane == 0, after, before).astype(bf16)
-
-
-def packed_rows(left, right, low, high):
-    depth, width = low.shape
+def corners_kernel(below_ref, above_ref, first_ref, last_ref):
+    width = below_ref.shape[1]
+    for k, ref in enumerate((below_ref, above_ref)):
+        first_ref[k] = ref[:, 0:LANES]
+        last_ref[k] = ref[:, width - LANES : width]
+
+
+def corners(below, above):
     return pl.pallas_call(
-        rows_kernel,
-        out_shape=[jax.ShapeDtypeStruct((depth, width + LANES), bf16)] * 2,
-        compiler_params=plain_params(),
-        name="rows",
-    )(left, right, low, high)
+        corners_kernel,
+        out_shape=[jax.ShapeDtypeStruct((2, below.shape[0], LANES), bf16)] * 2,
+        compiler_params=plain_params(),
+        name="corners",
+    )(below, above)
 
 
 def shifted(part, axis, back):
@@ -99,7 +96,7 @@
     return lax.ppermute(part, axis, [(i, i + 1) for i in range(count - 1)])
 
 
-def squares_kernel(image_ref, cells_ref, sums, low_ref, high_ref):
+def squares_kernel(image_ref, sums):
     depth, rows, width = image_ref.shape
     tiles = width // LANES
 
@@ -118,30 +115,16 @@
 
     lax.fori_loop(0, depth // KNOT * tiles, one, 0)
 
-    def ends(block, carry):
-        x = pl.multiple_of(block * KNOT, KNOT)
-        low = [cells_ref[x + k, 0:16, :].astype(f32)[0:1] for k in range(KNOT)]
-        high = [cells_ref[x + k, rows - 16 : rows, :].astype(f32)[15:16] for k in range(KNOT)]
-        low_ref[pl.ds(x, KNOT), :] = jnp.concatenate(low, axis=0)
-        high_ref[pl.ds(x, KNOT), :] = jnp.concatenate(high, axis=0)
-        return carry
-
-    lax.fori_loop(0, depth // KNOT, ends, 0)
-
-
-def squares(image, cells):
+
+def squares(image):
     depth, rows, width = image.shape
     return pl.pallas_call(
         squares_kernel,
-        out_shape=[
-            jax.ShapeDtypeStruct((width // LANES, depth * rows // KNOT**2, LANES), f32),
-            jax.ShapeDtypeStruct((depth, width), f32),
-            jax.ShapeDtypeStruct((depth, width), f32),
-        ],
+        out_shape=jax.ShapeDtypeStruct((width // LANES, depth * rows // KNOT**2, LANES), f32),
         compiler_params=plain_params(),
         cost_estimate=pl.CostEstimate(flops=3 * image.size, bytes_accessed=2 * image.size, transcendentals=0),
         name="squares",
-    )(image, cells)
+    )(image)
 
 
 def terms_kernel(
@@ -185,7 +168,7 @@
 
 
 def warp_kernel(
-    cells_ref, image_ref, shift_ref, beyond_ref, low_ref, high_ref, field, plane_ref, depth_ref,
+    cells_ref, image_ref, shift_ref, beyond_ref, low_ref, high_ref, before_ref, after_ref, field, plane_ref, depth_ref,
     diag_depth_ref, diag_plane_ref,
     residual_ref, depth_out, plane_out,
     ahead_ref, here_ref, behind_ref, wide, bands, rims, blocks, energy, held,
@@ -221,7 +204,11 @@
         for k in range(planes):
             wide[k * rows : (k + 1) * rows, 0:width] = cells_ref[k]
             wide[k * rows : (k + 1) * rows, width:] = beyond_ref[k]
-        wide[span:, :] = jnp.concatenate([low_ref[...].astype(f32), high_ref[...].astype(f32)], axis=0).astype(bf16)
+        rim = jnp.concatenate([low_ref[...].astype(f32), high_ref[...].astype(f32)], axis=0)
+        wide[span:, 0:width] = rim.astype(bf16)
+        lane = lax.broadcasted_iota(jnp.int32, (planes, LANES), 1)
+        rim = [jnp.where(lane == 0, after_ref[k].astype(f32), before_ref[k].astype(f32)) for k in range(2)]
+        wide[span:, width:] = jnp.concatenate(rim, axis=0).astype(bf16)
 
         def put(c, tile, values):
             for k in range(planes):
@@ -339,7 +326,9 @@
         plane_out[count // 2 :, 3 * RANK :] = jnp.full((count // 2, RANK), local, f32)
 
 
-def warp(cells, image, shift, beyond, low, high, field, plane, depth_factors, diag_depth, diag_plane, parts):
+def warp(
+    cells, image, shift, beyond, low, high, before, after, field, plane, depth_factors, diag_depth, diag_plane, parts
+):
     depth, rows, width = cells.shape
     nodes = plane.shape[1]
     tiles = width // LANES
@@ -358,6 +347,8 @@
             pl.BlockSpec((KNOT, rows, LANES), ahead),
             pl.BlockSpec((KNOT, low.shape[1]), lambda i: (jnp.minimum(i, count - 1), 0)),
             pl.BlockSpec((KNOT, high.shape[1]), lambda i: (jnp.minimum(i, count - 1), 0)),
+            pl.BlockSpec((2, KNOT, LANES), lambda i: (0, jnp.minimum(i, count - 1), 0)),
+            pl.BlockSpec((2, KNOT, LANES), lambda i: (0, jnp.minimum(i, count - 1), 0)),
             pl.BlockSpec(field.shape, lambda i: (0, 0, 0, 0)),
             pl.BlockSpec(plane.shape, whole),
             pl.BlockSpec(depth_factors.shape, whole),
@@ -386,7 +377,7 @@
         compiler_params=grid_params(),
         cost_estimate=pl.CostEstimate(flops=60 * cells.size, bytes_accessed=12 * cells.size, transcendentals=0),
         name="warp",
-    )(cells, image, shift, beyond, low, high, field, plane, depth_factors, diag_depth, diag_plane)
+    )(cells, image, shift, beyond, low, high, before, after, field, plane, depth_factors, diag_depth, diag_plane)
 
 
 def gather_kernel(depth_ref, *refs):
@@ -431,17 +422,19 @@
     n_gy, n_gz = lax.axis_size("gy"), lax.axis_size("gz")
     nodes_x, nodes_y = plane_factors.shape[2:]
     plane = jnp.transpose(plane_factors, (0, 2, 3, 1)).reshape(2, nodes_x * nodes_y, RANK)
-    first, last = end_columns(deformed)
+    first, last, low, high = ends(deformed)
+    above = shifted(low, "gy", True)
+    below = shifted(high, "gy", False)
     right = shifted(first, "gz", True)
     left = shifted(last, "gz", False)
-    sums, low, high = squares(image, deformed)
-    low, high = packed_rows(left, right, low, high)
-    above = shifted(low, "gy", True)
-    below = shifted(high, "gy", False)
+    sums = squares(image)
+    first, last = corners(below, above)
+    after = shifted(first, "gz", True)
+    before = shifted(last, "gz", False)
     field, diag_depth, diag_plane, beyond = terms(sums, plane, depth_factors, left, right, deformed.shape[0])
     residual, depth_terms, plane_terms = warp(
-        deformed, image, displacement, beyond, below, above, field, plane, depth_factors, diag_depth, diag_plane,
-        n_gy,
+        deformed, image, displacement, beyond, below, above, before, after, field, plane, depth_factors,
+        diag_depth, diag_plane, n_gy,
     )
     others = [
         lax.ppermute(plane_terms, "gz", [(i, (i + hop) % n_gz) for i in range(n_gz)]) for hop in range(1, n_gz)

time: 79.1 us -> 84.4 us (1.067)
  starting transfers between devices: 20.6 us -> 24.6 us
  waiting for transfers between devices: 7.95 us -> 9.27 us
    ppermute x2 -> x3, starting transfers between devices: 6.35 us -> 10.5 us  [shifted(): return lax.ppermute(part, axis, [(i, i + 1) for i in range(count - 1)])]
    all_to_all x1, starting transfers between devices: 6.35 us -> 5.02 us  [local(): depth_terms = lax.all_to_all(depth_terms, 'gy', 0, 0)]
    ppermute x2 -> x3, waiting for transfers between devices: 3.25 us -> 4.56 us  [shifted(): return lax.ppermute(part, axis, [(i + 1, i) for i in range(count - 1)])]
    ppermute x2 -> x3, starting transfers between devices: 2.58 us -> 3.88 us  [shifted(): return lax.ppermute(part, axis, [(i + 1, i) for i in range(count - 1)])]
  transfers between devices with their start and end apart: 8 -> 10, of which waited for: 5 -> 5; matrix products, arithmetic and copies ran while one was open for 0% -> 0% of each run, Pallas kernels for 3% -> 3%
where the time goes in v12:
time: 84.4 us; the launch traced here: 83.9 us
  Pallas kernels  34 us (40%)
  starting transfers between devices  24.6 us (29%)
  blocking collectives  10.9 us (13%)
  waiting for transfers between devices  9.27 us (11%)
  local copies, waits for them, and re-layouts  4.38 us (5%)
    pallas_call x1, Pallas kernels, warp(): pl.pallas_call(warp_kernel, grid=(count + 1,), in_specs=[pl.BlockSpec((KN...  30 us
    all_to_all x1, blocking collectives, local(): depth_terms = lax.all_to_all(depth_terms, 'gy', 0, 0)  10.9 us
    ppermute x3, starting transfers between devices, shifted(): return lax.ppermute(part, axis, [(i, i + 1) for i in range(count - 1)])  10.5 us
    ppermute x3, starting transfers between devices, local(): lax.ppermute(plane_terms, 'gz', [(i, (i + hop) % n_gz) for i in range(n_g...  5.17 us
    all_to_all x1, starting transfers between devices, local(): depth_terms = lax.all_to_all(depth_terms, 'gy', 0, 0)  5.02 us
    ppermute x3, waiting for transfers between devices, local(): lax.ppermute(plane_terms, 'gz', [(i, (i + hop) % n_gz) for i in range(n_g...  4.7 us
    ppermute x3, waiting for transfers between devices, shifted(): return lax.ppermute(part, axis, [(i + 1, i) for i in range(count - 1)])  4.56 us
    unnamed x12, local copies, waits for them, and re-layouts  4.38 us
  transfers between devices with their start and end apart: 10, of which 5 were waited for; matrix products, arithmetic and copies ran while one was open for 0% of the time, Pallas kernels for 3%

profile of v12, /device:TPU:0, one launch (start us, length us, event | category | flops | bytes accessed | tf_op | source)
XLA Modules:
  0.0 83.9 jit_solution(589080754690203509)
XLA Ops:
  0.6 0.0 copy-start
  0.6 2.2 %copy-done = bf16[64,64,512]{2,1,0:T(8,128)(2,1)S(1)} copy-done((bf16[64,64,512]{2,1,0:T(8,128)(2,1)S(1)}, bf16[64,64,512]{2,1,0:T(8,128)(2,1)}, u32[]{:S(2)}) %copy-start) | copy-done | bytes 4194328
  2.8 0.0 copy-start.4
  2.8 0.0 copy-start.1
  2.8 0.8 ends.1
  3.6 2.5 %collective-permute-start.2 = (bf16[64,512]{1,0:T(8,128)(2,1)S(1)}, bf16[64,512]{1,0:T(8,128)(2,1)S(1)}, u32[]{:S(2)}, u32[]{:S(2)}) collective-permute-start(bf16[64,512]{1,0:T(8,128)(2,1)S(1)} %get-tuple-element.23), channel_id=1, source_target_pairs={{0,4},{4,8},{8,12},{12,16},{16,20},{20,24},{24,28},{1,5},{5,9},{9,... | collective-permute-start | bytes 196616 | tf_op jit(solution)/shard_map/ppermute | solution.py:96
  6.1 1.3 %collective-permute-start.3 = (bf16[64,512]{1,0:T(8,128)(2,1)S(1)}, bf16[64,512]{1,0:T(8,128)(2,1)S(1)}, u32[]{:S(2)}, u32[]{:S(2)}) collective-permute-start(bf16[64,512]{1,0:T(8,128)(2,1)S(1)} %get-tuple-element.24), channel_id=1, source_target_pairs={{4,0},{8,4},{12,8},{16,12},{20,16},{24,20},{28,24},{5,1},{9,5},{13... | collective-permute-start | bytes 196616 | tf_op jit(solution)/shard_map/ppermute | solution.py:95
  7.4 0.0 collective-permute-done.2.below_ref.low_ref
  7.5 3.9 %collective-permute-done.3.above_ref.high_ref = bf16[64,512]{1,0:T(8,128)(2,1)S(1)} collective-permute-done((bf16[64,512]{1,0:T(8,128)(2,1)S(1)}, bf16[64,512]{1,0:T(8,128)(2,1)S(1)}, u32[]{:S(2)}, u32[]{:S(2)}) %collective-permute-start.3) | collective-permute-done | bytes 65568 | tf_op jit(solution)/shard_map/ppermute | solution.py:95
  11.4 3.5 %collective-permute-start.4 = (bf16[2,64,128]{2,1,0:T(8,128)(2,1)S(1)}, bf16[2,64,128]{2,1,0:T(8,128)(2,1)S(1)}, u32[]{:S(2)}, u32[]{:S(2)}) collective-permute-start(bf16[2,64,128]{2,1,0:T(8,128)(2,1)S(1)} %get-tuple-element.25), channel_id=1, source_target_pairs={{0,1},{1,2},{2,3},{4,5},{5,6},{6,7},{8,9},{9,10},{10,11},{12,13},{... | collective-permute-start | bytes 98312 | tf_op jit(solution)/shard_map/ppermute | solution.py:96
  14.9 1.3 %collective-permute-start.5 = (bf16[2,64,128]{2,1,0:T(8,128)(2,1)S(1)}, bf16[2,64,128]{2,1,0:T(8,128)(2,1)S(1)}, u32[]{:S(2)}, u32[]{:S(2)}) collective-permute-start(bf16[2,64,128]{2,1,0:T(8,128)(2,1)S(1)} %get-tuple-element.26), channel_id=1, source_target_pairs={{1,0},{2,1},{3,2},{5,4},{6,5},{7,6},{9,8},{10,9},{11,10},{13,12},{... | collective-permute-start | bytes 98312 | tf_op jit(solution)/shard_map/ppermute | solution.py:95
  16.2 4.5 %collective-permute-start = (bf16[64,128]{1,0:T(8,128)(2,1)S(1)}, bf16[64,128]{1,0:T(8,128)(2,1)S(1)}, u32[]{:S(2)}, u32[]{:S(2)}) collective-permute-start(bf16[64,128]{1,0:T(8,128)(2,1)S(1)} %get-tuple-element.20), channel_id=1, source_target_pairs={{0,1},{1,2},{2,3},{4,5},{5,6},{6,7},{8,9},{9,10},{10,11},{12,13},{... | collective-permute-start | bytes 49160 | tf_op jit(solution)/shard_map/ppermute | solution.py:96
  20.8 1.3 %collective-permute-start.1 = (bf16[64,128]{1,0:T(8,128)(2,1)S(1)}, bf16[64,128]{1,0:T(8,128)(2,1)S(1)}, u32[]{:S(2)}, u32[]{:S(2)}) collective-permute-start(bf16[64,128]{1,0:T(8,128)(2,1)S(1)} %get-tuple-element.21), channel_id=1, source_target_pairs={{1,0},{2,1},{3,2},{5,4},{6,5},{7,6},{9,8},{10,9},{11,10},{13,12},{... | collective-permute-start | bytes 49160 | tf_op jit(solution)/shard_map/ppermute | solution.py:95
  22.1 0.0 copy-start.2
  22.1 2.2 %copy-done.2 = bf16[64,64,512]{2,1,0:T(8,128)(2,1)S(1)} copy-done((bf16[64,64,512]{2,1,0:T(8,128)(2,1)S(1)}, bf16[64,64,512]{2,1,0:T(8,128)(2,1)}, u32[]{:S(2)}) %copy-start.2) | copy-done | bytes 4194328
  24.3 0.0 copy-start.5
  24.3 0.0 copy-start.3
  24.3 1.5 %squares.1.sums = f32[4,64,128]{2,1,0:T(8,128)S(1)} custom-call(bf16[64,64,512]{2,1,0:T(8,128)(2,1)S(1)} %copy-done.2), custom_call_target="tpu_custom_call" | custom-call | flops 6291456 | bytes 4194304 | tf_op jit(solution)/shard_map/squares/pallas_call | solution.py:121
  25.8 0.0 collective-permute-done.left_ref
  25.8 0.6 collective-permute-done.1.right_ref
  26.4 0.0 copy-done.4
  26.4 0.0 copy-done.5
  26.4 0.7 terms.1
  27.1 0.0 collective-permute-done.4.before_ref
  27.1 0.0 collective-permute-done.5.after_ref
  27.1 0.0 copy-done.1
  27.1 0.0 copy-done.3
  27.1 30.0 %warp.1 = (bf16[64,64,512]{2,1,0:T(8,128)(2,1)}, f32[8,16,512]{2,1,0:T(8,128)}, f32[64,128]{1,0:T(8,128)S(1)}) custom-call(bf16[64,64,512]{2,1,0:T(8,128)(2,1)S(1)} %copy-done.1, bf16[64,64,512]{2,1,0:T(8,128)(2,1)S(1)} %copy-done.3, bf16[3,64,64,512]{3,2,1,0:T(8,128)(2,1)} %shift_ref.1, bf16[64,64,128]{2,1,0:T(8,128)(2,1)S(1)} %get-tuple-element.22.beyond_ref, ...), custom_call_target="tpu_custom_call" | custom-call | flops 125829120 | bytes 25165824 | tf_op jit(solution)/shard_map/warp/pallas_call | solution.py:340
  57.1 5.0 %all-to-all-start = ((f32[8,16,512]{2,1,0:T(8,128)}), f32[8,16,512]{2,1,0:T(8,128)S(1)}, u32[]{:S(2)}, u32[]{:S(2)}) async-start(f32[8,16,512]{2,1,0:T(8,128)} %get-tuple-element.31), calls=%async_computation | async-start | bytes 524288 | tf_op jit(solution)/shard_map/all_to_all | solution.py:442
  62.1 4.2 %collective-permute-start.8 = (f32[64,128]{1,0:T(8,128)S(1)}, f32[64,128]{1,0:T(8,128)S(1)}, u32[]{:S(2)}, u32[]{:S(2)}) collective-permute-start(f32[64,128]{1,0:T(8,128)S(1)} %get-tuple-element.32.refs_0_), channel_id=1, source_target_pairs={{0,3},{1,0},{2,1},{3,2},{4,7},{5,4},{6,5},{7,6},{8,11},{9,8},{10,9... | collective-permute-start | bytes 98312 | tf_op jit(solution)/shard_map/ppermute | solution.py:440
  66.3 0.0 collective-permute-start.7
  66.3 1.0 %collective-permute-start.6 = (f32[64,128]{1,0:T(8,128)S(1)}, f32[64,128]{1,0:T(8,128)S(1)}, u32[]{:S(2)}, u32[]{:S(2)}) collective-permute-start(f32[64,128]{1,0:T(8,128)S(1)} %get-tuple-element.32.refs_0_), channel_id=1, source_target_pairs={{0,1},{1,2},{2,3},{3,0},{4,5},{5,6},{6,7},{7,4},{8,9},{9,10},{10,1... | collective-permute-start | bytes 98312 | tf_op jit(solution)/shard_map/ppermute | solution.py:440
  67.3 0.7 collective-permute-done.8.refs_3_
  68.0 3.5 %collective-permute-done.7.refs_2_ = f32[64,128]{1,0:T(8,128)S(1)} collective-permute-done((f32[64,128]{1,0:T(8,128)S(1)}, f32[64,128]{1,0:T(8,128)S(1)}, u32[]{:S(2)}, u32[]{:S(2)}) %collective-permute-start.7) | collective-permute-done | bytes 32800 | tf_op jit(solution)/shard_map/ppermute | solution.py:440
  71.4 0.6 collective-permute-done.6.refs_1_
  72.0 0.0 all-to-all-done.depth_ref
  72.0 0.1 gather.1
  72.1 10.9 %all_to_all.10.depth_ref = f32[8,16,512]{2,1,0:T(8,128)S(1)} all-to-all(f32[8,16,512]{2,1,0:T(8,128)S(1)} %get-tuple-element.33), channel_id=1, replica_groups=mesh['gy'=8,'gz'=4] {'gy'}, dimensions={0} | all-to-all | bytes 524288 | tf_op jit(solution)/shard_map/all_to_all | solution.py:452
  83.1 0.9 %steps.1 = (f32[2,32,512]{2,1,0:T(8,128)}, f32[2,64,32]{2,1,0:T(8,128)}) custom-call(f32[8,16,512]{2,1,0:T(8,128)S(1)} %all_to_all.10.depth_ref, f32[64,128]{1,0:T(8,128)S(1)} %get-tuple-element.34.plane_ref), custom_call_target="tpu_custom_call" | custom-call | tf_op jit(solution)/shard_map/steps/pallas_call | solution.py:454
  (1 shorter events, 0.0 us)
Async XLA Ops:
  0.6 2.2 %copy-start = (bf16[64,64,512]{2,1,0:T(8,128)(2,1)S(1)}, bf16[64,64,512]{2,1,0:T(8,128)(2,1)}, u32[]{:S(2)}) copy-start(bf16[64,64,512]{2,1,0:T(8,128)(2,1)} %cells_ref.3) | copy-start | bytes 12582916
  2.8 23.6 %copy-start.4 = (f32[2,32,512]{2,1,0:T(8,128)S(1)}, f32[2,32,512]{2,1,0:T(8,128)}, u32[]{:S(2)}) copy-start(f32[2,32,512]{2,1,0:T(8,128)} %depth_ref.3) | copy-start | bytes 393220
  2.8 24.3 %copy-start.1 = (bf16[64,64,512]{2,1,0:T(8,128)(2,1)S(1)}, bf16[64,64,512]{2,1,0:T(8,128)(2,1)}, u32[]{:S(2)}) copy-start(bf16[64,64,512]{2,1,0:T(8,128)(2,1)} %cells_ref.3) | copy-start | bytes 12582916
  3.6 3.8 %collective-permute-start.2 = (bf16[64,512]{1,0:T(8,128)(2,1)S(1)}, bf16[64,512]{1,0:T(8,128)(2,1)S(1)}, u32[]{:S(2)}, u32[]{:S(2)}) collective-permute-start(bf16[64,512]{1,0:T(8,128)(2,1)S(1)} %get-tuple-element.23), channel_id=1, source_target_pairs={{0,4},{4,8},{8,12},{12,16},{16,20},{20,24},{24,28},{1,5},{5,9},{9,... | collective-permute-start | bytes 196616 | tf_op jit(solution)/shard_map/ppermute | solution.py:96
  6.1 5.3 %collective-permute-start.3 = (bf16[64,512]{1,0:T(8,128)(2,1)S(1)}, bf16[64,512]{1,0:T(8,128)(2,1)S(1)}, u32[]{:S(2)}, u32[]{:S(2)}) collective-permute-start(bf16[64,512]{1,0:T(8,128)(2,1)S(1)} %get-tuple-element.24), channel_id=1, source_target_pairs={{4,0},{8,4},{12,8},{16,12},{20,16},{24,20},{28,24},{5,1},{9,5},{13... | collective-permute-start | bytes 196616 | tf_op jit(solution)/shard_map/ppermute | solution.py:95
  11.4 15.7 %collective-permute-start.4 = (bf16[2,64,128]{2,1,0:T(8,128)(2,1)S(1)}, bf16[2,64,128]{2,1,0:T(8,128)(2,1)S(1)}, u32[]{:S(2)}, u32[]{:S(2)}) collective-permute-start(bf16[2,64,128]{2,1,0:T(8,128)(2,1)S(1)} %get-tuple-element.25), channel_id=1, source_target_pairs={{0,1},{1,2},{2,3},{4,5},{5,6},{6,7},{8,9},{9,10},{10,11},{12,13},{... | collective-permute-start | bytes 98312 | tf_op jit(solution)/shard_map/ppermute | solution.py:96
  14.9 12.2 %collective-permute-start.5 = (bf16[2,64,128]{2,1,0:T(8,128)(2,1)S(1)}, bf16[2,64,128]{2,1,0:T(8,128)(2,1)S(1)}, u32[]{:S(2)}, u32[]{:S(2)}) collective-permute-start(bf16[2,64,128]{2,1,0:T(8,128)(2,1)S(1)} %get-tuple-element.26), channel_id=1, source_target_pairs={{1,0},{2,1},{3,2},{5,4},{6,5},{7,6},{9,8},{10,9},{11,10},{13,12},{... | collective-permute-start | bytes 98312 | tf_op jit(solution)/shard_map/ppermute | solution.py:95
  16.2 9.6 %collective-permute-start = (bf16[64,128]{1,0:T(8,128)(2,1)S(1)}, bf16[64,128]{1,0:T(8,128)(2,1)S(1)}, u32[]{:S(2)}, u32[]{:S(2)}) collective-permute-start(bf16[64,128]{1,0:T(8,128)(2,1)S(1)} %get-tuple-element.20), channel_id=1, source_target_pairs={{0,1},{1,2},{2,3},{4,5},{5,6},{6,7},{8,9},{9,10},{10,11},{12,13},{... | collective-permute-start | bytes 49160 | tf_op jit(solution)/shard_map/ppermute | solution.py:96
  20.8 5.6 %collective-permute-start.1 = (bf16[64,128]{1,0:T(8,128)(2,1)S(1)}, bf16[64,128]{1,0:T(8,128)(2,1)S(1)}, u32[]{:S(2)}, u32[]{:S(2)}) collective-permute-start(bf16[64,128]{1,0:T(8,128)(2,1)S(1)} %get-tuple-element.21), channel_id=1, source_target_pairs={{1,0},{2,1},{3,2},{5,4},{6,5},{7,6},{9,8},{10,9},{11,10},{13,12},{... | collective-permute-start | bytes 49160 | tf_op jit(solution)/shard_map/ppermute | solution.py:95
  22.1 2.2 %copy-start.2 = (bf16[64,64,512]{2,1,0:T(8,128)(2,1)S(1)}, bf16[64,64,512]{2,1,0:T(8,128)(2,1)}, u32[]{:S(2)}) copy-start(bf16[64,64,512]{2,1,0:T(8,128)(2,1)} %image_ref.3) | copy-start | bytes 12582916
  24.3 2.1 %copy-start.5 = (f32[2,32,8,8]{1,3,2,0:T(8,128)S(1)}, f32[2,32,8,8]{1,3,2,0:T(8,128)}, u32[]{:S(2)}) copy-start(f32[2,32,8,8]{1,3,2,0:T(8,128)} %param.8) | copy-start | bytes 49156
  24.3 2.9 %copy-start.3 = (bf16[64,64,512]{2,1,0:T(8,128)(2,1)S(1)}, bf16[64,64,512]{2,1,0:T(8,128)(2,1)}, u32[]{:S(2)}) copy-start(bf16[64,64,512]{2,1,0:T(8,128)(2,1)} %image_ref.3) | copy-start | bytes 12582916
  57.1 14.9 %all-to-all-start = ((f32[8,16,512]{2,1,0:T(8,128)}), f32[8,16,512]{2,1,0:T(8,128)S(1)}, u32[]{:S(2)}, u32[]{:S(2)}) async-start(f32[8,16,512]{2,1,0:T(8,128)} %get-tuple-element.31), calls=%async_computation | async-start | bytes 524288 | tf_op jit(solution)/shard_map/all_to_all | solution.py:442
  62.1 5.9 %collective-permute-start.8 = (f32[64,128]{1,0:T(8,128)S(1)}, f32[64,128]{1,0:T(8,128)S(1)}, u32[]{:S(2)}, u32[]{:S(2)}) collective-permute-start(f32[64,128]{1,0:T(8,128)S(1)} %get-tuple-element.32.refs_0_), channel_id=1, source_target_pairs={{0,3},{1,0},{2,1},{3,2},{4,7},{5,4},{6,5},{7,6},{8,11},{9,8},{10,9... | collective-permute-start | bytes 98312 | tf_op jit(solution)/shard_map/ppermute | solution.py:440
  66.3 5.2 %collective-permute-start.7 = (f32[64,128]{1,0:T(8,128)S(1)}, f32[64,128]{1,0:T(8,128)S(1)}, u32[]{:S(2)}, u32[]{:S(2)}) collective-permute-start(f32[64,128]{1,0:T(8,128)S(1)} %get-tuple-element.32.refs_0_), channel_id=1, source_target_pairs={{0,2},{1,3},{2,0},{3,1},{4,6},{5,7},{6,4},{7,5},{8,10},{9,11},{10,... | collective-permute-start | bytes 98312 | tf_op jit(solution)/shard_map/ppermute | solution.py:440
  66.3 5.7 %collective-permute-start.6 = (f32[64,128]{1,0:T(8,128)S(1)}, f32[64,128]{1,0:T(8,128)S(1)}, u32[]{:S(2)}, u32[]{:S(2)}) collective-permute-start(f32[64,128]{1,0:T(8,128)S(1)} %get-tuple-element.32.refs_0_), channel_id=1, source_target_pairs={{0,1},{1,2},{2,3},{3,0},{4,5},{5,6},{6,7},{7,4},{8,9},{9,10},{10,1... | collective-permute-start | bytes 98312 | tf_op jit(solution)/shard_map/ppermute | solution.py:440

commit v13 on v11

--- a/solution.py
+++ b/solution.py
@@ -44,7 +44,7 @@
     return pltpu.CompilerParams(vmem_limit_bytes=32000000)
 
 
-def columns_kernel(cells_ref, first_ref, last_ref):
+def ends_kernel(cells_ref, first_ref, last_ref, low_ref, high_ref):
     depth, rows, width = cells_ref.shape
     lane = lax.broadcasted_iota(jnp.int32, (rows, LANES), 1)
     first = jnp.zeros((rows, LANES), f32)
@@ -56,15 +56,20 @@
         last = jnp.where(lane == x, pltpu.roll(far, (x + 1) % LANES, 1), last)
     first_ref[...] = first.astype(bf16)
     last_ref[...] = last.astype(bf16)
-
-
-def end_columns(cells):
-    rows = cells.shape[1]
+    for x in range(0, depth, 16):
+        low = [cells_ref[x + k, 0:16, :].astype(f32)[0:1] for k in range(16)]
+        high = [cells_ref[x + k, rows - 16 : rows, :].astype(f32)[15:16] for k in range(16)]
+        low_ref[x : x + 16, :] = jnp.concatenate(low, axis=0).astype(bf16)
+        high_ref[x : x + 16, :] = jnp.concatenate(high, axis=0).astype(bf16)
+
+
+def ends(cells):
+    depth, rows, width = cells.shape
     return pl.pallas_call(
-        columns_kernel,
-        out_shape=[jax.ShapeDtypeStruct((rows, LANES), bf16)] * 2,
-        compiler_params=plain_params(),
-        name="columns",
+        ends_kernel,
+        out_shape=[jax.ShapeDtypeStruct((rows, LANES), bf16)] * 2 + [jax.ShapeDtypeStruct((depth, width), bf16)] * 2,
+        compiler_params=plain_params(),
+        name="ends",
     )(cells)
 
 
@@ -78,7 +83,7 @@
     for row, body, out in ((0, low_ref, low_out), (rows - 1, high_ref, high_out)):
         after = pltpu.roll(right, (LANES - row) % LANES, 1)
         before = pltpu.roll(left, LANES - 1 - row, 1)
-        out[:, 0:width] = body[...].astype(bf16)
+        out[:, 0:width] = body[...]
         out[:, width : width + LANES] = jnp.where(lane == 0, after, before).astype(bf16)
 
 
@@ -99,7 +104,7 @@
     return lax.ppermute(part, axis, [(i, i + 1) for i in range(count - 1)])
 
 
-def squares_kernel(image_ref, cells_ref, sums, low_ref, high_ref):
+def squares_kernel(image_ref, later_ref, sums):
     depth, rows, width = image_ref.shape
     tiles = width // LANES
 
@@ -118,30 +123,16 @@
 
     lax.fori_loop(0, depth // KNOT * tiles, one, 0)
 
-    def ends(block, carry):
-        x = pl.multiple_of(block * KNOT, KNOT)
-        low = [cells_ref[x + k, 0:16, :].astype(f32)[0:1] for k in range(KNOT)]
-        high = [cells_ref[x + k, rows - 16 : rows, :].astype(f32)[15:16] for k in range(KNOT)]
-        low_ref[pl.ds(x, KNOT), :] = jnp.concatenate(low, axis=0)
-        high_ref[pl.ds(x, KNOT), :] = jnp.concatenate(high, axis=0)
-        return carry
-
-    lax.fori_loop(0, depth // KNOT, ends, 0)
-
-
-def squares(image, cells):
+
+def squares(image, later):
     depth, rows, width = image.shape
     return pl.pallas_call(
         squares_kernel,
-        out_shape=[
-            jax.ShapeDtypeStruct((width // LANES, depth * rows // KNOT**2, LANES), f32),
-            jax.ShapeDtypeStruct((depth, width), f32),
-            jax.ShapeDtypeStruct((depth, width), f32),
-        ],
+        out_shape=jax.ShapeDtypeStruct((width // LANES, depth * rows // KNOT**2, LANES), f32),
         compiler_params=plain_params(),
         cost_estimate=pl.CostEstimate(flops=3 * image.size, bytes_accessed=2 * image.size, transcendentals=0),
         name="squares",
-    )(image, cells)
+    )(image, later)
 
 
 def terms_kernel(
@@ -431,13 +422,13 @@
     n_gy, n_gz = lax.axis_size("gy"), lax.axis_size("gz")
     nodes_x, nodes_y = plane_factors.shape[2:]
     plane = jnp.transpose(plane_factors, (0, 2, 3, 1)).reshape(2, nodes_x * nodes_y, RANK)
-    first, last = end_columns(deformed)
+    first, last, low, high = ends(deformed)
     right = shifted(first, "gz", True)
     left = shifted(last, "gz", False)
-    sums, low, high = squares(image, deformed)
     low, high = packed_rows(left, right, low, high)
     above = shifted(low, "gy", True)
     below = shifted(high, "gy", False)
+    sums = squares(image, low)
     field, diag_depth, diag_plane, beyond = terms(sums, plane, depth_factors, left, right, deformed.shape[0])
     residual, depth_terms, plane_terms = warp(
         deformed, image, displacement, beyond, below, above, field, plane, depth_factors, diag_depth, diag_plane,

time: 79.1 us -> 79.3 us (level)
    ppermute x2, waiting for transfers between devices: 3.25 us -> 4.21 us  [shifted(): return lax.ppermute(part, axis, [(i + 1, i) for i in range(count - 1)])]
  transfers between devices with their start and end apart: 8 -> 8, of which waited for: 5 -> 4; matrix products, arithmetic and copies ran while one was open for 0% -> 0% of each run, Pallas kernels for 3% -> 3%
where the time goes in v13:
time: 79.3 us; the launch traced here: 78.8 us
  Pallas kernels  34 us (43%)
  starting transfers between devices  20.3 us (26%)
  blocking collectives  10.9 us (14%)
  waiting for transfers between devices  8.47 us (11%)
  local copies, waits for them, and re-layouts  4.38 us (6%)
    pallas_call x1, Pallas kernels, warp(): pl.pallas_call(warp_kernel, grid=(count + 1,), in_specs=[pl.BlockSpec((KN...  29.8 us
    all_to_all x1, blocking collectives, local(): depth_terms = lax.all_to_all(depth_terms, 'gy', 0, 0)  10.9 us
    all_to_all x1, starting transfers between devices, local(): depth_terms = lax.all_to_all(depth_terms, 'gy', 0, 0)  6.7 us
    ppermute x2, starting transfers between devices, shifted(): return lax.ppermute(part, axis, [(i, i + 1) for i in range(count - 1)])  6.35 us
    ppermute x3, starting transfers between devices, local(): lax.ppermute(plane_terms, 'gz', [(i, (i + hop) % n_gz) for i in range(n_g...  4.62 us
    unnamed x12, local copies, waits for them, and re-layouts  4.38 us
    ppermute x2, waiting for transfers between devices, shifted(): return lax.ppermute(part, axis, [(i + 1, i) for i in range(count - 1)])  4.21 us
    ppermute x3, waiting for transfers between devices, local(): lax.ppermute(plane_terms, 'gz', [(i, (i + hop) % n_gz) for i in range(n_g...  4.13 us
  transfers between devices with their start and end apart: 8, of which 4 were waited for; matrix products, arithmetic and copies ran while one was open for 0% of the time, Pallas kernels for 3%

profile of v13, /device:TPU:0, one launch (start us, length us, event | category | flops | bytes accessed | tf_op | source)
XLA Modules:
  0.0 78.8 jit_solution(14078990423382731319)
XLA Ops:
  0.6 0.0 copy-start
  0.6 2.2 %copy-done = bf16[64,64,512]{2,1,0:T(8,128)(2,1)S(1)} copy-done((bf16[64,64,512]{2,1,0:T(8,128)(2,1)S(1)}, bf16[64,64,512]{2,1,0:T(8,128)(2,1)}, u32[]{:S(2)}) %copy-start) | copy-done | bytes 4194328
  2.8 0.0 copy-start.4
  2.8 0.0 copy-start.1
  2.8 0.8 %ends.1 = (bf16[64,128]{1,0:T(8,128)(2,1)S(1)}, bf16[64,128]{1,0:T(8,128)(2,1)S(1)}, bf16[64,512]{1,0:T(8,128)(2,1)S(1)}, bf16[64,512]{1,0:T(8,128)(2,1)S(1)}) custom-call(bf16[64,64,512]{2,1,0:T(8,128)(2,1)S(1)} %copy-done), custom_call_target="tpu_custom_call" | custom-call | tf_op jit(solution)/shard_map/ends/pallas_call | solution.py:68
  3.6 5.1 %collective-permute-start = (bf16[64,128]{1,0:T(8,128)(2,1)S(1)}, bf16[64,128]{1,0:T(8,128)(2,1)S(1)}, u32[]{:S(2)}, u32[]{:S(2)}) collective-permute-start(bf16[64,128]{1,0:T(8,128)(2,1)S(1)} %get-tuple-element.20), channel_id=1, source_target_pairs={{0,1},{1,2},{2,3},{4,5},{5,6},{6,7},{8,9},{9,10},{10,11},{12,13},{... | collective-permute-start | bytes 49160 | tf_op jit(solution)/shard_map/ppermute | solution.py:104
  8.7 1.3 %collective-permute-start.1 = (bf16[64,128]{1,0:T(8,128)(2,1)S(1)}, bf16[64,128]{1,0:T(8,128)(2,1)S(1)}, u32[]{:S(2)}, u32[]{:S(2)}) collective-permute-start(bf16[64,128]{1,0:T(8,128)(2,1)S(1)} %get-tuple-element.21), channel_id=1, source_target_pairs={{1,0},{2,1},{3,2},{5,4},{6,5},{7,6},{9,8},{10,9},{11,10},{13,12},{... | collective-permute-start | bytes 49160 | tf_op jit(solution)/shard_map/ppermute | solution.py:103
  10.0 0.1 collective-permute-done.left_ref
  10.1 4.2 %collective-permute-done.1.right_ref = bf16[64,128]{1,0:T(8,128)(2,1)S(1)} collective-permute-done((bf16[64,128]{1,0:T(8,128)(2,1)S(1)}, bf16[64,128]{1,0:T(8,128)(2,1)S(1)}, u32[]{:S(2)}, u32[]{:S(2)}) %collective-permute-start.1) | collective-permute-done | bytes 16416 | tf_op jit(solution)/shard_map/ppermute | solution.py:103
  14.3 0.2 rows.1
  14.5 1.3 %collective-permute-start.2 = (bf16[64,640]{1,0:T(8,128)(2,1)S(1)}, bf16[64,640]{1,0:T(8,128)(2,1)S(1)}, u32[]{:S(2)}, u32[]{:S(2)}) collective-permute-start(bf16[64,640]{1,0:T(8,128)(2,1)S(1)} %get-tuple-element.26), channel_id=1, source_target_pairs={{0,4},{4,8},{8,12},{12,16},{16,20},{20,24},{24,28},{1,5},{5,9},{9,... | collective-permute-start | bytes 245768 | tf_op jit(solution)/shard_map/ppermute | solution.py:104
  15.8 1.3 %collective-permute-start.3 = (bf16[64,640]{1,0:T(8,128)(2,1)S(1)}, bf16[64,640]{1,0:T(8,128)(2,1)S(1)}, u32[]{:S(2)}, u32[]{:S(2)}) collective-permute-start(bf16[64,640]{1,0:T(8,128)(2,1)S(1)} %get-tuple-element.24.later_ref), channel_id=1, source_target_pairs={{4,0},{8,4},{12,8},{16,12},{20,16},{24,20},{28,24},{5,1},{9,5},{13... | collective-permute-start | bytes 245768 | tf_op jit(solution)/shard_map/ppermute | solution.py:103
  17.1 0.0 copy-start.2
  17.1 2.2 %copy-done.2 = bf16[64,64,512]{2,1,0:T(8,128)(2,1)S(1)} copy-done((bf16[64,64,512]{2,1,0:T(8,128)(2,1)S(1)}, bf16[64,64,512]{2,1,0:T(8,128)(2,1)}, u32[]{:S(2)}) %copy-start.2) | copy-done | bytes 4194328
  19.3 0.0 copy-start.5
  19.3 0.0 copy-start.3
  19.3 1.5 %squares.1.sums = f32[4,64,128]{2,1,0:T(8,128)S(1)} custom-call(bf16[64,64,512]{2,1,0:T(8,128)(2,1)S(1)} %copy-done.2, bf16[64,640]{1,0:T(8,128)(2,1)S(1)} %get-tuple-element.24.later_ref), custom_call_target="tpu_custom_call" | custom-call | flops 6291456 | bytes 4194304 | tf_op jit(solution)/shard_map/squares/pallas_call | solution.py:129
  20.8 0.0 copy-done.4
  20.8 0.0 copy-done.5
  20.8 0.7 terms.1
  21.5 0.0 collective-permute-done.2.low_ref
  21.5 0.0 collective-permute-done.3.high_ref
  21.6 0.0 copy-done.1
  21.6 0.0 copy-done.3
  21.6 29.8 %warp.1 = (bf16[64,64,512]{2,1,0:T(8,128)(2,1)}, f32[8,16,512]{2,1,0:T(8,128)}, f32[64,128]{1,0:T(8,128)S(1)}) custom-call(bf16[64,64,512]{2,1,0:T(8,128)(2,1)S(1)} %copy-done.1, bf16[64,64,512]{2,1,0:T(8,128)(2,1)S(1)} %copy-done.3, bf16[3,64,64,512]{3,2,1,0:T(8,128)(2,1)} %shift_ref.1, bf16[64,64,128]{2,1,0:T(8,128)(2,1)S(1)} %get-tuple-element.25.beyond_ref, ...), custom_call_target="tpu_custom_call" | custom-call | flops 125829120 | bytes 25165824 | tf_op jit(solution)/shard_map/warp/pallas_call | solution.py:342
  51.4 6.7 %all-to-all-start = ((f32[8,16,512]{2,1,0:T(8,128)}), f32[8,16,512]{2,1,0:T(8,128)S(1)}, u32[]{:S(2)}, u32[]{:S(2)}) async-start(f32[8,16,512]{2,1,0:T(8,128)} %get-tuple-element.31), calls=%async_computation | async-start | bytes 524288 | tf_op jit(solution)/shard_map/all_to_all | solution.py:440
  58.1 1.8 %collective-permute-start.6 = (f32[64,128]{1,0:T(8,128)S(1)}, f32[64,128]{1,0:T(8,128)S(1)}, u32[]{:S(2)}, u32[]{:S(2)}) collective-permute-start(f32[64,128]{1,0:T(8,128)S(1)} %get-tuple-element.32.refs_0_), channel_id=1, source_target_pairs={{0,3},{1,0},{2,1},{3,2},{4,7},{5,4},{6,5},{7,6},{8,11},{9,8},{10,9... | collective-permute-start | bytes 98312 | tf_op jit(solution)/shard_map/ppermute | solution.py:438
  59.9 1.3 %collective-permute-start.5 = (f32[64,128]{1,0:T(8,128)S(1)}, f32[64,128]{1,0:T(8,128)S(1)}, u32[]{:S(2)}, u32[]{:S(2)}) collective-permute-start(f32[64,128]{1,0:T(8,128)S(1)} %get-tuple-element.32.refs_0_), channel_id=1, source_target_pairs={{0,2},{1,3},{2,0},{3,1},{4,6},{5,7},{6,4},{7,5},{8,10},{9,11},{10,... | collective-permute-start | bytes 98312 | tf_op jit(solution)/shard_map/ppermute | solution.py:438
  61.1 1.6 %collective-permute-start.4 = (f32[64,128]{1,0:T(8,128)S(1)}, f32[64,128]{1,0:T(8,128)S(1)}, u32[]{:S(2)}, u32[]{:S(2)}) collective-permute-start(f32[64,128]{1,0:T(8,128)S(1)} %get-tuple-element.32.refs_0_), channel_id=1, source_target_pairs={{0,1},{1,2},{2,3},{3,0},{4,5},{5,6},{6,7},{7,4},{8,9},{9,10},{10,1... | collective-permute-start | bytes 98312 | tf_op jit(solution)/shard_map/ppermute | solution.py:438
  62.7 0.0 collective-permute-done.6.refs_3_
  62.7 2.3 %collective-permute-done.5.refs_2_ = f32[64,128]{1,0:T(8,128)S(1)} collective-permute-done((f32[64,128]{1,0:T(8,128)S(1)}, f32[64,128]{1,0:T(8,128)S(1)}, u32[]{:S(2)}, u32[]{:S(2)}) %collective-permute-start.5) | collective-permute-done | bytes 32800 | tf_op jit(solution)/shard_map/ppermute | solution.py:438
  65.0 1.9 %collective-permute-done.4.refs_1_ = f32[64,128]{1,0:T(8,128)S(1)} collective-permute-done((f32[64,128]{1,0:T(8,128)S(1)}, f32[64,128]{1,0:T(8,128)S(1)}, u32[]{:S(2)}, u32[]{:S(2)}) %collective-permute-start.4) | collective-permute-done | bytes 32800 | tf_op jit(solution)/shard_map/ppermute | solution.py:438
  66.9 0.0 all-to-all-done.depth_ref
  66.9 0.1 gather.1
  67.0 10.9 %all_to_all.10.depth_ref = f32[8,16,512]{2,1,0:T(8,128)S(1)} all-to-all(f32[8,16,512]{2,1,0:T(8,128)S(1)} %get-tuple-element.33), channel_id=1, replica_groups=mesh['gy'=8,'gz'=4] {'gy'}, dimensions={0} | all-to-all | bytes 524288 | tf_op jit(solution)/shard_map/all_to_all | solution.py:450
  77.9 0.9 %steps.1 = (f32[2,32,512]{2,1,0:T(8,128)}, f32[2,64,32]{2,1,0:T(8,128)}) custom-call(f32[8,16,512]{2,1,0:T(8,128)S(1)} %all_to_all.10.depth_ref, f32[64,128]{1,0:T(8,128)S(1)} %get-tuple-element.34.plane_ref), custom_call_target="tpu_custom_call" | custom-call | tf_op jit(solution)/shard_map/steps/pallas_call | solution.py:452
Async XLA Ops:
  0.6 2.2 %copy-start = (bf16[64,64,512]{2,1,0:T(8,128)(2,1)S(1)}, bf16[64,64,512]{2,1,0:T(8,128)(2,1)}, u32[]{:S(2)}) copy-start(bf16[64,64,512]{2,1,0:T(8,128)(2,1)} %cells_ref.3) | copy-start | bytes 12582916
  2.8 18.0 %copy-start.4 = (f32[2,32,512]{2,1,0:T(8,128)S(1)}, f32[2,32,512]{2,1,0:T(8,128)}, u32[]{:S(2)}) copy-start(f32[2,32,512]{2,1,0:T(8,128)} %depth_ref.3) | copy-start | bytes 393220
  2.8 18.7 %copy-start.1 = (bf16[64,64,512]{2,1,0:T(8,128)(2,1)S(1)}, bf16[64,64,512]{2,1,0:T(8,128)(2,1)}, u32[]{:S(2)}) copy-start(bf16[64,64,512]{2,1,0:T(8,128)(2,1)} %cells_ref.3) | copy-start | bytes 12582916
  3.6 6.5 %collective-permute-start = (bf16[64,128]{1,0:T(8,128)(2,1)S(1)}, bf16[64,128]{1,0:T(8,128)(2,1)S(1)}, u32[]{:S(2)}, u32[]{:S(2)}) collective-permute-start(bf16[64,128]{1,0:T(8,128)(2,1)S(1)} %get-tuple-element.20), channel_id=1, source_target_pairs={{0,1},{1,2},{2,3},{4,5},{5,6},{6,7},{8,9},{9,10},{10,11},{12,13},{... | collective-permute-start | bytes 49160 | tf_op jit(solution)/shard_map/ppermute | solution.py:104
  8.7 5.6 %collective-permute-start.1 = (bf16[64,128]{1,0:T(8,128)(2,1)S(1)}, bf16[64,128]{1,0:T(8,128)(2,1)S(1)}, u32[]{:S(2)}, u32[]{:S(2)}) collective-permute-start(bf16[64,128]{1,0:T(8,128)(2,1)S(1)} %get-tuple-element.21), channel_id=1, source_target_pairs={{1,0},{2,1},{3,2},{5,4},{6,5},{7,6},{9,8},{10,9},{11,10},{13,12},{... | collective-permute-start | bytes 49160 | tf_op jit(solution)/shard_map/ppermute | solution.py:103
  14.5 7.0 %collective-permute-start.2 = (bf16[64,640]{1,0:T(8,128)(2,1)S(1)}, bf16[64,640]{1,0:T(8,128)(2,1)S(1)}, u32[]{:S(2)}, u32[]{:S(2)}) collective-permute-start(bf16[64,640]{1,0:T(8,128)(2,1)S(1)} %get-tuple-element.26), channel_id=1, source_target_pairs={{0,4},{4,8},{8,12},{12,16},{16,20},{20,24},{24,28},{1,5},{5,9},{9,... | collective-permute-start | bytes 245768 | tf_op jit(solution)/shard_map/ppermute | solution.py:104
  15.8 5.7 %collective-permute-start.3 = (bf16[64,640]{1,0:T(8,128)(2,1)S(1)}, bf16[64,640]{1,0:T(8,128)(2,1)S(1)}, u32[]{:S(2)}, u32[]{:S(2)}) collective-permute-start(bf16[64,640]{1,0:T(8,128)(2,1)S(1)} %get-tuple-element.24.later_ref), channel_id=1, source_target_pairs={{4,0},{8,4},{12,8},{16,12},{20,16},{24,20},{28,24},{5,1},{9,5},{13... | collective-permute-start | bytes 245768 | tf_op jit(solution)/shard_map/ppermute | solution.py:103
  17.1 2.2 %copy-start.2 = (bf16[64,64,512]{2,1,0:T(8,128)(2,1)S(1)}, bf16[64,64,512]{2,1,0:T(8,128)(2,1)}, u32[]{:S(2)}) copy-start(bf16[64,64,512]{2,1,0:T(8,128)(2,1)} %image_ref.3) | copy-start | bytes 12582916
  19.3 1.5 %copy-start.5 = (f32[2,32,8,8]{1,3,2,0:T(8,128)S(1)}, f32[2,32,8,8]{1,3,2,0:T(8,128)}, u32[]{:S(2)}) copy-start(f32[2,32,8,8]{1,3,2,0:T(8,128)} %param.8) | copy-start | bytes 49156
  19.3 2.3 %copy-start.3 = (bf16[64,64,512]{2,1,0:T(8,128)(2,1)S(1)}, bf16[64,64,512]{2,1,0:T(8,128)(2,1)}, u32[]{:S(2)}) copy-start(bf16[64,64,512]{2,1,0:T(8,128)(2,1)} %image_ref.3) | copy-start | bytes 12582916
  51.4 15.5 %all-to-all-start = ((f32[8,16,512]{2,1,0:T(8,128)}), f32[8,16,512]{2,1,0:T(8,128)S(1)}, u32[]{:S(2)}, u32[]{:S(2)}) async-start(f32[8,16,512]{2,1,0:T(8,128)} %get-tuple-element.31), calls=%async_computation | async-start | bytes 524288 | tf_op jit(solution)/shard_map/all_to_all | solution.py:440
  58.1 4.6 %collective-permute-start.6 = (f32[64,128]{1,0:T(8,128)S(1)}, f32[64,128]{1,0:T(8,128)S(1)}, u32[]{:S(2)}, u32[]{:S(2)}) collective-permute-start(f32[64,128]{1,0:T(8,128)S(1)} %get-tuple-element.32.refs_0_), channel_id=1, source_target_pairs={{0,3},{1,0},{2,1},{3,2},{4,7},{5,4},{6,5},{7,6},{8,11},{9,8},{10,9... | collective-permute-start | bytes 98312 | tf_op jit(solution)/shard_map/ppermute | solution.py:438
  59.9 5.1 %collective-permute-start.5 = (f32[64,128]{1,0:T(8,128)S(1)}, f32[64,128]{1,0:T(8,128)S(1)}, u32[]{:S(2)}, u32[]{:S(2)}) collective-permute-start(f32[64,128]{1,0:T(8,128)S(1)} %get-tuple-element.32.refs_0_), channel_id=1, source_target_pairs={{0,2},{1,3},{2,0},{3,1},{4,6},{5,7},{6,4},{7,5},{8,10},{9,11},{10,... | collective-permute-start | bytes 98312 | tf_op jit(solution)/shard_map/ppermute | solution.py:438
  61.1 5.7 %collective-permute-start.4 = (f32[64,128]{1,0:T(8,128)S(1)}, f32[64,128]{1,0:T(8,128)S(1)}, u32[]{:S(2)}, u32[]{:S(2)}) collective-permute-start(f32[64,128]{1,0:T(8,128)S(1)} %get-tuple-element.32.refs_0_), channel_id=1, source_target_pairs={{0,1},{1,2},{2,3},{3,0},{4,5},{5,6},{6,7},{7,4},{8,9},{9,10},{10,1... | collective-permute-start | bytes 98312 | tf_op jit(solution)/shard_map/ppermute | solution.py:438

commit v14 on v13

--- a/solution.py
+++ b/solution.py
@@ -69,6 +69,7 @@
         ends_kernel,
         out_shape=[jax.ShapeDtypeStruct((rows, LANES), bf16)] * 2 + [jax.ShapeDtypeStruct((depth, width), bf16)] * 2,
         compiler_params=plain_params(),
+        cost_estimate=pl.CostEstimate(flops=cells.size, bytes_accessed=2 * cells.size, transcendentals=0),
         name="ends",
     )(cells)
 
@@ -93,6 +94,7 @@
         rows_kernel,
         out_shape=[jax.ShapeDtypeStruct((depth, width + LANES), bf16)] * 2,
         compiler_params=plain_params(),
+        cost_estimate=pl.CostEstimate(flops=500000 * low.size, bytes_accessed=8 * low.size, transcendentals=0),
         name="rows",
     )(left, right, low, high)
 
@@ -321,13 +323,11 @@
         for p in range(parts):
             for k in range(4):
                 depth_out[p, k * share : (k + 1) * share, :] = kinds[k][p * share : (p + 1) * share]
-        local = jnp.sum(energy[...])
+            depth_out[p, 3 * share :, width // 2 :] = jnp.full((share, width // 2), jnp.sum(energy[...]), f32)
         kinds = [split_dot(sums[k], depth_ref[k], 1) for k in range(2)]
         kinds = kinds + [diag_plane_ref[0], diag_plane_ref[1]]
         for k in range(4):
             plane_out[:, k * RANK : (k + 1) * RANK] = kinds[k]
-        count = plane_out.shape[0]
-        plane_out[count // 2 :, 3 * RANK :] = jnp.full((count // 2, RANK), local, f32)
 
 
 def warp(cells, image, shift, beyond, low, high, field, plane, depth_factors, diag_depth, diag_plane, parts):
@@ -380,30 +380,25 @@
     )(cells, image, shift, beyond, low, high, field, plane, depth_factors, diag_depth, diag_plane)
 
 
-def gather_kernel(depth_ref, *refs):
+def gather_kernel(depth_ref, plane_ref, depth_out, plane_out):
+    total = jnp.sum(depth_ref[...], axis=0)
+    for p in range(depth_out.shape[0]):
+        depth_out[p] = total
+    cells = plane_ref.shape[0]
+    plane_out[...] = plane_ref[...]
+    energy = total[total.shape[0] - 1, total.shape[1] - 1]
+    plane_out[cells // 2 :, 3 * RANK :] = jnp.full((cells // 2, RANK), energy, f32)
+
+
+def step_kernel(full_z, node_count, depth_ref, *refs):
     depth_out, plane_out = refs[-2:]
-    total = jnp.sum(depth_ref[...], axis=0)
     found = [ref[...] for ref in refs[:-2]]
     while len(found) > 1:
         half = len(found) // 2
         found = [found[k] + found[k + half] for k in range(half)]
     planes = found[0]
-    plane_out[...] = planes
-    cells = planes.shape[0]
-    share, width = total.shape[0] // 4, total.shape[1]
-    row = lax.broadcasted_iota(jnp.int32, total.shape, 0)
-    lane = lax.broadcasted_iota(jnp.int32, total.shape, 1)
-    partial = planes[cells - 1, 4 * RANK - 1]
-    total = jnp.where((row >= 3 * share) & (lane >= width // 2), partial, total)
-    for p in range(depth_out.shape[0]):
-        depth_out[p] = total
-
-
-def step_kernel(full_z, node_count, depth_ref, plane_ref, depth_out, plane_out):
     parts, share, width = depth_ref.shape[0], depth_ref.shape[1] // 4, depth_ref.shape[2]
-    energy = depth_ref[0, 3 * share, width - 1]
-    for p in range(1, parts):
-        energy = energy + depth_ref[p, 3 * share, width - 1]
+    energy = planes[planes.shape[0] - 1, 4 * RANK - 1]
     lam_depth = damping * energy / full_z
     lam_plane = damping * RANK * energy / node_count
     for p in range(parts):
@@ -413,7 +408,6 @@
         rows = slice(p * share, (p + 1) * share)
         depth_out[0, rows, :] = got[0:share] / (got[2 * share : 3 * share] + lam_depth + epsilon)
         depth_out[1, rows, :] = got[share : 2 * share] / (levels + lam_depth + epsilon)
-    planes = plane_ref[...]
     plane_out[0] = planes[:, 0:RANK] / (planes[:, 2 * RANK : 3 * RANK] + lam_plane + epsilon)
     plane_out[1] = planes[:, RANK : 2 * RANK] / (planes[0:1, 3 * RANK :] + lam_plane + epsilon)
 
@@ -434,9 +428,6 @@
         deformed, image, displacement, beyond, below, above, field, plane, depth_factors, diag_depth, diag_plane,
         n_gy,
     )
-    others = [
-        lax.ppermute(plane_terms, "gz", [(i, (i + hop) % n_gz) for i in range(n_gz)]) for hop in range(1, n_gz)
-    ]
     depth_terms = lax.all_to_all(depth_terms, "gy", 0, 0)
     depth_terms, plane_terms = pl.pallas_call(
         gather_kernel,
@@ -446,8 +437,11 @@
         ],
         compiler_params=plain_params(),
         name="gather",
-    )(depth_terms, plane_terms, *others)
+    )(depth_terms, plane_terms)
     depth_terms = lax.all_to_all(depth_terms, "gy", 0, 0)
+    others = [
+        lax.ppermute(plane_terms, "gz", [(i, (i + hop) % n_gz) for i in range(n_gz)]) for hop in range(1, n_gz)
+    ]
     width = depth_factors.shape[2]
     step_depth, step_plane = pl.pallas_call(
         functools.partial(step_kernel, width * n_gz, nodes_x * nodes_y * n_gy),
@@ -457,7 +451,7 @@
         ],
         compiler_params=plain_params(),
         name="steps",
-    )(depth_terms, plane_terms)
+    )(depth_terms, plane_terms, *others)
     step_plane = jnp.transpose(step_plane.reshape(2, nodes_x, nodes_y, RANK), (0, 3, 1, 2))
     return residual, step_plane, step_depth
 

time: 79.3 us -> 77.9 us (0.982)
  starting transfers between devices: 20.3 us -> 17.3 us
  blocking collectives: 10.9 us -> 13.1 us
  local copies, waits for them, and re-layouts: 4.38 us -> 2.21 us
  waiting for transfers between devices: 8.47 us -> 9.67 us
    all_to_all x1, starting transfers between devices: 6.7 us -> 3.41 us  [local(): depth_terms = lax.all_to_all(depth_terms, 'gy', 0, 0)]
    unnamed x12 -> x10, local copies, waits for them, and re-layouts: 4.38 us -> 2.21 us
    all_to_all x1, blocking collectives: 10.9 us -> 13.1 us  [local(): depth_terms = lax.all_to_all(depth_terms, 'gy', 0, 0)]
    ppermute x2, waiting for transfers between devices: 4.21 us -> 5.41 us  [shifted(): return lax.ppermute(part, axis, [(i + 1, i) for i in range(count - 1)])]
  transfers between devices with their start and end apart: 8 -> 8, of which waited for: 4 -> 5; matrix products, arithmetic and copies ran while one was open for 0% -> 0% of each run, Pallas kernels for 3% -> 3%
where the time goes in v14:
time: 77.9 us; the launch traced here: 77.5 us
  Pallas kernels  34.5 us (44%)
  starting transfers between devices  17.3 us (22%)
  blocking collectives  13.1 us (17%)
  waiting for transfers between devices  9.67 us (12%)
  local copies, waits for them, and re-layouts  2.21 us (3%)
    pallas_call x1, Pallas kernels, warp(): pl.pallas_call(warp_kernel, grid=(count + 1,), in_specs=[pl.BlockSpec((KN...  29.7 us
    all_to_all x1, blocking collectives, local(): depth_terms = lax.all_to_all(depth_terms, 'gy', 0, 0)  13.1 us
    ppermute x2, starting transfers between devices, shifted(): return lax.ppermute(part, axis, [(i, i + 1) for i in range(count - 1)])  6.49 us
    ppermute x2, waiting for transfers between devices, shifted(): return lax.ppermute(part, axis, [(i + 1, i) for i in range(count - 1)])  5.41 us
    ppermute x3, starting transfers between devices, local(): lax.ppermute(plane_terms, 'gz', [(i, (i + hop) % n_gz) for i in range(n_g...  4.67 us
    ppermute x3, waiting for transfers between devices, local(): lax.ppermute(plane_terms, 'gz', [(i, (i + hop) % n_gz) for i in range(n_g...  4.13 us
    all_to_all x1, starting transfers between devices, local(): depth_terms = lax.all_to_all(depth_terms, 'gy', 0, 0)  3.41 us
    ppermute x2, starting transfers between devices, shifted(): return lax.ppermute(part, axis, [(i + 1, i) for i in range(count - 1)])  2.72 us
  transfers between devices with their start and end apart: 8, of which 5 were waited for; matrix products, arithmetic and copies ran while one was open for 0% of the time, Pallas kernels for 3%

profile of v14, /device:TPU:0, one launch (start us, length us, event | category | flops | bytes accessed | tf_op | source)
XLA Modules:
  0.0 77.5 jit_solution(13419445685604246661)
XLA Ops:
  0.6 0.0 copy-start
  0.6 2.2 %copy-done = bf16[64,64,512]{2,1,0:T(8,128)(2,1)S(1)} copy-done((bf16[64,64,512]{2,1,0:T(8,128)(2,1)S(1)}, bf16[64,64,512]{2,1,0:T(8,128)(2,1)}, u32[]{:S(2)}) %copy-start) | copy-done | bytes 4194328
  2.8 0.8 %ends.1 = (bf16[64,128]{1,0:T(8,128)(2,1)S(1)}, bf16[64,128]{1,0:T(8,128)(2,1)S(1)}, bf16[64,512]{1,0:T(8,128)(2,1)S(1)}, bf16[64,512]{1,0:T(8,128)(2,1)S(1)}) custom-call(bf16[64,64,512]{2,1,0:T(8,128)(2,1)S(1)} %copy-done), custom_call_target="tpu_custom_call" | custom-call | flops 2097152 | bytes 4194304 | tf_op jit(solution)/shard_map/ends/pallas_call | solution.py:68
  3.6 4.9 %collective-permute-start = (bf16[64,128]{1,0:T(8,128)(2,1)S(1)}, bf16[64,128]{1,0:T(8,128)(2,1)S(1)}, u32[]{:S(2)}, u32[]{:S(2)}) collective-permute-start(bf16[64,128]{1,0:T(8,128)(2,1)S(1)} %get-tuple-element.20), channel_id=1, source_target_pairs={{0,1},{1,2},{2,3},{4,5},{5,6},{6,7},{8,9},{9,10},{10,11},{12,13},{... | collective-permute-start | bytes 49160 | tf_op jit(solution)/shard_map/ppermute | solution.py:106
  8.6 1.3 %collective-permute-start.1 = (bf16[64,128]{1,0:T(8,128)(2,1)S(1)}, bf16[64,128]{1,0:T(8,128)(2,1)S(1)}, u32[]{:S(2)}, u32[]{:S(2)}) collective-permute-start(bf16[64,128]{1,0:T(8,128)(2,1)S(1)} %get-tuple-element.21), channel_id=1, source_target_pairs={{1,0},{2,1},{3,2},{5,4},{6,5},{7,6},{9,8},{10,9},{11,10},{13,12},{... | collective-permute-start | bytes 49160 | tf_op jit(solution)/shard_map/ppermute | solution.py:105
  9.9 0.1 collective-permute-done.left_ref
  10.0 4.2 %collective-permute-done.1.right_ref = bf16[64,128]{1,0:T(8,128)(2,1)S(1)} collective-permute-done((bf16[64,128]{1,0:T(8,128)(2,1)S(1)}, bf16[64,128]{1,0:T(8,128)(2,1)S(1)}, u32[]{:S(2)}, u32[]{:S(2)}) %collective-permute-start.1) | collective-permute-done | bytes 16416 | tf_op jit(solution)/shard_map/ppermute | solution.py:105
  14.2 0.0 copy-start.2
  14.2 0.2 rows.1
  14.4 0.0 copy-start.3
  14.4 0.0 copy-start.4
  14.4 0.0 copy-start.1
  14.4 1.6 %collective-permute-start.2 = (bf16[64,640]{1,0:T(8,128)(2,1)S(1)}, bf16[64,640]{1,0:T(8,128)(2,1)S(1)}, u32[]{:S(2)}, u32[]{:S(2)}) collective-permute-start(bf16[64,640]{1,0:T(8,128)(2,1)S(1)} %get-tuple-element.26), channel_id=1, source_target_pairs={{0,4},{4,8},{8,12},{12,16},{16,20},{20,24},{24,28},{1,5},{5,9},{9,... | collective-permute-start | bytes 245768 | tf_op jit(solution)/shard_map/ppermute | solution.py:106
  16.0 1.4 %collective-permute-start.3 = (bf16[64,640]{1,0:T(8,128)(2,1)S(1)}, bf16[64,640]{1,0:T(8,128)(2,1)S(1)}, u32[]{:S(2)}, u32[]{:S(2)}) collective-permute-start(bf16[64,640]{1,0:T(8,128)(2,1)S(1)} %get-tuple-element.24.later_ref), channel_id=1, source_target_pairs={{4,0},{8,4},{12,8},{16,12},{20,16},{24,20},{28,24},{5,1},{9,5},{13... | collective-permute-start | bytes 245768 | tf_op jit(solution)/shard_map/ppermute | solution.py:105
  17.4 0.0 copy-done.2
  17.4 1.5 %squares.1.sums = f32[4,64,128]{2,1,0:T(8,128)S(1)} custom-call(bf16[64,64,512]{2,1,0:T(8,128)(2,1)S(1)} %copy-done.2, bf16[64,640]{1,0:T(8,128)(2,1)S(1)} %get-tuple-element.24.later_ref), custom_call_target="tpu_custom_call" | custom-call | flops 6291456 | bytes 4194304 | tf_op jit(solution)/shard_map/squares/pallas_call | solution.py:131
  19.0 0.0 copy-done.3
  19.0 0.0 copy-done.4
  19.0 0.7 terms.1
  19.7 0.0 collective-permute-done.2.low_ref
  19.7 1.2 %collective-permute-done.3.high_ref = bf16[64,640]{1,0:T(8,128)(2,1)S(1)} collective-permute-done((bf16[64,640]{1,0:T(8,128)(2,1)S(1)}, bf16[64,640]{1,0:T(8,128)(2,1)S(1)}, u32[]{:S(2)}, u32[]{:S(2)}) %collective-permute-start.3) | collective-permute-done | bytes 81952 | tf_op jit(solution)/shard_map/ppermute | solution.py:105
  20.9 0.0 copy-done.1
  20.9 29.7 %warp.1 = (bf16[64,64,512]{2,1,0:T(8,128)(2,1)}, f32[8,16,512]{2,1,0:T(8,128)S(1)}, f32[64,128]{1,0:T(8,128)S(1)}) custom-call(bf16[64,64,512]{2,1,0:T(8,128)(2,1)S(1)} %copy-done.1, bf16[64,64,512]{2,1,0:T(8,128)(2,1)S(1)} %copy-done.2, bf16[3,64,64,512]{3,2,1,0:T(8,128)(2,1)} %shift_ref.1, bf16[64,64,128]{2,1,0:T(8,128)(2,1)S(1)} %get-tuple-element.25.beyond_ref, ...), custom_call_target="tpu_custom_call" | custom-call | flops 125829120 | bytes 25165824 | tf_op jit(solution)/shard_map/warp/pallas_call | solution.py:342
  50.6 13.1 %all_to_all.10.depth_ref = f32[8,16,512]{2,1,0:T(8,128)S(1)} all-to-all(f32[8,16,512]{2,1,0:T(8,128)S(1)} %get-tuple-element.31), channel_id=1, replica_groups=mesh['gy'=8,'gz'=4] {'gy'}, dimensions={0} | all-to-all | bytes 524288 | tf_op jit(solution)/shard_map/all_to_all | solution.py:431
  63.7 0.7 gather.1
  64.4 3.4 %all-to-all-start.1 = ((f32[8,16,512]{2,1,0:T(8,128)}), f32[8,16,512]{2,1,0:T(8,128)S(1)}, u32[]{:S(2)}, u32[]{:S(2)}) async-start(f32[8,16,512]{2,1,0:T(8,128)} %get-tuple-element.33), calls=%async_computation.1 | async-start | bytes 524288 | tf_op jit(solution)/shard_map/all_to_all | solution.py:441
  67.8 1.8 %collective-permute-start.6 = (f32[64,128]{1,0:T(8,128)S(1)}, f32[64,128]{1,0:T(8,128)S(1)}, u32[]{:S(2)}, u32[]{:S(2)}) collective-permute-start(f32[64,128]{1,0:T(8,128)S(1)} %get-tuple-element.34.refs_0_), channel_id=1, source_target_pairs={{0,3},{1,0},{2,1},{3,2},{4,7},{5,4},{6,5},{7,6},{8,11},{9,8},{10,9... | collective-permute-start | bytes 98312 | tf_op jit(solution)/shard_map/ppermute | solution.py:443
  69.6 1.3 %collective-permute-start.5 = (f32[64,128]{1,0:T(8,128)S(1)}, f32[64,128]{1,0:T(8,128)S(1)}, u32[]{:S(2)}, u32[]{:S(2)}) collective-permute-start(f32[64,128]{1,0:T(8,128)S(1)} %get-tuple-element.34.refs_0_), channel_id=1, source_target_pairs={{0,2},{1,3},{2,0},{3,1},{4,6},{5,7},{6,4},{7,5},{8,10},{9,11},{10,... | collective-permute-start | bytes 98312 | tf_op jit(solution)/shard_map/ppermute | solution.py:443
  70.9 1.6 %collective-permute-start.4 = (f32[64,128]{1,0:T(8,128)S(1)}, f32[64,128]{1,0:T(8,128)S(1)}, u32[]{:S(2)}, u32[]{:S(2)}) collective-permute-start(f32[64,128]{1,0:T(8,128)S(1)} %get-tuple-element.34.refs_0_), channel_id=1, source_target_pairs={{0,1},{1,2},{2,3},{3,0},{4,5},{5,6},{6,7},{7,4},{8,9},{9,10},{10,1... | collective-permute-start | bytes 98312 | tf_op jit(solution)/shard_map/ppermute | solution.py:443
  72.5 0.0 collective-permute-done.6.refs_3_
  72.5 2.1 %collective-permute-done.5.refs_2_ = f32[64,128]{1,0:T(8,128)S(1)} collective-permute-done((f32[64,128]{1,0:T(8,128)S(1)}, f32[64,128]{1,0:T(8,128)S(1)}, u32[]{:S(2)}, u32[]{:S(2)}) %collective-permute-start.5) | collective-permute-done | bytes 32800 | tf_op jit(solution)/shard_map/ppermute | solution.py:443
  74.6 2.0 %collective-permute-done.4.refs_1_ = f32[64,128]{1,0:T(8,128)S(1)} collective-permute-done((f32[64,128]{1,0:T(8,128)S(1)}, f32[64,128]{1,0:T(8,128)S(1)}, u32[]{:S(2)}, u32[]{:S(2)}) %collective-permute-start.4) | collective-permute-done | bytes 32800 | tf_op jit(solution)/shard_map/ppermute | solution.py:443
  76.6 0.0 all-to-all-done.1.depth_ref
  76.6 0.9 %steps.1 = (f32[2,32,512]{2,1,0:T(8,128)}, f32[2,64,32]{2,1,0:T(8,128)}) custom-call(f32[8,16,512]{2,1,0:T(8,128)S(1)} %all-to-all-done.1.depth_ref, f32[64,128]{1,0:T(8,128)S(1)} %get-tuple-element.34.refs_0_, f32[64,128]{1,0:T(8,128)S(1)} %collective-permute-done.4.refs_1_, f32[64,128]{1,0:T(8,128)S(1)} %collective-permute-done.5.refs_2_, ...), custom_call_target="tpu_custom_call" | custom-call | tf_op jit(solution)/shard_map/steps/pallas_call | solution.py:446
Async XLA Ops:
  0.6 2.2 %copy-start = (bf16[64,64,512]{2,1,0:T(8,128)(2,1)S(1)}, bf16[64,64,512]{2,1,0:T(8,128)(2,1)}, u32[]{:S(2)}) copy-start(bf16[64,64,512]{2,1,0:T(8,128)(2,1)} %cells_ref.3) | copy-start | bytes 12582916
  3.6 6.4 %collective-permute-start = (bf16[64,128]{1,0:T(8,128)(2,1)S(1)}, bf16[64,128]{1,0:T(8,128)(2,1)S(1)}, u32[]{:S(2)}, u32[]{:S(2)}) collective-permute-start(bf16[64,128]{1,0:T(8,128)(2,1)S(1)} %get-tuple-element.20), channel_id=1, source_target_pairs={{0,1},{1,2},{2,3},{4,5},{5,6},{6,7},{8,9},{9,10},{10,11},{12,13},{... | collective-permute-start | bytes 49160 | tf_op jit(solution)/shard_map/ppermute | solution.py:106
  8.6 5.6 %collective-permute-start.1 = (bf16[64,128]{1,0:T(8,128)(2,1)S(1)}, bf16[64,128]{1,0:T(8,128)(2,1)S(1)}, u32[]{:S(2)}, u32[]{:S(2)}) collective-permute-start(bf16[64,128]{1,0:T(8,128)(2,1)S(1)} %get-tuple-element.21), channel_id=1, source_target_pairs={{1,0},{2,1},{3,2},{5,4},{6,5},{7,6},{9,8},{10,9},{11,10},{13,12},{... | collective-permute-start | bytes 49160 | tf_op jit(solution)/shard_map/ppermute | solution.py:105
  14.2 3.2 %copy-start.2 = (bf16[64,64,512]{2,1,0:T(8,128)(2,1)S(1)}, bf16[64,64,512]{2,1,0:T(8,128)(2,1)}, u32[]{:S(2)}) copy-start(bf16[64,64,512]{2,1,0:T(8,128)(2,1)} %image_ref.3) | copy-start | bytes 12582916
  14.4 4.6 %copy-start.3 = (f32[2,32,512]{2,1,0:T(8,128)S(1)}, f32[2,32,512]{2,1,0:T(8,128)}, u32[]{:S(2)}) copy-start(f32[2,32,512]{2,1,0:T(8,128)} %depth_ref.3) | copy-start | bytes 393220
  14.4 4.6 %copy-start.4 = (f32[2,32,8,8]{1,3,2,0:T(8,128)S(1)}, f32[2,32,8,8]{1,3,2,0:T(8,128)}, u32[]{:S(2)}) copy-start(f32[2,32,8,8]{1,3,2,0:T(8,128)} %param.8) | copy-start | bytes 49156
  14.4 6.5 %copy-start.1 = (bf16[64,64,512]{2,1,0:T(8,128)(2,1)S(1)}, bf16[64,64,512]{2,1,0:T(8,128)(2,1)}, u32[]{:S(2)}) copy-start(bf16[64,64,512]{2,1,0:T(8,128)(2,1)} %cells_ref.3) | copy-start | bytes 12582916
  14.4 5.3 %collective-permute-start.2 = (bf16[64,640]{1,0:T(8,128)(2,1)S(1)}, bf16[64,640]{1,0:T(8,128)(2,1)S(1)}, u32[]{:S(2)}, u32[]{:S(2)}) collective-permute-start(bf16[64,640]{1,0:T(8,128)(2,1)S(1)} %get-tuple-element.26), channel_id=1, source_target_pairs={{0,4},{4,8},{8,12},{12,16},{16,20},{20,24},{24,28},{1,5},{5,9},{9,... | collective-permute-start | bytes 245768 | tf_op jit(solution)/shard_map/ppermute | solution.py:106
  16.0 4.9 %collective-permute-start.3 = (bf16[64,640]{1,0:T(8,128)(2,1)S(1)}, bf16[64,640]{1,0:T(8,128)(2,1)S(1)}, u32[]{:S(2)}, u32[]{:S(2)}) collective-permute-start(bf16[64,640]{1,0:T(8,128)(2,1)S(1)} %get-tuple-element.24.later_ref), channel_id=1, source_target_pairs={{4,0},{8,4},{12,8},{16,12},{20,16},{24,20},{28,24},{5,1},{9,5},{13... | collective-permute-start | bytes 245768 | tf_op jit(solution)/shard_map/ppermute | solution.py:105
  64.4 12.2 %all-to-all-start.1 = ((f32[8,16,512]{2,1,0:T(8,128)}), f32[8,16,512]{2,1,0:T(8,128)S(1)}, u32[]{:S(2)}, u32[]{:S(2)}) async-start(f32[8,16,512]{2,1,0:T(8,128)} %get-tuple-element.33), calls=%async_computation.1 | async-start | bytes 524288 | tf_op jit(solution)/shard_map/all_to_all | solution.py:441
  67.8 4.7 %collective-permute-start.6 = (f32[64,128]{1,0:T(8,128)S(1)}, f32[64,128]{1,0:T(8,128)S(1)}, u32[]{:S(2)}, u32[]{:S(2)}) collective-permute-start(f32[64,128]{1,0:T(8,128)S(1)} %get-tuple-element.34.refs_0_), channel_id=1, source_target_pairs={{0,3},{1,0},{2,1},{3,2},{4,7},{5,4},{6,5},{7,6},{8,11},{9,8},{10,9... | collective-permute-start | bytes 98312 | tf_op jit(solution)/shard_map/ppermute | solution.py:443
  69.6 5.0 %collective-permute-start.5 = (f32[64,128]{1,0:T(8,128)S(1)}, f32[64,128]{1,0:T(8,128)S(1)}, u32[]{:S(2)}, u32[]{:S(2)}) collective-permute-start(f32[64,128]{1,0:T(8,128)S(1)} %get-tuple-element.34.refs_0_), channel_id=1, source_target_pairs={{0,2},{1,3},{2,0},{3,1},{4,6},{5,7},{6,4},{7,5},{8,10},{9,11},{10,... | collective-permute-start | bytes 98312 | tf_op jit(solution)/shard_map/ppermute | solution.py:443
  70.9 5.7 %collective-permute-start.4 = (f32[64,128]{1,0:T(8,128)S(1)}, f32[64,128]{1,0:T(8,128)S(1)}, u32[]{:S(2)}, u32[]{:S(2)}) collective-permute-start(f32[64,128]{1,0:T(8,128)S(1)} %get-tuple-element.34.refs_0_), channel_id=1, source_target_pairs={{0,1},{1,2},{2,3},{3,0},{4,5},{5,6},{6,7},{7,4},{8,9},{9,10},{10,1... | collective-permute-start | bytes 98312 | tf_op jit(solution)/shard_map/ppermute | solution.py:443

commit v15 on v14

--- a/solution.py
+++ b/solution.py
@@ -181,7 +181,7 @@
     cells_ref, image_ref, shift_ref, beyond_ref, low_ref, high_ref, field, plane_ref, depth_ref,
     diag_depth_ref, diag_plane_ref,
     residual_ref, depth_out, plane_out,
-    ahead_ref, here_ref, behind_ref, wide, bands, rims, blocks, energy, held,
+    ahead_ref, here_ref, behind_ref, wide, bands, blocks, energy, held,
 ):
     step = pl.program_id(0)
     last = pl.num_programs(0) - 1
@@ -205,56 +205,64 @@
         bands[1] = (up - down).astype(bf16)
         energy[...] = jnp.zeros_like(energy)
         for c in range(3):
-            window[c][3 * block_rows - plane_rows : 3 * block_rows, :] = jnp.zeros((plane_rows, LANES), f32)
-
-    @pl.when(step < last)
-    def _():
-        slot = (step % 3) * block_rows
-        span = planes * rows
+            window[c][4 * block_rows - plane_rows :, :] = jnp.zeros((plane_rows, LANES), f32)
+
+    @pl.when(step < last - 1)
+    def _():
+        at = lax.broadcasted_iota(jnp.int32, (2 * TOP, width + LANES), 0)
+        low, high = low_ref[...].astype(f32), high_ref[...].astype(f32)
         for k in range(planes):
-            wide[k * rows : (k + 1) * rows, 0:width] = cells_ref[k]
-            wide[k * rows : (k + 1) * rows, width:] = beyond_ref[k]
-        wide[span:, :] = jnp.concatenate([low_ref[...].astype(f32), high_ref[...].astype(f32)], axis=0).astype(bf16)
-
-        def put(c, tile, values):
-            for k in range(planes):
-                first = pl.multiple_of(slot + k * plane_rows + tile * pitch, 8)
-                window[c][pl.ds(first + TOP, rows), :] = values[k * rows : (k + 1) * rows]
-            for side, row in enumerate((0, TOP + rows)):
-                rims[...] = values[span + side * planes : span + (side + 1) * planes]
-                for k in range(planes):
-                    first = pl.multiple_of(slot + k * plane_rows + tile * pitch, 8)
-                    window[c][pl.ds(first + row, 8), :] = jnp.broadcast_to(rims[k : k + 1], (8, LANES))
-
-        pieces = width // (2 * LANES)
-        for piece in range(pieces):
-            start = 2 * LANES * piece
-            after = wide[:, start : start + 3 * LANES]
-            if piece == 0:
-                before = jnp.concatenate([wide[:, width:], wide[:, 0 : 2 * LANES]], axis=1)
-            else:
-                before = wide[:, start - LANES : start + 2 * LANES]
-            ahead = jnp.dot(after, bands[0], preferred_element_type=f32)
-            behind = jnp.dot(before, bands[1], preferred_element_type=f32)
+            first = k * pitch
+            wide[first : first + rows, 0:LANES] = beyond_ref[k]
+            wide[first : first + rows, LANES : LANES + width] = cells_ref[k]
+            wide[first : first + rows, LANES + width :] = beyond_ref[k]
+            rim = jnp.where(at == TOP, high[k : k + 1], jnp.where(at == TOP - 1, low[k : k + 1], 0.0)).astype(bf16)
+            wide[first + rows : first + pitch, 0:LANES] = rim[:, width:]
+            wide[first + rows : first + pitch, LANES:] = rim
+
+    @pl.when(step >= last - 1)
+    def _():
+        wide[...] = jnp.zeros_like(wide)
+
+    slot = (step % 4) * block_rows
+    pieces = width // (2 * LANES)
+
+    def made(t):
+        plane = pl.ds(pl.multiple_of((t // pieces) * pitch, 16), pitch)
+        start = (t % pieces) * 2 * LANES
+        before = wide[plane, pl.ds(pl.multiple_of(start, LANES), 3 * LANES)]
+        after = wide[plane, pl.ds(pl.multiple_of(start + LANES, LANES), 3 * LANES)]
+        ahead = jnp.dot(after, bands[0], preferred_element_type=f32)
+        behind = jnp.dot(before, bands[1], preferred_element_type=f32)
+        return ahead, after[:, 0 : 2 * LANES].astype(f32), behind
+
+    def put(t, parts):
+        first = slot + (t // pieces) * plane_rows + (t % pieces) * 2 * pitch
+        for c in range(3):
             for half in range(2):
-                mine = slice(half * LANES, (half + 1) * LANES)
-                put(0, 2 * piece + half, ahead[:, mine])
-                put(1, 2 * piece + half, wide[:, start + half * LANES : start + (half + 1) * LANES].astype(f32))
-                put(2, 2 * piece + half, behind[:, mine])
-
-    @pl.when(step == last)
-    def _():
-        first = pl.multiple_of((step % 3) * block_rows, 8)
-        for c in range(3):
-            window[c][pl.ds(first, plane_rows), :] = jnp.zeros((plane_rows, LANES), f32)
-
-    @pl.when(step > 0)
-    def _():
-        mid = (step + 2) % 3
+                start = pl.multiple_of(first + half * pitch, 8)
+                values = parts[c][:, half * LANES : (half + 1) * LANES]
+                window[c][pl.ds(start + TOP, rows), :] = values[0:rows]
+                window[c][pl.ds(start, TOP), :] = values[rows : rows + TOP]
+                window[c][pl.ds(start + TOP + rows, TOP), :] = values[rows + TOP :]
+
+    turns = planes * pieces
+
+    @pl.when(step < 2)
+    def _():
+        def one(t, carry):
+            put(t, made(t))
+            return carry
+
+        lax.fori_loop(0, turns, one, 0)
+
+    @pl.when(step > 1)
+    def _():
+        mid = (step + 2) % 4
         first_rows = (
-            jnp.where(mid == 0, 3, mid) * block_rows - plane_rows,
+            jnp.where(mid == 0, 4, mid) * block_rows - plane_rows,
             mid * block_rows,
-            jnp.where(mid == 2, 0, mid + 1) * block_rows,
+            jnp.where(mid == 3, 0, mid + 1) * block_rows,
         )
 
         def one(t, total):
@@ -263,8 +271,9 @@
             at = pl.multiple_of(tile * LANES, LANES)
             top = pl.multiple_of(pair * 16, 16)
             origins = [first + tile * pitch + top + TOP for first in first_rows]
+            parts = made(t)
             for half in range(2):
-                node = (step - 1) * nodes + pair * 2 + half
+                node = (step - 2) * nodes + pair * 2 + half
                 mine = slice(8 * half, 8 * half + 8)
 
                 def taps(x):
@@ -309,9 +318,10 @@
                     before, here = here, after
                 for k, value in ((0, by_image), (1, plain)):
                     blocks[k, tile, pl.ds(node, 1), :] = jnp.sum(value, axis=0, keepdims=True)
+            put(t, parts)
             return total
 
-        energy[...] = lax.fori_loop(0, (rows // 16) * tiles, one, energy[...])
+        energy[...] = lax.fori_loop(0, turns, one, energy[...])
 
     @pl.when(step == last)
     def _():
@@ -335,17 +345,17 @@
     nodes = plane.shape[1]
     tiles = width // LANES
     count = depth // KNOT
-    behind = lambda i: (jnp.maximum(i - 1, 0), 0, 0)
+    behind = lambda i: (jnp.maximum(i - 2, 0), 0, 0)
     ahead = lambda i: (jnp.minimum(i, count - 1), 0, 0)
     flat = lambda i: (0, 0)
     whole = lambda i: (0, 0, 0)
     return pl.pallas_call(
         warp_kernel,
-        grid=(count + 1,),
+        grid=(count + 2,),
         in_specs=[
             pl.BlockSpec((KNOT, rows, width), ahead),
             pl.BlockSpec((KNOT, rows, width), behind),
-            pl.BlockSpec((3, KNOT, rows, width), lambda i: (0, jnp.maximum(i - 1, 0), 0, 0)),
+            pl.BlockSpec((3, KNOT, rows, width), lambda i: (0, jnp.maximum(i - 2, 0), 0, 0)),
             pl.BlockSpec((KNOT, rows, LANES), ahead),
             pl.BlockSpec((KNOT, low.shape[1]), lambda i: (jnp.minimum(i, count - 1), 0)),
             pl.BlockSpec((KNOT, high.shape[1]), lambda i: (jnp.minimum(i, count - 1), 0)),
@@ -366,10 +376,9 @@
             jax.ShapeDtypeStruct((nodes, 4 * RANK), f32),
         ],
         scratch_shapes=[
-            *[pltpu.VMEM((3 * KNOT * tiles * (rows + 2 * TOP), LANES), f32)] * 3,
-            pltpu.VMEM((KNOT * rows + 2 * KNOT, width + LANES), bf16),
+            *[pltpu.VMEM((4 * KNOT * tiles * (rows + 2 * TOP), LANES), f32)] * 3,
+            pltpu.VMEM((KNOT * (rows + 2 * TOP), width + 2 * LANES), bf16),
             pltpu.VMEM((2, 3 * LANES, 2 * LANES), bf16),
-            pltpu.VMEM((KNOT, LANES), f32),
             pltpu.VMEM((2, tiles, nodes, LANES), f32),
             pltpu.VMEM((8, LANES), f32),
             pltpu.VMEM((KNOT, 8, LANES), f32),
@@ -390,13 +399,8 @@
     plane_out[cells // 2 :, 3 * RANK :] = jnp.full((cells // 2, RANK), energy, f32)
 
 
-def step_kernel(full_z, node_count, depth_ref, *refs):
-    depth_out, plane_out = refs[-2:]
-    found = [ref[...] for ref in refs[:-2]]
-    while len(found) > 1:
-        half = len(found) // 2
-        found = [found[k] + found[k + half] for k in range(half)]
-    planes = found[0]
+def step_kernel(full_z, node_count, depth_ref, plane_ref, other_ref, depth_out, plane_out):
+    planes = plane_ref[...] + other_ref[...]
     parts, share, width = depth_ref.shape[0], depth_ref.shape[1] // 4, depth_ref.shape[2]
     energy = planes[planes.shape[0] - 1, 4 * RANK - 1]
     lam_depth = damping * energy / full_z
@@ -439,9 +443,12 @@
         name="gather",
     )(depth_terms, plane_terms)
     depth_terms = lax.all_to_all(depth_terms, "gy", 0, 0)
-    others = [
-        lax.ppermute(plane_terms, "gz", [(i, (i + hop) % n_gz) for i in range(n_gz)]) for hop in range(1, n_gz)
-    ]
+    hop = 1
+    while hop < n_gz:
+        other = lax.ppermute(plane_terms, "gz", [(i, i ^ hop) for i in range(n_gz)])
+        if 2 * hop < n_gz:
+            plane_terms = plane_terms + other
+        hop = 2 * hop
     width = depth_factors.shape[2]
     step_depth, step_plane = pl.pallas_call(
         functools.partial(step_kernel, width * n_gz, nodes_x * nodes_y * n_gy),
@@ -451,7 +458,7 @@
         ],
         compiler_params=plain_params(),
         name="steps",
-    )(depth_terms, plane_terms, *others)
+    )(depth_terms, plane_terms, other)
     step_plane = jnp.transpose(step_plane.reshape(2, nodes_x, nodes_y, RANK), (0, 3, 1, 2))
     return residual, step_plane, step_depth
 

time: 77.9 us -> 101 us (1.30)
  Pallas kernels: 34.5 us -> 57.9 us
    pallas_call x1, Pallas kernels: 29.7 us -> 53.1 us  [warp(): pl.pallas_call(warp_kernel, grid=(count + 2,), in_specs=[pl.BlockSpec((KN...]
    ppermute x3 -> x2, starting transfers between devices: 4.67 us -> 4.23 us  [local(): other = lax.ppermute(plane_terms, 'gz', [(i, i ^ hop) for i in range(n_gz)])]
    ppermute x3 -> x2, waiting for transfers between devices: 4.13 us -> 4.56 us  [local(): other = lax.ppermute(plane_terms, 'gz', [(i, i ^ hop) for i in range(n_gz)])]
  transfers between devices with their start and end apart: 8 -> 7, of which waited for: 5 -> 5; matrix products, arithmetic and copies ran while one was open for 0% -> 0% of each run, Pallas kernels for 3% -> 2%
where the time goes in v15:
time: 101 us
  Pallas kernels  57.9 us (57%)
  starting transfers between devices  16.8 us (17%)
  blocking collectives  13.1 us (13%)
  waiting for transfers between devices  10.1 us (10%)
  local copies, waits for them, and re-layouts  2.21 us (2%)
    pallas_call x1, Pallas kernels, warp(): pl.pallas_call(warp_kernel, grid=(count + 2,), in_specs=[pl.BlockSpec((KN...  53.1 us
    all_to_all x1, blocking collectives, local(): depth_terms = lax.all_to_all(depth_terms, 'gy', 0, 0)  13.1 us
    ppermute x2, starting transfers between devices, shifted(): return lax.ppermute(part, axis, [(i, i + 1) for i in range(count - 1)])  6.49 us
    ppermute x2, waiting for transfers between devices, shifted(): return lax.ppermute(part, axis, [(i + 1, i) for i in range(count - 1)])  5.41 us
    ppermute x2, waiting for transfers between devices, local(): other = lax.ppermute(plane_terms, 'gz', [(i, i ^ hop) for i in range(n_gz)])  4.56 us
    ppermute x2, starting transfers between devices, local(): other = lax.ppermute(plane_terms, 'gz', [(i, i ^ hop) for i in range(n_gz)])  4.23 us
    all_to_all x1, starting transfers between devices, local(): depth_terms = lax.all_to_all(depth_terms, 'gy', 0, 0)  3.41 us
    ppermute x2, starting transfers between devices, shifted(): return lax.ppermute(part, axis, [(i + 1, i) for i in range(count - 1)])  2.72 us
  transfers between devices with their start and end apart: 7, of which 5 were waited for; matrix products, arithmetic and copies ran while one was open for 0% of the time, Pallas kernels for 2%

profile of v15, /device:TPU:0, one launch (start us, length us, event | category | flops | bytes accessed | tf_op | source)
XLA Modules:
  0.0 100.9 jit_solution(4892063191838062718)
XLA Ops:
  0.6 0.0 copy-start
  0.6 2.2 %copy-done = bf16[64,64,512]{2,1,0:T(8,128)(2,1)S(1)} copy-done((bf16[64,64,512]{2,1,0:T(8,128)(2,1)S(1)}, bf16[64,64,512]{2,1,0:T(8,128)(2,1)}, u32[]{:S(2)}) %copy-start) | copy-done | bytes 4194328
  2.8 0.8 ends.1
  3.6 4.9 %collective-permute-start = (bf16[64,128]{1,0:T(8,128)(2,1)S(1)}, bf16[64,128]{1,0:T(8,128)(2,1)S(1)}, u32[]{:S(2)}, u32[]{:S(2)}) collective-permute-start(bf16[64,128]{1,0:T(8,128)(2,1)S(1)} %get-tuple-element.20), channel_id=1, source_target_pairs={{0,1},{1,2},{2,3},{4,5},{5,6},{6,7},{8,9},{9,10},{10,11},{12,13},{... | collective-permute-start | bytes 49160 | tf_op jit(solution)/shard_map/ppermute | solution.py:106
  8.6 1.3 %collective-permute-start.1 = (bf16[64,128]{1,0:T(8,128)(2,1)S(1)}, bf16[64,128]{1,0:T(8,128)(2,1)S(1)}, u32[]{:S(2)}, u32[]{:S(2)}) collective-permute-start(bf16[64,128]{1,0:T(8,128)(2,1)S(1)} %get-tuple-element.21), channel_id=1, source_target_pairs={{1,0},{2,1},{3,2},{5,4},{6,5},{7,6},{9,8},{10,9},{11,10},{13,12},{... | collective-permute-start | bytes 49160 | tf_op jit(solution)/shard_map/ppermute | solution.py:105
  9.9 0.1 collective-permute-done.left_ref
  10.0 4.2 %collective-permute-done.1.right_ref = bf16[64,128]{1,0:T(8,128)(2,1)S(1)} collective-permute-done((bf16[64,128]{1,0:T(8,128)(2,1)S(1)}, bf16[64,128]{1,0:T(8,128)(2,1)S(1)}, u32[]{:S(2)}, u32[]{:S(2)}) %collective-permute-start.1) | collective-permute-done | bytes 16416 | tf_op jit(solution)/shard_map/ppermute | solution.py:105
  14.2 0.0 copy-start.2
  14.2 0.2 rows.1
  14.4 0.0 copy-start.3
  14.4 0.0 copy-start.4
  14.4 0.0 copy-start.1
  14.4 1.6 %collective-permute-start.2 = (bf16[64,640]{1,0:T(8,128)(2,1)S(1)}, bf16[64,640]{1,0:T(8,128)(2,1)S(1)}, u32[]{:S(2)}, u32[]{:S(2)}) collective-permute-start(bf16[64,640]{1,0:T(8,128)(2,1)S(1)} %get-tuple-element.26), channel_id=1, source_target_pairs={{0,4},{4,8},{8,12},{12,16},{16,20},{20,24},{24,28},{1,5},{5,9},{9,... | collective-permute-start | bytes 245768 | tf_op jit(solution)/shard_map/ppermute | solution.py:106
  16.0 1.4 %collective-permute-start.3 = (bf16[64,640]{1,0:T(8,128)(2,1)S(1)}, bf16[64,640]{1,0:T(8,128)(2,1)S(1)}, u32[]{:S(2)}, u32[]{:S(2)}) collective-permute-start(bf16[64,640]{1,0:T(8,128)(2,1)S(1)} %get-tuple-element.24.later_ref), channel_id=1, source_target_pairs={{4,0},{8,4},{12,8},{16,12},{20,16},{24,20},{28,24},{5,1},{9,5},{13... | collective-permute-start | bytes 245768 | tf_op jit(solution)/shard_map/ppermute | solution.py:105
  17.4 0.0 copy-done.2
  17.4 1.5 %squares.1.sums = f32[4,64,128]{2,1,0:T(8,128)S(1)} custom-call(bf16[64,64,512]{2,1,0:T(8,128)(2,1)S(1)} %copy-done.2, bf16[64,640]{1,0:T(8,128)(2,1)S(1)} %get-tuple-element.24.later_ref), custom_call_target="tpu_custom_call" | custom-call | flops 6291456 | bytes 4194304 | tf_op jit(solution)/shard_map/squares/pallas_call | solution.py:131
  19.0 0.0 copy-done.3
  19.0 0.0 copy-done.4
  19.0 0.7 terms.1
  19.7 0.0 collective-permute-done.2.low_ref
  19.7 1.2 %collective-permute-done.3.high_ref = bf16[64,640]{1,0:T(8,128)(2,1)S(1)} collective-permute-done((bf16[64,640]{1,0:T(8,128)(2,1)S(1)}, bf16[64,640]{1,0:T(8,128)(2,1)S(1)}, u32[]{:S(2)}, u32[]{:S(2)}) %collective-permute-start.3) | collective-permute-done | bytes 81952 | tf_op jit(solution)/shard_map/ppermute | solution.py:105
  20.9 0.0 copy-done.1
  20.9 53.1 %warp.1 = (bf16[64,64,512]{2,1,0:T(8,128)(2,1)}, f32[8,16,512]{2,1,0:T(8,128)S(1)}, f32[64,128]{1,0:T(8,128)S(1)}) custom-call(bf16[64,64,512]{2,1,0:T(8,128)(2,1)S(1)} %copy-done.1, bf16[64,64,512]{2,1,0:T(8,128)(2,1)S(1)} %copy-done.2, bf16[3,64,64,512]{3,2,1,0:T(8,128)(2,1)} %shift_ref.1, bf16[64,64,128]{2,1,0:T(8,128)(2,1)S(1)} %get-tuple-element.25.beyond_ref, ...), custom_call_target="tpu_custom_call" | custom-call | flops 125829120 | bytes 25165824 | tf_op jit(solution)/shard_map/warp/pallas_call | solution.py:352
  74.0 13.1 %all_to_all.10.depth_ref = f32[8,16,512]{2,1,0:T(8,128)S(1)} all-to-all(f32[8,16,512]{2,1,0:T(8,128)S(1)} %get-tuple-element.31), channel_id=1, replica_groups=mesh['gy'=8,'gz'=4] {'gy'}, dimensions={0} | all-to-all | bytes 524288 | tf_op jit(solution)/shard_map/all_to_all | solution.py:435
  87.1 0.7 gather.1
  87.8 3.4 %all-to-all-start.1 = ((f32[8,16,512]{2,1,0:T(8,128)}), f32[8,16,512]{2,1,0:T(8,128)S(1)}, u32[]{:S(2)}, u32[]{:S(2)}) async-start(f32[8,16,512]{2,1,0:T(8,128)} %get-tuple-element.33), calls=%async_computation.1 | async-start | bytes 524288 | tf_op jit(solution)/shard_map/all_to_all | solution.py:445
  91.2 1.6 %collective-permute-start.4 = (f32[64,128]{1,0:T(8,128)S(1)}, f32[64,128]{1,0:T(8,128)S(1)}, u32[]{:S(2)}, u32[]{:S(2)}) collective-permute-start(f32[64,128]{1,0:T(8,128)S(1)} %get-tuple-element.34), channel_id=1, source_target_pairs={{0,1},{1,0},{2,3},{3,2},{4,5},{5,4},{6,7},{7,6},{8,9},{9,8},{10,11... | collective-permute-start | bytes 98312 | tf_op jit(solution)/shard_map/ppermute | solution.py:448
  92.9 2.3 %collective-permute-done.4 = f32[64,128]{1,0:T(8,128)S(1)} collective-permute-done((f32[64,128]{1,0:T(8,128)S(1)}, f32[64,128]{1,0:T(8,128)S(1)}, u32[]{:S(2)}, u32[]{:S(2)}) %collective-permute-start.4) | collective-permute-done | bytes 32800 | tf_op jit(solution)/shard_map/ppermute | solution.py:448
  95.2 2.6 %collective-permute-start.5 = (f32[64,128]{1,0:T(8,128)S(1)}, f32[64,128]{1,0:T(8,128)S(1)}, u32[]{:S(2)}, u32[]{:S(2)}) collective-permute-start(f32[64,128]{1,0:T(8,128)S(1)} %add.3.plane_ref), channel_id=1, source_target_pairs={{0,2},{1,3},{2,0},{3,1},{4,6},{5,7},{6,4},{7,5},{8,10},{9,11},{10,... | collective-permute-start | bytes 98312 | tf_op jit(solution)/shard_map/ppermute | solution.py:448
  97.8 2.2 %collective-permute-done.5.other_ref = f32[64,128]{1,0:T(8,128)S(1)} collective-permute-done((f32[64,128]{1,0:T(8,128)S(1)}, f32[64,128]{1,0:T(8,128)S(1)}, u32[]{:S(2)}, u32[]{:S(2)}) %collective-permute-start.5) | collective-permute-done | bytes 32800 | tf_op jit(solution)/shard_map/ppermute | solution.py:448
  100.0 0.0 all-to-all-done.1.depth_ref
  100.0 0.9 steps.1
  (1 shorter events, 0.0 us)
Async XLA Ops:
  0.6 2.2 %copy-start = (bf16[64,64,512]{2,1,0:T(8,128)(2,1)S(1)}, bf16[64,64,512]{2,1,0:T(8,128)(2,1)}, u32[]{:S(2)}) copy-start(bf16[64,64,512]{2,1,0:T(8,128)(2,1)} %cells_ref.3) | copy-start | bytes 12582916
  3.6 6.4 %collective-permute-start = (bf16[64,128]{1,0:T(8,128)(2,1)S(1)}, bf16[64,128]{1,0:T(8,128)(2,1)S(1)}, u32[]{:S(2)}, u32[]{:S(2)}) collective-permute-start(bf16[64,128]{1,0:T(8,128)(2,1)S(1)} %get-tuple-element.20), channel_id=1, source_target_pairs={{0,1},{1,2},{2,3},{4,5},{5,6},{6,7},{8,9},{9,10},{10,11},{12,13},{... | collective-permute-start | bytes 49160 | tf_op jit(solution)/shard_map/ppermute | solution.py:106
  8.6 5.6 %collective-permute-start.1 = (bf16[64,128]{1,0:T(8,128)(2,1)S(1)}, bf16[64,128]{1,0:T(8,128)(2,1)S(1)}, u32[]{:S(2)}, u32[]{:S(2)}) collective-permute-start(bf16[64,128]{1,0:T(8,128)(2,1)S(1)} %get-tuple-element.21), channel_id=1, source_target_pairs={{1,0},{2,1},{3,2},{5,4},{6,5},{7,6},{9,8},{10,9},{11,10},{13,12},{... | collective-permute-start | bytes 49160 | tf_op jit(solution)/shard_map/ppermute | solution.py:105
  14.2 3.2 %copy-start.2 = (bf16[64,64,512]{2,1,0:T(8,128)(2,1)S(1)}, bf16[64,64,512]{2,1,0:T(8,128)(2,1)}, u32[]{:S(2)}) copy-start(bf16[64,64,512]{2,1,0:T(8,128)(2,1)} %image_ref.3) | copy-start | bytes 12582916
  14.4 4.6 %copy-start.3 = (f32[2,32,512]{2,1,0:T(8,128)S(1)}, f32[2,32,512]{2,1,0:T(8,128)}, u32[]{:S(2)}) copy-start(f32[2,32,512]{2,1,0:T(8,128)} %depth_ref.3) | copy-start | bytes 393220
  14.4 4.6 %copy-start.4 = (f32[2,32,8,8]{1,3,2,0:T(8,128)S(1)}, f32[2,32,8,8]{1,3,2,0:T(8,128)}, u32[]{:S(2)}) copy-start(f32[2,32,8,8]{1,3,2,0:T(8,128)} %param.8) | copy-start | bytes 49156
  14.4 6.5 %copy-start.1 = (bf16[64,64,512]{2,1,0:T(8,128)(2,1)S(1)}, bf16[64,64,512]{2,1,0:T(8,128)(2,1)}, u32[]{:S(2)}) copy-start(bf16[64,64,512]{2,1,0:T(8,128)(2,1)} %cells_ref.3) | copy-start | bytes 12582916
  14.4 5.3 %collective-permute-start.2 = (bf16[64,640]{1,0:T(8,128)(2,1)S(1)}, bf16[64,640]{1,0:T(8,128)(2,1)S(1)}, u32[]{:S(2)}, u32[]{:S(2)}) collective-permute-start(bf16[64,640]{1,0:T(8,128)(2,1)S(1)} %get-tuple-element.26), channel_id=1, source_target_pairs={{0,4},{4,8},{8,12},{12,16},{16,20},{20,24},{24,28},{1,5},{5,9},{9,... | collective-permute-start | bytes 245768 | tf_op jit(solution)/shard_map/ppermute | solution.py:106
  16.0 4.9 %collective-permute-start.3 = (bf16[64,640]{1,0:T(8,128)(2,1)S(1)}, bf16[64,640]{1,0:T(8,128)(2,1)S(1)}, u32[]{:S(2)}, u32[]{:S(2)}) collective-permute-start(bf16[64,640]{1,0:T(8,128)(2,1)S(1)} %get-tuple-element.24.later_ref), channel_id=1, source_target_pairs={{4,0},{8,4},{12,8},{16,12},{20,16},{24,20},{28,24},{5,1},{9,5},{13... | collective-permute-start | bytes 245768 | tf_op jit(solution)/shard_map/ppermute | solution.py:105
  87.8 12.2 %all-to-all-start.1 = ((f32[8,16,512]{2,1,0:T(8,128)}), f32[8,16,512]{2,1,0:T(8,128)S(1)}, u32[]{:S(2)}, u32[]{:S(2)}) async-start(f32[8,16,512]{2,1,0:T(8,128)} %get-tuple-element.33), calls=%async_computation.1 | async-start | bytes 524288 | tf_op jit(solution)/shard_map/all_to_all | solution.py:445
  91.2 4.0 %collective-permute-start.4 = (f32[64,128]{1,0:T(8,128)S(1)}, f32[64,128]{1,0:T(8,128)S(1)}, u32[]{:S(2)}, u32[]{:S(2)}) collective-permute-start(f32[64,128]{1,0:T(8,128)S(1)} %get-tuple-element.34), channel_id=1, source_target_pairs={{0,1},{1,0},{2,3},{3,2},{4,5},{5,4},{6,7},{7,6},{8,9},{9,8},{10,11... | collective-permute-start | bytes 98312 | tf_op jit(solution)/shard_map/ppermute | solution.py:448
  95.2 4.8 %collective-permute-start.5 = (f32[64,128]{1,0:T(8,128)S(1)}, f32[64,128]{1,0:T(8,128)S(1)}, u32[]{:S(2)}, u32[]{:S(2)}) collective-permute-start(f32[64,128]{1,0:T(8,128)S(1)} %add.3.plane_ref), channel_id=1, source_target_pairs={{0,2},{1,3},{2,0},{3,1},{4,6},{5,7},{6,4},{7,5},{8,10},{9,11},{10,... | collective-permute-start | bytes 98312 | tf_op jit(solution)/shard_map/ppermute | solution.py:448

commit v16 on v13

--- a/solution.py
+++ b/solution.py
@@ -69,6 +69,7 @@
         ends_kernel,
         out_shape=[jax.ShapeDtypeStruct((rows, LANES), bf16)] * 2 + [jax.ShapeDtypeStruct((depth, width), bf16)] * 2,
         compiler_params=plain_params(),
+        cost_estimate=pl.CostEstimate(flops=cells.size, bytes_accessed=2 * cells.size, transcendentals=0),
         name="ends",
     )(cells)
 
@@ -93,6 +94,7 @@
         rows_kernel,
         out_shape=[jax.ShapeDtypeStruct((depth, width + LANES), bf16)] * 2,
         compiler_params=plain_params(),
+        cost_estimate=pl.CostEstimate(flops=500000 * low.size, bytes_accessed=8 * low.size, transcendentals=0),
         name="rows",
     )(left, right, low, high)
 
@@ -309,7 +311,7 @@
                     blocks[k, tile, pl.ds(node, 1), :] = jnp.sum(value, axis=0, keepdims=True)
             return total
 
-        energy[...] = lax.fori_loop(0, (rows // 16) * tiles, one, energy[...])
+        energy[...] = lax.fori_loop(0, (rows // 16) * tiles, one, energy[...], unroll=2)
 
     @pl.when(step == last)
     def _():
@@ -380,14 +382,9 @@
     )(cells, image, shift, beyond, low, high, field, plane, depth_factors, diag_depth, diag_plane)
 
 
-def gather_kernel(depth_ref, *refs):
-    depth_out, plane_out = refs[-2:]
+def gather_kernel(depth_ref, plane_ref, other_ref, depth_out, plane_out):
     total = jnp.sum(depth_ref[...], axis=0)
-    found = [ref[...] for ref in refs[:-2]]
-    while len(found) > 1:
-        half = len(found) // 2
-        found = [found[k] + found[k + half] for k in range(half)]
-    planes = found[0]
+    planes = plane_ref[...] + other_ref[...]
     plane_out[...] = planes
     cells = planes.shape[0]
     share, width = total.shape[0] // 4, total.shape[1]
@@ -434,10 +431,13 @@
         deformed, image, displacement, beyond, below, above, field, plane, depth_factors, diag_depth, diag_plane,
         n_gy,
     )
-    others = [
-        lax.ppermute(plane_terms, "gz", [(i, (i + hop) % n_gz) for i in range(n_gz)]) for hop in range(1, n_gz)
-    ]
     depth_terms = lax.all_to_all(depth_terms, "gy", 0, 0)
+    hop = 1
+    while hop < n_gz:
+        other = lax.ppermute(plane_terms, "gz", [(i, i ^ hop) for i in range(n_gz)])
+        if 2 * hop < n_gz:
+            plane_terms = plane_terms + other
+        hop = 2 * hop
     depth_terms, plane_terms = pl.pallas_call(
         gather_kernel,
         out_shape=[
@@ -446,7 +446,7 @@
         ],
         compiler_params=plain_params(),
         name="gather",
-    )(depth_terms, plane_terms, *others)
+    )(depth_terms, plane_terms, other)
     depth_terms = lax.all_to_all(depth_terms, "gy", 0, 0)
     width = depth_factors.shape[2]
     step_depth, step_plane = pl.pallas_call(

time: 79.3 us -> 78.2 us (0.986)
  local copies, waits for them, and re-layouts: 4.38 us -> 2.21 us
  waiting for transfers between devices: 8.47 us -> 10.2 us
    unnamed x12 -> x10, local copies, waits for them, and re-layouts: 4.38 us -> 2.21 us
    ppermute x2, waiting for transfers between devices: 4.21 us -> 5.41 us  [shifted(): return lax.ppermute(part, axis, [(i + 1, i) for i in range(count - 1)])]
    ppermute x3 -> x2, waiting for transfers between devices: 4.13 us -> 4.62 us  [local(): other = lax.ppermute(plane_terms, 'gz', [(i, i ^ hop) for i in range(n_gz)])]
    ppermute x3 -> x2, starting transfers between devices: 4.62 us -> 4.16 us  [local(): other = lax.ppermute(plane_terms, 'gz', [(i, i ^ hop) for i in range(n_gz)])]
  transfers between devices with their start and end apart: 8 -> 7, of which waited for: 4 -> 5; matrix products, arithmetic and copies ran while one was open for 0% -> 0% of each run, Pallas kernels for 3% -> 3%
where the time goes in v16:
time: 78.2 us; the launch traced here: 77.8 us
  Pallas kernels  34.1 us (44%)
  starting transfers between devices  19.7 us (25%)
  blocking collectives  10.9 us (14%)
  waiting for transfers between devices  10.2 us (13%)
  local copies, waits for them, and re-layouts  2.21 us (3%)
    pallas_call x1, Pallas kernels, warp(): pl.pallas_call(warp_kernel, grid=(count + 1,), in_specs=[pl.BlockSpec((KN...  29.9 us
    all_to_all x1, blocking collectives, local(): depth_terms = lax.all_to_all(depth_terms, 'gy', 0, 0)  10.9 us
    ppermute x2, starting transfers between devices, shifted(): return lax.ppermute(part, axis, [(i, i + 1) for i in range(count - 1)])  6.49 us
    all_to_all x1, starting transfers between devices, local(): depth_terms = lax.all_to_all(depth_terms, 'gy', 0, 0)  6.36 us
    ppermute x2, waiting for transfers between devices, shifted(): return lax.ppermute(part, axis, [(i + 1, i) for i in range(count - 1)])  5.41 us
    ppermute x2, waiting for transfers between devices, local(): other = lax.ppermute(plane_terms, 'gz', [(i, i ^ hop) for i in range(n_gz)])  4.62 us
    ppermute x2, starting transfers between devices, local(): other = lax.ppermute(plane_terms, 'gz', [(i, i ^ hop) for i in range(n_gz)])  4.16 us
    ppermute x2, starting transfers between devices, shifted(): return lax.ppermute(part, axis, [(i + 1, i) for i in range(count - 1)])  2.72 us
  transfers between devices with their start and end apart: 7, of which 5 were waited for; matrix products, arithmetic and copies ran while one was open for 0% of the time, Pallas kernels for 3%

profile of v16, /device:TPU:0, one launch (start us, length us, event | category | flops | bytes accessed | tf_op | source)
XLA Modules:
  0.0 77.8 jit_solution(1627268706890525702)
XLA Ops:
  0.6 0.0 copy-start
  0.6 2.2 %copy-done = bf16[64,64,512]{2,1,0:T(8,128)(2,1)S(1)} copy-done((bf16[64,64,512]{2,1,0:T(8,128)(2,1)S(1)}, bf16[64,64,512]{2,1,0:T(8,128)(2,1)}, u32[]{:S(2)}) %copy-start) | copy-done | bytes 4194328
  2.8 0.8 %ends.1 = (bf16[64,128]{1,0:T(8,128)(2,1)S(1)}, bf16[64,128]{1,0:T(8,128)(2,1)S(1)}, bf16[64,512]{1,0:T(8,128)(2,1)S(1)}, bf16[64,512]{1,0:T(8,128)(2,1)S(1)}) custom-call(bf16[64,64,512]{2,1,0:T(8,128)(2,1)S(1)} %copy-done), custom_call_target="tpu_custom_call" | custom-call | flops 2097152 | bytes 4194304 | tf_op jit(solution)/shard_map/ends/pallas_call | solution.py:68
  3.6 4.9 %collective-permute-start = (bf16[64,128]{1,0:T(8,128)(2,1)S(1)}, bf16[64,128]{1,0:T(8,128)(2,1)S(1)}, u32[]{:S(2)}, u32[]{:S(2)}) collective-permute-start(bf16[64,128]{1,0:T(8,128)(2,1)S(1)} %get-tuple-element.20), channel_id=1, source_target_pairs={{0,1},{1,2},{2,3},{4,5},{5,6},{6,7},{8,9},{9,10},{10,11},{12,13},{... | collective-permute-start | bytes 49160 | tf_op jit(solution)/shard_map/ppermute | solution.py:106
  8.6 1.3 %collective-permute-start.1 = (bf16[64,128]{1,0:T(8,128)(2,1)S(1)}, bf16[64,128]{1,0:T(8,128)(2,1)S(1)}, u32[]{:S(2)}, u32[]{:S(2)}) collective-permute-start(bf16[64,128]{1,0:T(8,128)(2,1)S(1)} %get-tuple-element.21), channel_id=1, source_target_pairs={{1,0},{2,1},{3,2},{5,4},{6,5},{7,6},{9,8},{10,9},{11,10},{13,12},{... | collective-permute-start | bytes 49160 | tf_op jit(solution)/shard_map/ppermute | solution.py:105
  9.9 0.1 collective-permute-done.left_ref
  10.0 4.2 %collective-permute-done.1.right_ref = bf16[64,128]{1,0:T(8,128)(2,1)S(1)} collective-permute-done((bf16[64,128]{1,0:T(8,128)(2,1)S(1)}, bf16[64,128]{1,0:T(8,128)(2,1)S(1)}, u32[]{:S(2)}, u32[]{:S(2)}) %collective-permute-start.1) | collective-permute-done | bytes 16416 | tf_op jit(solution)/shard_map/ppermute | solution.py:105
  14.2 0.0 copy-start.2
  14.2 0.2 rows.1
  14.4 0.0 copy-start.3
  14.4 0.0 copy-start.4
  14.4 0.0 copy-start.1
  14.4 1.6 %collective-permute-start.2 = (bf16[64,640]{1,0:T(8,128)(2,1)S(1)}, bf16[64,640]{1,0:T(8,128)(2,1)S(1)}, u32[]{:S(2)}, u32[]{:S(2)}) collective-permute-start(bf16[64,640]{1,0:T(8,128)(2,1)S(1)} %get-tuple-element.26), channel_id=1, source_target_pairs={{0,4},{4,8},{8,12},{12,16},{16,20},{20,24},{24,28},{1,5},{5,9},{9,... | collective-permute-start | bytes 245768 | tf_op jit(solution)/shard_map/ppermute | solution.py:106
  16.0 1.4 %collective-permute-start.3 = (bf16[64,640]{1,0:T(8,128)(2,1)S(1)}, bf16[64,640]{1,0:T(8,128)(2,1)S(1)}, u32[]{:S(2)}, u32[]{:S(2)}) collective-permute-start(bf16[64,640]{1,0:T(8,128)(2,1)S(1)} %get-tuple-element.24.later_ref), channel_id=1, source_target_pairs={{4,0},{8,4},{12,8},{16,12},{20,16},{24,20},{28,24},{5,1},{9,5},{13... | collective-permute-start | bytes 245768 | tf_op jit(solution)/shard_map/ppermute | solution.py:105
  17.4 0.0 copy-done.2
  17.4 1.5 %squares.1.sums = f32[4,64,128]{2,1,0:T(8,128)S(1)} custom-call(bf16[64,64,512]{2,1,0:T(8,128)(2,1)S(1)} %copy-done.2, bf16[64,640]{1,0:T(8,128)(2,1)S(1)} %get-tuple-element.24.later_ref), custom_call_target="tpu_custom_call" | custom-call | flops 6291456 | bytes 4194304 | tf_op jit(solution)/shard_map/squares/pallas_call | solution.py:131
  19.0 0.0 copy-done.3
  19.0 0.0 copy-done.4
  19.0 0.7 terms.1
  19.7 0.0 collective-permute-done.2.low_ref
  19.7 1.2 %collective-permute-done.3.high_ref = bf16[64,640]{1,0:T(8,128)(2,1)S(1)} collective-permute-done((bf16[64,640]{1,0:T(8,128)(2,1)S(1)}, bf16[64,640]{1,0:T(8,128)(2,1)S(1)}, u32[]{:S(2)}, u32[]{:S(2)}) %collective-permute-start.3) | collective-permute-done | bytes 81952 | tf_op jit(solution)/shard_map/ppermute | solution.py:105
  20.9 0.0 copy-done.1
  20.9 29.9 %warp.1 = (bf16[64,64,512]{2,1,0:T(8,128)(2,1)}, f32[8,16,512]{2,1,0:T(8,128)}, f32[64,128]{1,0:T(8,128)S(1)}) custom-call(bf16[64,64,512]{2,1,0:T(8,128)(2,1)S(1)} %copy-done.1, bf16[64,64,512]{2,1,0:T(8,128)(2,1)S(1)} %copy-done.2, bf16[3,64,64,512]{3,2,1,0:T(8,128)(2,1)} %shift_ref.1, bf16[64,64,128]{2,1,0:T(8,128)(2,1)S(1)} %get-tuple-element.25.beyond_ref, ...), custom_call_target="tpu_custom_call" | custom-call | flops 125829120 | bytes 25165824 | tf_op jit(solution)/shard_map/warp/pallas_call | solution.py:344
  50.8 6.4 %all-to-all-start = ((f32[8,16,512]{2,1,0:T(8,128)}), f32[8,16,512]{2,1,0:T(8,128)S(1)}, u32[]{:S(2)}, u32[]{:S(2)}) async-start(f32[8,16,512]{2,1,0:T(8,128)} %get-tuple-element.31), calls=%async_computation | async-start | bytes 524288 | tf_op jit(solution)/shard_map/all_to_all | solution.py:434
  57.2 1.6 %collective-permute-start.4 = (f32[64,128]{1,0:T(8,128)S(1)}, f32[64,128]{1,0:T(8,128)S(1)}, u32[]{:S(2)}, u32[]{:S(2)}) collective-permute-start(f32[64,128]{1,0:T(8,128)S(1)} %get-tuple-element.32), channel_id=1, source_target_pairs={{0,1},{1,0},{2,3},{3,2},{4,5},{5,4},{6,7},{7,6},{8,9},{9,8},{10,11... | collective-permute-start | bytes 98312 | tf_op jit(solution)/shard_map/ppermute | solution.py:437
  58.7 2.3 %collective-permute-done.4 = f32[64,128]{1,0:T(8,128)S(1)} collective-permute-done((f32[64,128]{1,0:T(8,128)S(1)}, f32[64,128]{1,0:T(8,128)S(1)}, u32[]{:S(2)}, u32[]{:S(2)}) %collective-permute-start.4) | collective-permute-done | bytes 32800 | tf_op jit(solution)/shard_map/ppermute | solution.py:437
  61.1 2.6 %collective-permute-start.5 = (f32[64,128]{1,0:T(8,128)S(1)}, f32[64,128]{1,0:T(8,128)S(1)}, u32[]{:S(2)}, u32[]{:S(2)}) collective-permute-start(f32[64,128]{1,0:T(8,128)S(1)} %add.3.plane_ref), channel_id=1, source_target_pairs={{0,2},{1,3},{2,0},{3,1},{4,6},{5,7},{6,4},{7,5},{8,10},{9,11},{10,... | collective-permute-start | bytes 98312 | tf_op jit(solution)/shard_map/ppermute | solution.py:437
  63.7 2.3 %collective-permute-done.5.other_ref = f32[64,128]{1,0:T(8,128)S(1)} collective-permute-done((f32[64,128]{1,0:T(8,128)S(1)}, f32[64,128]{1,0:T(8,128)S(1)}, u32[]{:S(2)}, u32[]{:S(2)}) %collective-permute-start.5) | collective-permute-done | bytes 32800 | tf_op jit(solution)/shard_map/ppermute | solution.py:437
  65.9 0.0 all-to-all-done.depth_ref
  65.9 0.1 gather.1
  66.1 10.9 %all_to_all.10.depth_ref = f32[8,16,512]{2,1,0:T(8,128)S(1)} all-to-all(f32[8,16,512]{2,1,0:T(8,128)S(1)} %get-tuple-element.33), channel_id=1, replica_groups=mesh['gy'=8,'gz'=4] {'gy'}, dimensions={0} | all-to-all | bytes 524288 | tf_op jit(solution)/shard_map/all_to_all | solution.py:450
  77.0 0.9 %steps.1 = (f32[2,32,512]{2,1,0:T(8,128)}, f32[2,64,32]{2,1,0:T(8,128)}) custom-call(f32[8,16,512]{2,1,0:T(8,128)S(1)} %all_to_all.10.depth_ref, f32[64,128]{1,0:T(8,128)S(1)} %get-tuple-element.34.plane_ref), custom_call_target="tpu_custom_call" | custom-call | tf_op jit(solution)/shard_map/steps/pallas_call | solution.py:452
  (1 shorter events, 0.0 us)
Async XLA Ops:
  0.6 2.2 %copy-start = (bf16[64,64,512]{2,1,0:T(8,128)(2,1)S(1)}, bf16[64,64,512]{2,1,0:T(8,128)(2,1)}, u32[]{:S(2)}) copy-start(bf16[64,64,512]{2,1,0:T(8,128)(2,1)} %cells_ref.3) | copy-start | bytes 12582916
  3.6 6.4 %collective-permute-start = (bf16[64,128]{1,0:T(8,128)(2,1)S(1)}, bf16[64,128]{1,0:T(8,128)(2,1)S(1)}, u32[]{:S(2)}, u32[]{:S(2)}) collective-permute-start(bf16[64,128]{1,0:T(8,128)(2,1)S(1)} %get-tuple-element.20), channel_id=1, source_target_pairs={{0,1},{1,2},{2,3},{4,5},{5,6},{6,7},{8,9},{9,10},{10,11},{12,13},{... | collective-permute-start | bytes 49160 | tf_op jit(solution)/shard_map/ppermute | solution.py:106
  8.6 5.6 %collective-permute-start.1 = (bf16[64,128]{1,0:T(8,128)(2,1)S(1)}, bf16[64,128]{1,0:T(8,128)(2,1)S(1)}, u32[]{:S(2)}, u32[]{:S(2)}) collective-permute-start(bf16[64,128]{1,0:T(8,128)(2,1)S(1)} %get-tuple-element.21), channel_id=1, source_target_pairs={{1,0},{2,1},{3,2},{5,4},{6,5},{7,6},{9,8},{10,9},{11,10},{13,12},{... | collective-permute-start | bytes 49160 | tf_op jit(solution)/shard_map/ppermute | solution.py:105
  14.2 3.2 %copy-start.2 = (bf16[64,64,512]{2,1,0:T(8,128)(2,1)S(1)}, bf16[64,64,512]{2,1,0:T(8,128)(2,1)}, u32[]{:S(2)}) copy-start(bf16[64,64,512]{2,1,0:T(8,128)(2,1)} %image_ref.3) | copy-start | bytes 12582916
  14.4 4.6 %copy-start.3 = (f32[2,32,512]{2,1,0:T(8,128)S(1)}, f32[2,32,512]{2,1,0:T(8,128)}, u32[]{:S(2)}) copy-start(f32[2,32,512]{2,1,0:T(8,128)} %depth_ref.3) | copy-start | bytes 393220
  14.4 4.6 %copy-start.4 = (f32[2,32,8,8]{1,3,2,0:T(8,128)S(1)}, f32[2,32,8,8]{1,3,2,0:T(8,128)}, u32[]{:S(2)}) copy-start(f32[2,32,8,8]{1,3,2,0:T(8,128)} %param.8) | copy-start | bytes 49156
  14.4 6.5 %copy-start.1 = (bf16[64,64,512]{2,1,0:T(8,128)(2,1)S(1)}, bf16[64,64,512]{2,1,0:T(8,128)(2,1)}, u32[]{:S(2)}) copy-start(bf16[64,64,512]{2,1,0:T(8,128)(2,1)} %cells_ref.3) | copy-start | bytes 12582916
  14.4 5.3 %collective-permute-start.2 = (bf16[64,640]{1,0:T(8,128)(2,1)S(1)}, bf16[64,640]{1,0:T(8,128)(2,1)S(1)}, u32[]{:S(2)}, u32[]{:S(2)}) collective-permute-start(bf16[64,640]{1,0:T(8,128)(2,1)S(1)} %get-tuple-element.26), channel_id=1, source_target_pairs={{0,4},{4,8},{8,12},{12,16},{16,20},{20,24},{24,28},{1,5},{5,9},{9,... | collective-permute-start | bytes 245768 | tf_op jit(solution)/shard_map/ppermute | solution.py:106
  16.0 4.9 %collective-permute-start.3 = (bf16[64,640]{1,0:T(8,128)(2,1)S(1)}, bf16[64,640]{1,0:T(8,128)(2,1)S(1)}, u32[]{:S(2)}, u32[]{:S(2)}) collective-permute-start(bf16[64,640]{1,0:T(8,128)(2,1)S(1)} %get-tuple-element.24.later_ref), channel_id=1, source_target_pairs={{4,0},{8,4},{12,8},{16,12},{20,16},{24,20},{28,24},{5,1},{9,5},{13... | collective-permute-start | bytes 245768 | tf_op jit(solution)/shard_map/ppermute | solution.py:105
  50.8 15.1 %all-to-all-start = ((f32[8,16,512]{2,1,0:T(8,128)}), f32[8,16,512]{2,1,0:T(8,128)S(1)}, u32[]{:S(2)}, u32[]{:S(2)}) async-start(f32[8,16,512]{2,1,0:T(8,128)} %get-tuple-element.31), calls=%async_computation | async-start | bytes 524288 | tf_op jit(solution)/shard_map/all_to_all | solution.py:434
  57.2 3.9 %collective-permute-start.4 = (f32[64,128]{1,0:T(8,128)S(1)}, f32[64,128]{1,0:T(8,128)S(1)}, u32[]{:S(2)}, u32[]{:S(2)}) collective-permute-start(f32[64,128]{1,0:T(8,128)S(1)} %get-tuple-element.32), channel_id=1, source_target_pairs={{0,1},{1,0},{2,3},{3,2},{4,5},{5,4},{6,7},{7,6},{8,9},{9,8},{10,11... | collective-permute-start | bytes 98312 | tf_op jit(solution)/shard_map/ppermute | solution.py:437
  61.1 4.9 %collective-permute-start.5 = (f32[64,128]{1,0:T(8,128)S(1)}, f32[64,128]{1,0:T(8,128)S(1)}, u32[]{:S(2)}, u32[]{:S(2)}) collective-permute-start(f32[64,128]{1,0:T(8,128)S(1)} %add.3.plane_ref), channel_id=1, source_target_pairs={{0,2},{1,3},{2,0},{3,1},{4,6},{5,7},{6,4},{7,5},{8,10},{9,11},{10,... | collective-permute-start | bytes 98312 | tf_op jit(solution)/shard_map/ppermute | solution.py:437

commit v17 on v16

--- a/solution.py
+++ b/solution.py
@@ -44,18 +44,42 @@
     return pltpu.CompilerParams(vmem_limit_bytes=32000000)
 
 
-def ends_kernel(cells_ref, first_ref, last_ref, low_ref, high_ref):
-    depth, rows, width = cells_ref.shape
+def columns_kernel(*refs):
+    first_ref, last_ref = refs[-2:]
+    chunks = (len(refs) - 2) // 2
+    rows = first_ref.shape[0]
     lane = lax.broadcasted_iota(jnp.int32, (rows, LANES), 1)
     first = jnp.zeros((rows, LANES), f32)
     last = jnp.zeros((rows, LANES), f32)
-    for x in range(depth):
-        near = cells_ref[x, :, 0:LANES].astype(f32)
-        far = cells_ref[x, :, width - LANES : width].astype(f32)
-        first = jnp.where(lane == x, pltpu.roll(near, x, 1), first)
-        last = jnp.where(lane == x, pltpu.roll(far, (x + 1) % LANES, 1), last)
+    for chunk in range(chunks):
+        near, far = refs[chunk], refs[chunks + chunk]
+        for k in range(near.shape[0]):
+            x = chunk * near.shape[0] + k
+            first = jnp.where(lane == x, pltpu.roll(near[k].astype(f32), x, 1), first)
+            last = jnp.where(lane == x, pltpu.roll(far[k].astype(f32), (x + 1) % LANES, 1), last)
     first_ref[...] = first.astype(bf16)
     last_ref[...] = last.astype(bf16)
+
+
+def end_columns(cells):
+    depth, rows, width = cells.shape
+    tiles = width // LANES
+    chunks = 4
+    block = (depth // chunks, rows, LANES)
+    places = [(chunk, tile) for tile in (0, tiles - 1) for chunk in range(chunks)]
+    return pl.pallas_call(
+        columns_kernel,
+        grid=(1,),
+        in_specs=[pl.BlockSpec(block, functools.partial(lambda c, t, i: (c, 0, t), c, t)) for c, t in places],
+        out_specs=[pl.BlockSpec((rows, LANES), lambda i: (0, 0))] * 2,
+        out_shape=[jax.ShapeDtypeStruct((rows, LANES), bf16)] * 2,
+        compiler_params=pltpu.CompilerParams(vmem_limit_bytes=60000000),
+        name="columns",
+    )(*[cells] * len(places))
+
+
+def ends_kernel(cells_ref, low_ref, high_ref):
+    depth, rows = cells_ref.shape[0:2]
     for x in range(0, depth, 16):
         low = [cells_ref[x + k, 0:16, :].astype(f32)[0:1] for k in range(16)]
         high = [cells_ref[x + k, rows - 16 : rows, :].astype(f32)[15:16] for k in range(16)]
@@ -67,25 +91,30 @@
     depth, rows, width = cells.shape
     return pl.pallas_call(
         ends_kernel,
-        out_shape=[jax.ShapeDtypeStruct((rows, LANES), bf16)] * 2 + [jax.ShapeDtypeStruct((depth, width), bf16)] * 2,
+        out_shape=[jax.ShapeDtypeStruct((depth, width), bf16)] * 2,
         compiler_params=plain_params(),
         cost_estimate=pl.CostEstimate(flops=cells.size, bytes_accessed=2 * cells.size, transcendentals=0),
         name="ends",
     )(cells)
 
 
-def rows_kernel(left_ref, right_ref, low_ref, high_ref, low_out, high_out):
+def rows_kernel(left_ref, right_ref, low_ref, high_ref, across_out, inside_out):
     depth, width = low_ref.shape
     rows = left_ref.shape[0]
+    odd = lax.axis_index("gy") % 2 == 1
     lane = lax.broadcasted_iota(jnp.int32, (depth, LANES), 1)
     pad = jnp.zeros((LANES - rows, LANES), f32)
     left = jnp.transpose(jnp.concatenate([left_ref[...].astype(f32), pad], axis=0))[0:depth]
     right = jnp.transpose(jnp.concatenate([right_ref[...].astype(f32), pad], axis=0))[0:depth]
-    for row, body, out in ((0, low_ref, low_out), (rows - 1, high_ref, high_out)):
+    bodies, beyond = [], []
+    for row, body in ((0, low_ref), (rows - 1, high_ref)):
         after = pltpu.roll(right, (LANES - row) % LANES, 1)
         before = pltpu.roll(left, LANES - 1 - row, 1)
-        out[:, 0:width] = body[...]
-        out[:, width : width + LANES] = jnp.where(lane == 0, after, before).astype(bf16)
+        bodies.append(body[...].astype(f32))
+        beyond.append(jnp.where(lane == 0, after, before))
+    for out, first, second in ((across_out, 1, 0), (inside_out, 0, 1)):
+        out[:, 0:width] = jnp.where(odd, bodies[first], bodies[second]).astype(bf16)
+        out[:, width : width + LANES] = jnp.where(odd, beyond[first], beyond[second]).astype(bf16)
 
 
 def packed_rows(left, right, low, high):
@@ -104,6 +133,12 @@
     if back:
         return lax.ppermute(part, axis, [(i + 1, i) for i in range(count - 1)])
     return lax.ppermute(part, axis, [(i, i + 1) for i in range(count - 1)])
+
+
+def swapped(part, axis, start):
+    count = lax.axis_size(axis)
+    pairs = [(i, i + 1) for i in range(start, count - 1, 2)]
+    return lax.ppermute(part, axis, pairs + [(j, i) for i, j in pairs])
 
 
 def squares_kernel(image_ref, later_ref, sums):
@@ -178,7 +213,7 @@
 
 
 def warp_kernel(
-    cells_ref, image_ref, shift_ref, beyond_ref, low_ref, high_ref, field, plane_ref, depth_ref,
+    cells_ref, image_ref, shift_ref, beyond_ref, across_ref, inside_ref, field, plane_ref, depth_ref,
     diag_depth_ref, diag_plane_ref,
     residual_ref, depth_out, plane_out,
     ahead_ref, here_ref, behind_ref, wide, bands, rims, blocks, energy, held,
@@ -214,7 +249,10 @@
         for k in range(planes):
             wide[k * rows : (k + 1) * rows, 0:width] = cells_ref[k]
             wide[k * rows : (k + 1) * rows, width:] = beyond_ref[k]
-        wide[span:, :] = jnp.concatenate([low_ref[...].astype(f32), high_ref[...].astype(f32)], axis=0).astype(bf16)
+        odd = lax.axis_index("gy") % 2 == 1
+        across, inside = across_ref[...].astype(f32), inside_ref[...].astype(f32)
+        low, high = jnp.where(odd, inside, across), jnp.where(odd, across, inside)
+        wide[span:, :] = jnp.concatenate([low, high], axis=0).astype(bf16)
 
         def put(c, tile, values):
             for k in range(planes):
@@ -332,7 +370,7 @@
         plane_out[count // 2 :, 3 * RANK :] = jnp.full((count // 2, RANK), local, f32)
 
 
-def warp(cells, image, shift, beyond, low, high, field, plane, depth_factors, diag_depth, diag_plane, parts):
+def warp(cells, image, shift, beyond, across, inside, field, plane, depth_factors, diag_depth, diag_plane, parts):
     depth, rows, width = cells.shape
     nodes = plane.shape[1]
     tiles = width // LANES
@@ -349,8 +387,8 @@
             pl.BlockSpec((KNOT, rows, width), behind),
             pl.BlockSpec((3, KNOT, rows, width), lambda i: (0, jnp.maximum(i - 1, 0), 0, 0)),
             pl.BlockSpec((KNOT, rows, LANES), ahead),
-            pl.BlockSpec((KNOT, low.shape[1]), lambda i: (jnp.minimum(i, count - 1), 0)),
-            pl.BlockSpec((KNOT, high.shape[1]), lambda i: (jnp.minimum(i, count - 1), 0)),
+            pl.BlockSpec((KNOT, across.shape[1]), lambda i: (jnp.minimum(i, count - 1), 0)),
+            pl.BlockSpec((KNOT, inside.shape[1]), lambda i: (jnp.minimum(i, count - 1), 0)),
             pl.BlockSpec(field.shape, lambda i: (0, 0, 0, 0)),
             pl.BlockSpec(plane.shape, whole),
             pl.BlockSpec(depth_factors.shape, whole),
@@ -379,7 +417,7 @@
         compiler_params=grid_params(),
         cost_estimate=pl.CostEstimate(flops=60 * cells.size, bytes_accessed=12 * cells.size, transcendentals=0),
         name="warp",
-    )(cells, image, shift, beyond, low, high, field, plane, depth_factors, diag_depth, diag_plane)
+    )(cells, image, shift, beyond, across, inside, field, plane, depth_factors, diag_depth, diag_plane)
 
 
 def gather_kernel(depth_ref, plane_ref, other_ref, depth_out, plane_out):
@@ -419,16 +457,18 @@
     n_gy, n_gz = lax.axis_size("gy"), lax.axis_size("gz")
     nodes_x, nodes_y = plane_factors.shape[2:]
     plane = jnp.transpose(plane_factors, (0, 2, 3, 1)).reshape(2, nodes_x * nodes_y, RANK)
-    first, last, low, high = ends(deformed)
+    first, last = end_columns(deformed)
     right = shifted(first, "gz", True)
     left = shifted(last, "gz", False)
-    low, high = packed_rows(left, right, low, high)
-    above = shifted(low, "gy", True)
-    below = shifted(high, "gy", False)
-    sums = squares(image, low)
+    low, high = ends(deformed)
+    across, inside = packed_rows(left, right, low, high)
+    later = across
+    inside = swapped(inside, "gy", 0)
+    across = swapped(across, "gy", 1)
+    sums = squares(image, later)
     field, diag_depth, diag_plane, beyond = terms(sums, plane, depth_factors, left, right, deformed.shape[0])
     residual, depth_terms, plane_terms = warp(
-        deformed, image, displacement, beyond, below, above, field, plane, depth_factors, diag_depth, diag_plane,
+        deformed, image, displacement, beyond, across, inside, field, plane, depth_factors, diag_depth, diag_plane,
         n_gy,
     )
     depth_terms = lax.all_to_all(depth_terms, "gy", 0, 0)

time: 78.2 us -> 75.8 us (0.969)
  starting transfers between devices: 19.7 us -> 17.4 us
  Pallas kernels: 34.1 us -> 36.4 us
  waiting for transfers between devices: 10.2 us -> 8.93 us
  local copies, waits for them, and re-layouts: 2.21 us -> 1.13 us
    pallas_call x1 -> x2, Pallas kernels: 0.82 us -> 3.13 us  [the longest x1 2.93 us: end_columns(): pl.pallas_call(columns_kernel, grid=(1,), in_specs=[pl.BlockSpec(block, f...]
    ppermute x2 -> x1, starting transfers between devices: 6.49 us -> 4.92 us  [shifted(): return lax.ppermute(part, axis, [(i, i + 1) for i in range(count - 1)])]
    ppermute x2 -> x1, starting transfers between devices: 2.72 us -> 1.29 us  [shifted(): return lax.ppermute(part, axis, [(i + 1, i) for i in range(count - 1)])]
    ppermute x2 -> x1, waiting for transfers between devices: 5.41 us -> 4.21 us  [shifted(): return lax.ppermute(part, axis, [(i + 1, i) for i in range(count - 1)])]
    unnamed x10 -> x8, local copies, waits for them, and re-layouts: 2.21 us -> 1.13 us
    ppermute x0 -> x2, starting transfers between devices: none -> 0.87 us  [swapped(): return lax.ppermute(part, axis, pairs + [(j, i) for i, j in pairs])]
  transfers between devices with their start and end apart: 7 -> 7, of which waited for: 5 -> 4; matrix products, arithmetic and copies ran while one was open for 0% -> 0% of each run, Pallas kernels for 3% -> 3%
where the time goes in v17:
time: 75.8 us; the launch traced here: 75.5 us
  Pallas kernels  36.4 us (48%)
  starting transfers between devices  17.4 us (23%)
  blocking collectives  10.9 us (14%)
  waiting for transfers between devices  8.93 us (12%)
  local copies, waits for them, and re-layouts  1.13 us (1%)
  between operations  0.76 us (1%)
    pallas_call x1, Pallas kernels, warp(): pl.pallas_call(warp_kernel, grid=(count + 1,), in_specs=[pl.BlockSpec((KN...  30 us
    all_to_all x1, blocking collectives, local(): depth_terms = lax.all_to_all(depth_terms, 'gy', 0, 0)  10.9 us
    all_to_all x1, starting transfers between devices, local(): depth_terms = lax.all_to_all(depth_terms, 'gy', 0, 0)  6.09 us
    ppermute x1, starting transfers between devices, shifted(): return lax.ppermute(part, axis, [(i, i + 1) for i in range(count - 1)])  4.92 us
    ppermute x2, waiting for transfers between devices, local(): other = lax.ppermute(plane_terms, 'gz', [(i, i ^ hop) for i in range(n_gz)])  4.59 us
    ppermute x1, waiting for transfers between devices, shifted(): return lax.ppermute(part, axis, [(i + 1, i) for i in range(count - 1)])  4.21 us
    ppermute x2, starting transfers between devices, local(): other = lax.ppermute(plane_terms, 'gz', [(i, i ^ hop) for i in range(n_gz)])  4.19 us
    pallas_call x1, Pallas kernels, end_columns(): pl.pallas_call(columns_kernel, grid=(1,), in_specs=[pl.BlockSpec(block, f...  2.93 us
  transfers between devices with their start and end apart: 7, of which 4 were waited for; matrix products, arithmetic and copies ran while one was open for 0% of the time, Pallas kernels for 3%

profile of v17, /device:TPU:0, one launch (start us, length us, event | category | flops | bytes accessed | tf_op | source)
XLA Modules:
  0.0 75.5 jit_solution(13311395350677207338)
XLA Ops:
  0.6 0.0 copy-start
  0.6 2.9 %columns.1 = (bf16[64,128]{1,0:T(8,128)(2,1)}, bf16[64,128]{1,0:T(8,128)(2,1)}) custom-call(bf16[64,64,512]{2,1,0:T(8,128)(2,1)} %cells_ref.3, bf16[64,64,512]{2,1,0:T(8,128)(2,1)} %cells_ref.3, bf16[64,64,512]{2,1,0:T(8,128)(2,1)} %cells_ref.3, bf16[64,64,512]{2,1,0:T(8,128)(2,1)} %cells_ref.3, bf16[64,64,512]{2,1,0:T(8,128)(2,1)} %cells_ref.3, ...), custom_call_target="tpu_custom_call" | custom-call | tf_op jit(solution)/shard_map/columns/pallas_call | solution.py:70
  3.6 4.9 %collective-permute-start = (bf16[64,128]{1,0:T(8,128)(2,1)}, bf16[64,128]{1,0:T(8,128)(2,1)S(1)}, u32[]{:S(2)}, u32[]{:S(2)}) collective-permute-start(bf16[64,128]{1,0:T(8,128)(2,1)} %get-tuple-element.20), channel_id=1, source_target_pairs={{0,1},{1,2},{2,3},{4,5},{5,6},{6,7},{8,9},{9,10},{10,11},{12,13},{... | collective-permute-start | bytes 49160 | tf_op jit(solution)/shard_map/ppermute | solution.py:135
  8.5 1.3 %collective-permute-start.1 = (bf16[64,128]{1,0:T(8,128)(2,1)}, bf16[64,128]{1,0:T(8,128)(2,1)S(1)}, u32[]{:S(2)}, u32[]{:S(2)}) collective-permute-start(bf16[64,128]{1,0:T(8,128)(2,1)} %get-tuple-element.21), channel_id=1, source_target_pairs={{1,0},{2,1},{3,2},{5,4},{6,5},{7,6},{9,8},{10,9},{11,10},{13,12},{... | collective-permute-start | bytes 49160 | tf_op jit(solution)/shard_map/ppermute | solution.py:134
  9.8 0.0 copy-done
  9.8 0.2 ends.1
  10.0 0.1 collective-permute-done.left_ref
  10.1 4.2 %collective-permute-done.1.right_ref = bf16[64,128]{1,0:T(8,128)(2,1)S(1)} collective-permute-done((bf16[64,128]{1,0:T(8,128)(2,1)}, bf16[64,128]{1,0:T(8,128)(2,1)S(1)}, u32[]{:S(2)}, u32[]{:S(2)}) %collective-permute-start.1) | collective-permute-done | bytes 16416 | tf_op jit(solution)/shard_map/ppermute | solution.py:134
  14.3 0.0 copy-start.1
  14.3 0.2 rows.1
  14.5 0.0 copy-start.2
  14.5 0.0 copy-start.3
  14.5 0.1 collective-permute-start.3
  14.6 0.8 %collective-permute-start.2 = (bf16[64,640]{1,0:T(8,128)(2,1)S(1)}, bf16[64,640]{1,0:T(8,128)(2,1)S(1)}, u32[]{:S(2)}, u32[]{:S(2)}) collective-permute-start(bf16[64,640]{1,0:T(8,128)(2,1)S(1)} %get-tuple-element.24.later_ref), channel_id=1, source_target_pairs={{4,8},{12,16},{20,24},{8,4},{16,12},{24,20},{5,9},{13,17},{21,25},... | collective-permute-start | bytes 245768 | tf_op jit(solution)/shard_map/ppermute | solution.py:141
  15.4 1.1 %copy-done.1 = bf16[64,64,512]{2,1,0:T(8,128)(2,1)S(1)} copy-done((bf16[64,64,512]{2,1,0:T(8,128)(2,1)S(1)}, bf16[64,64,512]{2,1,0:T(8,128)(2,1)}, u32[]{:S(2)}) %copy-start.1) | copy-done | bytes 4194328
  16.5 1.5 %squares.1.sums = f32[4,64,128]{2,1,0:T(8,128)S(1)} custom-call(bf16[64,64,512]{2,1,0:T(8,128)(2,1)S(1)} %copy-done.1, bf16[64,640]{1,0:T(8,128)(2,1)S(1)} %get-tuple-element.24.later_ref), custom_call_target="tpu_custom_call" | custom-call | flops 6291456 | bytes 4194304 | tf_op jit(solution)/shard_map/squares/pallas_call | solution.py:166
  18.0 0.0 copy-done.2
  18.0 0.0 copy-done.3
  18.1 0.7 terms.1
  18.8 0.0 collective-permute-done.3.inside_ref
  18.8 0.0 collective-permute-done.2.across_ref
  18.8 30.0 %warp.1 = (bf16[64,64,512]{2,1,0:T(8,128)(2,1)}, f32[8,16,512]{2,1,0:T(8,128)}, f32[64,128]{1,0:T(8,128)S(1)}) custom-call(bf16[64,64,512]{2,1,0:T(8,128)(2,1)S(1)} %copy-done, bf16[64,64,512]{2,1,0:T(8,128)(2,1)S(1)} %copy-done.1, bf16[3,64,64,512]{3,2,1,0:T(8,128)(2,1)} %shift_ref.1, bf16[64,64,128]{2,1,0:T(8,128)(2,1)S(1)} %get-tuple-element.25.beyond_ref, ...), custom_call_target="tpu_custom_call" | custom-call | flops 125829120 | bytes 25165824 | tf_op jit(solution)/shard_map/warp/pallas_call | solution.py:382
  48.7 6.1 %all-to-all-start = ((f32[8,16,512]{2,1,0:T(8,128)}), f32[8,16,512]{2,1,0:T(8,128)S(1)}, u32[]{:S(2)}, u32[]{:S(2)}) async-start(f32[8,16,512]{2,1,0:T(8,128)} %get-tuple-element.31), calls=%async_computation | async-start | bytes 524288 | tf_op jit(solution)/shard_map/all_to_all | solution.py:474
  54.8 1.6 %collective-permute-start.4 = (f32[64,128]{1,0:T(8,128)S(1)}, f32[64,128]{1,0:T(8,128)S(1)}, u32[]{:S(2)}, u32[]{:S(2)}) collective-permute-start(f32[64,128]{1,0:T(8,128)S(1)} %get-tuple-element.32), channel_id=1, source_target_pairs={{0,1},{1,0},{2,3},{3,2},{4,5},{5,4},{6,7},{7,6},{8,9},{9,8},{10,11... | collective-permute-start | bytes 98312 | tf_op jit(solution)/shard_map/ppermute | solution.py:477
  56.4 2.3 %collective-permute-done.4 = f32[64,128]{1,0:T(8,128)S(1)} collective-permute-done((f32[64,128]{1,0:T(8,128)S(1)}, f32[64,128]{1,0:T(8,128)S(1)}, u32[]{:S(2)}, u32[]{:S(2)}) %collective-permute-start.4) | collective-permute-done | bytes 32800 | tf_op jit(solution)/shard_map/ppermute | solution.py:477
  58.7 2.6 %collective-permute-start.5 = (f32[64,128]{1,0:T(8,128)S(1)}, f32[64,128]{1,0:T(8,128)S(1)}, u32[]{:S(2)}, u32[]{:S(2)}) collective-permute-start(f32[64,128]{1,0:T(8,128)S(1)} %add.3.plane_ref), channel_id=1, source_target_pairs={{0,2},{1,3},{2,0},{3,1},{4,6},{5,7},{6,4},{7,5},{8,10},{9,11},{10,... | collective-permute-start | bytes 98312 | tf_op jit(solution)/shard_map/ppermute | solution.py:477
  61.3 2.3 %collective-permute-done.5.other_ref = f32[64,128]{1,0:T(8,128)S(1)} collective-permute-done((f32[64,128]{1,0:T(8,128)S(1)}, f32[64,128]{1,0:T(8,128)S(1)}, u32[]{:S(2)}, u32[]{:S(2)}) %collective-permute-start.5) | collective-permute-done | bytes 32800 | tf_op jit(solution)/shard_map/ppermute | solution.py:477
  63.6 0.0 all-to-all-done.depth_ref
  63.6 0.1 gather.1
  63.7 10.9 %all_to_all.10.depth_ref = f32[8,16,512]{2,1,0:T(8,128)S(1)} all-to-all(f32[8,16,512]{2,1,0:T(8,128)S(1)} %get-tuple-element.33), channel_id=1, replica_groups=mesh['gy'=8,'gz'=4] {'gy'}, dimensions={0} | all-to-all | bytes 524288 | tf_op jit(solution)/shard_map/all_to_all | solution.py:490
  74.6 0.9 %steps.1 = (f32[2,32,512]{2,1,0:T(8,128)}, f32[2,64,32]{2,1,0:T(8,128)}) custom-call(f32[8,16,512]{2,1,0:T(8,128)S(1)} %all_to_all.10.depth_ref, f32[64,128]{1,0:T(8,128)S(1)} %get-tuple-element.34.plane_ref), custom_call_target="tpu_custom_call" | custom-call | tf_op jit(solution)/shard_map/steps/pallas_call | solution.py:492
  (1 shorter events, 0.0 us)
Async XLA Ops:
  0.6 9.2 %copy-start = (bf16[64,64,512]{2,1,0:T(8,128)(2,1)S(1)}, bf16[64,64,512]{2,1,0:T(8,128)(2,1)}, u32[]{:S(2)}) copy-start(bf16[64,64,512]{2,1,0:T(8,128)(2,1)} %cells_ref.3) | copy-start | bytes 12582916
  3.6 6.6 %collective-permute-start = (bf16[64,128]{1,0:T(8,128)(2,1)}, bf16[64,128]{1,0:T(8,128)(2,1)S(1)}, u32[]{:S(2)}, u32[]{:S(2)}) collective-permute-start(bf16[64,128]{1,0:T(8,128)(2,1)} %get-tuple-element.20), channel_id=1, source_target_pairs={{0,1},{1,2},{2,3},{4,5},{5,6},{6,7},{8,9},{9,10},{10,11},{12,13},{... | collective-permute-start | bytes 49160 | tf_op jit(solution)/shard_map/ppermute | solution.py:135
  8.5 5.8 %collective-permute-start.1 = (bf16[64,128]{1,0:T(8,128)(2,1)}, bf16[64,128]{1,0:T(8,128)(2,1)S(1)}, u32[]{:S(2)}, u32[]{:S(2)}) collective-permute-start(bf16[64,128]{1,0:T(8,128)(2,1)} %get-tuple-element.21), channel_id=1, source_target_pairs={{1,0},{2,1},{3,2},{5,4},{6,5},{7,6},{9,8},{10,9},{11,10},{13,12},{... | collective-permute-start | bytes 49160 | tf_op jit(solution)/shard_map/ppermute | solution.py:134
  14.3 2.2 %copy-start.1 = (bf16[64,64,512]{2,1,0:T(8,128)(2,1)S(1)}, bf16[64,64,512]{2,1,0:T(8,128)(2,1)}, u32[]{:S(2)}) copy-start(bf16[64,64,512]{2,1,0:T(8,128)(2,1)} %image_ref.3) | copy-start | bytes 12582916
  14.5 3.5 %copy-start.2 = (f32[2,32,512]{2,1,0:T(8,128)S(1)}, f32[2,32,512]{2,1,0:T(8,128)}, u32[]{:S(2)}) copy-start(f32[2,32,512]{2,1,0:T(8,128)} %depth_ref.3) | copy-start | bytes 393220
  14.5 3.5 %copy-start.3 = (f32[2,32,8,8]{1,3,2,0:T(8,128)S(1)}, f32[2,32,8,8]{1,3,2,0:T(8,128)}, u32[]{:S(2)}) copy-start(f32[2,32,8,8]{1,3,2,0:T(8,128)} %param.8) | copy-start | bytes 49156
  14.5 4.2 %collective-permute-start.3 = (bf16[64,640]{1,0:T(8,128)(2,1)S(1)}, bf16[64,640]{1,0:T(8,128)(2,1)S(1)}, u32[]{:S(2)}, u32[]{:S(2)}) collective-permute-start(bf16[64,640]{1,0:T(8,128)(2,1)S(1)} %get-tuple-element.26), channel_id=1, source_target_pairs={{0,4},{8,12},{16,20},{24,28},{4,0},{12,8},{20,16},{28,24},{1,5},{9... | collective-permute-start | bytes 245768 | tf_op jit(solution)/shard_map/ppermute | solution.py:141
  14.6 4.2 %collective-permute-start.2 = (bf16[64,640]{1,0:T(8,128)(2,1)S(1)}, bf16[64,640]{1,0:T(8,128)(2,1)S(1)}, u32[]{:S(2)}, u32[]{:S(2)}) collective-permute-start(bf16[64,640]{1,0:T(8,128)(2,1)S(1)} %get-tuple-element.24.later_ref), channel_id=1, source_target_pairs={{4,8},{12,16},{20,24},{8,4},{16,12},{24,20},{5,9},{13,17},{21,25},... | collective-permute-start | bytes 245768 | tf_op jit(solution)/shard_map/ppermute | solution.py:141
  48.7 14.9 %all-to-all-start = ((f32[8,16,512]{2,1,0:T(8,128)}), f32[8,16,512]{2,1,0:T(8,128)S(1)}, u32[]{:S(2)}, u32[]{:S(2)}) async-start(f32[8,16,512]{2,1,0:T(8,128)} %get-tuple-element.31), calls=%async_computation | async-start | bytes 524288 | tf_op jit(solution)/shard_map/all_to_all | solution.py:474
  54.8 3.9 %collective-permute-start.4 = (f32[64,128]{1,0:T(8,128)S(1)}, f32[64,128]{1,0:T(8,128)S(1)}, u32[]{:S(2)}, u32[]{:S(2)}) collective-permute-start(f32[64,128]{1,0:T(8,128)S(1)} %get-tuple-element.32), channel_id=1, source_target_pairs={{0,1},{1,0},{2,3},{3,2},{4,5},{5,4},{6,7},{7,6},{8,9},{9,8},{10,11... | collective-permute-start | bytes 98312 | tf_op jit(solution)/shard_map/ppermute | solution.py:477
  58.7 4.9 %collective-permute-start.5 = (f32[64,128]{1,0:T(8,128)S(1)}, f32[64,128]{1,0:T(8,128)S(1)}, u32[]{:S(2)}, u32[]{:S(2)}) collective-permute-start(f32[64,128]{1,0:T(8,128)S(1)} %add.3.plane_ref), channel_id=1, source_target_pairs={{0,2},{1,3},{2,0},{3,1},{4,6},{5,7},{6,4},{7,5},{8,10},{9,11},{10,... | collective-permute-start | bytes 98312 | tf_op jit(solution)/shard_map/ppermute | solution.py:477

commit v18 on v17

--- a/solution.py
+++ b/solution.py
@@ -45,9 +45,9 @@
 
 
 def columns_kernel(*refs):
-    first_ref, last_ref = refs[-2:]
+    inner_ref, outer_ref = refs[-2:]
     chunks = (len(refs) - 2) // 2
-    rows = first_ref.shape[0]
+    rows = inner_ref.shape[0]
     lane = lax.broadcasted_iota(jnp.int32, (rows, LANES), 1)
     first = jnp.zeros((rows, LANES), f32)
     last = jnp.zeros((rows, LANES), f32)
@@ -57,8 +57,9 @@
             x = chunk * near.shape[0] + k
             first = jnp.where(lane == x, pltpu.roll(near[k].astype(f32), x, 1), first)
             last = jnp.where(lane == x, pltpu.roll(far[k].astype(f32), (x + 1) % LANES, 1), last)
-    first_ref[...] = first.astype(bf16)
-    last_ref[...] = last.astype(bf16)
+    odd = lax.axis_index("gz") % 2 == 1
+    inner_ref[...] = jnp.where(odd, first, last).astype(bf16)
+    outer_ref[...] = jnp.where(odd, last, first).astype(bf16)
 
 
 def end_columns(cells):
@@ -98,14 +99,21 @@
     )(cells)
 
 
-def rows_kernel(left_ref, right_ref, low_ref, high_ref, across_out, inside_out):
+def z_sides(inner_ref, outer_ref):
+    odd = lax.axis_index("gz") % 2 == 1
+    inner, outer = inner_ref[...].astype(f32), outer_ref[...].astype(f32)
+    return jnp.where(odd, inner, outer), jnp.where(odd, outer, inner)
+
+
+def rows_kernel(inner_ref, outer_ref, low_ref, high_ref, across_out, inside_out):
     depth, width = low_ref.shape
-    rows = left_ref.shape[0]
+    rows = inner_ref.shape[0]
     odd = lax.axis_index("gy") % 2 == 1
     lane = lax.broadcasted_iota(jnp.int32, (depth, LANES), 1)
     pad = jnp.zeros((LANES - rows, LANES), f32)
-    left = jnp.transpose(jnp.concatenate([left_ref[...].astype(f32), pad], axis=0))[0:depth]
-    right = jnp.transpose(jnp.concatenate([right_ref[...].astype(f32), pad], axis=0))[0:depth]
+    left, right = z_sides(inner_ref, outer_ref)
+    left = jnp.transpose(jnp.concatenate([left, pad], axis=0))[0:depth]
+    right = jnp.transpose(jnp.concatenate([right, pad], axis=0))[0:depth]
     bodies, beyond = [], []
     for row, body in ((0, low_ref), (rows - 1, high_ref)):
         after = pltpu.roll(right, (LANES - row) % LANES, 1)
@@ -117,7 +125,7 @@
         out[:, width : width + LANES] = jnp.where(odd, beyond[first], beyond[second]).astype(bf16)
 
 
-def packed_rows(left, right, low, high):
+def packed_rows(inner, outer, low, high):
     depth, width = low.shape
     return pl.pallas_call(
         rows_kernel,
@@ -125,14 +133,7 @@
         compiler_params=plain_params(),
         cost_estimate=pl.CostEstimate(flops=500000 * low.size, bytes_accessed=8 * low.size, transcendentals=0),
         name="rows",
-    )(left, right, low, high)
-
-
-def shifted(part, axis, back):
-    count = lax.axis_size(axis)
-    if back:
-        return lax.ppermute(part, axis, [(i + 1, i) for i in range(count - 1)])
-    return lax.ppermute(part, axis, [(i, i + 1) for i in range(count - 1)])
+    )(inner, outer, low, high)
 
 
 def swapped(part, axis, start):
@@ -173,10 +174,10 @@
 
 
 def terms_kernel(
-    sums, plane_ref, depth_ref, left_ref, right_ref, field_ref, diag_depth_ref, diag_plane_ref, beyond_ref
+    sums, plane_ref, depth_ref, inner_ref, outer_ref, field_ref, diag_depth_ref, diag_plane_ref, beyond_ref
 ):
     tiles = sums.shape[0]
-    left, right = left_ref[...].astype(f32), right_ref[...].astype(f32)
+    left, right = z_sides(inner_ref, outer_ref)
     lane = lax.broadcasted_iota(jnp.int32, left.shape, 1)
     for x in range(beyond_ref.shape[0]):
         after = pltpu.roll(right, (LANES - x) % LANES, 1)
@@ -196,7 +197,7 @@
     diag_plane_ref[1] = dot(cells, second * second, ((1,), (1,)))
 
 
-def terms(sums, plane, depth_factors, left, right, depth):
+def terms(sums, plane, depth_factors, inner, outer, depth):
     nodes, width = plane.shape[1], depth_factors.shape[2]
     return pl.pallas_call(
         terms_kernel,
@@ -204,12 +205,12 @@
             jax.ShapeDtypeStruct((2, width // LANES, nodes, LANES), f32),
             jax.ShapeDtypeStruct((2, RANK, width), f32),
             jax.ShapeDtypeStruct((2, nodes, RANK), f32),
-            jax.ShapeDtypeStruct((depth,) + left.shape, bf16),
+            jax.ShapeDtypeStruct((depth,) + inner.shape, bf16),
         ],
         compiler_params=plain_params(),
         cost_estimate=pl.CostEstimate(flops=40 * nodes * RANK * width, bytes_accessed=1 << 20, transcendentals=0),
         name="terms",
-    )(sums, plane, depth_factors, left, right)
+    )(sums, plane, depth_factors, inner, outer)
 
 
 def warp_kernel(
@@ -422,19 +423,19 @@
 
 def gather_kernel(depth_ref, plane_ref, other_ref, depth_out, plane_out):
     total = jnp.sum(depth_ref[...], axis=0)
-    planes = plane_ref[...] + other_ref[...]
+    planes = plane_ref[...]
     plane_out[...] = planes
     cells = planes.shape[0]
     share, width = total.shape[0] // 4, total.shape[1]
     row = lax.broadcasted_iota(jnp.int32, total.shape, 0)
     lane = lax.broadcasted_iota(jnp.int32, total.shape, 1)
-    partial = planes[cells - 1, 4 * RANK - 1]
+    partial = planes[cells - 1, 4 * RANK - 1] + other_ref[other_ref.shape[0] - 1, 4 * RANK - 1]
     total = jnp.where((row >= 3 * share) & (lane >= width // 2), partial, total)
     for p in range(depth_out.shape[0]):
         depth_out[p] = total
 
 
-def step_kernel(full_z, node_count, depth_ref, plane_ref, depth_out, plane_out):
+def step_kernel(full_z, node_count, depth_ref, plane_ref, other_ref, depth_out, plane_out):
     parts, share, width = depth_ref.shape[0], depth_ref.shape[1] // 4, depth_ref.shape[2]
     energy = depth_ref[0, 3 * share, width - 1]
     for p in range(1, parts):
@@ -448,7 +449,7 @@
         rows = slice(p * share, (p + 1) * share)
         depth_out[0, rows, :] = got[0:share] / (got[2 * share : 3 * share] + lam_depth + epsilon)
         depth_out[1, rows, :] = got[share : 2 * share] / (levels + lam_depth + epsilon)
-    planes = plane_ref[...]
+    planes = plane_ref[...] + other_ref[...]
     plane_out[0] = planes[:, 0:RANK] / (planes[:, 2 * RANK : 3 * RANK] + lam_plane + epsilon)
     plane_out[1] = planes[:, RANK : 2 * RANK] / (planes[0:1, 3 * RANK :] + lam_plane + epsilon)
 
@@ -457,27 +458,27 @@
     n_gy, n_gz = lax.axis_size("gy"), lax.axis_size("gz")
     nodes_x, nodes_y = plane_factors.shape[2:]
     plane = jnp.transpose(plane_factors, (0, 2, 3, 1)).reshape(2, nodes_x * nodes_y, RANK)
-    first, last = end_columns(deformed)
-    right = shifted(first, "gz", True)
-    left = shifted(last, "gz", False)
+    inner, outer = end_columns(deformed)
+    inner = swapped(inner, "gz", 0)
+    outer = swapped(outer, "gz", 1)
     low, high = ends(deformed)
-    across, inside = packed_rows(left, right, low, high)
+    across, inside = packed_rows(inner, outer, low, high)
     later = across
     inside = swapped(inside, "gy", 0)
     across = swapped(across, "gy", 1)
     sums = squares(image, later)
-    field, diag_depth, diag_plane, beyond = terms(sums, plane, depth_factors, left, right, deformed.shape[0])
+    field, diag_depth, diag_plane, beyond = terms(sums, plane, depth_factors, inner, outer, deformed.shape[0])
     residual, depth_terms, plane_terms = warp(
         deformed, image, displacement, beyond, across, inside, field, plane, depth_factors, diag_depth, diag_plane,
         n_gy,
     )
     depth_terms = lax.all_to_all(depth_terms, "gy", 0, 0)
     hop = 1
-    while hop < n_gz:
-        other = lax.ppermute(plane_terms, "gz", [(i, i ^ hop) for i in range(n_gz)])
-        if 2 * hop < n_gz:
-            plane_terms = plane_terms + other
+    while 2 * hop < n_gz:
+        plane_terms = plane_terms + lax.ppermute(plane_terms, "gz", [(i, i ^ hop) for i in range(n_gz)])
         hop = 2 * hop
+    pairs = [(i, i ^ hop) for i in range(n_gz)]
+    energy = lax.ppermute(plane_terms[-8:], "gz", pairs)
     depth_terms, plane_terms = pl.pallas_call(
         gather_kernel,
         out_shape=[
@@ -486,8 +487,9 @@
         ],
         compiler_params=plain_params(),
         name="gather",
-    )(depth_terms, plane_terms, other)
+    )(depth_terms, plane_terms, energy)
     depth_terms = lax.all_to_all(depth_terms, "gy", 0, 0)
+    other = lax.ppermute(plane_terms, "gz", pairs)
     width = depth_factors.shape[2]
     step_depth, step_plane = pl.pallas_call(
         functools.partial(step_kernel, width * n_gz, nodes_x * nodes_y * n_gy),
@@ -497,7 +499,7 @@
         ],
         compiler_params=plain_params(),
         name="steps",
-    )(depth_terms, plane_terms)
+    )(depth_terms, plane_terms, other)
     step_plane = jnp.transpose(step_plane.reshape(2, nodes_x, nodes_y, RANK), (0, 3, 1, 2))
     return residual, step_plane, step_depth
 

time: 75.8 us -> 74.3 us (0.980)
  blocking collectives: 10.9 us -> 0 us
  starting transfers between devices: 17.4 us -> 26.2 us
    all_to_all x1 -> x0, blocking collectives: 10.9 us -> none  [local(): depth_terms = lax.all_to_all(depth_terms, 'gy', 0, 0)]
    all_to_all x1 -> x2, starting transfers between devices: 6.09 us -> 10.7 us  [local(): depth_terms = lax.all_to_all(depth_terms, 'gy', 0, 0)]
    ppermute x2 -> x4, starting transfers between devices: 0.87 us -> 4.54 us  [swapped(): return lax.ppermute(part, axis, pairs + [(j, i) for i, j in pairs])]
    ppermute x4 -> x3, waiting for transfers between devices: 8.92 us -> 5.71 us  [the longest x1 2.07 us: local(): other = lax.ppermute(plane_terms, 'gz', pairs)]
    all_to_all x1 -> x2, waiting for transfers between devices: 0.01 us -> 1.95 us  [local(): depth_terms = lax.all_to_all(depth_terms, 'gy', 0, 0)]
    ppermute x2 -> x4, waiting for transfers between devices: 0.01 us -> 1.06 us  [swapped(): return lax.ppermute(part, axis, pairs + [(j, i) for i, j in pairs])]
    ppermute x4 -> x3, starting transfers between devices: 10.4 us -> 10.9 us  [the longest x1 4.58 us: local(): lax.ppermute(plane_terms, 'gz', [(i, i ^ hop) for i in range(n_gz)])]
  transfers between devices with their start and end apart: 7 -> 9, of which waited for: 4 -> 5; matrix products, arithmetic and copies ran while one was open for 0% -> 0% of each run, Pallas kernels for 3% -> 3%
where the time goes in v18:
time: 74.3 us; the launch traced here: 73.9 us
  Pallas kernels  37.1 us (50%)
  starting transfers between devices  26.2 us (35%)
  waiting for transfers between devices  8.73 us (12%)
  local copies, waits for them, and re-layouts  1.13 us (2%)
  between operations  0.75 us (1%)
    pallas_call x1, Pallas kernels, warp(): pl.pallas_call(warp_kernel, grid=(count + 1,), in_specs=[pl.BlockSpec((KN...  30 us
    all_to_all x2, starting transfers between devices, local(): depth_terms = lax.all_to_all(depth_terms, 'gy', 0, 0)  10.7 us
    ppermute x1, starting transfers between devices, local(): lax.ppermute(plane_terms, 'gz', [(i, i ^ hop) for i in range(n_gz)])  4.58 us
    ppermute x4, starting transfers between devices, swapped(): return lax.ppermute(part, axis, pairs + [(j, i) for i, j in pairs])  4.54 us
    ppermute x1, starting transfers between devices, local(): energy = lax.ppermute(plane_terms[-8:], 'gz', pairs)  3.37 us
    pallas_call x1, Pallas kernels, end_columns(): pl.pallas_call(columns_kernel, grid=(1,), in_specs=[pl.BlockSpec(block, f...  2.94 us
    ppermute x1, starting transfers between devices, local(): other = lax.ppermute(plane_terms, 'gz', pairs)  2.92 us
    ppermute x1, waiting for transfers between devices, local(): other = lax.ppermute(plane_terms, 'gz', pairs)  2.07 us
  transfers between devices with their start and end apart: 9, of which 5 were waited for; matrix products, arithmetic and copies ran while one was open for 0% of the time, Pallas kernels for 3%

profile of v18, /device:TPU:0, one launch (start us, length us, event | category | flops | bytes accessed | tf_op | source)
XLA Modules:
  0.0 73.9 jit_solution(5507393130715799316)
XLA Ops:
  0.6 0.0 copy-start
  0.6 2.9 %columns.1 = (bf16[64,128]{1,0:T(8,128)(2,1)}, bf16[64,128]{1,0:T(8,128)(2,1)}) custom-call(bf16[64,64,512]{2,1,0:T(8,128)(2,1)} %cells_ref.3, bf16[64,64,512]{2,1,0:T(8,128)(2,1)} %cells_ref.3, bf16[64,64,512]{2,1,0:T(8,128)(2,1)} %cells_ref.3, bf16[64,64,512]{2,1,0:T(8,128)(2,1)} %cells_ref.3, bf16[64,64,512]{2,1,0:T(8,128)(2,1)} %cells_ref.3, ...), custom_call_target="tpu_custom_call" | custom-call | tf_op jit(solution)/shard_map/columns/pallas_call | solution.py:71
  3.6 3.0 %collective-permute-start = (bf16[64,128]{1,0:T(8,128)(2,1)}, bf16[64,128]{1,0:T(8,128)(2,1)S(1)}, u32[]{:S(2)}, u32[]{:S(2)}) collective-permute-start(bf16[64,128]{1,0:T(8,128)(2,1)} %get-tuple-element.20), channel_id=1, source_target_pairs={{0,1},{2,3},{1,0},{3,2},{4,5},{6,7},{5,4},{7,6},{8,9},{10,11},{9,8... | collective-permute-start | bytes 49160 | tf_op jit(solution)/shard_map/ppermute | solution.py:142
  6.6 0.7 collective-permute-start.1
  7.3 0.0 copy-done
  7.3 0.2 ends.1
  7.5 1.1 %collective-permute-done.inner_ref = bf16[64,128]{1,0:T(8,128)(2,1)S(1)} collective-permute-done((bf16[64,128]{1,0:T(8,128)(2,1)}, bf16[64,128]{1,0:T(8,128)(2,1)S(1)}, u32[]{:S(2)}, u32[]{:S(2)}) %collective-permute-start) | collective-permute-done | bytes 16416 | tf_op jit(solution)/shard_map/ppermute | solution.py:142
  8.5 0.0 collective-permute-done.1.outer_ref
  8.5 0.0 copy-start.1
  8.5 0.2 rows.1
  8.7 0.0 copy-start.2
  8.7 0.0 copy-start.3
  8.7 0.1 collective-permute-start.3
  8.8 0.8 %collective-permute-start.2 = (bf16[64,640]{1,0:T(8,128)(2,1)S(1)}, bf16[64,640]{1,0:T(8,128)(2,1)S(1)}, u32[]{:S(2)}, u32[]{:S(2)}) collective-permute-start(bf16[64,640]{1,0:T(8,128)(2,1)S(1)} %get-tuple-element.24.later_ref), channel_id=1, source_target_pairs={{4,8},{12,16},{20,24},{8,4},{16,12},{24,20},{5,9},{13,17},{21,25},... | collective-permute-start | bytes 245768 | tf_op jit(solution)/shard_map/ppermute | solution.py:142
  9.6 1.1 %copy-done.1 = bf16[64,64,512]{2,1,0:T(8,128)(2,1)S(1)} copy-done((bf16[64,64,512]{2,1,0:T(8,128)(2,1)S(1)}, bf16[64,64,512]{2,1,0:T(8,128)(2,1)}, u32[]{:S(2)}) %copy-start.1) | copy-done | bytes 4194328
  10.7 1.5 %squares.1.sums = f32[4,64,128]{2,1,0:T(8,128)S(1)} custom-call(bf16[64,64,512]{2,1,0:T(8,128)(2,1)S(1)} %copy-done.1, bf16[64,640]{1,0:T(8,128)(2,1)S(1)} %get-tuple-element.24.later_ref), custom_call_target="tpu_custom_call" | custom-call | flops 6291456 | bytes 4194304 | tf_op jit(solution)/shard_map/squares/pallas_call | solution.py:167
  12.2 0.0 copy-done.2
  12.2 0.0 copy-done.3
  12.3 0.7 terms.1
  12.9 0.0 collective-permute-done.3.inside_ref
  13.0 0.0 collective-permute-done.2.across_ref
  13.0 30.0 %warp.1 = (bf16[64,64,512]{2,1,0:T(8,128)(2,1)}, f32[8,16,512]{2,1,0:T(8,128)}, f32[64,128]{1,0:T(8,128)S(1)}) custom-call(bf16[64,64,512]{2,1,0:T(8,128)(2,1)S(1)} %copy-done, bf16[64,64,512]{2,1,0:T(8,128)(2,1)S(1)} %copy-done.1, bf16[3,64,64,512]{3,2,1,0:T(8,128)(2,1)} %shift_ref.1, bf16[64,64,128]{2,1,0:T(8,128)(2,1)S(1)} %get-tuple-element.25.beyond_ref, ...), custom_call_target="tpu_custom_call" | custom-call | flops 125829120 | bytes 25165824 | tf_op jit(solution)/shard_map/warp/pallas_call | solution.py:383
  42.9 6.5 %all-to-all-start = ((f32[8,16,512]{2,1,0:T(8,128)}), f32[8,16,512]{2,1,0:T(8,128)S(1)}, u32[]{:S(2)}, u32[]{:S(2)}) async-start(f32[8,16,512]{2,1,0:T(8,128)} %get-tuple-element.31), calls=%async_computation | async-start | bytes 524288 | tf_op jit(solution)/shard_map/all_to_all | solution.py:475
  49.5 4.6 %collective-permute-start.4 = (f32[64,128]{1,0:T(8,128)S(1)}, f32[64,128]{1,0:T(8,128)S(1)}, u32[]{:S(2)}, u32[]{:S(2)}) collective-permute-start(f32[64,128]{1,0:T(8,128)S(1)} %get-tuple-element.32), channel_id=1, source_target_pairs={{0,1},{1,0},{2,3},{3,2},{4,5},{5,4},{6,7},{7,6},{8,9},{9,8},{10,11... | collective-permute-start | bytes 98312 | tf_op jit(solution)/shard_map/ppermute | solution.py:478
  54.0 2.1 %collective-permute-done.4 = f32[64,128]{1,0:T(8,128)S(1)} collective-permute-done((f32[64,128]{1,0:T(8,128)S(1)}, f32[64,128]{1,0:T(8,128)S(1)}, u32[]{:S(2)}, u32[]{:S(2)}) %collective-permute-start.4) | collective-permute-done | bytes 32800 | tf_op jit(solution)/shard_map/ppermute | solution.py:478
  56.1 3.4 %collective-permute-start.5 = (f32[8,128]{1,0:T(8,128)S(1)}, f32[8,128]{1,0:T(8,128)S(1)}, u32[]{:S(2)}, u32[]{:S(2)}) collective-permute-start(f32[8,128]{1,0:T(8,128)S(1)} %slice.4), channel_id=1, source_target_pairs={{0,2},{1,3},{2,0},{3,1},{4,6},{5,7},{6,4},{7,5},{8,10},{9,11},{10,... | collective-permute-start | bytes 12296 | tf_op jit(solution)/shard_map/ppermute | solution.py:481
  59.5 1.6 %collective-permute-done.5.other_ref = f32[8,128]{1,0:T(8,128)S(1)} collective-permute-done((f32[8,128]{1,0:T(8,128)S(1)}, f32[8,128]{1,0:T(8,128)S(1)}, u32[]{:S(2)}, u32[]{:S(2)}) %collective-permute-start.5) | collective-permute-done | bytes 4128 | tf_op jit(solution)/shard_map/ppermute | solution.py:481
  61.1 0.0 all-to-all-done.depth_ref
  61.1 0.8 %gather.1 = (f32[8,16,512]{2,1,0:T(8,128)}, f32[64,128]{1,0:T(8,128)S(1)}) custom-call(f32[8,16,512]{2,1,0:T(8,128)S(1)} %all-to-all-done.depth_ref, f32[64,128]{1,0:T(8,128)S(1)} %add.3.plane_ref, f32[8,128]{1,0:T(8,128)S(1)} %collective-permute-done.5.other_ref), custom_call_target="tpu_custom_call" | custom-call | tf_op jit(solution)/shard_map/gather/pallas_call | solution.py:482
  61.9 4.2 %all-to-all-start.1 = ((f32[8,16,512]{2,1,0:T(8,128)}), f32[8,16,512]{2,1,0:T(8,128)S(1)}, u32[]{:S(2)}, u32[]{:S(2)}) async-start(f32[8,16,512]{2,1,0:T(8,128)} %get-tuple-element.33), calls=%async_computation.1 | async-start | bytes 524288 | tf_op jit(solution)/shard_map/all_to_all | solution.py:491
  66.1 2.9 %collective-permute-start.6 = (f32[64,128]{1,0:T(8,128)S(1)}, f32[64,128]{1,0:T(8,128)S(1)}, u32[]{:S(2)}, u32[]{:S(2)}) collective-permute-start(f32[64,128]{1,0:T(8,128)S(1)} %get-tuple-element.34.plane_ref), channel_id=1, source_target_pairs={{0,2},{1,3},{2,0},{3,1},{4,6},{5,7},{6,4},{7,5},{8,10},{9,11},{10,... | collective-permute-start | bytes 98312 | tf_op jit(solution)/shard_map/ppermute | solution.py:492
  69.0 2.1 %collective-permute-done.6.other_ref = f32[64,128]{1,0:T(8,128)S(1)} collective-permute-done((f32[64,128]{1,0:T(8,128)S(1)}, f32[64,128]{1,0:T(8,128)S(1)}, u32[]{:S(2)}, u32[]{:S(2)}) %collective-permute-start.6) | collective-permute-done | bytes 32800 | tf_op jit(solution)/shard_map/ppermute | solution.py:492
  71.1 1.9 %all-to-all-done.1.depth_ref = f32[8,16,512]{2,1,0:T(8,128)S(1)} async-done(((f32[8,16,512]{2,1,0:T(8,128)}), f32[8,16,512]{2,1,0:T(8,128)S(1)}, u32[]{:S(2)}, u32[]{:S(2)}) %all-to-all-start.1) | async-done | bytes 262176 | tf_op jit(solution)/shard_map/all_to_all | solution.py:491
  73.0 0.9 %steps.1 = (f32[2,32,512]{2,1,0:T(8,128)}, f32[2,64,32]{2,1,0:T(8,128)}) custom-call(f32[8,16,512]{2,1,0:T(8,128)S(1)} %all-to-all-done.1.depth_ref, f32[64,128]{1,0:T(8,128)S(1)} %get-tuple-element.34.plane_ref, f32[64,128]{1,0:T(8,128)S(1)} %collective-permute-done.6.other_ref), custom_call_target="tpu_custom_call" | custom-call | tf_op jit(solution)/shard_map/steps/pallas_call | solution.py:494
  (2 shorter events, 0.0 us)
Async XLA Ops:
  0.6 6.6 %copy-start = (bf16[64,64,512]{2,1,0:T(8,128)(2,1)S(1)}, bf16[64,64,512]{2,1,0:T(8,128)(2,1)}, u32[]{:S(2)}) copy-start(bf16[64,64,512]{2,1,0:T(8,128)(2,1)} %cells_ref.3) | copy-start | bytes 12582916
  3.6 5.0 %collective-permute-start = (bf16[64,128]{1,0:T(8,128)(2,1)}, bf16[64,128]{1,0:T(8,128)(2,1)S(1)}, u32[]{:S(2)}, u32[]{:S(2)}) collective-permute-start(bf16[64,128]{1,0:T(8,128)(2,1)} %get-tuple-element.20), channel_id=1, source_target_pairs={{0,1},{2,3},{1,0},{3,2},{4,5},{6,7},{5,4},{7,6},{8,9},{10,11},{9,8... | collective-permute-start | bytes 49160 | tf_op jit(solution)/shard_map/ppermute | solution.py:142
  6.6 1.9 %collective-permute-start.1 = (bf16[64,128]{1,0:T(8,128)(2,1)}, bf16[64,128]{1,0:T(8,128)(2,1)S(1)}, u32[]{:S(2)}, u32[]{:S(2)}) collective-permute-start(bf16[64,128]{1,0:T(8,128)(2,1)} %get-tuple-element.21), channel_id=1, source_target_pairs={{1,2},{2,1},{5,6},{6,5},{9,10},{10,9},{13,14},{14,13},{17,18},{18,... | collective-permute-start | bytes 49160 | tf_op jit(solution)/shard_map/ppermute | solution.py:142
  8.5 2.2 %copy-start.1 = (bf16[64,64,512]{2,1,0:T(8,128)(2,1)S(1)}, bf16[64,64,512]{2,1,0:T(8,128)(2,1)}, u32[]{:S(2)}) copy-start(bf16[64,64,512]{2,1,0:T(8,128)(2,1)} %image_ref.3) | copy-start | bytes 12582916
  8.7 3.5 %copy-start.2 = (f32[2,32,512]{2,1,0:T(8,128)S(1)}, f32[2,32,512]{2,1,0:T(8,128)}, u32[]{:S(2)}) copy-start(f32[2,32,512]{2,1,0:T(8,128)} %depth_ref.3) | copy-start | bytes 393220
  8.7 3.5 %copy-start.3 = (f32[2,32,8,8]{1,3,2,0:T(8,128)S(1)}, f32[2,32,8,8]{1,3,2,0:T(8,128)}, u32[]{:S(2)}) copy-start(f32[2,32,8,8]{1,3,2,0:T(8,128)} %param.8) | copy-start | bytes 49156
  8.7 4.2 %collective-permute-start.3 = (bf16[64,640]{1,0:T(8,128)(2,1)S(1)}, bf16[64,640]{1,0:T(8,128)(2,1)S(1)}, u32[]{:S(2)}, u32[]{:S(2)}) collective-permute-start(bf16[64,640]{1,0:T(8,128)(2,1)S(1)} %get-tuple-element.26), channel_id=1, source_target_pairs={{0,4},{8,12},{16,20},{24,28},{4,0},{12,8},{20,16},{28,24},{1,5},{9... | collective-permute-start | bytes 245768 | tf_op jit(solution)/shard_map/ppermute | solution.py:142
  8.8 4.1 %collective-permute-start.2 = (bf16[64,640]{1,0:T(8,128)(2,1)S(1)}, bf16[64,640]{1,0:T(8,128)(2,1)S(1)}, u32[]{:S(2)}, u32[]{:S(2)}) collective-permute-start(bf16[64,640]{1,0:T(8,128)(2,1)S(1)} %get-tuple-element.24.later_ref), channel_id=1, source_target_pairs={{4,8},{12,16},{20,24},{8,4},{16,12},{24,20},{5,9},{13,17},{21,25},... | collective-permute-start | bytes 245768 | tf_op jit(solution)/shard_map/ppermute | solution.py:142
  42.9 18.2 %all-to-all-start = ((f32[8,16,512]{2,1,0:T(8,128)}), f32[8,16,512]{2,1,0:T(8,128)S(1)}, u32[]{:S(2)}, u32[]{:S(2)}) async-start(f32[8,16,512]{2,1,0:T(8,128)} %get-tuple-element.31), calls=%async_computation | async-start | bytes 524288 | tf_op jit(solution)/shard_map/all_to_all | solution.py:475
  49.5 6.6 %collective-permute-start.4 = (f32[64,128]{1,0:T(8,128)S(1)}, f32[64,128]{1,0:T(8,128)S(1)}, u32[]{:S(2)}, u32[]{:S(2)}) collective-permute-start(f32[64,128]{1,0:T(8,128)S(1)} %get-tuple-element.32), channel_id=1, source_target_pairs={{0,1},{1,0},{2,3},{3,2},{4,5},{5,4},{6,7},{7,6},{8,9},{9,8},{10,11... | collective-permute-start | bytes 98312 | tf_op jit(solution)/shard_map/ppermute | solution.py:478
  56.1 5.0 %collective-permute-start.5 = (f32[8,128]{1,0:T(8,128)S(1)}, f32[8,128]{1,0:T(8,128)S(1)}, u32[]{:S(2)}, u32[]{:S(2)}) collective-permute-start(f32[8,128]{1,0:T(8,128)S(1)} %slice.4), channel_id=1, source_target_pairs={{0,2},{1,3},{2,0},{3,1},{4,6},{5,7},{6,4},{7,5},{8,10},{9,11},{10,... | collective-permute-start | bytes 12296 | tf_op jit(solution)/shard_map/ppermute | solution.py:481
  61.9 11.1 %all-to-all-start.1 = ((f32[8,16,512]{2,1,0:T(8,128)}), f32[8,16,512]{2,1,0:T(8,128)S(1)}, u32[]{:S(2)}, u32[]{:S(2)}) async-start(f32[8,16,512]{2,1,0:T(8,128)} %get-tuple-element.33), calls=%async_computation.1 | async-start | bytes 524288 | tf_op jit(solution)/shard_map/all_to_all | solution.py:491
  66.1 5.0 %collective-permute-start.6 = (f32[64,128]{1,0:T(8,128)S(1)}, f32[64,128]{1,0:T(8,128)S(1)}, u32[]{:S(2)}, u32[]{:S(2)}) collective-permute-start(f32[64,128]{1,0:T(8,128)S(1)} %get-tuple-element.34.plane_ref), channel_id=1, source_target_pairs={{0,2},{1,3},{2,0},{3,1},{4,6},{5,7},{6,4},{7,5},{8,10},{9,11},{10,... | collective-permute-start | bytes 98312 | tf_op jit(solution)/shard_map/ppermute | solution.py:492

commit v19 on v18

--- a/solution.py
+++ b/solution.py
@@ -79,24 +79,33 @@
     )(*[cells] * len(places))
 
 
-def ends_kernel(cells_ref, low_ref, high_ref):
-    depth, rows = cells_ref.shape[0:2]
-    for x in range(0, depth, 16):
-        low = [cells_ref[x + k, 0:16, :].astype(f32)[0:1] for k in range(16)]
-        high = [cells_ref[x + k, rows - 16 : rows, :].astype(f32)[15:16] for k in range(16)]
-        low_ref[x : x + 16, :] = jnp.concatenate(low, axis=0).astype(bf16)
-        high_ref[x : x + 16, :] = jnp.concatenate(high, axis=0).astype(bf16)
+def ends_kernel(*refs):
+    low_ref, high_ref = refs[-2:]
+    chunks = (len(refs) - 2) // 2
+    for chunk in range(chunks):
+        near, far = refs[chunk], refs[chunks + chunk]
+        planes = near.shape[0]
+        low = [near[k].astype(f32)[0:1] for k in range(planes)]
+        high = [far[k].astype(f32)[15:16] for k in range(planes)]
+        low_ref[chunk * planes : (chunk + 1) * planes, :] = jnp.concatenate(low, axis=0).astype(bf16)
+        high_ref[chunk * planes : (chunk + 1) * planes, :] = jnp.concatenate(high, axis=0).astype(bf16)
 
 
 def ends(cells):
     depth, rows, width = cells.shape
+    chunks = 4
+    block = (depth // chunks, 16, width)
+    places = [(chunk, row) for row in (0, rows // 16 - 1) for chunk in range(chunks)]
     return pl.pallas_call(
         ends_kernel,
+        grid=(1,),
+        in_specs=[pl.BlockSpec(block, functools.partial(lambda c, r, i: (c, r, 0), c, r)) for c, r in places],
+        out_specs=[pl.BlockSpec((depth, width), lambda i: (0, 0))] * 2,
         out_shape=[jax.ShapeDtypeStruct((depth, width), bf16)] * 2,
-        compiler_params=plain_params(),
+        compiler_params=pltpu.CompilerParams(vmem_limit_bytes=60000000),
         cost_estimate=pl.CostEstimate(flops=cells.size, bytes_accessed=2 * cells.size, transcendentals=0),
         name="ends",
-    )(cells)
+    )(*[cells] * len(places))
 
 
 def z_sides(inner_ref, outer_ref):
@@ -421,21 +430,26 @@
     )(cells, image, shift, beyond, across, inside, field, plane, depth_factors, diag_depth, diag_plane)
 
 
-def gather_kernel(depth_ref, plane_ref, other_ref, depth_out, plane_out):
+def gather_kernel(depth_ref, *refs):
+    depth_out, plane_out = refs[-2:]
     total = jnp.sum(depth_ref[...], axis=0)
-    planes = plane_ref[...]
+    found = [ref[...] for ref in refs[:-2]]
+    while len(found) > 1:
+        half = len(found) // 2
+        found = [found[k] + found[k + half] for k in range(half)]
+    planes = found[0]
     plane_out[...] = planes
     cells = planes.shape[0]
     share, width = total.shape[0] // 4, total.shape[1]
     row = lax.broadcasted_iota(jnp.int32, total.shape, 0)
     lane = lax.broadcasted_iota(jnp.int32, total.shape, 1)
-    partial = planes[cells - 1, 4 * RANK - 1] + other_ref[other_ref.shape[0] - 1, 4 * RANK - 1]
+    partial = planes[cells - 1, 4 * RANK - 1]
     total = jnp.where((row >= 3 * share) & (lane >= width // 2), partial, total)
     for p in range(depth_out.shape[0]):
         depth_out[p] = total
 
 
-def step_kernel(full_z, node_count, depth_ref, plane_ref, other_ref, depth_out, plane_out):
+def step_kernel(full_z, node_count, depth_ref, plane_ref, depth_out, plane_out):
     parts, share, width = depth_ref.shape[0], depth_ref.shape[1] // 4, depth_ref.shape[2]
     energy = depth_ref[0, 3 * share, width - 1]
     for p in range(1, parts):
@@ -449,7 +463,7 @@
         rows = slice(p * share, (p + 1) * share)
         depth_out[0, rows, :] = got[0:share] / (got[2 * share : 3 * share] + lam_depth + epsilon)
         depth_out[1, rows, :] = got[share : 2 * share] / (levels + lam_depth + epsilon)
-    planes = plane_ref[...] + other_ref[...]
+    planes = plane_ref[...]
     plane_out[0] = planes[:, 0:RANK] / (planes[:, 2 * RANK : 3 * RANK] + lam_plane + epsilon)
     plane_out[1] = planes[:, RANK : 2 * RANK] / (planes[0:1, 3 * RANK :] + lam_plane + epsilon)
 
@@ -473,12 +487,9 @@
         n_gy,
     )
     depth_terms = lax.all_to_all(depth_terms, "gy", 0, 0)
-    hop = 1
-    while 2 * hop < n_gz:
-        plane_terms = plane_terms + lax.ppermute(plane_terms, "gz", [(i, i ^ hop) for i in range(n_gz)])
-        hop = 2 * hop
-    pairs = [(i, i ^ hop) for i in range(n_gz)]
-    energy = lax.ppermute(plane_terms[-8:], "gz", pairs)
+    others = [
+        lax.ppermute(plane_terms, "gz", [(i, (i + hop) % n_gz) for i in range(n_gz)]) for hop in range(1, n_gz)
+    ]
     depth_terms, plane_terms = pl.pallas_call(
         gather_kernel,
         out_shape=[
@@ -487,9 +498,8 @@
         ],
         compiler_params=plain_params(),
         name="gather",
-    )(depth_terms, plane_terms, energy)
+    )(depth_terms, plane_terms, *others)
     depth_terms = lax.all_to_all(depth_terms, "gy", 0, 0)
-    other = lax.ppermute(plane_terms, "gz", pairs)
     width = depth_factors.shape[2]
     step_depth, step_plane = pl.pallas_call(
         functools.partial(step_kernel, width * n_gz, nodes_x * nodes_y * n_gy),
@@ -499,7 +509,7 @@
         ],
         compiler_params=plain_params(),
         name="steps",
-    )(depth_terms, plane_terms, other)
+    )(depth_terms, plane_terms)
     step_plane = jnp.transpose(step_plane.reshape(2, nodes_x, nodes_y, RANK), (0, 3, 1, 2))
     return residual, step_plane, step_depth
 

time: 74.3 us -> 75.8 us (1.020)
  blocking collectives: 0 us -> 10.9 us
  starting transfers between devices: 26.2 us -> 18.1 us
  waiting for transfers between devices: 8.73 us -> 4.3 us
  local copies, waits for them, and re-layouts: 1.13 us -> 2.79 us
  Pallas kernels: 37.1 us -> 38.5 us
    all_to_all x0 -> x1, blocking collectives: none -> 10.9 us  [local(): depth_terms = lax.all_to_all(depth_terms, 'gy', 0, 0)]
    all_to_all x2 -> x1, starting transfers between devices: 10.7 us -> 6.25 us  [local(): depth_terms = lax.all_to_all(depth_terms, 'gy', 0, 0)]
    ppermute x3, starting transfers between devices: 10.9 us -> 7.29 us  [local(): lax.ppermute(plane_terms, 'gz', [(i, (i + hop) % n_gz) for i in range(n_g...]
    pallas_call x1, Pallas kernels: 0.19 us -> 2.36 us  [ends(): pl.pallas_call(ends_kernel, grid=(1,), in_specs=[pl.BlockSpec(block, func...]
    all_to_all x2 -> x1, waiting for transfers between devices: 1.95 us -> 0.01 us  [local(): depth_terms = lax.all_to_all(depth_terms, 'gy', 0, 0)]
    unnamed x8 -> x12, local copies, waits for them, and re-layouts: 1.12 us -> 2.79 us
    ppermute x3, waiting for transfers between devices: 5.71 us -> 4.29 us  [local(): lax.ppermute(plane_terms, 'gz', [(i, (i + hop) % n_gz) for i in range(n_g...]
    ppermute x4, waiting for transfers between devices: 1.06 us -> 0.01 us  [swapped(): return lax.ppermute(part, axis, pairs + [(j, i) for i, j in pairs])]
  transfers between devices with their start and end apart: 9 -> 8, of which waited for: 5 -> 2; matrix products, arithmetic and copies ran while one was open for 0% -> 0% of each run, Pallas kernels for 3% -> 6%
where the time goes in v19:
time: 75.8 us; the launch traced here: 75.3 us
  Pallas kernels  38.5 us (51%)
  starting transfers between devices  18.1 us (24%)
  blocking collectives  10.9 us (14%)
  waiting for transfers between devices  4.3 us (6%)
  local copies, waits for them, and re-layouts  2.79 us (4%)
  between operations  0.76 us (1%)
    pallas_call x1, Pallas kernels, warp(): pl.pallas_call(warp_kernel, grid=(count + 1,), in_specs=[pl.BlockSpec((KN...  29.9 us
    all_to_all x1, blocking collectives, local(): depth_terms = lax.all_to_all(depth_terms, 'gy', 0, 0)  10.9 us
    ppermute x3, starting transfers between devices, local(): lax.ppermute(plane_terms, 'gz', [(i, (i + hop) % n_gz) for i in range(n_g...  7.29 us
    all_to_all x1, starting transfers between devices, local(): depth_terms = lax.all_to_all(depth_terms, 'gy', 0, 0)  6.25 us
    ppermute x4, starting transfers between devices, swapped(): return lax.ppermute(part, axis, pairs + [(j, i) for i, j in pairs])  4.54 us
    ppermute x3, waiting for transfers between devices, local(): lax.ppermute(plane_terms, 'gz', [(i, (i + hop) % n_gz) for i in range(n_g...  4.29 us
    pallas_call x1, Pallas kernels, end_columns(): pl.pallas_call(columns_kernel, grid=(1,), in_specs=[pl.BlockSpec(block, f...  2.79 us
    unnamed x12, local copies, waits for them, and re-layouts  2.79 us
  transfers between devices with their start and end apart: 8, of which 2 were waited for; matrix products, arithmetic and copies ran while one was open for 0% of the time, Pallas kernels for 6%

profile of v19, /device:TPU:0, one launch (start us, length us, event | category | flops | bytes accessed | tf_op | source)
XLA Modules:
  0.0 75.3 jit_solution(11402210065037110901)
XLA Ops:
  0.6 2.8 %columns.1 = (bf16[64,128]{1,0:T(8,128)(2,1)}, bf16[64,128]{1,0:T(8,128)(2,1)}) custom-call(bf16[64,64,512]{2,1,0:T(8,128)(2,1)} %cells_ref.1, bf16[64,64,512]{2,1,0:T(8,128)(2,1)} %cells_ref.1, bf16[64,64,512]{2,1,0:T(8,128)(2,1)} %cells_ref.1, bf16[64,64,512]{2,1,0:T(8,128)(2,1)} %cells_ref.1, bf16[64,64,512]{2,1,0:T(8,128)(2,1)} %cells_ref.1, ...), custom_call_target="tpu_custom_call" | custom-call | tf_op jit(solution)/shard_map/columns/pallas_call | solution.py:71
  3.4 3.0 %collective-permute-start = (bf16[64,128]{1,0:T(8,128)(2,1)}, bf16[64,128]{1,0:T(8,128)(2,1)S(1)}, u32[]{:S(2)}, u32[]{:S(2)}) collective-permute-start(bf16[64,128]{1,0:T(8,128)(2,1)} %get-tuple-element.20), channel_id=1, source_target_pairs={{0,1},{2,3},{1,0},{3,2},{4,5},{6,7},{5,4},{7,6},{8,9},{10,11},{9,8... | collective-permute-start | bytes 49160 | tf_op jit(solution)/shard_map/ppermute | solution.py:151
  6.4 0.7 collective-permute-start.1
  7.1 2.4 %ends.1 = (bf16[64,512]{1,0:T(8,128)(2,1)}, bf16[64,512]{1,0:T(8,128)(2,1)}) custom-call(bf16[64,64,512]{2,1,0:T(8,128)(2,1)} %cells_ref.1, bf16[64,64,512]{2,1,0:T(8,128)(2,1)} %cells_ref.1, bf16[64,64,512]{2,1,0:T(8,128)(2,1)} %cells_ref.1, bf16[64,64,512]{2,1,0:T(8,128)(2,1)} %cells_ref.1, bf16[64,64,512]{2,1,0:T(8,128)(2,1)} %cells_ref.1, ...), custom_call_target="tpu_custom_call" | custom-call | flops 2097152 | bytes 4194304 | tf_op jit(solution)/shard_map/ends/pallas_call | solution.py:99
  9.5 0.0 collective-permute-done.inner_ref
  9.5 0.0 collective-permute-done.1.outer_ref
  9.5 0.0 copy-start.4
  9.5 0.8 %copy-done.4 = bf16[64,512]{1,0:T(8,128)(2,1)S(1)} copy-done((bf16[64,512]{1,0:T(8,128)(2,1)S(1)}, bf16[64,512]{1,0:T(8,128)(2,1)}, u32[]{:S(2)}) %copy-start.4) | copy-done | bytes 65560
  10.3 0.0 copy-start.5
  10.3 0.8 %copy-done.5 = bf16[64,512]{1,0:T(8,128)(2,1)S(1)} copy-done((bf16[64,512]{1,0:T(8,128)(2,1)S(1)}, bf16[64,512]{1,0:T(8,128)(2,1)}, u32[]{:S(2)}) %copy-start.5) | copy-done | bytes 65560
  11.2 0.0 copy-start.1
  11.2 0.2 rows.1
  11.3 0.0 copy-start.2
  11.3 0.0 copy-start.3
  11.3 0.0 copy-start
  11.4 0.1 collective-permute-start.3
  11.4 0.8 %collective-permute-start.2 = (bf16[64,640]{1,0:T(8,128)(2,1)S(1)}, bf16[64,640]{1,0:T(8,128)(2,1)S(1)}, u32[]{:S(2)}, u32[]{:S(2)}) collective-permute-start(bf16[64,640]{1,0:T(8,128)(2,1)S(1)} %get-tuple-element.24.later_ref), channel_id=1, source_target_pairs={{4,8},{12,16},{20,24},{8,4},{16,12},{24,20},{5,9},{13,17},{21,25},... | collective-permute-start | bytes 245768 | tf_op jit(solution)/shard_map/ppermute | solution.py:151
  12.2 1.1 %copy-done.1 = bf16[64,64,512]{2,1,0:T(8,128)(2,1)S(1)} copy-done((bf16[64,64,512]{2,1,0:T(8,128)(2,1)S(1)}, bf16[64,64,512]{2,1,0:T(8,128)(2,1)}, u32[]{:S(2)}) %copy-start.1) | copy-done | bytes 4194328
  13.3 1.5 %squares.1.sums = f32[4,64,128]{2,1,0:T(8,128)S(1)} custom-call(bf16[64,64,512]{2,1,0:T(8,128)(2,1)S(1)} %copy-done.1, bf16[64,640]{1,0:T(8,128)(2,1)S(1)} %get-tuple-element.24.later_ref), custom_call_target="tpu_custom_call" | custom-call | flops 6291456 | bytes 4194304 | tf_op jit(solution)/shard_map/squares/pallas_call | solution.py:176
  14.9 0.0 copy-done.2
  14.9 0.0 copy-done.3
  14.9 0.7 terms.1
  15.6 0.0 collective-permute-done.3.inside_ref
  15.6 0.0 collective-permute-done.2.across_ref
  15.6 0.0 copy-done
  15.6 29.9 %warp.1 = (bf16[64,64,512]{2,1,0:T(8,128)(2,1)}, f32[8,16,512]{2,1,0:T(8,128)}, f32[64,128]{1,0:T(8,128)S(1)}) custom-call(bf16[64,64,512]{2,1,0:T(8,128)(2,1)S(1)} %copy-done, bf16[64,64,512]{2,1,0:T(8,128)(2,1)S(1)} %copy-done.1, bf16[3,64,64,512]{3,2,1,0:T(8,128)(2,1)} %shift_ref.1, bf16[64,64,128]{2,1,0:T(8,128)(2,1)S(1)} %get-tuple-element.25.beyond_ref, ...), custom_call_target="tpu_custom_call" | custom-call | flops 125829120 | bytes 25165824 | tf_op jit(solution)/shard_map/warp/pallas_call | solution.py:392
  45.5 6.2 %all-to-all-start = ((f32[8,16,512]{2,1,0:T(8,128)}), f32[8,16,512]{2,1,0:T(8,128)S(1)}, u32[]{:S(2)}, u32[]{:S(2)}) async-start(f32[8,16,512]{2,1,0:T(8,128)} %get-tuple-element.31), calls=%async_computation | async-start | bytes 524288 | tf_op jit(solution)/shard_map/all_to_all | solution.py:489
  51.8 3.0 %collective-permute-start.6 = (f32[64,128]{1,0:T(8,128)S(1)}, f32[64,128]{1,0:T(8,128)S(1)}, u32[]{:S(2)}, u32[]{:S(2)}) collective-permute-start(f32[64,128]{1,0:T(8,128)S(1)} %get-tuple-element.32.refs_0_), channel_id=1, source_target_pairs={{0,3},{1,0},{2,1},{3,2},{4,7},{5,4},{6,5},{7,6},{8,11},{9,8},{10,9... | collective-permute-start | bytes 98312 | tf_op jit(solution)/shard_map/ppermute | solution.py:491
  54.7 2.9 %collective-permute-start.5 = (f32[64,128]{1,0:T(8,128)S(1)}, f32[64,128]{1,0:T(8,128)S(1)}, u32[]{:S(2)}, u32[]{:S(2)}) collective-permute-start(f32[64,128]{1,0:T(8,128)S(1)} %get-tuple-element.32.refs_0_), channel_id=1, source_target_pairs={{0,2},{1,3},{2,0},{3,1},{4,6},{5,7},{6,4},{7,5},{8,10},{9,11},{10,... | collective-permute-start | bytes 98312 | tf_op jit(solution)/shard_map/ppermute | solution.py:491
  57.6 1.4 %collective-permute-start.4 = (f32[64,128]{1,0:T(8,128)S(1)}, f32[64,128]{1,0:T(8,128)S(1)}, u32[]{:S(2)}, u32[]{:S(2)}) collective-permute-start(f32[64,128]{1,0:T(8,128)S(1)} %get-tuple-element.32.refs_0_), channel_id=1, source_target_pairs={{0,1},{1,2},{2,3},{3,0},{4,5},{5,6},{6,7},{7,4},{8,9},{9,10},{10,1... | collective-permute-start | bytes 98312 | tf_op jit(solution)/shard_map/ppermute | solution.py:491
  59.1 0.0 collective-permute-done.6.refs_3_
  59.1 1.3 %collective-permute-done.5.refs_2_ = f32[64,128]{1,0:T(8,128)S(1)} collective-permute-done((f32[64,128]{1,0:T(8,128)S(1)}, f32[64,128]{1,0:T(8,128)S(1)}, u32[]{:S(2)}, u32[]{:S(2)}) %collective-permute-start.5) | collective-permute-done | bytes 32800 | tf_op jit(solution)/shard_map/ppermute | solution.py:491
  60.3 3.0 %collective-permute-done.4.refs_1_ = f32[64,128]{1,0:T(8,128)S(1)} collective-permute-done((f32[64,128]{1,0:T(8,128)S(1)}, f32[64,128]{1,0:T(8,128)S(1)}, u32[]{:S(2)}, u32[]{:S(2)}) %collective-permute-start.4) | collective-permute-done | bytes 32800 | tf_op jit(solution)/shard_map/ppermute | solution.py:491
  63.3 0.0 all-to-all-done.depth_ref
  63.4 0.1 gather.1
  63.5 10.9 %all_to_all.10.depth_ref = f32[8,16,512]{2,1,0:T(8,128)S(1)} all-to-all(f32[8,16,512]{2,1,0:T(8,128)S(1)} %get-tuple-element.33), channel_id=1, replica_groups=mesh['gy'=8,'gz'=4] {'gy'}, dimensions={0} | all-to-all | bytes 524288 | tf_op jit(solution)/shard_map/all_to_all | solution.py:502
  74.4 0.9 %steps.1 = (f32[2,32,512]{2,1,0:T(8,128)}, f32[2,64,32]{2,1,0:T(8,128)}) custom-call(f32[8,16,512]{2,1,0:T(8,128)S(1)} %all_to_all.10.depth_ref, f32[64,128]{1,0:T(8,128)S(1)} %get-tuple-element.34.plane_ref), custom_call_target="tpu_custom_call" | custom-call | tf_op jit(solution)/shard_map/steps/pallas_call | solution.py:504
Async XLA Ops:
  3.4 6.0 %collective-permute-start = (bf16[64,128]{1,0:T(8,128)(2,1)}, bf16[64,128]{1,0:T(8,128)(2,1)S(1)}, u32[]{:S(2)}, u32[]{:S(2)}) collective-permute-start(bf16[64,128]{1,0:T(8,128)(2,1)} %get-tuple-element.20), channel_id=1, source_target_pairs={{0,1},{2,3},{1,0},{3,2},{4,5},{6,7},{5,4},{7,6},{8,9},{10,11},{9,8... | collective-permute-start | bytes 49160 | tf_op jit(solution)/shard_map/ppermute | solution.py:151
  6.4 3.0 %collective-permute-start.1 = (bf16[64,128]{1,0:T(8,128)(2,1)}, bf16[64,128]{1,0:T(8,128)(2,1)S(1)}, u32[]{:S(2)}, u32[]{:S(2)}) collective-permute-start(bf16[64,128]{1,0:T(8,128)(2,1)} %get-tuple-element.21), channel_id=1, source_target_pairs={{1,2},{2,1},{5,6},{6,5},{9,10},{10,9},{13,14},{14,13},{17,18},{18,... | collective-permute-start | bytes 49160 | tf_op jit(solution)/shard_map/ppermute | solution.py:151
  9.5 0.8 %copy-start.4 = (bf16[64,512]{1,0:T(8,128)(2,1)S(1)}, bf16[64,512]{1,0:T(8,128)(2,1)}, u32[]{:S(2)}) copy-start(bf16[64,512]{1,0:T(8,128)(2,1)} %get-tuple-element.22.low_ref) | copy-start | bytes 196612
  10.3 0.8 %copy-start.5 = (bf16[64,512]{1,0:T(8,128)(2,1)S(1)}, bf16[64,512]{1,0:T(8,128)(2,1)}, u32[]{:S(2)}) copy-start(bf16[64,512]{1,0:T(8,128)(2,1)} %get-tuple-element.23.high_ref) | copy-start | bytes 196612
  11.2 2.2 %copy-start.1 = (bf16[64,64,512]{2,1,0:T(8,128)(2,1)S(1)}, bf16[64,64,512]{2,1,0:T(8,128)(2,1)}, u32[]{:S(2)}) copy-start(bf16[64,64,512]{2,1,0:T(8,128)(2,1)} %image_ref.3) | copy-start | bytes 12582916
  11.3 3.5 %copy-start.2 = (f32[2,32,512]{2,1,0:T(8,128)S(1)}, f32[2,32,512]{2,1,0:T(8,128)}, u32[]{:S(2)}) copy-start(f32[2,32,512]{2,1,0:T(8,128)} %depth_ref.3) | copy-start | bytes 393220
  11.3 3.5 %copy-start.3 = (f32[2,32,8,8]{1,3,2,0:T(8,128)S(1)}, f32[2,32,8,8]{1,3,2,0:T(8,128)}, u32[]{:S(2)}) copy-start(f32[2,32,8,8]{1,3,2,0:T(8,128)} %param.8) | copy-start | bytes 49156
  11.3 4.2 %copy-start = (bf16[64,64,512]{2,1,0:T(8,128)(2,1)S(1)}, bf16[64,64,512]{2,1,0:T(8,128)(2,1)}, u32[]{:S(2)}) copy-start(bf16[64,64,512]{2,1,0:T(8,128)(2,1)} %cells_ref.1) | copy-start | bytes 12582916
  11.4 4.2 %collective-permute-start.3 = (bf16[64,640]{1,0:T(8,128)(2,1)S(1)}, bf16[64,640]{1,0:T(8,128)(2,1)S(1)}, u32[]{:S(2)}, u32[]{:S(2)}) collective-permute-start(bf16[64,640]{1,0:T(8,128)(2,1)S(1)} %get-tuple-element.26), channel_id=1, source_target_pairs={{0,4},{8,12},{16,20},{24,28},{4,0},{12,8},{20,16},{28,24},{1,5},{9... | collective-permute-start | bytes 245768 | tf_op jit(solution)/shard_map/ppermute | solution.py:151
  11.4 4.1 %collective-permute-start.2 = (bf16[64,640]{1,0:T(8,128)(2,1)S(1)}, bf16[64,640]{1,0:T(8,128)(2,1)S(1)}, u32[]{:S(2)}, u32[]{:S(2)}) collective-permute-start(bf16[64,640]{1,0:T(8,128)(2,1)S(1)} %get-tuple-element.24.later_ref), channel_id=1, source_target_pairs={{4,8},{12,16},{20,24},{8,4},{16,12},{24,20},{5,9},{13,17},{21,25},... | collective-permute-start | bytes 245768 | tf_op jit(solution)/shard_map/ppermute | solution.py:151
  45.5 17.8 %all-to-all-start = ((f32[8,16,512]{2,1,0:T(8,128)}), f32[8,16,512]{2,1,0:T(8,128)S(1)}, u32[]{:S(2)}, u32[]{:S(2)}) async-start(f32[8,16,512]{2,1,0:T(8,128)} %get-tuple-element.31), calls=%async_computation | async-start | bytes 524288 | tf_op jit(solution)/shard_map/all_to_all | solution.py:489
  51.8 7.3 %collective-permute-start.6 = (f32[64,128]{1,0:T(8,128)S(1)}, f32[64,128]{1,0:T(8,128)S(1)}, u32[]{:S(2)}, u32[]{:S(2)}) collective-permute-start(f32[64,128]{1,0:T(8,128)S(1)} %get-tuple-element.32.refs_0_), channel_id=1, source_target_pairs={{0,3},{1,0},{2,1},{3,2},{4,7},{5,4},{6,5},{7,6},{8,11},{9,8},{10,9... | collective-permute-start | bytes 98312 | tf_op jit(solution)/shard_map/ppermute | solution.py:491
  54.7 5.6 %collective-permute-start.5 = (f32[64,128]{1,0:T(8,128)S(1)}, f32[64,128]{1,0:T(8,128)S(1)}, u32[]{:S(2)}, u32[]{:S(2)}) collective-permute-start(f32[64,128]{1,0:T(8,128)S(1)} %get-tuple-element.32.refs_0_), channel_id=1, source_target_pairs={{0,2},{1,3},{2,0},{3,1},{4,6},{5,7},{6,4},{7,5},{8,10},{9,11},{10,... | collective-permute-start | bytes 98312 | tf_op jit(solution)/shard_map/ppermute | solution.py:491
  57.6 5.7 %collective-permute-start.4 = (f32[64,128]{1,0:T(8,128)S(1)}, f32[64,128]{1,0:T(8,128)S(1)}, u32[]{:S(2)}, u32[]{:S(2)}) collective-permute-start(f32[64,128]{1,0:T(8,128)S(1)} %get-tuple-element.32.refs_0_), channel_id=1, source_target_pairs={{0,1},{1,2},{2,3},{3,0},{4,5},{5,6},{6,7},{7,4},{8,9},{9,10},{10,1... | collective-permute-start | bytes 98312 | tf_op jit(solution)/shard_map/ppermute | solution.py:491

commit v20 on v19

--- a/solution.py
+++ b/solution.py
@@ -79,33 +79,24 @@
     )(*[cells] * len(places))
 
 
-def ends_kernel(*refs):
-    low_ref, high_ref = refs[-2:]
-    chunks = (len(refs) - 2) // 2
-    for chunk in range(chunks):
-        near, far = refs[chunk], refs[chunks + chunk]
-        planes = near.shape[0]
-        low = [near[k].astype(f32)[0:1] for k in range(planes)]
-        high = [far[k].astype(f32)[15:16] for k in range(planes)]
-        low_ref[chunk * planes : (chunk + 1) * planes, :] = jnp.concatenate(low, axis=0).astype(bf16)
-        high_ref[chunk * planes : (chunk + 1) * planes, :] = jnp.concatenate(high, axis=0).astype(bf16)
+def ends_kernel(cells_ref, low_ref, high_ref):
+    depth, rows = cells_ref.shape[0:2]
+    for x in range(0, depth, 16):
+        low = [cells_ref[x + k, 0:16, :].astype(f32)[0:1] for k in range(16)]
+        high = [cells_ref[x + k, rows - 16 : rows, :].astype(f32)[15:16] for k in range(16)]
+        low_ref[x : x + 16, :] = jnp.concatenate(low, axis=0).astype(bf16)
+        high_ref[x : x + 16, :] = jnp.concatenate(high, axis=0).astype(bf16)
 
 
 def ends(cells):
     depth, rows, width = cells.shape
-    chunks = 4
-    block = (depth // chunks, 16, width)
-    places = [(chunk, row) for row in (0, rows // 16 - 1) for chunk in range(chunks)]
     return pl.pallas_call(
         ends_kernel,
-        grid=(1,),
-        in_specs=[pl.BlockSpec(block, functools.partial(lambda c, r, i: (c, r, 0), c, r)) for c, r in places],
-        out_specs=[pl.BlockSpec((depth, width), lambda i: (0, 0))] * 2,
         out_shape=[jax.ShapeDtypeStruct((depth, width), bf16)] * 2,
-        compiler_params=pltpu.CompilerParams(vmem_limit_bytes=60000000),
+        compiler_params=plain_params(),
         cost_estimate=pl.CostEstimate(flops=cells.size, bytes_accessed=2 * cells.size, transcendentals=0),
         name="ends",
-    )(*[cells] * len(places))
+    )(cells)
 
 
 def z_sides(inner_ref, outer_ref):
@@ -226,7 +217,7 @@
     cells_ref, image_ref, shift_ref, beyond_ref, across_ref, inside_ref, field, plane_ref, depth_ref,
     diag_depth_ref, diag_plane_ref,
     residual_ref, depth_out, plane_out,
-    ahead_ref, here_ref, behind_ref, wide, bands, rims, blocks, energy, held,
+    ahead_ref, here_ref, behind_ref, wide, bands, blocks, energy, held,
 ):
     step = pl.program_id(0)
     last = pl.num_programs(0) - 1
@@ -255,24 +246,24 @@
     @pl.when(step < last)
     def _():
         slot = (step % 3) * block_rows
-        span = planes * rows
-        for k in range(planes):
-            wide[k * rows : (k + 1) * rows, 0:width] = cells_ref[k]
-            wide[k * rows : (k + 1) * rows, width:] = beyond_ref[k]
         odd = lax.axis_index("gy") % 2 == 1
         across, inside = across_ref[...].astype(f32), inside_ref[...].astype(f32)
         low, high = jnp.where(odd, inside, across), jnp.where(odd, across, inside)
-        wide[span:, :] = jnp.concatenate([low, high], axis=0).astype(bf16)
+        at = lax.broadcasted_iota(jnp.int32, (2 * TOP, width + LANES), 0)
+        for k in range(planes):
+            first = k * pitch
+            wide[first : first + rows, 0:width] = cells_ref[k]
+            wide[first : first + rows, width:] = beyond_ref[k]
+            rim = jnp.where(at == TOP, high[k : k + 1], jnp.where(at == TOP - 1, low[k : k + 1], 0.0))
+            wide[first + rows : first + pitch, :] = rim.astype(bf16)
 
         def put(c, tile, values):
             for k in range(planes):
                 first = pl.multiple_of(slot + k * plane_rows + tile * pitch, 8)
-                window[c][pl.ds(first + TOP, rows), :] = values[k * rows : (k + 1) * rows]
-            for side, row in enumerate((0, TOP + rows)):
-                rims[...] = values[span + side * planes : span + (side + 1) * planes]
-                for k in range(planes):
-                    first = pl.multiple_of(slot + k * plane_rows + tile * pitch, 8)
-                    window[c][pl.ds(first + row, 8), :] = jnp.broadcast_to(rims[k : k + 1], (8, LANES))
+                mine = values[k * pitch : (k + 1) * pitch]
+                window[c][pl.ds(first + TOP, rows), :] = mine[0:rows]
+                window[c][pl.ds(first, TOP), :] = mine[rows : rows + TOP]
+                window[c][pl.ds(first + TOP + rows, TOP), :] = mine[rows + TOP :]
 
         pieces = width // (2 * LANES)
         for piece in range(pieces):
@@ -417,9 +408,8 @@
         ],
         scratch_shapes=[
             *[pltpu.VMEM((3 * KNOT * tiles * (rows + 2 * TOP), LANES), f32)] * 3,
-            pltpu.VMEM((KNOT * rows + 2 * KNOT, width + LANES), bf16),
+            pltpu.VMEM((KNOT * (rows + 2 * TOP), width + LANES), bf16),
             pltpu.VMEM((2, 3 * LANES, 2 * LANES), bf16),
-            pltpu.VMEM((KNOT, LANES), f32),
             pltpu.VMEM((2, tiles, nodes, LANES), f32),
             pltpu.VMEM((8, LANES), f32),
             pltpu.VMEM((KNOT, 8, LANES), f32),

time: 75.8 us -> 73.6 us (0.971)
  Pallas kernels: 38.5 us -> 36.6 us
  local copies, waits for them, and re-layouts: 2.79 us -> 1.12 us
  starting transfers between devices: 18.1 us -> 19.1 us
    pallas_call x1, Pallas kernels: 2.36 us -> 0.19 us  [ends(): pl.pallas_call(ends_kernel, out_shape=[jax.ShapeDtypeStruct((depth, width...]
    unnamed x12 -> x8, local copies, waits for them, and re-layouts: 2.79 us -> 1.12 us
    ppermute x4, waiting for transfers between devices: 0.01 us -> 1.06 us  [swapped(): return lax.ppermute(part, axis, pairs + [(j, i) for i, j in pairs])]
    ppermute x3, starting transfers between devices: 7.29 us -> 8.07 us  [local(): lax.ppermute(plane_terms, 'gz', [(i, (i + hop) % n_gz) for i in range(n_g...]
  transfers between devices with their start and end apart: 8 -> 8, of which waited for: 2 -> 3; matrix products, arithmetic and copies ran while one was open for 0% -> 0% of each run, Pallas kernels for 6% -> 3%
where the time goes in v20:
time: 73.6 us; the launch traced here: 73.3 us
  Pallas kernels  36.6 us (50%)
  starting transfers between devices  19.1 us (26%)
  blocking collectives  10.9 us (15%)
  waiting for transfers between devices  4.83 us (7%)
  local copies, waits for them, and re-layouts  1.12 us (2%)
  between operations  0.76 us (1%)
    pallas_call x1, Pallas kernels, warp(): pl.pallas_call(warp_kernel, grid=(count + 1,), in_specs=[pl.BlockSpec((KN...  30.1 us
    all_to_all x1, blocking collectives, local(): depth_terms = lax.all_to_all(depth_terms, 'gy', 0, 0)  10.9 us
    ppermute x3, starting transfers between devices, local(): lax.ppermute(plane_terms, 'gz', [(i, (i + hop) % n_gz) for i in range(n_g...  8.07 us
    all_to_all x1, starting transfers between devices, local(): depth_terms = lax.all_to_all(depth_terms, 'gy', 0, 0)  6.53 us
    ppermute x4, starting transfers between devices, swapped(): return lax.ppermute(part, axis, pairs + [(j, i) for i, j in pairs])  4.54 us
    ppermute x3, waiting for transfers between devices, local(): lax.ppermute(plane_terms, 'gz', [(i, (i + hop) % n_gz) for i in range(n_g...  3.76 us
    pallas_call x1, Pallas kernels, end_columns(): pl.pallas_call(columns_kernel, grid=(1,), in_specs=[pl.BlockSpec(block, f...  2.94 us
    pallas_call x1, Pallas kernels, squares(): pl.pallas_call(squares_kernel, out_shape=jax.ShapeDtypeStruct((width // L...  1.5 us
  transfers between devices with their start and end apart: 8, of which 3 were waited for; matrix products, arithmetic and copies ran while one was open for 0% of the time, Pallas kernels for 3%

profile of v20, /device:TPU:0, one launch (start us, length us, event | category | flops | bytes accessed | tf_op | source)
XLA Modules:
  0.0 73.3 jit_solution(2236965671230894927)
XLA Ops:
  0.6 0.0 copy-start
  0.6 2.9 %columns.1 = (bf16[64,128]{1,0:T(8,128)(2,1)}, bf16[64,128]{1,0:T(8,128)(2,1)}) custom-call(bf16[64,64,512]{2,1,0:T(8,128)(2,1)} %cells_ref.3, bf16[64,64,512]{2,1,0:T(8,128)(2,1)} %cells_ref.3, bf16[64,64,512]{2,1,0:T(8,128)(2,1)} %cells_ref.3, bf16[64,64,512]{2,1,0:T(8,128)(2,1)} %cells_ref.3, bf16[64,64,512]{2,1,0:T(8,128)(2,1)} %cells_ref.3, ...), custom_call_target="tpu_custom_call" | custom-call | tf_op jit(solution)/shard_map/columns/pallas_call | solution.py:71
  3.6 3.0 %collective-permute-start = (bf16[64,128]{1,0:T(8,128)(2,1)}, bf16[64,128]{1,0:T(8,128)(2,1)S(1)}, u32[]{:S(2)}, u32[]{:S(2)}) collective-permute-start(bf16[64,128]{1,0:T(8,128)(2,1)} %get-tuple-element.20), channel_id=1, source_target_pairs={{0,1},{2,3},{1,0},{3,2},{4,5},{6,7},{5,4},{7,6},{8,9},{10,11},{9,8... | collective-permute-start | bytes 49160 | tf_op jit(solution)/shard_map/ppermute | solution.py:142
  6.6 0.7 collective-permute-start.1
  7.3 0.0 copy-done
  7.3 0.2 ends.1
  7.5 1.1 %collective-permute-done.inner_ref = bf16[64,128]{1,0:T(8,128)(2,1)S(1)} collective-permute-done((bf16[64,128]{1,0:T(8,128)(2,1)}, bf16[64,128]{1,0:T(8,128)(2,1)S(1)}, u32[]{:S(2)}, u32[]{:S(2)}) %collective-permute-start) | collective-permute-done | bytes 16416 | tf_op jit(solution)/shard_map/ppermute | solution.py:142
  8.5 0.0 collective-permute-done.1.outer_ref
  8.5 0.0 copy-start.1
  8.5 0.2 rows.1
  8.7 0.0 copy-start.2
  8.7 0.0 copy-start.3
  8.7 0.1 collective-permute-start.3
  8.8 0.8 %collective-permute-start.2 = (bf16[64,640]{1,0:T(8,128)(2,1)S(1)}, bf16[64,640]{1,0:T(8,128)(2,1)S(1)}, u32[]{:S(2)}, u32[]{:S(2)}) collective-permute-start(bf16[64,640]{1,0:T(8,128)(2,1)S(1)} %get-tuple-element.24.later_ref), channel_id=1, source_target_pairs={{4,8},{12,16},{20,24},{8,4},{16,12},{24,20},{5,9},{13,17},{21,25},... | collective-permute-start | bytes 245768 | tf_op jit(solution)/shard_map/ppermute | solution.py:142
  9.6 1.1 %copy-done.1 = bf16[64,64,512]{2,1,0:T(8,128)(2,1)S(1)} copy-done((bf16[64,64,512]{2,1,0:T(8,128)(2,1)S(1)}, bf16[64,64,512]{2,1,0:T(8,128)(2,1)}, u32[]{:S(2)}) %copy-start.1) | copy-done | bytes 4194328
  10.7 1.5 %squares.1.sums = f32[4,64,128]{2,1,0:T(8,128)S(1)} custom-call(bf16[64,64,512]{2,1,0:T(8,128)(2,1)S(1)} %copy-done.1, bf16[64,640]{1,0:T(8,128)(2,1)S(1)} %get-tuple-element.24.later_ref), custom_call_target="tpu_custom_call" | custom-call | flops 6291456 | bytes 4194304 | tf_op jit(solution)/shard_map/squares/pallas_call | solution.py:167
  12.2 0.0 copy-done.2
  12.2 0.0 copy-done.3
  12.3 0.7 terms.1
  12.9 0.0 collective-permute-done.3.inside_ref
  13.0 0.0 collective-permute-done.2.across_ref
  13.0 30.1 %warp.1 = (bf16[64,64,512]{2,1,0:T(8,128)(2,1)}, f32[8,16,512]{2,1,0:T(8,128)}, f32[64,128]{1,0:T(8,128)S(1)}) custom-call(bf16[64,64,512]{2,1,0:T(8,128)(2,1)S(1)} %copy-done, bf16[64,64,512]{2,1,0:T(8,128)(2,1)S(1)} %copy-done.1, bf16[3,64,64,512]{3,2,1,0:T(8,128)(2,1)} %shift_ref.1, bf16[64,64,128]{2,1,0:T(8,128)(2,1)S(1)} %get-tuple-element.25.beyond_ref, ...), custom_call_target="tpu_custom_call" | custom-call | flops 125829120 | bytes 25165824 | tf_op jit(solution)/shard_map/warp/pallas_call | solution.py:383
  43.0 6.5 %all-to-all-start = ((f32[8,16,512]{2,1,0:T(8,128)}), f32[8,16,512]{2,1,0:T(8,128)S(1)}, u32[]{:S(2)}, u32[]{:S(2)}) async-start(f32[8,16,512]{2,1,0:T(8,128)} %get-tuple-element.31), calls=%async_computation | async-start | bytes 524288 | tf_op jit(solution)/shard_map/all_to_all | solution.py:479
  49.6 3.6 %collective-permute-start.6 = (f32[64,128]{1,0:T(8,128)S(1)}, f32[64,128]{1,0:T(8,128)S(1)}, u32[]{:S(2)}, u32[]{:S(2)}) collective-permute-start(f32[64,128]{1,0:T(8,128)S(1)} %get-tuple-element.32.refs_0_), channel_id=1, source_target_pairs={{0,3},{1,0},{2,1},{3,2},{4,7},{5,4},{6,5},{7,6},{8,11},{9,8},{10,9... | collective-permute-start | bytes 98312 | tf_op jit(solution)/shard_map/ppermute | solution.py:481
  53.2 2.5 %collective-permute-start.5 = (f32[64,128]{1,0:T(8,128)S(1)}, f32[64,128]{1,0:T(8,128)S(1)}, u32[]{:S(2)}, u32[]{:S(2)}) collective-permute-start(f32[64,128]{1,0:T(8,128)S(1)} %get-tuple-element.32.refs_0_), channel_id=1, source_target_pairs={{0,2},{1,3},{2,0},{3,1},{4,6},{5,7},{6,4},{7,5},{8,10},{9,11},{10,... | collective-permute-start | bytes 98312 | tf_op jit(solution)/shard_map/ppermute | solution.py:481
  55.7 2.0 %collective-permute-start.4 = (f32[64,128]{1,0:T(8,128)S(1)}, f32[64,128]{1,0:T(8,128)S(1)}, u32[]{:S(2)}, u32[]{:S(2)}) collective-permute-start(f32[64,128]{1,0:T(8,128)S(1)} %get-tuple-element.32.refs_0_), channel_id=1, source_target_pairs={{0,1},{1,2},{2,3},{3,0},{4,5},{5,6},{6,7},{7,4},{8,9},{9,10},{10,1... | collective-permute-start | bytes 98312 | tf_op jit(solution)/shard_map/ppermute | solution.py:481
  57.6 0.0 collective-permute-done.6.refs_3_
  57.7 0.7 collective-permute-done.5.refs_2_
  58.4 3.0 %collective-permute-done.4.refs_1_ = f32[64,128]{1,0:T(8,128)S(1)} collective-permute-done((f32[64,128]{1,0:T(8,128)S(1)}, f32[64,128]{1,0:T(8,128)S(1)}, u32[]{:S(2)}, u32[]{:S(2)}) %collective-permute-start.4) | collective-permute-done | bytes 32800 | tf_op jit(solution)/shard_map/ppermute | solution.py:481
  61.4 0.0 all-to-all-done.depth_ref
  61.4 0.1 gather.1
  61.5 10.9 %all_to_all.10.depth_ref = f32[8,16,512]{2,1,0:T(8,128)S(1)} all-to-all(f32[8,16,512]{2,1,0:T(8,128)S(1)} %get-tuple-element.33), channel_id=1, replica_groups=mesh['gy'=8,'gz'=4] {'gy'}, dimensions={0} | all-to-all | bytes 524288 | tf_op jit(solution)/shard_map/all_to_all | solution.py:492
  72.4 0.9 %steps.1 = (f32[2,32,512]{2,1,0:T(8,128)}, f32[2,64,32]{2,1,0:T(8,128)}) custom-call(f32[8,16,512]{2,1,0:T(8,128)S(1)} %all_to_all.10.depth_ref, f32[64,128]{1,0:T(8,128)S(1)} %get-tuple-element.34.plane_ref), custom_call_target="tpu_custom_call" | custom-call | tf_op jit(solution)/shard_map/steps/pallas_call | solution.py:494
Async XLA Ops:
  0.6 6.6 %copy-start = (bf16[64,64,512]{2,1,0:T(8,128)(2,1)S(1)}, bf16[64,64,512]{2,1,0:T(8,128)(2,1)}, u32[]{:S(2)}) copy-start(bf16[64,64,512]{2,1,0:T(8,128)(2,1)} %cells_ref.3) | copy-start | bytes 12582916
  3.6 5.0 %collective-permute-start = (bf16[64,128]{1,0:T(8,128)(2,1)}, bf16[64,128]{1,0:T(8,128)(2,1)S(1)}, u32[]{:S(2)}, u32[]{:S(2)}) collective-permute-start(bf16[64,128]{1,0:T(8,128)(2,1)} %get-tuple-element.20), channel_id=1, source_target_pairs={{0,1},{2,3},{1,0},{3,2},{4,5},{6,7},{5,4},{7,6},{8,9},{10,11},{9,8... | collective-permute-start | bytes 49160 | tf_op jit(solution)/shard_map/ppermute | solution.py:142
  6.6 1.9 %collective-permute-start.1 = (bf16[64,128]{1,0:T(8,128)(2,1)}, bf16[64,128]{1,0:T(8,128)(2,1)S(1)}, u32[]{:S(2)}, u32[]{:S(2)}) collective-permute-start(bf16[64,128]{1,0:T(8,128)(2,1)} %get-tuple-element.21), channel_id=1, source_target_pairs={{1,2},{2,1},{5,6},{6,5},{9,10},{10,9},{13,14},{14,13},{17,18},{18,... | collective-permute-start | bytes 49160 | tf_op jit(solution)/shard_map/ppermute | solution.py:142
  8.5 2.2 %copy-start.1 = (bf16[64,64,512]{2,1,0:T(8,128)(2,1)S(1)}, bf16[64,64,512]{2,1,0:T(8,128)(2,1)}, u32[]{:S(2)}) copy-start(bf16[64,64,512]{2,1,0:T(8,128)(2,1)} %image_ref.3) | copy-start | bytes 12582916
  8.7 3.5 %copy-start.2 = (f32[2,32,512]{2,1,0:T(8,128)S(1)}, f32[2,32,512]{2,1,0:T(8,128)}, u32[]{:S(2)}) copy-start(f32[2,32,512]{2,1,0:T(8,128)} %depth_ref.3) | copy-start | bytes 393220
  8.7 3.5 %copy-start.3 = (f32[2,32,8,8]{1,3,2,0:T(8,128)S(1)}, f32[2,32,8,8]{1,3,2,0:T(8,128)}, u32[]{:S(2)}) copy-start(f32[2,32,8,8]{1,3,2,0:T(8,128)} %param.8) | copy-start | bytes 49156
  8.7 4.2 %collective-permute-start.3 = (bf16[64,640]{1,0:T(8,128)(2,1)S(1)}, bf16[64,640]{1,0:T(8,128)(2,1)S(1)}, u32[]{:S(2)}, u32[]{:S(2)}) collective-permute-start(bf16[64,640]{1,0:T(8,128)(2,1)S(1)} %get-tuple-element.26), channel_id=1, source_target_pairs={{0,4},{8,12},{16,20},{24,28},{4,0},{12,8},{20,16},{28,24},{1,5},{9... | collective-permute-start | bytes 245768 | tf_op jit(solution)/shard_map/ppermute | solution.py:142
  8.8 4.1 %collective-permute-start.2 = (bf16[64,640]{1,0:T(8,128)(2,1)S(1)}, bf16[64,640]{1,0:T(8,128)(2,1)S(1)}, u32[]{:S(2)}, u32[]{:S(2)}) collective-permute-start(bf16[64,640]{1,0:T(8,128)(2,1)S(1)} %get-tuple-element.24.later_ref), channel_id=1, source_target_pairs={{4,8},{12,16},{20,24},{8,4},{16,12},{24,20},{5,9},{13,17},{21,25},... | collective-permute-start | bytes 245768 | tf_op jit(solution)/shard_map/ppermute | solution.py:142
  43.0 18.4 %all-to-all-start = ((f32[8,16,512]{2,1,0:T(8,128)}), f32[8,16,512]{2,1,0:T(8,128)S(1)}, u32[]{:S(2)}, u32[]{:S(2)}) async-start(f32[8,16,512]{2,1,0:T(8,128)} %get-tuple-element.31), calls=%async_computation | async-start | bytes 524288 | tf_op jit(solution)/shard_map/all_to_all | solution.py:479
  49.6 8.1 %collective-permute-start.6 = (f32[64,128]{1,0:T(8,128)S(1)}, f32[64,128]{1,0:T(8,128)S(1)}, u32[]{:S(2)}, u32[]{:S(2)}) collective-permute-start(f32[64,128]{1,0:T(8,128)S(1)} %get-tuple-element.32.refs_0_), channel_id=1, source_target_pairs={{0,3},{1,0},{2,1},{3,2},{4,7},{5,4},{6,5},{7,6},{8,11},{9,8},{10,9... | collective-permute-start | bytes 98312 | tf_op jit(solution)/shard_map/ppermute | solution.py:481
  53.2 5.2 %collective-permute-start.5 = (f32[64,128]{1,0:T(8,128)S(1)}, f32[64,128]{1,0:T(8,128)S(1)}, u32[]{:S(2)}, u32[]{:S(2)}) collective-permute-start(f32[64,128]{1,0:T(8,128)S(1)} %get-tuple-element.32.refs_0_), channel_id=1, source_target_pairs={{0,2},{1,3},{2,0},{3,1},{4,6},{5,7},{6,4},{7,5},{8,10},{9,11},{10,... | collective-permute-start | bytes 98312 | tf_op jit(solution)/shard_map/ppermute | solution.py:481
  55.7 5.7 %collective-permute-start.4 = (f32[64,128]{1,0:T(8,128)S(1)}, f32[64,128]{1,0:T(8,128)S(1)}, u32[]{:S(2)}, u32[]{:S(2)}) collective-permute-start(f32[64,128]{1,0:T(8,128)S(1)} %get-tuple-element.32.refs_0_), channel_id=1, source_target_pairs={{0,1},{1,2},{2,3},{3,0},{4,5},{5,6},{6,7},{7,4},{8,9},{9,10},{10,1... | collective-permute-start | bytes 98312 | tf_op jit(solution)/shard_map/ppermute | solution.py:481

commit v21 on v20

--- a/solution.py
+++ b/solution.py
@@ -214,7 +214,7 @@
 
 
 def warp_kernel(
-    cells_ref, image_ref, shift_ref, beyond_ref, across_ref, inside_ref, field, plane_ref, depth_ref,
+    cells_ref, image_ref, shift_x_ref, shift_y_ref, shift_z_ref, beyond_ref, across_ref, inside_ref, field, plane_ref, depth_ref,
     diag_depth_ref, diag_plane_ref,
     residual_ref, depth_out, plane_out,
     ahead_ref, here_ref, behind_ref, wide, bands, blocks, energy, held,
@@ -225,6 +225,7 @@
     nodes = rows // KNOT
     tiles = width // LANES
     window = (ahead_ref, here_ref, behind_ref)
+    shifts = (shift_x_ref, shift_y_ref, shift_z_ref)
     pitch = rows + 2 * TOP
     plane_rows = tiles * pitch
     block_rows = planes * plane_rows
@@ -321,7 +322,7 @@
                 for k in range(planes):
                     after = taps(k + 2)
                     place = (k, pl.ds(top, 16), pl.ds(at, LANES))
-                    sx, sy, sz = (shift_ref[(axis,) + place].astype(f32)[mine] for axis in range(3))
+                    sx, sy, sz = (ref[(0,) + place].astype(f32)[mine] for ref in shifts)
                     image = image_ref[place].astype(f32)[mine]
                     px, py, pz = sx > 0, sy > 0, sz > 0
                     ax, ay = jnp.abs(sx), jnp.abs(sy)
@@ -359,9 +360,14 @@
         sums = [joined(blocks.at[k]) for k in range(2)]
         kinds = [split_dot(plane_ref[k], sums[k], 0) for k in range(2)]
         kinds = kinds + [diag_depth_ref[0], diag_depth_ref[1]]
+        half = width // 2
         for p in range(parts):
-            for k in range(4):
-                depth_out[p, k * share : (k + 1) * share, :] = kinds[k][p * share : (p + 1) * share]
+            rows = slice(p * share, (p + 1) * share)
+            for k in range(2):
+                mine = slice(k * share, (k + 1) * share)
+                depth_out[p, mine, 0:width] = kinds[k][rows]
+                depth_out[p, mine, width : width + half] = kinds[2][rows, k * half : (k + 1) * half]
+                depth_out[p, mine, width + half :] = kinds[3][rows, 0:LANES]
         local = jnp.sum(energy[...])
         kinds = [split_dot(sums[k], depth_ref[k], 1) for k in range(2)]
         kinds = kinds + [diag_plane_ref[0], diag_plane_ref[1]]
@@ -386,7 +392,9 @@
         in_specs=[
             pl.BlockSpec((KNOT, rows, width), ahead),
             pl.BlockSpec((KNOT, rows, width), behind),
-            pl.BlockSpec((3, KNOT, rows, width), lambda i: (0, jnp.maximum(i - 1, 0), 0, 0)),
+            pl.BlockSpec((1, KNOT, rows, width), lambda i: (0, jnp.maximum(i - 1, 0), 0, 0)),
+            pl.BlockSpec((1, KNOT, rows, width), lambda i: (1, jnp.maximum(i - 1, 0), 0, 0)),
+            pl.BlockSpec((1, KNOT, rows, width), lambda i: (2, jnp.maximum(i - 1, 0), 0, 0)),
             pl.BlockSpec((KNOT, rows, LANES), ahead),
             pl.BlockSpec((KNOT, across.shape[1]), lambda i: (jnp.minimum(i, count - 1), 0)),
             pl.BlockSpec((KNOT, inside.shape[1]), lambda i: (jnp.minimum(i, count - 1), 0)),
@@ -398,12 +406,12 @@
         ],
         out_specs=[
             pl.BlockSpec((KNOT, rows, width), behind),
-            pl.BlockSpec((parts, 4 * RANK // parts, width), whole),
+            pl.BlockSpec((parts, 2 * RANK // parts, width + width // 2 + LANES), whole),
             pl.BlockSpec((nodes, 4 * RANK), flat),
         ],
         out_shape=[
             jax.ShapeDtypeStruct(cells.shape, bf16),
-            jax.ShapeDtypeStruct((parts, 4 * RANK // parts, width), f32),
+            jax.ShapeDtypeStruct((parts, 2 * RANK // parts, width + width // 2 + LANES), f32),
             jax.ShapeDtypeStruct((nodes, 4 * RANK), f32),
         ],
         scratch_shapes=[
@@ -417,7 +425,7 @@
         compiler_params=grid_params(),
         cost_estimate=pl.CostEstimate(flops=60 * cells.size, bytes_accessed=12 * cells.size, transcendentals=0),
         name="warp",
-    )(cells, image, shift, beyond, across, inside, field, plane, depth_factors, diag_depth, diag_plane)
+    )(cells, image, shift, shift, shift, beyond, across, inside, field, plane, depth_factors, diag_depth, diag_plane)
 
 
 def gather_kernel(depth_ref, *refs):
@@ -430,29 +438,31 @@
     planes = found[0]
     plane_out[...] = planes
     cells = planes.shape[0]
-    share, width = total.shape[0] // 4, total.shape[1]
+    share, width = total.shape[0] // 2, total.shape[1]
     row = lax.broadcasted_iota(jnp.int32, total.shape, 0)
     lane = lax.broadcasted_iota(jnp.int32, total.shape, 1)
     partial = planes[cells - 1, 4 * RANK - 1]
-    total = jnp.where((row >= 3 * share) & (lane >= width // 2), partial, total)
+    total = jnp.where((row >= share) & (lane >= width - LANES), partial, total)
     for p in range(depth_out.shape[0]):
         depth_out[p] = total
 
 
 def step_kernel(full_z, node_count, depth_ref, plane_ref, depth_out, plane_out):
-    parts, share, width = depth_ref.shape[0], depth_ref.shape[1] // 4, depth_ref.shape[2]
-    energy = depth_ref[0, 3 * share, width - 1]
+    parts, share, width = depth_ref.shape[0], depth_ref.shape[1] // 2, depth_out.shape[2]
+    half = width // 2
+    energy = depth_ref[0, share, width + half]
     for p in range(1, parts):
-        energy = energy + depth_ref[p, 3 * share, width - 1]
+        energy = energy + depth_ref[p, share, width + half]
     lam_depth = damping * energy / full_z
     lam_plane = damping * RANK * energy / node_count
     for p in range(parts):
         got = depth_ref[p]
-        levels = got[3 * share :, 0 : width // 2]
-        levels = jnp.concatenate([levels, levels], axis=1)
         rows = slice(p * share, (p + 1) * share)
-        depth_out[0, rows, :] = got[0:share] / (got[2 * share : 3 * share] + lam_depth + epsilon)
-        depth_out[1, rows, :] = got[share : 2 * share] / (levels + lam_depth + epsilon)
+        first, second = got[0:share], got[share:]
+        squared = jnp.concatenate([first[:, width : width + half], second[:, width : width + half]], axis=1)
+        levels = jnp.concatenate([first[:, width + half :]] * (width // LANES), axis=1)
+        depth_out[0, rows, :] = first[:, 0:width] / (squared + lam_depth + epsilon)
+        depth_out[1, rows, :] = second[:, 0:width] / (levels + lam_depth + epsilon)
     planes = plane_ref[...]
     plane_out[0] = planes[:, 0:RANK] / (planes[:, 2 * RANK : 3 * RANK] + lam_plane + epsilon)
     plane_out[1] = planes[:, RANK : 2 * RANK] / (planes[0:1, 3 * RANK :] + lam_plane + epsilon)

time: 73.6 us -> 73.2 us (level)
  no operation moved by 1% of the time
where the time goes in v21:
time: 73.2 us; the launch traced here: 72.9 us
  Pallas kernels  36.5 us (50%)
  starting transfers between devices  19.1 us (26%)
  blocking collectives  10.5 us (14%)
  waiting for transfers between devices  4.83 us (7%)
  local copies, waits for them, and re-layouts  1.12 us (2%)
  between operations  0.76 us (1%)
    pallas_call x1, Pallas kernels, warp(): pl.pallas_call(warp_kernel, grid=(count + 1,), in_specs=[pl.BlockSpec((KN...  30.1 us
    all_to_all x1, blocking collectives, local(): depth_terms = lax.all_to_all(depth_terms, 'gy', 0, 0)  10.5 us
    ppermute x3, starting transfers between devices, local(): lax.ppermute(plane_terms, 'gz', [(i, (i + hop) % n_gz) for i in range(n_g...  8.06 us
    all_to_all x1, starting transfers between devices, local(): depth_terms = lax.all_to_all(depth_terms, 'gy', 0, 0)  6.54 us
    ppermute x4, starting transfers between devices, swapped(): return lax.ppermute(part, axis, pairs + [(j, i) for i, j in pairs])  4.54 us
    ppermute x3, waiting for transfers between devices, local(): lax.ppermute(plane_terms, 'gz', [(i, (i + hop) % n_gz) for i in range(n_g...  3.76 us
    pallas_call x1, Pallas kernels, end_columns(): pl.pallas_call(columns_kernel, grid=(1,), in_specs=[pl.BlockSpec(block, f...  2.94 us
    pallas_call x1, Pallas kernels, squares(): pl.pallas_call(squares_kernel, out_shape=jax.ShapeDtypeStruct((width // L...  1.5 us
  transfers between devices with their start and end apart: 8, of which 3 were waited for; matrix products, arithmetic and copies ran while one was open for 0% of the time, Pallas kernels for 3%

profile of v21, /device:TPU:0, one launch (start us, length us, event | category | flops | bytes accessed | tf_op | source)
XLA Modules:
  0.0 72.9 jit_solution(6931409168086380029)
XLA Ops:
  0.6 0.0 copy-start
  0.6 2.9 %columns.1 = (bf16[64,128]{1,0:T(8,128)(2,1)}, bf16[64,128]{1,0:T(8,128)(2,1)}) custom-call(bf16[64,64,512]{2,1,0:T(8,128)(2,1)} %cells_ref.3, bf16[64,64,512]{2,1,0:T(8,128)(2,1)} %cells_ref.3, bf16[64,64,512]{2,1,0:T(8,128)(2,1)} %cells_ref.3, bf16[64,64,512]{2,1,0:T(8,128)(2,1)} %cells_ref.3, bf16[64,64,512]{2,1,0:T(8,128)(2,1)} %cells_ref.3, ...), custom_call_target="tpu_custom_call" | custom-call | tf_op jit(solution)/shard_map/columns/pallas_call | solution.py:71
  3.6 3.0 %collective-permute-start = (bf16[64,128]{1,0:T(8,128)(2,1)}, bf16[64,128]{1,0:T(8,128)(2,1)S(1)}, u32[]{:S(2)}, u32[]{:S(2)}) collective-permute-start(bf16[64,128]{1,0:T(8,128)(2,1)} %get-tuple-element.20), channel_id=1, source_target_pairs={{0,1},{2,3},{1,0},{3,2},{4,5},{6,7},{5,4},{7,6},{8,9},{10,11},{9,8... | collective-permute-start | bytes 49160 | tf_op jit(solution)/shard_map/ppermute | solution.py:142
  6.6 0.7 collective-permute-start.1
  7.3 0.0 copy-done
  7.3 0.2 ends.1
  7.5 1.1 %collective-permute-done.inner_ref = bf16[64,128]{1,0:T(8,128)(2,1)S(1)} collective-permute-done((bf16[64,128]{1,0:T(8,128)(2,1)}, bf16[64,128]{1,0:T(8,128)(2,1)S(1)}, u32[]{:S(2)}, u32[]{:S(2)}) %collective-permute-start) | collective-permute-done | bytes 16416 | tf_op jit(solution)/shard_map/ppermute | solution.py:142
  8.5 0.0 collective-permute-done.1.outer_ref
  8.5 0.0 copy-start.1
  8.5 0.2 rows.1
  8.7 0.0 copy-start.2
  8.7 0.0 copy-start.3
  8.7 0.1 collective-permute-start.3
  8.8 0.8 %collective-permute-start.2 = (bf16[64,640]{1,0:T(8,128)(2,1)S(1)}, bf16[64,640]{1,0:T(8,128)(2,1)S(1)}, u32[]{:S(2)}, u32[]{:S(2)}) collective-permute-start(bf16[64,640]{1,0:T(8,128)(2,1)S(1)} %get-tuple-element.24.later_ref), channel_id=1, source_target_pairs={{4,8},{12,16},{20,24},{8,4},{16,12},{24,20},{5,9},{13,17},{21,25},... | collective-permute-start | bytes 245768 | tf_op jit(solution)/shard_map/ppermute | solution.py:142
  9.6 1.1 %copy-done.1 = bf16[64,64,512]{2,1,0:T(8,128)(2,1)S(1)} copy-done((bf16[64,64,512]{2,1,0:T(8,128)(2,1)S(1)}, bf16[64,64,512]{2,1,0:T(8,128)(2,1)}, u32[]{:S(2)}) %copy-start.1) | copy-done | bytes 4194328
  10.7 1.5 %squares.1.sums = f32[4,64,128]{2,1,0:T(8,128)S(1)} custom-call(bf16[64,64,512]{2,1,0:T(8,128)(2,1)S(1)} %copy-done.1, bf16[64,640]{1,0:T(8,128)(2,1)S(1)} %get-tuple-element.24.later_ref), custom_call_target="tpu_custom_call" | custom-call | flops 6291456 | bytes 4194304 | tf_op jit(solution)/shard_map/squares/pallas_call | solution.py:167
  12.2 0.0 copy-done.2
  12.2 0.0 copy-done.3
  12.3 0.7 terms.1
  12.9 0.0 collective-permute-done.3.inside_ref
  13.0 0.0 collective-permute-done.2.across_ref
  13.0 30.1 %warp.1 = (bf16[64,64,512]{2,1,0:T(8,128)(2,1)}, f32[8,8,896]{2,1,0:T(8,128)}, f32[64,128]{1,0:T(8,128)S(1)}) custom-call(bf16[64,64,512]{2,1,0:T(8,128)(2,1)S(1)} %copy-done, bf16[64,64,512]{2,1,0:T(8,128)(2,1)S(1)} %copy-done.1, bf16[3,64,64,512]{3,2,1,0:T(8,128)(2,1)} %shift_z_ref.1, bf16[3,64,64,512]{3,2,1,0:T(8,128)(2,1)} %shift_z_ref.1, ...), custom_call_target="tpu_custom_call" | custom-call | flops 125829120 | bytes 25165824 | tf_op jit(solution)/shard_map/warp/pallas_call | solution.py:389
  43.0 6.5 %all-to-all-start = ((f32[8,8,896]{2,1,0:T(8,128)}), f32[8,8,896]{2,1,0:T(8,128)S(1)}, u32[]{:S(2)}, u32[]{:S(2)}) async-start(f32[8,8,896]{2,1,0:T(8,128)} %get-tuple-element.31), calls=%async_computation | async-start | bytes 458752 | tf_op jit(solution)/shard_map/all_to_all | solution.py:489
  49.6 3.6 %collective-permute-start.6 = (f32[64,128]{1,0:T(8,128)S(1)}, f32[64,128]{1,0:T(8,128)S(1)}, u32[]{:S(2)}, u32[]{:S(2)}) collective-permute-start(f32[64,128]{1,0:T(8,128)S(1)} %get-tuple-element.32.refs_0_), channel_id=1, source_target_pairs={{0,3},{1,0},{2,1},{3,2},{4,7},{5,4},{6,5},{7,6},{8,11},{9,8},{10,9... | collective-permute-start | bytes 98312 | tf_op jit(solution)/shard_map/ppermute | solution.py:491
  53.2 2.5 %collective-permute-start.5 = (f32[64,128]{1,0:T(8,128)S(1)}, f32[64,128]{1,0:T(8,128)S(1)}, u32[]{:S(2)}, u32[]{:S(2)}) collective-permute-start(f32[64,128]{1,0:T(8,128)S(1)} %get-tuple-element.32.refs_0_), channel_id=1, source_target_pairs={{0,2},{1,3},{2,0},{3,1},{4,6},{5,7},{6,4},{7,5},{8,10},{9,11},{10,... | collective-permute-start | bytes 98312 | tf_op jit(solution)/shard_map/ppermute | solution.py:491
  55.7 2.0 %collective-permute-start.4 = (f32[64,128]{1,0:T(8,128)S(1)}, f32[64,128]{1,0:T(8,128)S(1)}, u32[]{:S(2)}, u32[]{:S(2)}) collective-permute-start(f32[64,128]{1,0:T(8,128)S(1)} %get-tuple-element.32.refs_0_), channel_id=1, source_target_pairs={{0,1},{1,2},{2,3},{3,0},{4,5},{5,6},{6,7},{7,4},{8,9},{9,10},{10,1... | collective-permute-start | bytes 98312 | tf_op jit(solution)/shard_map/ppermute | solution.py:491
  57.6 0.0 collective-permute-done.6.refs_3_
  57.6 0.7 %collective-permute-done.5.refs_2_ = f32[64,128]{1,0:T(8,128)S(1)} collective-permute-done((f32[64,128]{1,0:T(8,128)S(1)}, f32[64,128]{1,0:T(8,128)S(1)}, u32[]{:S(2)}, u32[]{:S(2)}) %collective-permute-start.5) | collective-permute-done | bytes 32800 | tf_op jit(solution)/shard_map/ppermute | solution.py:491
  58.4 3.0 %collective-permute-done.4.refs_1_ = f32[64,128]{1,0:T(8,128)S(1)} collective-permute-done((f32[64,128]{1,0:T(8,128)S(1)}, f32[64,128]{1,0:T(8,128)S(1)}, u32[]{:S(2)}, u32[]{:S(2)}) %collective-permute-start.4) | collective-permute-done | bytes 32800 | tf_op jit(solution)/shard_map/ppermute | solution.py:491
  61.4 0.0 all-to-all-done.depth_ref
  61.4 0.1 gather.1
  61.5 10.5 %all_to_all.10.depth_ref = f32[8,8,896]{2,1,0:T(8,128)S(1)} all-to-all(f32[8,8,896]{2,1,0:T(8,128)S(1)} %get-tuple-element.33), channel_id=1, replica_groups=mesh['gy'=8,'gz'=4] {'gy'}, dimensions={0} | all-to-all | bytes 458752 | tf_op jit(solution)/shard_map/all_to_all | solution.py:502
  72.1 0.8 %steps.1 = (f32[2,32,512]{2,1,0:T(8,128)}, f32[2,64,32]{2,1,0:T(8,128)}) custom-call(f32[8,8,896]{2,1,0:T(8,128)S(1)} %all_to_all.10.depth_ref, f32[64,128]{1,0:T(8,128)S(1)} %get-tuple-element.34.plane_ref), custom_call_target="tpu_custom_call" | custom-call | tf_op jit(solution)/shard_map/steps/pallas_call | solution.py:504
Async XLA Ops:
  0.6 6.6 %copy-start = (bf16[64,64,512]{2,1,0:T(8,128)(2,1)S(1)}, bf16[64,64,512]{2,1,0:T(8,128)(2,1)}, u32[]{:S(2)}) copy-start(bf16[64,64,512]{2,1,0:T(8,128)(2,1)} %cells_ref.3) | copy-start | bytes 12582916
  3.6 5.0 %collective-permute-start = (bf16[64,128]{1,0:T(8,128)(2,1)}, bf16[64,128]{1,0:T(8,128)(2,1)S(1)}, u32[]{:S(2)}, u32[]{:S(2)}) collective-permute-start(bf16[64,128]{1,0:T(8,128)(2,1)} %get-tuple-element.20), channel_id=1, source_target_pairs={{0,1},{2,3},{1,0},{3,2},{4,5},{6,7},{5,4},{7,6},{8,9},{10,11},{9,8... | collective-permute-start | bytes 49160 | tf_op jit(solution)/shard_map/ppermute | solution.py:142
  6.6 1.9 %collective-permute-start.1 = (bf16[64,128]{1,0:T(8,128)(2,1)}, bf16[64,128]{1,0:T(8,128)(2,1)S(1)}, u32[]{:S(2)}, u32[]{:S(2)}) collective-permute-start(bf16[64,128]{1,0:T(8,128)(2,1)} %get-tuple-element.21), channel_id=1, source_target_pairs={{1,2},{2,1},{5,6},{6,5},{9,10},{10,9},{13,14},{14,13},{17,18},{18,... | collective-permute-start | bytes 49160 | tf_op jit(solution)/shard_map/ppermute | solution.py:142
  8.5 2.2 %copy-start.1 = (bf16[64,64,512]{2,1,0:T(8,128)(2,1)S(1)}, bf16[64,64,512]{2,1,0:T(8,128)(2,1)}, u32[]{:S(2)}) copy-start(bf16[64,64,512]{2,1,0:T(8,128)(2,1)} %image_ref.3) | copy-start | bytes 12582916
  8.7 3.5 %copy-start.2 = (f32[2,32,512]{2,1,0:T(8,128)S(1)}, f32[2,32,512]{2,1,0:T(8,128)}, u32[]{:S(2)}) copy-start(f32[2,32,512]{2,1,0:T(8,128)} %depth_ref.3) | copy-start | bytes 393220
  8.7 3.5 %copy-start.3 = (f32[2,32,8,8]{1,3,2,0:T(8,128)S(1)}, f32[2,32,8,8]{1,3,2,0:T(8,128)}, u32[]{:S(2)}) copy-start(f32[2,32,8,8]{1,3,2,0:T(8,128)} %param.8) | copy-start | bytes 49156
  8.7 4.2 %collective-permute-start.3 = (bf16[64,640]{1,0:T(8,128)(2,1)S(1)}, bf16[64,640]{1,0:T(8,128)(2,1)S(1)}, u32[]{:S(2)}, u32[]{:S(2)}) collective-permute-start(bf16[64,640]{1,0:T(8,128)(2,1)S(1)} %get-tuple-element.26), channel_id=1, source_target_pairs={{0,4},{8,12},{16,20},{24,28},{4,0},{12,8},{20,16},{28,24},{1,5},{9... | collective-permute-start | bytes 245768 | tf_op jit(solution)/shard_map/ppermute | solution.py:142
  8.8 4.1 %collective-permute-start.2 = (bf16[64,640]{1,0:T(8,128)(2,1)S(1)}, bf16[64,640]{1,0:T(8,128)(2,1)S(1)}, u32[]{:S(2)}, u32[]{:S(2)}) collective-permute-start(bf16[64,640]{1,0:T(8,128)(2,1)S(1)} %get-tuple-element.24.later_ref), channel_id=1, source_target_pairs={{4,8},{12,16},{20,24},{8,4},{16,12},{24,20},{5,9},{13,17},{21,25},... | collective-permute-start | bytes 245768 | tf_op jit(solution)/shard_map/ppermute | solution.py:142
  43.0 18.4 %all-to-all-start = ((f32[8,8,896]{2,1,0:T(8,128)}), f32[8,8,896]{2,1,0:T(8,128)S(1)}, u32[]{:S(2)}, u32[]{:S(2)}) async-start(f32[8,8,896]{2,1,0:T(8,128)} %get-tuple-element.31), calls=%async_computation | async-start | bytes 458752 | tf_op jit(solution)/shard_map/all_to_all | solution.py:489
  49.6 8.1 %collective-permute-start.6 = (f32[64,128]{1,0:T(8,128)S(1)}, f32[64,128]{1,0:T(8,128)S(1)}, u32[]{:S(2)}, u32[]{:S(2)}) collective-permute-start(f32[64,128]{1,0:T(8,128)S(1)} %get-tuple-element.32.refs_0_), channel_id=1, source_target_pairs={{0,3},{1,0},{2,1},{3,2},{4,7},{5,4},{6,5},{7,6},{8,11},{9,8},{10,9... | collective-permute-start | bytes 98312 | tf_op jit(solution)/shard_map/ppermute | solution.py:491
  53.2 5.2 %collective-permute-start.5 = (f32[64,128]{1,0:T(8,128)S(1)}, f32[64,128]{1,0:T(8,128)S(1)}, u32[]{:S(2)}, u32[]{:S(2)}) collective-permute-start(f32[64,128]{1,0:T(8,128)S(1)} %get-tuple-element.32.refs_0_), channel_id=1, source_target_pairs={{0,2},{1,3},{2,0},{3,1},{4,6},{5,7},{6,4},{7,5},{8,10},{9,11},{10,... | collective-permute-start | bytes 98312 | tf_op jit(solution)/shard_map/ppermute | solution.py:491
  55.7 5.7 %collective-permute-start.4 = (f32[64,128]{1,0:T(8,128)S(1)}, f32[64,128]{1,0:T(8,128)S(1)}, u32[]{:S(2)}, u32[]{:S(2)}) collective-permute-start(f32[64,128]{1,0:T(8,128)S(1)} %get-tuple-element.32.refs_0_), channel_id=1, source_target_pairs={{0,1},{1,2},{2,3},{3,0},{4,5},{5,6},{6,7},{7,4},{8,9},{9,10},{10,1... | collective-permute-start | bytes 98312 | tf_op jit(solution)/shard_map/ppermute | solution.py:491

commit v22 on v21

--- a/solution.py
+++ b/solution.py
@@ -79,13 +79,15 @@
     )(*[cells] * len(places))
 
 
-def ends_kernel(cells_ref, low_ref, high_ref):
+def ends_kernel(cells_ref, across_ref, inside_ref):
     depth, rows = cells_ref.shape[0:2]
+    odd = lax.axis_index("gy") % 2 == 1
     for x in range(0, depth, 16):
         low = [cells_ref[x + k, 0:16, :].astype(f32)[0:1] for k in range(16)]
         high = [cells_ref[x + k, rows - 16 : rows, :].astype(f32)[15:16] for k in range(16)]
-        low_ref[x : x + 16, :] = jnp.concatenate(low, axis=0).astype(bf16)
-        high_ref[x : x + 16, :] = jnp.concatenate(high, axis=0).astype(bf16)
+        low, high = jnp.concatenate(low, axis=0), jnp.concatenate(high, axis=0)
+        across_ref[x : x + 16, :] = jnp.where(odd, high, low).astype(bf16)
+        inside_ref[x : x + 16, :] = jnp.where(odd, low, high).astype(bf16)
 
 
 def ends(cells):
@@ -105,35 +107,30 @@
     return jnp.where(odd, inner, outer), jnp.where(odd, outer, inner)
 
 
-def rows_kernel(inner_ref, outer_ref, low_ref, high_ref, across_out, inside_out):
-    depth, width = low_ref.shape
-    rows = inner_ref.shape[0]
+def corners_kernel(inner_ref, outer_ref, across_out, inside_out):
+    rows, depth = inner_ref.shape[0], across_out.shape[0]
     odd = lax.axis_index("gy") % 2 == 1
     lane = lax.broadcasted_iota(jnp.int32, (depth, LANES), 1)
     pad = jnp.zeros((LANES - rows, LANES), f32)
     left, right = z_sides(inner_ref, outer_ref)
     left = jnp.transpose(jnp.concatenate([left, pad], axis=0))[0:depth]
     right = jnp.transpose(jnp.concatenate([right, pad], axis=0))[0:depth]
-    bodies, beyond = [], []
-    for row, body in ((0, low_ref), (rows - 1, high_ref)):
-        after = pltpu.roll(right, (LANES - row) % LANES, 1)
-        before = pltpu.roll(left, LANES - 1 - row, 1)
-        bodies.append(body[...].astype(f32))
-        beyond.append(jnp.where(lane == 0, after, before))
-    for out, first, second in ((across_out, 1, 0), (inside_out, 0, 1)):
-        out[:, 0:width] = jnp.where(odd, bodies[first], bodies[second]).astype(bf16)
-        out[:, width : width + LANES] = jnp.where(odd, beyond[first], beyond[second]).astype(bf16)
-
-
-def packed_rows(inner, outer, low, high):
-    depth, width = low.shape
+    low, high = (
+        jnp.where(lane == 0, pltpu.roll(right, (LANES - row) % LANES, 1), pltpu.roll(left, LANES - 1 - row, 1))
+        for row in (0, rows - 1)
+    )
+    across_out[...] = jnp.where(odd, high, low).astype(bf16)
+    inside_out[...] = jnp.where(odd, low, high).astype(bf16)
+
+
+def corners(inner, outer, depth):
     return pl.pallas_call(
-        rows_kernel,
-        out_shape=[jax.ShapeDtypeStruct((depth, width + LANES), bf16)] * 2,
+        corners_kernel,
+        out_shape=[jax.ShapeDtypeStruct((depth, LANES), bf16)] * 2,
         compiler_params=plain_params(),
-        cost_estimate=pl.CostEstimate(flops=500000 * low.size, bytes_accessed=8 * low.size, transcendentals=0),
-        name="rows",
-    )(inner, outer, low, high)
+        cost_estimate=pl.CostEstimate(flops=1 << 34, bytes_accessed=1 << 17, transcendentals=0),
+        name="corners",
+    )(inner, outer)
 
 
 def swapped(part, axis, start):
@@ -214,7 +211,8 @@
 
 
 def warp_kernel(
-    cells_ref, image_ref, shift_x_ref, shift_y_ref, shift_z_ref, beyond_ref, across_ref, inside_ref, field, plane_ref, depth_ref,
+    cells_ref, image_ref, shift_x_ref, shift_y_ref, shift_z_ref, beyond_ref, across_ref, inside_ref,
+    across_tile_ref, inside_tile_ref, field, plane_ref, depth_ref,
     diag_depth_ref, diag_plane_ref,
     residual_ref, depth_out, plane_out,
     ahead_ref, here_ref, behind_ref, wide, bands, blocks, energy, held,
@@ -248,7 +246,10 @@
     def _():
         slot = (step % 3) * block_rows
         odd = lax.axis_index("gy") % 2 == 1
-        across, inside = across_ref[...].astype(f32), inside_ref[...].astype(f32)
+        across, inside = (
+            jnp.concatenate([row[...].astype(f32), tile[...].astype(f32)], axis=1)
+            for row, tile in ((across_ref, across_tile_ref), (inside_ref, inside_tile_ref))
+        )
         low, high = jnp.where(odd, inside, across), jnp.where(odd, across, inside)
         at = lax.broadcasted_iota(jnp.int32, (2 * TOP, width + LANES), 0)
         for k in range(planes):
@@ -377,7 +378,10 @@
         plane_out[count // 2 :, 3 * RANK :] = jnp.full((count // 2, RANK), local, f32)
 
 
-def warp(cells, image, shift, beyond, across, inside, field, plane, depth_factors, diag_depth, diag_plane, parts):
+def warp(
+    cells, image, shift, beyond, across, inside, across_tile, inside_tile, field, plane, depth_factors, diag_depth,
+    diag_plane, parts
+):
     depth, rows, width = cells.shape
     nodes = plane.shape[1]
     tiles = width // LANES
@@ -398,6 +402,8 @@
             pl.BlockSpec((KNOT, rows, LANES), ahead),
             pl.BlockSpec((KNOT, across.shape[1]), lambda i: (jnp.minimum(i, count - 1), 0)),
             pl.BlockSpec((KNOT, inside.shape[1]), lambda i: (jnp.minimum(i, count - 1), 0)),
+            pl.BlockSpec((KNOT, LANES), lambda i: (jnp.minimum(i, count - 1), 0)),
+            pl.BlockSpec((KNOT, LANES), lambda i: (jnp.minimum(i, count - 1), 0)),
             pl.BlockSpec(field.shape, lambda i: (0, 0, 0, 0)),
             pl.BlockSpec(plane.shape, whole),
             pl.BlockSpec(depth_factors.shape, whole),
@@ -425,7 +431,7 @@
         compiler_params=grid_params(),
         cost_estimate=pl.CostEstimate(flops=60 * cells.size, bytes_accessed=12 * cells.size, transcendentals=0),
         name="warp",
-    )(cells, image, shift, shift, shift, beyond, across, inside, field, plane, depth_factors, diag_depth, diag_plane)
+    )(cells, image, shift, shift, shift, beyond, across, inside, across_tile, inside_tile, field, plane, depth_factors, diag_depth, diag_plane)
 
 
 def gather_kernel(depth_ref, *refs):
@@ -475,16 +481,17 @@
     inner, outer = end_columns(deformed)
     inner = swapped(inner, "gz", 0)
     outer = swapped(outer, "gz", 1)
-    low, high = ends(deformed)
-    across, inside = packed_rows(inner, outer, low, high)
-    later = across
+    across, inside = ends(deformed)
     inside = swapped(inside, "gy", 0)
     across = swapped(across, "gy", 1)
-    sums = squares(image, later)
+    across_tile, inside_tile = corners(inner, outer, deformed.shape[0])
+    sums = squares(image, across_tile)
+    inside_tile = swapped(inside_tile, "gy", 0)
+    across_tile = swapped(across_tile, "gy", 1)
     field, diag_depth, diag_plane, beyond = terms(sums, plane, depth_factors, inner, outer, deformed.shape[0])
     residual, depth_terms, plane_terms = warp(
-        deformed, image, displacement, beyond, across, inside, field, plane, depth_factors, diag_depth, diag_plane,
-        n_gy,
+        deformed, image, displacement, beyond, across, inside, across_tile, inside_tile, field, plane, depth_factors,
+        diag_depth, diag_plane, n_gy,
     )
     depth_terms = lax.all_to_all(depth_terms, "gy", 0, 0)
     others = [

time: 73.2 us -> 73.8 us (level)
  local copies, waits for them, and re-layouts: 1.12 us -> 0.02 us
  waiting for transfers between devices: 4.83 us -> 5.63 us
  starting transfers between devices: 19.1 us -> 19.9 us
    ppermute x4 -> x6, starting transfers between devices: 4.54 us -> 8 us  [swapped(): return lax.ppermute(part, axis, pairs + [(j, i) for i, j in pairs])]
    ppermute x3, starting transfers between devices: 8.06 us -> 5.96 us  [local(): lax.ppermute(plane_terms, 'gz', [(i, (i + hop) % n_gz) for i in range(n_g...]
    ppermute x3, waiting for transfers between devices: 3.76 us -> 5.62 us  [local(): lax.ppermute(plane_terms, 'gz', [(i, (i + hop) % n_gz) for i in range(n_g...]
    unnamed x8, local copies, waits for them, and re-layouts: 1.12 us -> 0.02 us
    ppermute x4 -> x6, waiting for transfers between devices: 1.06 us -> 0.02 us  [swapped(): return lax.ppermute(part, axis, pairs + [(j, i) for i, j in pairs])]
  transfers between devices with their start and end apart: 8 -> 10, of which waited for: 3 -> 3; matrix products, arithmetic and copies ran while one was open for 0% -> 0% of each run, Pallas kernels for 3% -> 4%
where the time goes in v22:
time: 73.8 us; the launch traced here: 73.5 us
  Pallas kernels  36.6 us (50%)
  starting transfers between devices  19.9 us (27%)
  blocking collectives  10.6 us (14%)
  waiting for transfers between devices  5.63 us (8%)
  between operations  0.79 us (1%)
    pallas_call x1, Pallas kernels, warp(): pl.pallas_call(warp_kernel, grid=(count + 1,), in_specs=[pl.BlockSpec((KN...  30.1 us
    all_to_all x1, blocking collectives, local(): depth_terms = lax.all_to_all(depth_terms, 'gy', 0, 0)  10.6 us
    ppermute x6, starting transfers between devices, swapped(): return lax.ppermute(part, axis, pairs + [(j, i) for i, j in pairs])  8 us
    all_to_all x1, starting transfers between devices, local(): depth_terms = lax.all_to_all(depth_terms, 'gy', 0, 0)  5.96 us
    ppermute x3, starting transfers between devices, local(): lax.ppermute(plane_terms, 'gz', [(i, (i + hop) % n_gz) for i in range(n_g...  5.96 us
    ppermute x3, waiting for transfers between devices, local(): lax.ppermute(plane_terms, 'gz', [(i, (i + hop) % n_gz) for i in range(n_g...  5.62 us
    pallas_call x1, Pallas kernels, end_columns(): pl.pallas_call(columns_kernel, grid=(1,), in_specs=[pl.BlockSpec(block, f...  2.94 us
    pallas_call x1, Pallas kernels, squares(): pl.pallas_call(squares_kernel, out_shape=jax.ShapeDtypeStruct((width // L...  1.52 us
  transfers between devices with their start and end apart: 10, of which 3 were waited for; matrix products, arithmetic and copies ran while one was open for 0% of the time, Pallas kernels for 4%

profile of v22, /device:TPU:0, one launch (start us, length us, event | category | flops | bytes accessed | tf_op | source)
XLA Modules:
  0.0 73.5 jit_solution(3348087035359096509)
XLA Ops:
  0.6 0.0 copy-start
  0.6 2.9 %columns.1 = (bf16[64,128]{1,0:T(8,128)(2,1)}, bf16[64,128]{1,0:T(8,128)(2,1)}) custom-call(bf16[64,64,512]{2,1,0:T(8,128)(2,1)} %cells_ref.3, bf16[64,64,512]{2,1,0:T(8,128)(2,1)} %cells_ref.3, bf16[64,64,512]{2,1,0:T(8,128)(2,1)} %cells_ref.3, bf16[64,64,512]{2,1,0:T(8,128)(2,1)} %cells_ref.3, bf16[64,64,512]{2,1,0:T(8,128)(2,1)} %cells_ref.3, ...), custom_call_target="tpu_custom_call" | custom-call | tf_op jit(solution)/shard_map/columns/pallas_call | solution.py:71
  3.6 3.0 %collective-permute-start = (bf16[64,128]{1,0:T(8,128)(2,1)}, bf16[64,128]{1,0:T(8,128)(2,1)S(1)}, u32[]{:S(2)}, u32[]{:S(2)}) collective-permute-start(bf16[64,128]{1,0:T(8,128)(2,1)} %get-tuple-element.20), channel_id=1, source_target_pairs={{0,1},{2,3},{1,0},{3,2},{4,5},{6,7},{5,4},{7,6},{8,9},{10,11},{9,8... | collective-permute-start | bytes 49160 | tf_op jit(solution)/shard_map/ppermute | solution.py:139
  6.6 0.7 collective-permute-start.1
  7.3 0.0 copy-done
  7.3 0.2 ends.1
  7.5 0.7 collective-permute-start.2
  8.2 0.0 copy-start.1
  8.2 2.9 %collective-permute-start.3 = (bf16[64,512]{1,0:T(8,128)(2,1)S(1)}, bf16[64,512]{1,0:T(8,128)(2,1)S(1)}, u32[]{:S(2)}, u32[]{:S(2)}) collective-permute-start(bf16[64,512]{1,0:T(8,128)(2,1)S(1)} %get-tuple-element.25), channel_id=1, source_target_pairs={{0,4},{8,12},{16,20},{24,28},{4,0},{12,8},{20,16},{28,24},{1,5},{9... | collective-permute-start | bytes 196616 | tf_op jit(solution)/shard_map/ppermute | solution.py:139
  11.1 0.0 collective-permute-done.inner_ref
  11.1 0.0 collective-permute-done.1.outer_ref
  11.1 0.2 corners.1
  11.3 0.0 copy-start.2
  11.3 0.0 copy-start.3
  11.3 0.1 collective-permute-start.5
  11.4 0.7 collective-permute-start.4
  12.0 0.0 copy-done.1
  12.1 1.5 %squares.1.sums = f32[4,64,128]{2,1,0:T(8,128)S(1)} custom-call(bf16[64,64,512]{2,1,0:T(8,128)(2,1)S(1)} %copy-done.1, bf16[64,128]{1,0:T(8,128)(2,1)S(1)} %get-tuple-element.22.later_ref), custom_call_target="tpu_custom_call" | custom-call | flops 6291456 | bytes 4194304 | tf_op jit(solution)/shard_map/squares/pallas_call | solution.py:164
  13.6 0.0 copy-done.2
  13.6 0.0 copy-done.3
  13.6 0.7 terms.1
  14.3 0.0 collective-permute-done.5.inside_tile_ref
  14.3 0.0 collective-permute-done.4.across_tile_ref
  14.3 0.0 collective-permute-done.2.across_ref
  14.3 0.0 collective-permute-done.3.inside_ref
  14.3 30.1 %warp.1 = (bf16[64,64,512]{2,1,0:T(8,128)(2,1)}, f32[8,8,896]{2,1,0:T(8,128)}, f32[64,128]{1,0:T(8,128)S(1)}) custom-call(bf16[64,64,512]{2,1,0:T(8,128)(2,1)S(1)} %copy-done, bf16[64,64,512]{2,1,0:T(8,128)(2,1)S(1)} %copy-done.1, bf16[3,64,64,512]{3,2,1,0:T(8,128)(2,1)} %shift_z_ref.1, bf16[3,64,64,512]{3,2,1,0:T(8,128)(2,1)} %shift_z_ref.1, ...), custom_call_target="tpu_custom_call" | custom-call | flops 125829120 | bytes 25165824 | tf_op jit(solution)/shard_map/warp/pallas_call | solution.py:393
  44.4 6.0 %all-to-all-start = ((f32[8,8,896]{2,1,0:T(8,128)}), f32[8,8,896]{2,1,0:T(8,128)S(1)}, u32[]{:S(2)}, u32[]{:S(2)}) async-start(f32[8,8,896]{2,1,0:T(8,128)} %get-tuple-element.31), calls=%async_computation | async-start | bytes 458752 | tf_op jit(solution)/shard_map/all_to_all | solution.py:496
  50.4 2.5 %collective-permute-start.8 = (f32[64,128]{1,0:T(8,128)S(1)}, f32[64,128]{1,0:T(8,128)S(1)}, u32[]{:S(2)}, u32[]{:S(2)}) collective-permute-start(f32[64,128]{1,0:T(8,128)S(1)} %get-tuple-element.32.refs_0_), channel_id=1, source_target_pairs={{0,3},{1,0},{2,1},{3,2},{4,7},{5,4},{6,5},{7,6},{8,11},{9,8},{10,9... | collective-permute-start | bytes 98312 | tf_op jit(solution)/shard_map/ppermute | solution.py:498
  52.9 3.4 %collective-permute-start.7 = (f32[64,128]{1,0:T(8,128)S(1)}, f32[64,128]{1,0:T(8,128)S(1)}, u32[]{:S(2)}, u32[]{:S(2)}) collective-permute-start(f32[64,128]{1,0:T(8,128)S(1)} %get-tuple-element.32.refs_0_), channel_id=1, source_target_pairs={{0,2},{1,3},{2,0},{3,1},{4,6},{5,7},{6,4},{7,5},{8,10},{9,11},{10,... | collective-permute-start | bytes 98312 | tf_op jit(solution)/shard_map/ppermute | solution.py:498
  56.3 0.1 collective-permute-start.6
  56.4 0.5 collective-permute-done.8.refs_3_
  56.9 2.6 %collective-permute-done.7.refs_2_ = f32[64,128]{1,0:T(8,128)S(1)} collective-permute-done((f32[64,128]{1,0:T(8,128)S(1)}, f32[64,128]{1,0:T(8,128)S(1)}, u32[]{:S(2)}, u32[]{:S(2)}) %collective-permute-start.7) | collective-permute-done | bytes 32800 | tf_op jit(solution)/shard_map/ppermute | solution.py:498
  59.4 2.5 %collective-permute-done.6.refs_1_ = f32[64,128]{1,0:T(8,128)S(1)} collective-permute-done((f32[64,128]{1,0:T(8,128)S(1)}, f32[64,128]{1,0:T(8,128)S(1)}, u32[]{:S(2)}, u32[]{:S(2)}) %collective-permute-start.6) | collective-permute-done | bytes 32800 | tf_op jit(solution)/shard_map/ppermute | solution.py:498
  62.0 0.0 all-to-all-done.depth_ref
  62.0 0.1 gather.1
  62.1 10.6 %all_to_all.10.depth_ref = f32[8,8,896]{2,1,0:T(8,128)S(1)} all-to-all(f32[8,8,896]{2,1,0:T(8,128)S(1)} %get-tuple-element.33), channel_id=1, replica_groups=mesh['gy'=8,'gz'=4] {'gy'}, dimensions={0} | all-to-all | bytes 458752 | tf_op jit(solution)/shard_map/all_to_all | solution.py:509
  72.7 0.8 %steps.1 = (f32[2,32,512]{2,1,0:T(8,128)}, f32[2,64,32]{2,1,0:T(8,128)}) custom-call(f32[8,8,896]{2,1,0:T(8,128)S(1)} %all_to_all.10.depth_ref, f32[64,128]{1,0:T(8,128)S(1)} %get-tuple-element.34.plane_ref), custom_call_target="tpu_custom_call" | custom-call | tf_op jit(solution)/shard_map/steps/pallas_call | solution.py:511
Async XLA Ops:
  0.6 6.6 %copy-start = (bf16[64,64,512]{2,1,0:T(8,128)(2,1)S(1)}, bf16[64,64,512]{2,1,0:T(8,128)(2,1)}, u32[]{:S(2)}) copy-start(bf16[64,64,512]{2,1,0:T(8,128)(2,1)} %cells_ref.3) | copy-start | bytes 12582916
  3.6 7.5 %collective-permute-start = (bf16[64,128]{1,0:T(8,128)(2,1)}, bf16[64,128]{1,0:T(8,128)(2,1)S(1)}, u32[]{:S(2)}, u32[]{:S(2)}) collective-permute-start(bf16[64,128]{1,0:T(8,128)(2,1)} %get-tuple-element.20), channel_id=1, source_target_pairs={{0,1},{2,3},{1,0},{3,2},{4,5},{6,7},{5,4},{7,6},{8,9},{10,11},{9,8... | collective-permute-start | bytes 49160 | tf_op jit(solution)/shard_map/ppermute | solution.py:139
  6.6 4.5 %collective-permute-start.1 = (bf16[64,128]{1,0:T(8,128)(2,1)}, bf16[64,128]{1,0:T(8,128)(2,1)S(1)}, u32[]{:S(2)}, u32[]{:S(2)}) collective-permute-start(bf16[64,128]{1,0:T(8,128)(2,1)} %get-tuple-element.21), channel_id=1, source_target_pairs={{1,2},{2,1},{5,6},{6,5},{9,10},{10,9},{13,14},{14,13},{17,18},{18,... | collective-permute-start | bytes 49160 | tf_op jit(solution)/shard_map/ppermute | solution.py:139
  7.5 6.8 %collective-permute-start.2 = (bf16[64,512]{1,0:T(8,128)(2,1)S(1)}, bf16[64,512]{1,0:T(8,128)(2,1)S(1)}, u32[]{:S(2)}, u32[]{:S(2)}) collective-permute-start(bf16[64,512]{1,0:T(8,128)(2,1)S(1)} %get-tuple-element.24), channel_id=1, source_target_pairs={{4,8},{12,16},{20,24},{8,4},{16,12},{24,20},{5,9},{13,17},{21,25},... | collective-permute-start | bytes 196616 | tf_op jit(solution)/shard_map/ppermute | solution.py:139
  8.2 3.9 %copy-start.1 = (bf16[64,64,512]{2,1,0:T(8,128)(2,1)S(1)}, bf16[64,64,512]{2,1,0:T(8,128)(2,1)}, u32[]{:S(2)}) copy-start(bf16[64,64,512]{2,1,0:T(8,128)(2,1)} %image_ref.3) | copy-start | bytes 12582916
  8.2 6.2 %collective-permute-start.3 = (bf16[64,512]{1,0:T(8,128)(2,1)S(1)}, bf16[64,512]{1,0:T(8,128)(2,1)S(1)}, u32[]{:S(2)}, u32[]{:S(2)}) collective-permute-start(bf16[64,512]{1,0:T(8,128)(2,1)S(1)} %get-tuple-element.25), channel_id=1, source_target_pairs={{0,4},{8,12},{16,20},{24,28},{4,0},{12,8},{20,16},{28,24},{1,5},{9... | collective-permute-start | bytes 196616 | tf_op jit(solution)/shard_map/ppermute | solution.py:139
  11.3 2.3 %copy-start.2 = (f32[2,32,512]{2,1,0:T(8,128)S(1)}, f32[2,32,512]{2,1,0:T(8,128)}, u32[]{:S(2)}) copy-start(f32[2,32,512]{2,1,0:T(8,128)} %depth_ref.3) | copy-start | bytes 393220
  11.3 2.3 %copy-start.3 = (f32[2,32,8,8]{1,3,2,0:T(8,128)S(1)}, f32[2,32,8,8]{1,3,2,0:T(8,128)}, u32[]{:S(2)}) copy-start(f32[2,32,8,8]{1,3,2,0:T(8,128)} %param.8) | copy-start | bytes 49156
  11.3 3.0 %collective-permute-start.5 = (bf16[64,128]{1,0:T(8,128)(2,1)S(1)}, bf16[64,128]{1,0:T(8,128)(2,1)S(1)}, u32[]{:S(2)}, u32[]{:S(2)}) collective-permute-start(bf16[64,128]{1,0:T(8,128)(2,1)S(1)} %get-tuple-element.26), channel_id=1, source_target_pairs={{0,4},{8,12},{16,20},{24,28},{4,0},{12,8},{20,16},{28,24},{1,5},{9... | collective-permute-start | bytes 49160 | tf_op jit(solution)/shard_map/ppermute | solution.py:139
  11.4 2.9 %collective-permute-start.4 = (bf16[64,128]{1,0:T(8,128)(2,1)S(1)}, bf16[64,128]{1,0:T(8,128)(2,1)S(1)}, u32[]{:S(2)}, u32[]{:S(2)}) collective-permute-start(bf16[64,128]{1,0:T(8,128)(2,1)S(1)} %get-tuple-element.22.later_ref), channel_id=1, source_target_pairs={{4,8},{12,16},{20,24},{8,4},{16,12},{24,20},{5,9},{13,17},{21,25},... | collective-permute-start | bytes 49160 | tf_op jit(solution)/shard_map/ppermute | solution.py:139
  44.4 17.5 %all-to-all-start = ((f32[8,8,896]{2,1,0:T(8,128)}), f32[8,8,896]{2,1,0:T(8,128)S(1)}, u32[]{:S(2)}, u32[]{:S(2)}) async-start(f32[8,8,896]{2,1,0:T(8,128)} %get-tuple-element.31), calls=%async_computation | async-start | bytes 458752 | tf_op jit(solution)/shard_map/all_to_all | solution.py:496
  50.4 6.5 %collective-permute-start.8 = (f32[64,128]{1,0:T(8,128)S(1)}, f32[64,128]{1,0:T(8,128)S(1)}, u32[]{:S(2)}, u32[]{:S(2)}) collective-permute-start(f32[64,128]{1,0:T(8,128)S(1)} %get-tuple-element.32.refs_0_), channel_id=1, source_target_pairs={{0,3},{1,0},{2,1},{3,2},{4,7},{5,4},{6,5},{7,6},{8,11},{9,8},{10,9... | collective-permute-start | bytes 98312 | tf_op jit(solution)/shard_map/ppermute | solution.py:498
  52.9 6.6 %collective-permute-start.7 = (f32[64,128]{1,0:T(8,128)S(1)}, f32[64,128]{1,0:T(8,128)S(1)}, u32[]{:S(2)}, u32[]{:S(2)}) collective-permute-start(f32[64,128]{1,0:T(8,128)S(1)} %get-tuple-element.32.refs_0_), channel_id=1, source_target_pairs={{0,2},{1,3},{2,0},{3,1},{4,6},{5,7},{6,4},{7,5},{8,10},{9,11},{10,... | collective-permute-start | bytes 98312 | tf_op jit(solution)/shard_map/ppermute | solution.py:498
  56.3 5.7 %collective-permute-start.6 = (f32[64,128]{1,0:T(8,128)S(1)}, f32[64,128]{1,0:T(8,128)S(1)}, u32[]{:S(2)}, u32[]{:S(2)}) collective-permute-start(f32[64,128]{1,0:T(8,128)S(1)} %get-tuple-element.32.refs_0_), channel_id=1, source_target_pairs={{0,1},{1,2},{2,3},{3,0},{4,5},{5,6},{6,7},{7,4},{8,9},{9,10},{10,1... | collective-permute-start | bytes 98312 | tf_op jit(solution)/shard_map/ppermute | solution.py:498

commit v23 on v22

--- a/solution.py
+++ b/solution.py
@@ -495,7 +495,7 @@
     )
     depth_terms = lax.all_to_all(depth_terms, "gy", 0, 0)
     others = [
-        lax.ppermute(plane_terms, "gz", [(i, (i + hop) % n_gz) for i in range(n_gz)]) for hop in range(1, n_gz)
+        lax.ppermute(plane_terms, "gz", [(i, i ^ hop) for i in range(n_gz)]) for hop in range(1, n_gz)
     ]
     depth_terms, plane_terms = pl.pallas_call(
         gather_kernel,

time: 73.8 us -> 72 us (0.976)
  waiting for transfers between devices: 5.63 us -> 3.93 us
    ppermute x3, waiting for transfers between devices: 5.62 us -> 3.91 us  [local(): lax.ppermute(plane_terms, 'gz', [(i, i ^ hop) for i in range(n_gz)])]
  transfers between devices with their start and end apart: 10 -> 10, of which waited for: 3 -> 2; matrix products, arithmetic and copies ran while one was open for 0% -> 0% of each run, Pallas kernels for 4% -> 4%
where the time goes in v23:
time: 72 us; the launch traced here: 71.7 us
  Pallas kernels  36.6 us (51%)
  starting transfers between devices  19.8 us (28%)
  blocking collectives  10.6 us (15%)
  waiting for transfers between devices  3.93 us (5%)
  between operations  0.79 us (1%)
    pallas_call x1, Pallas kernels, warp(): pl.pallas_call(warp_kernel, grid=(count + 1,), in_specs=[pl.BlockSpec((KN...  30.1 us
    all_to_all x1, blocking collectives, local(): depth_terms = lax.all_to_all(depth_terms, 'gy', 0, 0)  10.6 us
    ppermute x6, starting transfers between devices, swapped(): return lax.ppermute(part, axis, pairs + [(j, i) for i, j in pairs])  8 us
    all_to_all x1, starting transfers between devices, local(): depth_terms = lax.all_to_all(depth_terms, 'gy', 0, 0)  5.96 us
    ppermute x3, starting transfers between devices, local(): lax.ppermute(plane_terms, 'gz', [(i, i ^ hop) for i in range(n_gz)])  5.86 us
    ppermute x3, waiting for transfers between devices, local(): lax.ppermute(plane_terms, 'gz', [(i, i ^ hop) for i in range(n_gz)])  3.91 us
    pallas_call x1, Pallas kernels, end_columns(): pl.pallas_call(columns_kernel, grid=(1,), in_specs=[pl.BlockSpec(block, f...  2.94 us
    pallas_call x1, Pallas kernels, squares(): pl.pallas_call(squares_kernel, out_shape=jax.ShapeDtypeStruct((width // L...  1.52 us
  transfers between devices with their start and end apart: 10, of which 2 were waited for; matrix products, arithmetic and copies ran while one was open for 0% of the time, Pallas kernels for 4%

profile of v23, /device:TPU:0, one launch (start us, length us, event | category | flops | bytes accessed | tf_op | source)
XLA Modules:
  0.0 71.7 jit_solution(8794177845504861126)
XLA Ops:
  0.6 0.0 copy-start
  0.6 2.9 %columns.1 = (bf16[64,128]{1,0:T(8,128)(2,1)}, bf16[64,128]{1,0:T(8,128)(2,1)}) custom-call(bf16[64,64,512]{2,1,0:T(8,128)(2,1)} %cells_ref.3, bf16[64,64,512]{2,1,0:T(8,128)(2,1)} %cells_ref.3, bf16[64,64,512]{2,1,0:T(8,128)(2,1)} %cells_ref.3, bf16[64,64,512]{2,1,0:T(8,128)(2,1)} %cells_ref.3, bf16[64,64,512]{2,1,0:T(8,128)(2,1)} %cells_ref.3, ...), custom_call_target="tpu_custom_call" | custom-call | tf_op jit(solution)/shard_map/columns/pallas_call | solution.py:71
  3.6 3.0 %collective-permute-start = (bf16[64,128]{1,0:T(8,128)(2,1)}, bf16[64,128]{1,0:T(8,128)(2,1)S(1)}, u32[]{:S(2)}, u32[]{:S(2)}) collective-permute-start(bf16[64,128]{1,0:T(8,128)(2,1)} %get-tuple-element.20), channel_id=1, source_target_pairs={{0,1},{2,3},{1,0},{3,2},{4,5},{6,7},{5,4},{7,6},{8,9},{10,11},{9,8... | collective-permute-start | bytes 49160 | tf_op jit(solution)/shard_map/ppermute | solution.py:139
  6.6 0.7 collective-permute-start.1
  7.3 0.0 copy-done
  7.3 0.2 ends.1
  7.5 0.7 collective-permute-start.2
  8.2 0.0 copy-start.1
  8.2 2.9 %collective-permute-start.3 = (bf16[64,512]{1,0:T(8,128)(2,1)S(1)}, bf16[64,512]{1,0:T(8,128)(2,1)S(1)}, u32[]{:S(2)}, u32[]{:S(2)}) collective-permute-start(bf16[64,512]{1,0:T(8,128)(2,1)S(1)} %get-tuple-element.25), channel_id=1, source_target_pairs={{0,4},{8,12},{16,20},{24,28},{4,0},{12,8},{20,16},{28,24},{1,5},{9... | collective-permute-start | bytes 196616 | tf_op jit(solution)/shard_map/ppermute | solution.py:139
  11.1 0.0 collective-permute-done.inner_ref
  11.1 0.0 collective-permute-done.1.outer_ref
  11.1 0.2 corners.1
  11.3 0.0 copy-start.2
  11.3 0.0 copy-start.3
  11.3 0.1 collective-permute-start.5
  11.4 0.7 collective-permute-start.4
  12.0 0.0 copy-done.1
  12.1 1.5 %squares.1.sums = f32[4,64,128]{2,1,0:T(8,128)S(1)} custom-call(bf16[64,64,512]{2,1,0:T(8,128)(2,1)S(1)} %copy-done.1, bf16[64,128]{1,0:T(8,128)(2,1)S(1)} %get-tuple-element.22.later_ref), custom_call_target="tpu_custom_call" | custom-call | flops 6291456 | bytes 4194304 | tf_op jit(solution)/shard_map/squares/pallas_call | solution.py:164
  13.6 0.0 copy-done.2
  13.6 0.0 copy-done.3
  13.6 0.7 terms.1
  14.3 0.0 collective-permute-done.5.inside_tile_ref
  14.3 0.0 collective-permute-done.4.across_tile_ref
  14.3 0.0 collective-permute-done.2.across_ref
  14.3 0.0 collective-permute-done.3.inside_ref
  14.3 30.1 %warp.1 = (bf16[64,64,512]{2,1,0:T(8,128)(2,1)}, f32[8,8,896]{2,1,0:T(8,128)}, f32[64,128]{1,0:T(8,128)S(1)}) custom-call(bf16[64,64,512]{2,1,0:T(8,128)(2,1)S(1)} %copy-done, bf16[64,64,512]{2,1,0:T(8,128)(2,1)S(1)} %copy-done.1, bf16[3,64,64,512]{3,2,1,0:T(8,128)(2,1)} %shift_z_ref.1, bf16[3,64,64,512]{3,2,1,0:T(8,128)(2,1)} %shift_z_ref.1, ...), custom_call_target="tpu_custom_call" | custom-call | flops 125829120 | bytes 25165824 | tf_op jit(solution)/shard_map/warp/pallas_call | solution.py:393
  44.4 6.0 %all-to-all-start = ((f32[8,8,896]{2,1,0:T(8,128)}), f32[8,8,896]{2,1,0:T(8,128)S(1)}, u32[]{:S(2)}, u32[]{:S(2)}) async-start(f32[8,8,896]{2,1,0:T(8,128)} %get-tuple-element.31), calls=%async_computation | async-start | bytes 458752 | tf_op jit(solution)/shard_map/all_to_all | solution.py:496
  50.4 2.5 %collective-permute-start.8 = (f32[64,128]{1,0:T(8,128)S(1)}, f32[64,128]{1,0:T(8,128)S(1)}, u32[]{:S(2)}, u32[]{:S(2)}) collective-permute-start(f32[64,128]{1,0:T(8,128)S(1)} %get-tuple-element.32.refs_0_), channel_id=1, source_target_pairs={{0,3},{1,2},{2,1},{3,0},{4,7},{5,6},{6,5},{7,4},{8,11},{9,10},{10,... | collective-permute-start | bytes 98312 | tf_op jit(solution)/shard_map/ppermute | solution.py:498
  52.9 3.4 %collective-permute-start.7 = (f32[64,128]{1,0:T(8,128)S(1)}, f32[64,128]{1,0:T(8,128)S(1)}, u32[]{:S(2)}, u32[]{:S(2)}) collective-permute-start(f32[64,128]{1,0:T(8,128)S(1)} %get-tuple-element.32.refs_0_), channel_id=1, source_target_pairs={{0,2},{1,3},{2,0},{3,1},{4,6},{5,7},{6,4},{7,5},{8,10},{9,11},{10,... | collective-permute-start | bytes 98312 | tf_op jit(solution)/shard_map/ppermute | solution.py:498
  56.3 0.0 collective-permute-start.6
  56.3 0.0 collective-permute-done.8.refs_3_
  56.3 3.2 %collective-permute-done.7.refs_2_ = f32[64,128]{1,0:T(8,128)S(1)} collective-permute-done((f32[64,128]{1,0:T(8,128)S(1)}, f32[64,128]{1,0:T(8,128)S(1)}, u32[]{:S(2)}, u32[]{:S(2)}) %collective-permute-start.7) | collective-permute-done | bytes 32800 | tf_op jit(solution)/shard_map/ppermute | solution.py:498
  59.4 0.7 %collective-permute-done.6.refs_1_ = f32[64,128]{1,0:T(8,128)S(1)} collective-permute-done((f32[64,128]{1,0:T(8,128)S(1)}, f32[64,128]{1,0:T(8,128)S(1)}, u32[]{:S(2)}, u32[]{:S(2)}) %collective-permute-start.6) | collective-permute-done | bytes 32800 | tf_op jit(solution)/shard_map/ppermute | solution.py:498
  60.2 0.0 all-to-all-done.depth_ref
  60.2 0.1 gather.1
  60.3 10.6 %all_to_all.10.depth_ref = f32[8,8,896]{2,1,0:T(8,128)S(1)} all-to-all(f32[8,8,896]{2,1,0:T(8,128)S(1)} %get-tuple-element.33), channel_id=1, replica_groups=mesh['gy'=8,'gz'=4] {'gy'}, dimensions={0} | all-to-all | bytes 458752 | tf_op jit(solution)/shard_map/all_to_all | solution.py:509
  70.9 0.8 %steps.1 = (f32[2,32,512]{2,1,0:T(8,128)}, f32[2,64,32]{2,1,0:T(8,128)}) custom-call(f32[8,8,896]{2,1,0:T(8,128)S(1)} %all_to_all.10.depth_ref, f32[64,128]{1,0:T(8,128)S(1)} %get-tuple-element.34.plane_ref), custom_call_target="tpu_custom_call" | custom-call | tf_op jit(solution)/shard_map/steps/pallas_call | solution.py:511
Async XLA Ops:
  0.6 6.6 %copy-start = (bf16[64,64,512]{2,1,0:T(8,128)(2,1)S(1)}, bf16[64,64,512]{2,1,0:T(8,128)(2,1)}, u32[]{:S(2)}) copy-start(bf16[64,64,512]{2,1,0:T(8,128)(2,1)} %cells_ref.3) | copy-start | bytes 12582916
  3.6 7.5 %collective-permute-start = (bf16[64,128]{1,0:T(8,128)(2,1)}, bf16[64,128]{1,0:T(8,128)(2,1)S(1)}, u32[]{:S(2)}, u32[]{:S(2)}) collective-permute-start(bf16[64,128]{1,0:T(8,128)(2,1)} %get-tuple-element.20), channel_id=1, source_target_pairs={{0,1},{2,3},{1,0},{3,2},{4,5},{6,7},{5,4},{7,6},{8,9},{10,11},{9,8... | collective-permute-start | bytes 49160 | tf_op jit(solution)/shard_map/ppermute | solution.py:139
  6.6 4.5 %collective-permute-start.1 = (bf16[64,128]{1,0:T(8,128)(2,1)}, bf16[64,128]{1,0:T(8,128)(2,1)S(1)}, u32[]{:S(2)}, u32[]{:S(2)}) collective-permute-start(bf16[64,128]{1,0:T(8,128)(2,1)} %get-tuple-element.21), channel_id=1, source_target_pairs={{1,2},{2,1},{5,6},{6,5},{9,10},{10,9},{13,14},{14,13},{17,18},{18,... | collective-permute-start | bytes 49160 | tf_op jit(solution)/shard_map/ppermute | solution.py:139
  7.5 6.8 %collective-permute-start.2 = (bf16[64,512]{1,0:T(8,128)(2,1)S(1)}, bf16[64,512]{1,0:T(8,128)(2,1)S(1)}, u32[]{:S(2)}, u32[]{:S(2)}) collective-permute-start(bf16[64,512]{1,0:T(8,128)(2,1)S(1)} %get-tuple-element.24), channel_id=1, source_target_pairs={{4,8},{12,16},{20,24},{8,4},{16,12},{24,20},{5,9},{13,17},{21,25},... | collective-permute-start | bytes 196616 | tf_op jit(solution)/shard_map/ppermute | solution.py:139
  8.2 3.9 %copy-start.1 = (bf16[64,64,512]{2,1,0:T(8,128)(2,1)S(1)}, bf16[64,64,512]{2,1,0:T(8,128)(2,1)}, u32[]{:S(2)}) copy-start(bf16[64,64,512]{2,1,0:T(8,128)(2,1)} %image_ref.3) | copy-start | bytes 12582916
  8.2 6.2 %collective-permute-start.3 = (bf16[64,512]{1,0:T(8,128)(2,1)S(1)}, bf16[64,512]{1,0:T(8,128)(2,1)S(1)}, u32[]{:S(2)}, u32[]{:S(2)}) collective-permute-start(bf16[64,512]{1,0:T(8,128)(2,1)S(1)} %get-tuple-element.25), channel_id=1, source_target_pairs={{0,4},{8,12},{16,20},{24,28},{4,0},{12,8},{20,16},{28,24},{1,5},{9... | collective-permute-start | bytes 196616 | tf_op jit(solution)/shard_map/ppermute | solution.py:139
  11.3 2.3 %copy-start.2 = (f32[2,32,512]{2,1,0:T(8,128)S(1)}, f32[2,32,512]{2,1,0:T(8,128)}, u32[]{:S(2)}) copy-start(f32[2,32,512]{2,1,0:T(8,128)} %depth_ref.3) | copy-start | bytes 393220
  11.3 2.3 %copy-start.3 = (f32[2,32,8,8]{1,3,2,0:T(8,128)S(1)}, f32[2,32,8,8]{1,3,2,0:T(8,128)}, u32[]{:S(2)}) copy-start(f32[2,32,8,8]{1,3,2,0:T(8,128)} %param.8) | copy-start | bytes 49156
  11.3 3.0 %collective-permute-start.5 = (bf16[64,128]{1,0:T(8,128)(2,1)S(1)}, bf16[64,128]{1,0:T(8,128)(2,1)S(1)}, u32[]{:S(2)}, u32[]{:S(2)}) collective-permute-start(bf16[64,128]{1,0:T(8,128)(2,1)S(1)} %get-tuple-element.26), channel_id=1, source_target_pairs={{0,4},{8,12},{16,20},{24,28},{4,0},{12,8},{20,16},{28,24},{1,5},{9... | collective-permute-start | bytes 49160 | tf_op jit(solution)/shard_map/ppermute | solution.py:139
  11.4 2.9 %collective-permute-start.4 = (bf16[64,128]{1,0:T(8,128)(2,1)S(1)}, bf16[64,128]{1,0:T(8,128)(2,1)S(1)}, u32[]{:S(2)}, u32[]{:S(2)}) collective-permute-start(bf16[64,128]{1,0:T(8,128)(2,1)S(1)} %get-tuple-element.22.later_ref), channel_id=1, source_target_pairs={{4,8},{12,16},{20,24},{8,4},{16,12},{24,20},{5,9},{13,17},{21,25},... | collective-permute-start | bytes 49160 | tf_op jit(solution)/shard_map/ppermute | solution.py:139
  44.4 15.7 %all-to-all-start = ((f32[8,8,896]{2,1,0:T(8,128)}), f32[8,8,896]{2,1,0:T(8,128)S(1)}, u32[]{:S(2)}, u32[]{:S(2)}) async-start(f32[8,8,896]{2,1,0:T(8,128)} %get-tuple-element.31), calls=%async_computation | async-start | bytes 458752 | tf_op jit(solution)/shard_map/all_to_all | solution.py:496
  50.4 5.9 %collective-permute-start.8 = (f32[64,128]{1,0:T(8,128)S(1)}, f32[64,128]{1,0:T(8,128)S(1)}, u32[]{:S(2)}, u32[]{:S(2)}) collective-permute-start(f32[64,128]{1,0:T(8,128)S(1)} %get-tuple-element.32.refs_0_), channel_id=1, source_target_pairs={{0,3},{1,2},{2,1},{3,0},{4,7},{5,6},{6,5},{7,4},{8,11},{9,10},{10,... | collective-permute-start | bytes 98312 | tf_op jit(solution)/shard_map/ppermute | solution.py:498
  52.9 6.6 %collective-permute-start.7 = (f32[64,128]{1,0:T(8,128)S(1)}, f32[64,128]{1,0:T(8,128)S(1)}, u32[]{:S(2)}, u32[]{:S(2)}) collective-permute-start(f32[64,128]{1,0:T(8,128)S(1)} %get-tuple-element.32.refs_0_), channel_id=1, source_target_pairs={{0,2},{1,3},{2,0},{3,1},{4,6},{5,7},{6,4},{7,5},{8,10},{9,11},{10,... | collective-permute-start | bytes 98312 | tf_op jit(solution)/shard_map/ppermute | solution.py:498
  56.3 3.9 %collective-permute-start.6 = (f32[64,128]{1,0:T(8,128)S(1)}, f32[64,128]{1,0:T(8,128)S(1)}, u32[]{:S(2)}, u32[]{:S(2)}) collective-permute-start(f32[64,128]{1,0:T(8,128)S(1)} %get-tuple-element.32.refs_0_), channel_id=1, source_target_pairs={{0,1},{1,0},{2,3},{3,2},{4,5},{5,4},{6,7},{7,6},{8,9},{9,8},{10,11... | collective-permute-start | bytes 98312 | tf_op jit(solution)/shard_map/ppermute | solution.py:498

commit v24 on v23

--- a/solution.py
+++ b/solution.py
@@ -34,10 +34,6 @@
 
 def joined(ref):
     return jnp.concatenate([ref[tile] for tile in range(ref.shape[0])], axis=1)
-
-
-def grid_params():
-    return pltpu.CompilerParams(dimension_semantics=("arbitrary",), vmem_limit_bytes=40000000)
 
 
 def plain_params():
@@ -211,11 +207,12 @@
 
 
 def warp_kernel(
-    cells_ref, image_ref, shift_x_ref, shift_y_ref, shift_z_ref, beyond_ref, across_ref, inside_ref,
+    cells_ref, image_hbm, shift_hbm, beyond_ref, across_ref, inside_ref,
     across_tile_ref, inside_tile_ref, field, plane_ref, depth_ref,
     diag_depth_ref, diag_plane_ref,
-    residual_ref, depth_out, plane_out,
+    residual_hbm, depth_out, plane_out,
     ahead_ref, here_ref, behind_ref, wide, bands, blocks, energy, held,
+    image_ref, shift_ref, residual_ref, got, sent,
 ):
     step = pl.program_id(0)
     last = pl.num_programs(0) - 1
@@ -223,7 +220,6 @@
     nodes = rows // KNOT
     tiles = width // LANES
     window = (ahead_ref, here_ref, behind_ref)
-    shifts = (shift_x_ref, shift_y_ref, shift_z_ref)
     pitch = rows + 2 * TOP
     plane_rows = tiles * pitch
     block_rows = planes * plane_rows
@@ -241,6 +237,23 @@
         energy[...] = jnp.zeros_like(energy)
         for c in range(3):
             window[c][3 * block_rows - plane_rows : 3 * block_rows, :] = jnp.zeros((plane_rows, LANES), f32)
+
+    def fetched(n):
+        slot, part = n % 2, pl.ds(n * planes, planes)
+        copies = [
+            pltpu.make_async_copy(shift_hbm.at[axis, part], shift_ref.at[slot, axis], got.at[slot, axis])
+            for axis in range(3)
+        ]
+        return copies + [pltpu.make_async_copy(image_hbm.at[part], image_ref.at[slot], got.at[slot, 3])]
+
+    def leaving(n):
+        slot, part = n % 2, pl.ds(n * planes, planes)
+        return pltpu.make_async_copy(residual_ref.at[slot], residual_hbm.at[part], sent.at[slot])
+
+    @pl.when(step < last)
+    def _():
+        for copy in fetched(step):
+            copy.start()
 
     @pl.when(step < last)
     def _():
@@ -291,6 +304,15 @@
 
     @pl.when(step > 0)
     def _():
+        block = step - 1
+        here_slot = block % 2
+        for copy in fetched(block):
+            copy.wait()
+
+        @pl.when(block > 1)
+        def _():
+            leaving(block - 2).wait()
+
         mid = (step + 2) % 3
         first_rows = (
             jnp.where(mid == 0, 3, mid) * block_rows - plane_rows,
@@ -323,8 +345,8 @@
                 for k in range(planes):
                     after = taps(k + 2)
                     place = (k, pl.ds(top, 16), pl.ds(at, LANES))
-                    sx, sy, sz = (ref[(0,) + place].astype(f32)[mine] for ref in shifts)
-                    image = image_ref[place].astype(f32)[mine]
+                    sx, sy, sz = (shift_ref[(here_slot, axis) + place].astype(f32)[mine] for axis in range(3))
+                    image = image_ref[(here_slot,) + place].astype(f32)[mine]
                     px, py, pz = sx > 0, sy > 0, sz > 0
                     ax, ay = jnp.abs(sx), jnp.abs(sy)
 
@@ -343,7 +365,7 @@
                     if half == 0:
                         held[k] = misfit
                     else:
-                        residual_ref[place] = jnp.concatenate([held[k], misfit], axis=0).astype(bf16)
+                        residual_ref[(here_slot,) + place] = jnp.concatenate([held[k], misfit], axis=0).astype(bf16)
                     by_image = by_image + misfit * image
                     plain = plain + misfit
                     total = total + misfit * misfit
@@ -352,7 +374,8 @@
                     blocks[k, tile, pl.ds(node, 1), :] = jnp.sum(value, axis=0, keepdims=True)
             return total
 
-        energy[...] = lax.fori_loop(0, (rows // 16) * tiles, one, energy[...], unroll=2)
+        energy[...] = lax.fori_loop(0, (rows // 16) * tiles, one, energy[...])
+        leaving(block).start()
 
     @pl.when(step == last)
     def _():
@@ -376,6 +399,8 @@
             plane_out[:, k * RANK : (k + 1) * RANK] = kinds[k]
         count = plane_out.shape[0]
         plane_out[count // 2 :, 3 * RANK :] = jnp.full((count // 2, RANK), local, f32)
+        leaving(last - 2).wait()
+        leaving(last - 1).wait()
 
 
 def warp(
@@ -386,7 +411,6 @@
     nodes = plane.shape[1]
     tiles = width // LANES
     count = depth // KNOT
-    behind = lambda i: (jnp.maximum(i - 1, 0), 0, 0)
     ahead = lambda i: (jnp.minimum(i, count - 1), 0, 0)
     flat = lambda i: (0, 0)
     whole = lambda i: (0, 0, 0)
@@ -395,10 +419,8 @@
         grid=(count + 1,),
         in_specs=[
             pl.BlockSpec((KNOT, rows, width), ahead),
-            pl.BlockSpec((KNOT, rows, width), behind),
-            pl.BlockSpec((1, KNOT, rows, width), lambda i: (0, jnp.maximum(i - 1, 0), 0, 0)),
-            pl.BlockSpec((1, KNOT, rows, width), lambda i: (1, jnp.maximum(i - 1, 0), 0, 0)),
-            pl.BlockSpec((1, KNOT, rows, width), lambda i: (2, jnp.maximum(i - 1, 0), 0, 0)),
+            pl.BlockSpec(memory_space=pl.ANY),
+            pl.BlockSpec(memory_space=pl.ANY),
             pl.BlockSpec((KNOT, rows, LANES), ahead),
             pl.BlockSpec((KNOT, across.shape[1]), lambda i: (jnp.minimum(i, count - 1), 0)),
             pl.BlockSpec((KNOT, inside.shape[1]), lambda i: (jnp.minimum(i, count - 1), 0)),
@@ -411,7 +433,7 @@
             pl.BlockSpec(diag_plane.shape, whole),
         ],
         out_specs=[
-            pl.BlockSpec((KNOT, rows, width), behind),
+            pl.BlockSpec(memory_space=pl.ANY),
             pl.BlockSpec((parts, 2 * RANK // parts, width + width // 2 + LANES), whole),
             pl.BlockSpec((nodes, 4 * RANK), flat),
         ],
@@ -427,11 +449,16 @@
             pltpu.VMEM((2, tiles, nodes, LANES), f32),
             pltpu.VMEM((8, LANES), f32),
             pltpu.VMEM((KNOT, 8, LANES), f32),
-        ],
-        compiler_params=grid_params(),
+            pltpu.VMEM((2, KNOT, rows, width), bf16),
+            pltpu.VMEM((2, 3, KNOT, rows, width), bf16),
+            pltpu.VMEM((2, KNOT, rows, width), bf16),
+            pltpu.SemaphoreType.DMA((2, 4)),
+            pltpu.SemaphoreType.DMA((2,)),
+        ],
+        compiler_params=pltpu.CompilerParams(dimension_semantics=("arbitrary",), vmem_limit_bytes=53000000),
         cost_estimate=pl.CostEstimate(flops=60 * cells.size, bytes_accessed=12 * cells.size, transcendentals=0),
         name="warp",
-    )(cells, image, shift, shift, shift, beyond, across, inside, across_tile, inside_tile, field, plane, depth_factors, diag_depth, diag_plane)
+    )(cells, image, shift, beyond, across, inside, across_tile, inside_tile, field, plane, depth_factors, diag_depth, diag_plane)
 
 
 def gather_kernel(depth_ref, *refs):

time: 72 us -> 71.7 us (level)
  no operation moved by 1% of the time
where the time goes in v24:
time: 71.7 us; the launch traced here: 71.3 us
  Pallas kernels  36.2 us (50%)
  starting transfers between devices  19.8 us (28%)
  blocking collectives  10.6 us (15%)
  waiting for transfers between devices  3.93 us (5%)
  between operations  0.8 us (1%)
    pallas_call x1, Pallas kernels, warp(): pl.pallas_call(warp_kernel, grid=(count + 1,), in_specs=[pl.BlockSpec((KN...  29.7 us
    all_to_all x1, blocking collectives, local(): depth_terms = lax.all_to_all(depth_terms, 'gy', 0, 0)  10.6 us
    ppermute x6, starting transfers between devices, swapped(): return lax.ppermute(part, axis, pairs + [(j, i) for i, j in pairs])  8 us
    all_to_all x1, starting transfers between devices, local(): depth_terms = lax.all_to_all(depth_terms, 'gy', 0, 0)  5.97 us
    ppermute x3, starting transfers between devices, local(): lax.ppermute(plane_terms, 'gz', [(i, i ^ hop) for i in range(n_gz)])  5.86 us
    ppermute x3, waiting for transfers between devices, local(): lax.ppermute(plane_terms, 'gz', [(i, i ^ hop) for i in range(n_gz)])  3.91 us
    pallas_call x1, Pallas kernels, end_columns(): pl.pallas_call(columns_kernel, grid=(1,), in_specs=[pl.BlockSpec(block, f...  2.94 us
    pallas_call x1, Pallas kernels, squares(): pl.pallas_call(squares_kernel, out_shape=jax.ShapeDtypeStruct((width // L...  1.52 us
  transfers between devices with their start and end apart: 10, of which 2 were waited for; matrix products, arithmetic and copies ran while one was open for 0% of the time, Pallas kernels for 4%

profile of v24, /device:TPU:0, one launch (start us, length us, event | category | flops | bytes accessed | tf_op | source)
XLA Modules:
  0.0 71.3 jit_solution(12864736812305778249)
XLA Ops:
  0.6 0.0 copy-start
  0.6 2.9 %columns.1 = (bf16[64,128]{1,0:T(8,128)(2,1)}, bf16[64,128]{1,0:T(8,128)(2,1)}) custom-call(bf16[64,64,512]{2,1,0:T(8,128)(2,1)} %cells_ref.3, bf16[64,64,512]{2,1,0:T(8,128)(2,1)} %cells_ref.3, bf16[64,64,512]{2,1,0:T(8,128)(2,1)} %cells_ref.3, bf16[64,64,512]{2,1,0:T(8,128)(2,1)} %cells_ref.3, bf16[64,64,512]{2,1,0:T(8,128)(2,1)} %cells_ref.3, ...), custom_call_target="tpu_custom_call" | custom-call | tf_op jit(solution)/shard_map/columns/pallas_call | solution.py:67
  3.6 3.0 %collective-permute-start = (bf16[64,128]{1,0:T(8,128)(2,1)}, bf16[64,128]{1,0:T(8,128)(2,1)S(1)}, u32[]{:S(2)}, u32[]{:S(2)}) collective-permute-start(bf16[64,128]{1,0:T(8,128)(2,1)} %get-tuple-element.20), channel_id=1, source_target_pairs={{0,1},{2,3},{1,0},{3,2},{4,5},{6,7},{5,4},{7,6},{8,9},{10,11},{9,8... | collective-permute-start | bytes 49160 | tf_op jit(solution)/shard_map/ppermute | solution.py:135
  6.6 0.7 collective-permute-start.1
  7.3 0.0 copy-done
  7.3 0.2 ends.1
  7.5 0.7 collective-permute-start.2
  8.2 0.0 copy-start.1
  8.2 2.9 %collective-permute-start.3 = (bf16[64,512]{1,0:T(8,128)(2,1)S(1)}, bf16[64,512]{1,0:T(8,128)(2,1)S(1)}, u32[]{:S(2)}, u32[]{:S(2)}) collective-permute-start(bf16[64,512]{1,0:T(8,128)(2,1)S(1)} %get-tuple-element.25), channel_id=1, source_target_pairs={{0,4},{8,12},{16,20},{24,28},{4,0},{12,8},{20,16},{28,24},{1,5},{9... | collective-permute-start | bytes 196616 | tf_op jit(solution)/shard_map/ppermute | solution.py:135
  11.1 0.0 collective-permute-done.inner_ref
  11.1 0.0 collective-permute-done.1.outer_ref
  11.1 0.2 corners.1
  11.3 0.0 copy-start.2
  11.3 0.0 copy-start.3
  11.3 0.1 collective-permute-start.5
  11.4 0.7 collective-permute-start.4
  12.0 0.0 copy-done.1
  12.1 1.5 %squares.1.sums = f32[4,64,128]{2,1,0:T(8,128)S(1)} custom-call(bf16[64,64,512]{2,1,0:T(8,128)(2,1)S(1)} %copy-done.1, bf16[64,128]{1,0:T(8,128)(2,1)S(1)} %get-tuple-element.22.later_ref), custom_call_target="tpu_custom_call" | custom-call | flops 6291456 | bytes 4194304 | tf_op jit(solution)/shard_map/squares/pallas_call | solution.py:160
  13.6 0.0 copy-done.2
  13.6 0.0 copy-done.3
  13.6 0.7 terms.1
  14.3 0.0 collective-permute-done.5.inside_tile_ref
  14.3 0.0 collective-permute-done.4.across_tile_ref
  14.3 0.0 collective-permute-done.2.across_ref
  14.3 0.0 collective-permute-done.3.inside_ref
  14.3 29.7 %warp.1 = (bf16[64,64,512]{2,1,0:T(8,128)(2,1)}, f32[8,8,896]{2,1,0:T(8,128)}, f32[64,128]{1,0:T(8,128)S(1)}) custom-call(bf16[64,64,512]{2,1,0:T(8,128)(2,1)} %cells_ref.3, bf16[64,64,512]{2,1,0:T(8,128)(2,1)} %image_hbm.1, bf16[3,64,64,512]{3,2,1,0:T(8,128)(2,1)} %shift_hbm.1, bf16[64,64,128]{2,1,0:T(8,128)(2,1)S(1)} %get-tuple-element.23.beyond_ref, ...), custom_call_target="tpu_custom_call" | custom-call | flops 125829120 | bytes 25165824 | tf_op jit(solution)/shard_map/warp/pallas_call | solution.py:417
  44.1 6.0 %all-to-all-start = ((f32[8,8,896]{2,1,0:T(8,128)}), f32[8,8,896]{2,1,0:T(8,128)S(1)}, u32[]{:S(2)}, u32[]{:S(2)}) async-start(f32[8,8,896]{2,1,0:T(8,128)} %get-tuple-element.31), calls=%async_computation | async-start | bytes 458752 | tf_op jit(solution)/shard_map/all_to_all | solution.py:523
  50.0 2.5 %collective-permute-start.8 = (f32[64,128]{1,0:T(8,128)S(1)}, f32[64,128]{1,0:T(8,128)S(1)}, u32[]{:S(2)}, u32[]{:S(2)}) collective-permute-start(f32[64,128]{1,0:T(8,128)S(1)} %get-tuple-element.32.refs_0_), channel_id=1, source_target_pairs={{0,3},{1,2},{2,1},{3,0},{4,7},{5,6},{6,5},{7,4},{8,11},{9,10},{10,... | collective-permute-start | bytes 98312 | tf_op jit(solution)/shard_map/ppermute | solution.py:525
  52.5 3.4 %collective-permute-start.7 = (f32[64,128]{1,0:T(8,128)S(1)}, f32[64,128]{1,0:T(8,128)S(1)}, u32[]{:S(2)}, u32[]{:S(2)}) collective-permute-start(f32[64,128]{1,0:T(8,128)S(1)} %get-tuple-element.32.refs_0_), channel_id=1, source_target_pairs={{0,2},{1,3},{2,0},{3,1},{4,6},{5,7},{6,4},{7,5},{8,10},{9,11},{10,... | collective-permute-start | bytes 98312 | tf_op jit(solution)/shard_map/ppermute | solution.py:525
  55.9 0.0 collective-permute-start.6
  55.9 0.0 collective-permute-done.8.refs_3_
  55.9 3.2 %collective-permute-done.7.refs_2_ = f32[64,128]{1,0:T(8,128)S(1)} collective-permute-done((f32[64,128]{1,0:T(8,128)S(1)}, f32[64,128]{1,0:T(8,128)S(1)}, u32[]{:S(2)}, u32[]{:S(2)}) %collective-permute-start.7) | collective-permute-done | bytes 32800 | tf_op jit(solution)/shard_map/ppermute | solution.py:525
  59.1 0.7 %collective-permute-done.6.refs_1_ = f32[64,128]{1,0:T(8,128)S(1)} collective-permute-done((f32[64,128]{1,0:T(8,128)S(1)}, f32[64,128]{1,0:T(8,128)S(1)}, u32[]{:S(2)}, u32[]{:S(2)}) %collective-permute-start.6) | collective-permute-done | bytes 32800 | tf_op jit(solution)/shard_map/ppermute | solution.py:525
  59.8 0.0 all-to-all-done.depth_ref
  59.8 0.1 gather.1
  59.9 10.6 %all_to_all.10.depth_ref = f32[8,8,896]{2,1,0:T(8,128)S(1)} all-to-all(f32[8,8,896]{2,1,0:T(8,128)S(1)} %get-tuple-element.33), channel_id=1, replica_groups=mesh['gy'=8,'gz'=4] {'gy'}, dimensions={0} | all-to-all | bytes 458752 | tf_op jit(solution)/shard_map/all_to_all | solution.py:536
  70.5 0.8 %steps.1 = (f32[2,32,512]{2,1,0:T(8,128)}, f32[2,64,32]{2,1,0:T(8,128)}) custom-call(f32[8,8,896]{2,1,0:T(8,128)S(1)} %all_to_all.10.depth_ref, f32[64,128]{1,0:T(8,128)S(1)} %get-tuple-element.34.plane_ref), custom_call_target="tpu_custom_call" | custom-call | tf_op jit(solution)/shard_map/steps/pallas_call | solution.py:538
Async XLA Ops:
  0.6 6.6 %copy-start = (bf16[64,64,512]{2,1,0:T(8,128)(2,1)S(1)}, bf16[64,64,512]{2,1,0:T(8,128)(2,1)}, u32[]{:S(2)}) copy-start(bf16[64,64,512]{2,1,0:T(8,128)(2,1)} %cells_ref.3) | copy-start | bytes 12582916
  3.6 7.5 %collective-permute-start = (bf16[64,128]{1,0:T(8,128)(2,1)}, bf16[64,128]{1,0:T(8,128)(2,1)S(1)}, u32[]{:S(2)}, u32[]{:S(2)}) collective-permute-start(bf16[64,128]{1,0:T(8,128)(2,1)} %get-tuple-element.20), channel_id=1, source_target_pairs={{0,1},{2,3},{1,0},{3,2},{4,5},{6,7},{5,4},{7,6},{8,9},{10,11},{9,8... | collective-permute-start | bytes 49160 | tf_op jit(solution)/shard_map/ppermute | solution.py:135
  6.6 4.5 %collective-permute-start.1 = (bf16[64,128]{1,0:T(8,128)(2,1)}, bf16[64,128]{1,0:T(8,128)(2,1)S(1)}, u32[]{:S(2)}, u32[]{:S(2)}) collective-permute-start(bf16[64,128]{1,0:T(8,128)(2,1)} %get-tuple-element.21), channel_id=1, source_target_pairs={{1,2},{2,1},{5,6},{6,5},{9,10},{10,9},{13,14},{14,13},{17,18},{18,... | collective-permute-start | bytes 49160 | tf_op jit(solution)/shard_map/ppermute | solution.py:135
  7.5 6.8 %collective-permute-start.2 = (bf16[64,512]{1,0:T(8,128)(2,1)S(1)}, bf16[64,512]{1,0:T(8,128)(2,1)S(1)}, u32[]{:S(2)}, u32[]{:S(2)}) collective-permute-start(bf16[64,512]{1,0:T(8,128)(2,1)S(1)} %get-tuple-element.24), channel_id=1, source_target_pairs={{4,8},{12,16},{20,24},{8,4},{16,12},{24,20},{5,9},{13,17},{21,25},... | collective-permute-start | bytes 196616 | tf_op jit(solution)/shard_map/ppermute | solution.py:135
  8.2 3.9 %copy-start.1 = (bf16[64,64,512]{2,1,0:T(8,128)(2,1)S(1)}, bf16[64,64,512]{2,1,0:T(8,128)(2,1)}, u32[]{:S(2)}) copy-start(bf16[64,64,512]{2,1,0:T(8,128)(2,1)} %image_hbm.1) | copy-start | bytes 12582916
  8.2 6.2 %collective-permute-start.3 = (bf16[64,512]{1,0:T(8,128)(2,1)S(1)}, bf16[64,512]{1,0:T(8,128)(2,1)S(1)}, u32[]{:S(2)}, u32[]{:S(2)}) collective-permute-start(bf16[64,512]{1,0:T(8,128)(2,1)S(1)} %get-tuple-element.25), channel_id=1, source_target_pairs={{0,4},{8,12},{16,20},{24,28},{4,0},{12,8},{20,16},{28,24},{1,5},{9... | collective-permute-start | bytes 196616 | tf_op jit(solution)/shard_map/ppermute | solution.py:135
  11.3 2.3 %copy-start.2 = (f32[2,32,512]{2,1,0:T(8,128)S(1)}, f32[2,32,512]{2,1,0:T(8,128)}, u32[]{:S(2)}) copy-start(f32[2,32,512]{2,1,0:T(8,128)} %depth_ref.3) | copy-start | bytes 393220
  11.3 2.3 %copy-start.3 = (f32[2,32,8,8]{1,3,2,0:T(8,128)S(1)}, f32[2,32,8,8]{1,3,2,0:T(8,128)}, u32[]{:S(2)}) copy-start(f32[2,32,8,8]{1,3,2,0:T(8,128)} %param.8) | copy-start | bytes 49156
  11.3 3.0 %collective-permute-start.5 = (bf16[64,128]{1,0:T(8,128)(2,1)S(1)}, bf16[64,128]{1,0:T(8,128)(2,1)S(1)}, u32[]{:S(2)}, u32[]{:S(2)}) collective-permute-start(bf16[64,128]{1,0:T(8,128)(2,1)S(1)} %get-tuple-element.26), channel_id=1, source_target_pairs={{0,4},{8,12},{16,20},{24,28},{4,0},{12,8},{20,16},{28,24},{1,5},{9... | collective-permute-start | bytes 49160 | tf_op jit(solution)/shard_map/ppermute | solution.py:135
  11.4 2.9 %collective-permute-start.4 = (bf16[64,128]{1,0:T(8,128)(2,1)S(1)}, bf16[64,128]{1,0:T(8,128)(2,1)S(1)}, u32[]{:S(2)}, u32[]{:S(2)}) collective-permute-start(bf16[64,128]{1,0:T(8,128)(2,1)S(1)} %get-tuple-element.22.later_ref), channel_id=1, source_target_pairs={{4,8},{12,16},{20,24},{8,4},{16,12},{24,20},{5,9},{13,17},{21,25},... | collective-permute-start | bytes 49160 | tf_op jit(solution)/shard_map/ppermute | solution.py:135
  44.1 15.8 %all-to-all-start = ((f32[8,8,896]{2,1,0:T(8,128)}), f32[8,8,896]{2,1,0:T(8,128)S(1)}, u32[]{:S(2)}, u32[]{:S(2)}) async-start(f32[8,8,896]{2,1,0:T(8,128)} %get-tuple-element.31), calls=%async_computation | async-start | bytes 458752 | tf_op jit(solution)/shard_map/all_to_all | solution.py:523
  50.0 5.9 %collective-permute-start.8 = (f32[64,128]{1,0:T(8,128)S(1)}, f32[64,128]{1,0:T(8,128)S(1)}, u32[]{:S(2)}, u32[]{:S(2)}) collective-permute-start(f32[64,128]{1,0:T(8,128)S(1)} %get-tuple-element.32.refs_0_), channel_id=1, source_target_pairs={{0,3},{1,2},{2,1},{3,0},{4,7},{5,6},{6,5},{7,4},{8,11},{9,10},{10,... | collective-permute-start | bytes 98312 | tf_op jit(solution)/shard_map/ppermute | solution.py:525
  52.5 6.6 %collective-permute-start.7 = (f32[64,128]{1,0:T(8,128)S(1)}, f32[64,128]{1,0:T(8,128)S(1)}, u32[]{:S(2)}, u32[]{:S(2)}) collective-permute-start(f32[64,128]{1,0:T(8,128)S(1)} %get-tuple-element.32.refs_0_), channel_id=1, source_target_pairs={{0,2},{1,3},{2,0},{3,1},{4,6},{5,7},{6,4},{7,5},{8,10},{9,11},{10,... | collective-permute-start | bytes 98312 | tf_op jit(solution)/shard_map/ppermute | solution.py:525
  55.9 3.9 %collective-permute-start.6 = (f32[64,128]{1,0:T(8,128)S(1)}, f32[64,128]{1,0:T(8,128)S(1)}, u32[]{:S(2)}, u32[]{:S(2)}) collective-permute-start(f32[64,128]{1,0:T(8,128)S(1)} %get-tuple-element.32.refs_0_), channel_id=1, source_target_pairs={{0,1},{1,0},{2,3},{3,2},{4,5},{5,4},{6,7},{7,6},{8,9},{9,8},{10,11... | collective-permute-start | bytes 98312 | tf_op jit(solution)/shard_map/ppermute | solution.py:525

commit v25 on v24

--- a/solution.py
+++ b/solution.py
@@ -40,58 +40,47 @@
     return pltpu.CompilerParams(vmem_limit_bytes=32000000)
 
 
-def columns_kernel(*refs):
-    inner_ref, outer_ref = refs[-2:]
-    chunks = (len(refs) - 2) // 2
-    rows = inner_ref.shape[0]
+def ends_kernel(cells_hbm, inner_ref, outer_ref, across_ref, inside_ref, cells, got):
+    depth, rows, width = cells.shape
+    chunks = got.shape[0]
+    planes = depth // chunks
+
+    def fetched(n):
+        part = pl.ds(n * planes, planes)
+        return pltpu.make_async_copy(cells_hbm.at[part], cells.at[part], got.at[n])
+
+    for n in range(chunks):
+        fetched(n).start()
+    odd_y, odd_z = lax.axis_index("gy") % 2 == 1, lax.axis_index("gz") % 2 == 1
     lane = lax.broadcasted_iota(jnp.int32, (rows, LANES), 1)
     first = jnp.zeros((rows, LANES), f32)
     last = jnp.zeros((rows, LANES), f32)
-    for chunk in range(chunks):
-        near, far = refs[chunk], refs[chunks + chunk]
-        for k in range(near.shape[0]):
-            x = chunk * near.shape[0] + k
-            first = jnp.where(lane == x, pltpu.roll(near[k].astype(f32), x, 1), first)
-            last = jnp.where(lane == x, pltpu.roll(far[k].astype(f32), (x + 1) % LANES, 1), last)
-    odd = lax.axis_index("gz") % 2 == 1
-    inner_ref[...] = jnp.where(odd, first, last).astype(bf16)
-    outer_ref[...] = jnp.where(odd, last, first).astype(bf16)
-
-
-def end_columns(cells):
-    depth, rows, width = cells.shape
-    tiles = width // LANES
-    chunks = 4
-    block = (depth // chunks, rows, LANES)
-    places = [(chunk, tile) for tile in (0, tiles - 1) for chunk in range(chunks)]
-    return pl.pallas_call(
-        columns_kernel,
-        grid=(1,),
-        in_specs=[pl.BlockSpec(block, functools.partial(lambda c, t, i: (c, 0, t), c, t)) for c, t in places],
-        out_specs=[pl.BlockSpec((rows, LANES), lambda i: (0, 0))] * 2,
-        out_shape=[jax.ShapeDtypeStruct((rows, LANES), bf16)] * 2,
-        compiler_params=pltpu.CompilerParams(vmem_limit_bytes=60000000),
-        name="columns",
-    )(*[cells] * len(places))
-
-
-def ends_kernel(cells_ref, across_ref, inside_ref):
-    depth, rows = cells_ref.shape[0:2]
-    odd = lax.axis_index("gy") % 2 == 1
-    for x in range(0, depth, 16):
-        low = [cells_ref[x + k, 0:16, :].astype(f32)[0:1] for k in range(16)]
-        high = [cells_ref[x + k, rows - 16 : rows, :].astype(f32)[15:16] for k in range(16)]
-        low, high = jnp.concatenate(low, axis=0), jnp.concatenate(high, axis=0)
-        across_ref[x : x + 16, :] = jnp.where(odd, high, low).astype(bf16)
-        inside_ref[x : x + 16, :] = jnp.where(odd, low, high).astype(bf16)
+    for n in range(chunks):
+        fetched(n).wait()
+        for x in range(n * planes, (n + 1) * planes):
+            near = cells[x, :, 0:LANES].astype(f32)
+            far = cells[x, :, width - LANES : width].astype(f32)
+            first = jnp.where(lane == x, pltpu.roll(near, x, 1), first)
+            last = jnp.where(lane == x, pltpu.roll(far, (x + 1) % LANES, 1), last)
+        if (n + 1) * planes % 16 == 0:
+            x = (n + 1) * planes - 16
+            low = [cells[x + k, 0:16, :].astype(f32)[0:1] for k in range(16)]
+            high = [cells[x + k, rows - 16 : rows, :].astype(f32)[15:16] for k in range(16)]
+            low, high = jnp.concatenate(low, axis=0), jnp.concatenate(high, axis=0)
+            across_ref[x : x + 16, :] = jnp.where(odd_y, high, low).astype(bf16)
+            inside_ref[x : x + 16, :] = jnp.where(odd_y, low, high).astype(bf16)
+    inner_ref[...] = jnp.where(odd_z, first, last).astype(bf16)
+    outer_ref[...] = jnp.where(odd_z, last, first).astype(bf16)
 
 
 def ends(cells):
     depth, rows, width = cells.shape
     return pl.pallas_call(
         ends_kernel,
-        out_shape=[jax.ShapeDtypeStruct((depth, width), bf16)] * 2,
-        compiler_params=plain_params(),
+        in_specs=[pl.BlockSpec(memory_space=pl.ANY)],
+        out_shape=[jax.ShapeDtypeStruct((rows, LANES), bf16)] * 2 + [jax.ShapeDtypeStruct((depth, width), bf16)] * 2,
+        scratch_shapes=[pltpu.VMEM(cells.shape, bf16), pltpu.SemaphoreType.DMA((depth // KNOT,))],
+        compiler_params=pltpu.CompilerParams(vmem_limit_bytes=61000000),
         cost_estimate=pl.CostEstimate(flops=cells.size, bytes_accessed=2 * cells.size, transcendentals=0),
         name="ends",
     )(cells)
@@ -505,10 +494,9 @@
     n_gy, n_gz = lax.axis_size("gy"), lax.axis_size("gz")
     nodes_x, nodes_y = plane_factors.shape[2:]
     plane = jnp.transpose(plane_factors, (0, 2, 3, 1)).reshape(2, nodes_x * nodes_y, RANK)
-    inner, outer = end_columns(deformed)
+    inner, outer, across, inside = ends(deformed)
     inner = swapped(inner, "gz", 0)
     outer = swapped(outer, "gz", 1)
-    across, inside = ends(deformed)
     inside = swapped(inside, "gy", 0)
     across = swapped(across, "gy", 1)
     across_tile, inside_tile = corners(inner, outer, deformed.shape[0])

time: 71.7 us -> 71.7 us (level)
    pallas_call x2 -> x1, Pallas kernels: 3.14 us -> 3.09 us  [ends(): pl.pallas_call(ends_kernel, in_specs=[pl.BlockSpec(memory_space=pl.ANY)],...]
  transfers between devices with their start and end apart: 10 -> 10, of which waited for: 2 -> 2; matrix products, arithmetic and copies ran while one was open for 0% -> 0% of each run, Pallas kernels for 4% -> 3%
where the time goes in v25:
time: 71.7 us; the launch traced here: 71.3 us
  Pallas kernels  36.1 us (50%)
  starting transfers between devices  19.9 us (28%)
  blocking collectives  10.6 us (15%)
  waiting for transfers between devices  3.93 us (5%)
  between operations  0.78 us (1%)
    pallas_call x1, Pallas kernels, warp(): pl.pallas_call(warp_kernel, grid=(count + 1,), in_specs=[pl.BlockSpec((KN...  29.7 us
    all_to_all x1, blocking collectives, local(): depth_terms = lax.all_to_all(depth_terms, 'gy', 0, 0)  10.6 us
    ppermute x6, starting transfers between devices, swapped(): return lax.ppermute(part, axis, pairs + [(j, i) for i, j in pairs])  8.07 us
    all_to_all x1, starting transfers between devices, local(): depth_terms = lax.all_to_all(depth_terms, 'gy', 0, 0)  5.98 us
    ppermute x3, starting transfers between devices, local(): lax.ppermute(plane_terms, 'gz', [(i, i ^ hop) for i in range(n_gz)])  5.86 us
    ppermute x3, waiting for transfers between devices, local(): lax.ppermute(plane_terms, 'gz', [(i, i ^ hop) for i in range(n_gz)])  3.91 us
    pallas_call x1, Pallas kernels, ends(): pl.pallas_call(ends_kernel, in_specs=[pl.BlockSpec(memory_space=pl.ANY)],...  3.09 us
    pallas_call x1, Pallas kernels, squares(): pl.pallas_call(squares_kernel, out_shape=jax.ShapeDtypeStruct((width // L...  1.52 us
  transfers between devices with their start and end apart: 10, of which 2 were waited for; matrix products, arithmetic and copies ran while one was open for 0% of the time, Pallas kernels for 3%

profile of v25, /device:TPU:0, one launch (start us, length us, event | category | flops | bytes accessed | tf_op | source)
XLA Modules:
  0.0 71.3 jit_solution(11733978040375503168)
XLA Ops:
  0.6 3.1 %ends.1 = (bf16[64,128]{1,0:T(8,128)(2,1)}, bf16[64,128]{1,0:T(8,128)(2,1)}, bf16[64,512]{1,0:T(8,128)(2,1)}, bf16[64,512]{1,0:T(8,128)(2,1)}) custom-call(bf16[64,64,512]{2,1,0:T(8,128)(2,1)} %cells_ref.1), custom_call_target="tpu_custom_call" | custom-call | flops 2097152 | bytes 4194304 | tf_op jit(solution)/shard_map/ends/pallas_call | solution.py:78
  3.7 3.1 %collective-permute-start = (bf16[64,128]{1,0:T(8,128)(2,1)}, bf16[64,128]{1,0:T(8,128)(2,1)S(1)}, u32[]{:S(2)}, u32[]{:S(2)}) collective-permute-start(bf16[64,128]{1,0:T(8,128)(2,1)} %get-tuple-element.20), channel_id=1, source_target_pairs={{0,1},{2,3},{1,0},{3,2},{4,5},{6,7},{5,4},{7,6},{8,9},{10,11},{9,8... | collective-permute-start | bytes 49160 | tf_op jit(solution)/shard_map/ppermute | solution.py:124
  6.8 0.7 collective-permute-start.1
  7.5 0.7 collective-permute-start.2
  8.1 0.0 copy-start
  8.2 2.9 %collective-permute-start.3 = (bf16[64,512]{1,0:T(8,128)(2,1)}, bf16[64,512]{1,0:T(8,128)(2,1)S(1)}, u32[]{:S(2)}, u32[]{:S(2)}) collective-permute-start(bf16[64,512]{1,0:T(8,128)(2,1)} %get-tuple-element.25), channel_id=1, source_target_pairs={{0,4},{8,12},{16,20},{24,28},{4,0},{12,8},{20,16},{28,24},{1,5},{9... | collective-permute-start | bytes 196616 | tf_op jit(solution)/shard_map/ppermute | solution.py:124
  11.1 0.0 collective-permute-done.inner_ref
  11.1 0.0 collective-permute-done.1.outer_ref
  11.1 0.2 corners.1
  11.3 0.0 copy-start.1
  11.3 0.0 copy-start.2
  11.3 0.1 collective-permute-start.5
  11.4 0.7 collective-permute-start.4
  12.0 0.0 copy-done
  12.0 1.5 %squares.1.sums = f32[4,64,128]{2,1,0:T(8,128)S(1)} custom-call(bf16[64,64,512]{2,1,0:T(8,128)(2,1)S(1)} %copy-done, bf16[64,128]{1,0:T(8,128)(2,1)S(1)} %get-tuple-element.22.later_ref), custom_call_target="tpu_custom_call" | custom-call | flops 6291456 | bytes 4194304 | tf_op jit(solution)/shard_map/squares/pallas_call | solution.py:149
  13.6 0.0 copy-done.1
  13.6 0.0 copy-done.2
  13.6 0.7 terms.1
  14.3 0.0 collective-permute-done.5.inside_tile_ref
  14.3 0.0 collective-permute-done.4.across_tile_ref
  14.3 0.0 collective-permute-done.2.across_ref
  14.3 0.0 collective-permute-done.3.inside_ref
  14.3 29.7 %warp.1 = (bf16[64,64,512]{2,1,0:T(8,128)(2,1)}, f32[8,8,896]{2,1,0:T(8,128)}, f32[64,128]{1,0:T(8,128)S(1)}) custom-call(bf16[64,64,512]{2,1,0:T(8,128)(2,1)} %cells_ref.1, bf16[64,64,512]{2,1,0:T(8,128)(2,1)} %image_hbm.1, bf16[3,64,64,512]{3,2,1,0:T(8,128)(2,1)} %shift_hbm.1, bf16[64,64,128]{2,1,0:T(8,128)(2,1)S(1)} %get-tuple-element.23.beyond_ref, ...), custom_call_target="tpu_custom_call" | custom-call | flops 125829120 | bytes 25165824 | tf_op jit(solution)/shard_map/warp/pallas_call | solution.py:406
  44.0 6.0 %all-to-all-start = ((f32[8,8,896]{2,1,0:T(8,128)}), f32[8,8,896]{2,1,0:T(8,128)S(1)}, u32[]{:S(2)}, u32[]{:S(2)}) async-start(f32[8,8,896]{2,1,0:T(8,128)} %get-tuple-element.31), calls=%async_computation | async-start | bytes 458752 | tf_op jit(solution)/shard_map/all_to_all | solution.py:511
  50.0 2.5 %collective-permute-start.8 = (f32[64,128]{1,0:T(8,128)S(1)}, f32[64,128]{1,0:T(8,128)S(1)}, u32[]{:S(2)}, u32[]{:S(2)}) collective-permute-start(f32[64,128]{1,0:T(8,128)S(1)} %get-tuple-element.32.refs_0_), channel_id=1, source_target_pairs={{0,3},{1,2},{2,1},{3,0},{4,7},{5,6},{6,5},{7,4},{8,11},{9,10},{10,... | collective-permute-start | bytes 98312 | tf_op jit(solution)/shard_map/ppermute | solution.py:513
  52.5 3.4 %collective-permute-start.7 = (f32[64,128]{1,0:T(8,128)S(1)}, f32[64,128]{1,0:T(8,128)S(1)}, u32[]{:S(2)}, u32[]{:S(2)}) collective-permute-start(f32[64,128]{1,0:T(8,128)S(1)} %get-tuple-element.32.refs_0_), channel_id=1, source_target_pairs={{0,2},{1,3},{2,0},{3,1},{4,6},{5,7},{6,4},{7,5},{8,10},{9,11},{10,... | collective-permute-start | bytes 98312 | tf_op jit(solution)/shard_map/ppermute | solution.py:513
  55.9 0.0 collective-permute-start.6
  55.9 0.0 collective-permute-done.8.refs_3_
  55.9 3.2 %collective-permute-done.7.refs_2_ = f32[64,128]{1,0:T(8,128)S(1)} collective-permute-done((f32[64,128]{1,0:T(8,128)S(1)}, f32[64,128]{1,0:T(8,128)S(1)}, u32[]{:S(2)}, u32[]{:S(2)}) %collective-permute-start.7) | collective-permute-done | bytes 32800 | tf_op jit(solution)/shard_map/ppermute | solution.py:513
  59.1 0.7 %collective-permute-done.6.refs_1_ = f32[64,128]{1,0:T(8,128)S(1)} collective-permute-done((f32[64,128]{1,0:T(8,128)S(1)}, f32[64,128]{1,0:T(8,128)S(1)}, u32[]{:S(2)}, u32[]{:S(2)}) %collective-permute-start.6) | collective-permute-done | bytes 32800 | tf_op jit(solution)/shard_map/ppermute | solution.py:513
  59.8 0.0 all-to-all-done.depth_ref
  59.8 0.1 gather.1
  59.9 10.6 %all_to_all.10.depth_ref = f32[8,8,896]{2,1,0:T(8,128)S(1)} all-to-all(f32[8,8,896]{2,1,0:T(8,128)S(1)} %get-tuple-element.33), channel_id=1, replica_groups=mesh['gy'=8,'gz'=4] {'gy'}, dimensions={0} | all-to-all | bytes 458752 | tf_op jit(solution)/shard_map/all_to_all | solution.py:524
  70.5 0.8 %steps.1 = (f32[2,32,512]{2,1,0:T(8,128)}, f32[2,64,32]{2,1,0:T(8,128)}) custom-call(f32[8,8,896]{2,1,0:T(8,128)S(1)} %all_to_all.10.depth_ref, f32[64,128]{1,0:T(8,128)S(1)} %get-tuple-element.34.plane_ref), custom_call_target="tpu_custom_call" | custom-call | tf_op jit(solution)/shard_map/steps/pallas_call | solution.py:526
Async XLA Ops:
  3.7 7.3 %collective-permute-start = (bf16[64,128]{1,0:T(8,128)(2,1)}, bf16[64,128]{1,0:T(8,128)(2,1)S(1)}, u32[]{:S(2)}, u32[]{:S(2)}) collective-permute-start(bf16[64,128]{1,0:T(8,128)(2,1)} %get-tuple-element.20), channel_id=1, source_target_pairs={{0,1},{2,3},{1,0},{3,2},{4,5},{6,7},{5,4},{7,6},{8,9},{10,11},{9,8... | collective-permute-start | bytes 49160 | tf_op jit(solution)/shard_map/ppermute | solution.py:124
  6.8 4.3 %collective-permute-start.1 = (bf16[64,128]{1,0:T(8,128)(2,1)}, bf16[64,128]{1,0:T(8,128)(2,1)S(1)}, u32[]{:S(2)}, u32[]{:S(2)}) collective-permute-start(bf16[64,128]{1,0:T(8,128)(2,1)} %get-tuple-element.21), channel_id=1, source_target_pairs={{1,2},{2,1},{5,6},{6,5},{9,10},{10,9},{13,14},{14,13},{17,18},{18,... | collective-permute-start | bytes 49160 | tf_op jit(solution)/shard_map/ppermute | solution.py:124
  7.5 6.8 %collective-permute-start.2 = (bf16[64,512]{1,0:T(8,128)(2,1)}, bf16[64,512]{1,0:T(8,128)(2,1)S(1)}, u32[]{:S(2)}, u32[]{:S(2)}) collective-permute-start(bf16[64,512]{1,0:T(8,128)(2,1)} %get-tuple-element.24), channel_id=1, source_target_pairs={{4,8},{12,16},{20,24},{8,4},{16,12},{24,20},{5,9},{13,17},{21,25},... | collective-permute-start | bytes 196616 | tf_op jit(solution)/shard_map/ppermute | solution.py:124
  8.1 3.9 %copy-start = (bf16[64,64,512]{2,1,0:T(8,128)(2,1)S(1)}, bf16[64,64,512]{2,1,0:T(8,128)(2,1)}, u32[]{:S(2)}) copy-start(bf16[64,64,512]{2,1,0:T(8,128)(2,1)} %image_hbm.1) | copy-start | bytes 12582916
  8.2 6.2 %collective-permute-start.3 = (bf16[64,512]{1,0:T(8,128)(2,1)}, bf16[64,512]{1,0:T(8,128)(2,1)S(1)}, u32[]{:S(2)}, u32[]{:S(2)}) collective-permute-start(bf16[64,512]{1,0:T(8,128)(2,1)} %get-tuple-element.25), channel_id=1, source_target_pairs={{0,4},{8,12},{16,20},{24,28},{4,0},{12,8},{20,16},{28,24},{1,5},{9... | collective-permute-start | bytes 196616 | tf_op jit(solution)/shard_map/ppermute | solution.py:124
  11.3 2.3 %copy-start.1 = (f32[2,32,512]{2,1,0:T(8,128)S(1)}, f32[2,32,512]{2,1,0:T(8,128)}, u32[]{:S(2)}) copy-start(f32[2,32,512]{2,1,0:T(8,128)} %depth_ref.3) | copy-start | bytes 393220
  11.3 2.3 %copy-start.2 = (f32[2,32,8,8]{1,3,2,0:T(8,128)S(1)}, f32[2,32,8,8]{1,3,2,0:T(8,128)}, u32[]{:S(2)}) copy-start(f32[2,32,8,8]{1,3,2,0:T(8,128)} %param.8) | copy-start | bytes 49156
  11.3 3.0 %collective-permute-start.5 = (bf16[64,128]{1,0:T(8,128)(2,1)S(1)}, bf16[64,128]{1,0:T(8,128)(2,1)S(1)}, u32[]{:S(2)}, u32[]{:S(2)}) collective-permute-start(bf16[64,128]{1,0:T(8,128)(2,1)S(1)} %get-tuple-element.26), channel_id=1, source_target_pairs={{0,4},{8,12},{16,20},{24,28},{4,0},{12,8},{20,16},{28,24},{1,5},{9... | collective-permute-start | bytes 49160 | tf_op jit(solution)/shard_map/ppermute | solution.py:124
  11.4 2.9 %collective-permute-start.4 = (bf16[64,128]{1,0:T(8,128)(2,1)S(1)}, bf16[64,128]{1,0:T(8,128)(2,1)S(1)}, u32[]{:S(2)}, u32[]{:S(2)}) collective-permute-start(bf16[64,128]{1,0:T(8,128)(2,1)S(1)} %get-tuple-element.22.later_ref), channel_id=1, source_target_pairs={{4,8},{12,16},{20,24},{8,4},{16,12},{24,20},{5,9},{13,17},{21,25},... | collective-permute-start | bytes 49160 | tf_op jit(solution)/shard_map/ppermute | solution.py:124
  44.0 15.8 %all-to-all-start = ((f32[8,8,896]{2,1,0:T(8,128)}), f32[8,8,896]{2,1,0:T(8,128)S(1)}, u32[]{:S(2)}, u32[]{:S(2)}) async-start(f32[8,8,896]{2,1,0:T(8,128)} %get-tuple-element.31), calls=%async_computation | async-start | bytes 458752 | tf_op jit(solution)/shard_map/all_to_all | solution.py:511
  50.0 5.9 %collective-permute-start.8 = (f32[64,128]{1,0:T(8,128)S(1)}, f32[64,128]{1,0:T(8,128)S(1)}, u32[]{:S(2)}, u32[]{:S(2)}) collective-permute-start(f32[64,128]{1,0:T(8,128)S(1)} %get-tuple-element.32.refs_0_), channel_id=1, source_target_pairs={{0,3},{1,2},{2,1},{3,0},{4,7},{5,6},{6,5},{7,4},{8,11},{9,10},{10,... | collective-permute-start | bytes 98312 | tf_op jit(solution)/shard_map/ppermute | solution.py:513
  52.5 6.6 %collective-permute-start.7 = (f32[64,128]{1,0:T(8,128)S(1)}, f32[64,128]{1,0:T(8,128)S(1)}, u32[]{:S(2)}, u32[]{:S(2)}) collective-permute-start(f32[64,128]{1,0:T(8,128)S(1)} %get-tuple-element.32.refs_0_), channel_id=1, source_target_pairs={{0,2},{1,3},{2,0},{3,1},{4,6},{5,7},{6,4},{7,5},{8,10},{9,11},{10,... | collective-permute-start | bytes 98312 | tf_op jit(solution)/shard_map/ppermute | solution.py:513
  55.9 3.9 %collective-permute-start.6 = (f32[64,128]{1,0:T(8,128)S(1)}, f32[64,128]{1,0:T(8,128)S(1)}, u32[]{:S(2)}, u32[]{:S(2)}) collective-permute-start(f32[64,128]{1,0:T(8,128)S(1)} %get-tuple-element.32.refs_0_), channel_id=1, source_target_pairs={{0,1},{1,0},{2,3},{3,2},{4,5},{5,4},{6,7},{7,6},{8,9},{9,8},{10,11... | collective-permute-start | bytes 98312 | tf_op jit(solution)/shard_map/ppermute | solution.py:513

commit v26 on v25

--- a/solution.py
+++ b/solution.py
@@ -330,9 +330,9 @@
                 brightness = jnp.broadcast_to(field[1, tile, pl.ds(node, 1), :], (8, LANES))
                 by_image = jnp.zeros((8, LANES), f32)
                 plain = jnp.zeros((8, LANES), f32)
-                before, here = taps(0), taps(1)
+                here = taps(1)
                 for k in range(planes):
-                    after = taps(k + 2)
+                    before, after = taps(k), taps(k + 2)
                     place = (k, pl.ds(top, 16), pl.ds(at, LANES))
                     sx, sy, sz = (shift_ref[(here_slot, axis) + place].astype(f32)[mine] for axis in range(3))
                     image = image_ref[(here_slot,) + place].astype(f32)[mine]
@@ -358,7 +358,7 @@
                     by_image = by_image + misfit * image
                     plain = plain + misfit
                     total = total + misfit * misfit
-                    before, here = here, after
+                    here = after
                 for k, value in ((0, by_image), (1, plain)):
                     blocks[k, tile, pl.ds(node, 1), :] = jnp.sum(value, axis=0, keepdims=True)
             return total

time: 71.7 us -> 71.7 us (level)
  no operation moved by 1% of the time
where the time goes in v26:
time: 71.7 us; the launch traced here: 71.4 us
  Pallas kernels  36.1 us (50%)
  starting transfers between devices  19.9 us (28%)
  blocking collectives  10.6 us (15%)
  waiting for transfers between devices  3.93 us (5%)
  between operations  0.78 us (1%)
    pallas_call x1, Pallas kernels, warp(): pl.pallas_call(warp_kernel, grid=(count + 1,), in_specs=[pl.BlockSpec((KN...  29.7 us
    all_to_all x1, blocking collectives, local(): depth_terms = lax.all_to_all(depth_terms, 'gy', 0, 0)  10.6 us
    ppermute x6, starting transfers between devices, swapped(): return lax.ppermute(part, axis, pairs + [(j, i) for i, j in pairs])  8.07 us
    all_to_all x1, starting transfers between devices, local(): depth_terms = lax.all_to_all(depth_terms, 'gy', 0, 0)  5.98 us
    ppermute x3, starting transfers between devices, local(): lax.ppermute(plane_terms, 'gz', [(i, i ^ hop) for i in range(n_gz)])  5.86 us
    ppermute x3, waiting for transfers between devices, local(): lax.ppermute(plane_terms, 'gz', [(i, i ^ hop) for i in range(n_gz)])  3.91 us
    pallas_call x1, Pallas kernels, ends(): pl.pallas_call(ends_kernel, in_specs=[pl.BlockSpec(memory_space=pl.ANY)],...  3.09 us
    pallas_call x1, Pallas kernels, squares(): pl.pallas_call(squares_kernel, out_shape=jax.ShapeDtypeStruct((width // L...  1.52 us
  transfers between devices with their start and end apart: 10, of which 2 were waited for; matrix products, arithmetic and copies ran while one was open for 0% of the time, Pallas kernels for 3%

profile of v26, /device:TPU:0, one launch (start us, length us, event | category | flops | bytes accessed | tf_op | source)
XLA Modules:
  0.0 71.4 jit_solution(14858159475085106160)
XLA Ops:
  0.6 3.1 %ends.1 = (bf16[64,128]{1,0:T(8,128)(2,1)}, bf16[64,128]{1,0:T(8,128)(2,1)}, bf16[64,512]{1,0:T(8,128)(2,1)}, bf16[64,512]{1,0:T(8,128)(2,1)}) custom-call(bf16[64,64,512]{2,1,0:T(8,128)(2,1)} %cells_ref.1), custom_call_target="tpu_custom_call" | custom-call | flops 2097152 | bytes 4194304 | tf_op jit(solution)/shard_map/ends/pallas_call | solution.py:78
  3.7 3.1 %collective-permute-start = (bf16[64,128]{1,0:T(8,128)(2,1)}, bf16[64,128]{1,0:T(8,128)(2,1)S(1)}, u32[]{:S(2)}, u32[]{:S(2)}) collective-permute-start(bf16[64,128]{1,0:T(8,128)(2,1)} %get-tuple-element.20), channel_id=1, source_target_pairs={{0,1},{2,3},{1,0},{3,2},{4,5},{6,7},{5,4},{7,6},{8,9},{10,11},{9,8... | collective-permute-start | bytes 49160 | tf_op jit(solution)/shard_map/ppermute | solution.py:124
  6.8 0.7 collective-permute-start.1
  7.5 0.7 collective-permute-start.2
  8.1 0.0 copy-start
  8.2 2.9 %collective-permute-start.3 = (bf16[64,512]{1,0:T(8,128)(2,1)}, bf16[64,512]{1,0:T(8,128)(2,1)S(1)}, u32[]{:S(2)}, u32[]{:S(2)}) collective-permute-start(bf16[64,512]{1,0:T(8,128)(2,1)} %get-tuple-element.25), channel_id=1, source_target_pairs={{0,4},{8,12},{16,20},{24,28},{4,0},{12,8},{20,16},{28,24},{1,5},{9... | collective-permute-start | bytes 196616 | tf_op jit(solution)/shard_map/ppermute | solution.py:124
  11.1 0.0 collective-permute-done.inner_ref
  11.1 0.0 collective-permute-done.1.outer_ref
  11.1 0.2 corners.1
  11.3 0.0 copy-start.1
  11.3 0.0 copy-start.2
  11.3 0.1 collective-permute-start.5
  11.4 0.7 collective-permute-start.4
  12.0 0.0 copy-done
  12.0 1.5 %squares.1.sums = f32[4,64,128]{2,1,0:T(8,128)S(1)} custom-call(bf16[64,64,512]{2,1,0:T(8,128)(2,1)S(1)} %copy-done, bf16[64,128]{1,0:T(8,128)(2,1)S(1)} %get-tuple-element.22.later_ref), custom_call_target="tpu_custom_call" | custom-call | flops 6291456 | bytes 4194304 | tf_op jit(solution)/shard_map/squares/pallas_call | solution.py:149
  13.6 0.0 copy-done.1
  13.6 0.0 copy-done.2
  13.6 0.7 terms.1
  14.3 0.0 collective-permute-done.5.inside_tile_ref
  14.3 0.0 collective-permute-done.4.across_tile_ref
  14.3 0.0 collective-permute-done.2.across_ref
  14.3 0.0 collective-permute-done.3.inside_ref
  14.3 29.7 %warp.1 = (bf16[64,64,512]{2,1,0:T(8,128)(2,1)}, f32[8,8,896]{2,1,0:T(8,128)}, f32[64,128]{1,0:T(8,128)S(1)}) custom-call(bf16[64,64,512]{2,1,0:T(8,128)(2,1)} %cells_ref.1, bf16[64,64,512]{2,1,0:T(8,128)(2,1)} %image_hbm.1, bf16[3,64,64,512]{3,2,1,0:T(8,128)(2,1)} %shift_hbm.1, bf16[64,64,128]{2,1,0:T(8,128)(2,1)S(1)} %get-tuple-element.23.beyond_ref, ...), custom_call_target="tpu_custom_call" | custom-call | flops 125829120 | bytes 25165824 | tf_op jit(solution)/shard_map/warp/pallas_call | solution.py:406
  44.1 6.0 %all-to-all-start = ((f32[8,8,896]{2,1,0:T(8,128)}), f32[8,8,896]{2,1,0:T(8,128)S(1)}, u32[]{:S(2)}, u32[]{:S(2)}) async-start(f32[8,8,896]{2,1,0:T(8,128)} %get-tuple-element.31), calls=%async_computation | async-start | bytes 458752 | tf_op jit(solution)/shard_map/all_to_all | solution.py:511
  50.0 2.5 %collective-permute-start.8 = (f32[64,128]{1,0:T(8,128)S(1)}, f32[64,128]{1,0:T(8,128)S(1)}, u32[]{:S(2)}, u32[]{:S(2)}) collective-permute-start(f32[64,128]{1,0:T(8,128)S(1)} %get-tuple-element.32.refs_0_), channel_id=1, source_target_pairs={{0,3},{1,2},{2,1},{3,0},{4,7},{5,6},{6,5},{7,4},{8,11},{9,10},{10,... | collective-permute-start | bytes 98312 | tf_op jit(solution)/shard_map/ppermute | solution.py:513
  52.5 3.4 %collective-permute-start.7 = (f32[64,128]{1,0:T(8,128)S(1)}, f32[64,128]{1,0:T(8,128)S(1)}, u32[]{:S(2)}, u32[]{:S(2)}) collective-permute-start(f32[64,128]{1,0:T(8,128)S(1)} %get-tuple-element.32.refs_0_), channel_id=1, source_target_pairs={{0,2},{1,3},{2,0},{3,1},{4,6},{5,7},{6,4},{7,5},{8,10},{9,11},{10,... | collective-permute-start | bytes 98312 | tf_op jit(solution)/shard_map/ppermute | solution.py:513
  55.9 0.0 collective-permute-start.6
  55.9 0.0 collective-permute-done.8.refs_3_
  55.9 3.2 %collective-permute-done.7.refs_2_ = f32[64,128]{1,0:T(8,128)S(1)} collective-permute-done((f32[64,128]{1,0:T(8,128)S(1)}, f32[64,128]{1,0:T(8,128)S(1)}, u32[]{:S(2)}, u32[]{:S(2)}) %collective-permute-start.7) | collective-permute-done | bytes 32800 | tf_op jit(solution)/shard_map/ppermute | solution.py:513
  59.1 0.7 %collective-permute-done.6.refs_1_ = f32[64,128]{1,0:T(8,128)S(1)} collective-permute-done((f32[64,128]{1,0:T(8,128)S(1)}, f32[64,128]{1,0:T(8,128)S(1)}, u32[]{:S(2)}, u32[]{:S(2)}) %collective-permute-start.6) | collective-permute-done | bytes 32800 | tf_op jit(solution)/shard_map/ppermute | solution.py:513
  59.8 0.0 all-to-all-done.depth_ref
  59.8 0.1 gather.1
  59.9 10.6 %all_to_all.10.depth_ref = f32[8,8,896]{2,1,0:T(8,128)S(1)} all-to-all(f32[8,8,896]{2,1,0:T(8,128)S(1)} %get-tuple-element.33), channel_id=1, replica_groups=mesh['gy'=8,'gz'=4] {'gy'}, dimensions={0} | all-to-all | bytes 458752 | tf_op jit(solution)/shard_map/all_to_all | solution.py:524
  70.5 0.8 %steps.1 = (f32[2,32,512]{2,1,0:T(8,128)}, f32[2,64,32]{2,1,0:T(8,128)}) custom-call(f32[8,8,896]{2,1,0:T(8,128)S(1)} %all_to_all.10.depth_ref, f32[64,128]{1,0:T(8,128)S(1)} %get-tuple-element.34.plane_ref), custom_call_target="tpu_custom_call" | custom-call | tf_op jit(solution)/shard_map/steps/pallas_call | solution.py:526
Async XLA Ops:
  3.7 7.3 %collective-permute-start = (bf16[64,128]{1,0:T(8,128)(2,1)}, bf16[64,128]{1,0:T(8,128)(2,1)S(1)}, u32[]{:S(2)}, u32[]{:S(2)}) collective-permute-start(bf16[64,128]{1,0:T(8,128)(2,1)} %get-tuple-element.20), channel_id=1, source_target_pairs={{0,1},{2,3},{1,0},{3,2},{4,5},{6,7},{5,4},{7,6},{8,9},{10,11},{9,8... | collective-permute-start | bytes 49160 | tf_op jit(solution)/shard_map/ppermute | solution.py:124
  6.8 4.3 %collective-permute-start.1 = (bf16[64,128]{1,0:T(8,128)(2,1)}, bf16[64,128]{1,0:T(8,128)(2,1)S(1)}, u32[]{:S(2)}, u32[]{:S(2)}) collective-permute-start(bf16[64,128]{1,0:T(8,128)(2,1)} %get-tuple-element.21), channel_id=1, source_target_pairs={{1,2},{2,1},{5,6},{6,5},{9,10},{10,9},{13,14},{14,13},{17,18},{18,... | collective-permute-start | bytes 49160 | tf_op jit(solution)/shard_map/ppermute | solution.py:124
  7.5 6.8 %collective-permute-start.2 = (bf16[64,512]{1,0:T(8,128)(2,1)}, bf16[64,512]{1,0:T(8,128)(2,1)S(1)}, u32[]{:S(2)}, u32[]{:S(2)}) collective-permute-start(bf16[64,512]{1,0:T(8,128)(2,1)} %get-tuple-element.24), channel_id=1, source_target_pairs={{4,8},{12,16},{20,24},{8,4},{16,12},{24,20},{5,9},{13,17},{21,25},... | collective-permute-start | bytes 196616 | tf_op jit(solution)/shard_map/ppermute | solution.py:124
  8.1 3.9 %copy-start = (bf16[64,64,512]{2,1,0:T(8,128)(2,1)S(1)}, bf16[64,64,512]{2,1,0:T(8,128)(2,1)}, u32[]{:S(2)}) copy-start(bf16[64,64,512]{2,1,0:T(8,128)(2,1)} %image_hbm.1) | copy-start | bytes 12582916
  8.2 6.2 %collective-permute-start.3 = (bf16[64,512]{1,0:T(8,128)(2,1)}, bf16[64,512]{1,0:T(8,128)(2,1)S(1)}, u32[]{:S(2)}, u32[]{:S(2)}) collective-permute-start(bf16[64,512]{1,0:T(8,128)(2,1)} %get-tuple-element.25), channel_id=1, source_target_pairs={{0,4},{8,12},{16,20},{24,28},{4,0},{12,8},{20,16},{28,24},{1,5},{9... | collective-permute-start | bytes 196616 | tf_op jit(solution)/shard_map/ppermute | solution.py:124
  11.3 2.3 %copy-start.1 = (f32[2,32,512]{2,1,0:T(8,128)S(1)}, f32[2,32,512]{2,1,0:T(8,128)}, u32[]{:S(2)}) copy-start(f32[2,32,512]{2,1,0:T(8,128)} %depth_ref.3) | copy-start | bytes 393220
  11.3 2.3 %copy-start.2 = (f32[2,32,8,8]{1,3,2,0:T(8,128)S(1)}, f32[2,32,8,8]{1,3,2,0:T(8,128)}, u32[]{:S(2)}) copy-start(f32[2,32,8,8]{1,3,2,0:T(8,128)} %param.8) | copy-start | bytes 49156
  11.3 3.0 %collective-permute-start.5 = (bf16[64,128]{1,0:T(8,128)(2,1)S(1)}, bf16[64,128]{1,0:T(8,128)(2,1)S(1)}, u32[]{:S(2)}, u32[]{:S(2)}) collective-permute-start(bf16[64,128]{1,0:T(8,128)(2,1)S(1)} %get-tuple-element.26), channel_id=1, source_target_pairs={{0,4},{8,12},{16,20},{24,28},{4,0},{12,8},{20,16},{28,24},{1,5},{9... | collective-permute-start | bytes 49160 | tf_op jit(solution)/shard_map/ppermute | solution.py:124
  11.4 2.9 %collective-permute-start.4 = (bf16[64,128]{1,0:T(8,128)(2,1)S(1)}, bf16[64,128]{1,0:T(8,128)(2,1)S(1)}, u32[]{:S(2)}, u32[]{:S(2)}) collective-permute-start(bf16[64,128]{1,0:T(8,128)(2,1)S(1)} %get-tuple-element.22.later_ref), channel_id=1, source_target_pairs={{4,8},{12,16},{20,24},{8,4},{16,12},{24,20},{5,9},{13,17},{21,25},... | collective-permute-start | bytes 49160 | tf_op jit(solution)/shard_map/ppermute | solution.py:124
  44.1 15.8 %all-to-all-start = ((f32[8,8,896]{2,1,0:T(8,128)}), f32[8,8,896]{2,1,0:T(8,128)S(1)}, u32[]{:S(2)}, u32[]{:S(2)}) async-start(f32[8,8,896]{2,1,0:T(8,128)} %get-tuple-element.31), calls=%async_computation | async-start | bytes 458752 | tf_op jit(solution)/shard_map/all_to_all | solution.py:511
  50.0 5.9 %collective-permute-start.8 = (f32[64,128]{1,0:T(8,128)S(1)}, f32[64,128]{1,0:T(8,128)S(1)}, u32[]{:S(2)}, u32[]{:S(2)}) collective-permute-start(f32[64,128]{1,0:T(8,128)S(1)} %get-tuple-element.32.refs_0_), channel_id=1, source_target_pairs={{0,3},{1,2},{2,1},{3,0},{4,7},{5,6},{6,5},{7,4},{8,11},{9,10},{10,... | collective-permute-start | bytes 98312 | tf_op jit(solution)/shard_map/ppermute | solution.py:513
  52.5 6.6 %collective-permute-start.7 = (f32[64,128]{1,0:T(8,128)S(1)}, f32[64,128]{1,0:T(8,128)S(1)}, u32[]{:S(2)}, u32[]{:S(2)}) collective-permute-start(f32[64,128]{1,0:T(8,128)S(1)} %get-tuple-element.32.refs_0_), channel_id=1, source_target_pairs={{0,2},{1,3},{2,0},{3,1},{4,6},{5,7},{6,4},{7,5},{8,10},{9,11},{10,... | collective-permute-start | bytes 98312 | tf_op jit(solution)/shard_map/ppermute | solution.py:513
  55.9 3.9 %collective-permute-start.6 = (f32[64,128]{1,0:T(8,128)S(1)}, f32[64,128]{1,0:T(8,128)S(1)}, u32[]{:S(2)}, u32[]{:S(2)}) collective-permute-start(f32[64,128]{1,0:T(8,128)S(1)} %get-tuple-element.32.refs_0_), channel_id=1, source_target_pairs={{0,1},{1,0},{2,3},{3,2},{4,5},{5,4},{6,7},{7,6},{8,9},{9,8},{10,11... | collective-permute-start | bytes 98312 | tf_op jit(solution)/shard_map/ppermute | solution.py:513

commit v27 on v26

--- a/solution.py
+++ b/solution.py
@@ -248,10 +248,12 @@
     def _():
         slot = (step % 3) * block_rows
         odd = lax.axis_index("gy") % 2 == 1
-        across, inside = (
-            jnp.concatenate([row[...].astype(f32), tile[...].astype(f32)], axis=1)
-            for row, tile in ((across_ref, across_tile_ref), (inside_ref, inside_tile_ref))
-        )
+
+        def rim_rows(row, tile):
+            both = jnp.concatenate([row[...].astype(f32), tile[...].astype(f32)], axis=1)
+            return jnp.where(step % 2 == 0, both[0:planes], both[planes:])
+
+        across, inside = rim_rows(across_ref, across_tile_ref), rim_rows(inside_ref, inside_tile_ref)
         low, high = jnp.where(odd, inside, across), jnp.where(odd, across, inside)
         at = lax.broadcasted_iota(jnp.int32, (2 * TOP, width + LANES), 0)
         for k in range(planes):
@@ -411,10 +413,10 @@
             pl.BlockSpec(memory_space=pl.ANY),
             pl.BlockSpec(memory_space=pl.ANY),
             pl.BlockSpec((KNOT, rows, LANES), ahead),
-            pl.BlockSpec((KNOT, across.shape[1]), lambda i: (jnp.minimum(i, count - 1), 0)),
-            pl.BlockSpec((KNOT, inside.shape[1]), lambda i: (jnp.minimum(i, count - 1), 0)),
-            pl.BlockSpec((KNOT, LANES), lambda i: (jnp.minimum(i, count - 1), 0)),
-            pl.BlockSpec((KNOT, LANES), lambda i: (jnp.minimum(i, count - 1), 0)),
+            pl.BlockSpec((2 * KNOT, across.shape[1]), lambda i: (jnp.minimum(i, count - 1) // 2, 0)),
+            pl.BlockSpec((2 * KNOT, inside.shape[1]), lambda i: (jnp.minimum(i, count - 1) // 2, 0)),
+            pl.BlockSpec((2 * KNOT, LANES), lambda i: (jnp.minimum(i, count - 1) // 2, 0)),
+            pl.BlockSpec((2 * KNOT, LANES), lambda i: (jnp.minimum(i, count - 1) // 2, 0)),
             pl.BlockSpec(field.shape, lambda i: (0, 0, 0, 0)),
             pl.BlockSpec(plane.shape, whole),
             pl.BlockSpec(depth_factors.shape, whole),

time: 71.7 us -> 71.7 us (level)
  no operation moved by 1% of the time
where the time goes in v27:
time: 71.7 us; the launch traced here: 71.4 us
  Pallas kernels  36.1 us (50%)
  starting transfers between devices  19.9 us (28%)
  blocking collectives  10.6 us (15%)
  waiting for transfers between devices  3.93 us (5%)
  between operations  0.78 us (1%)
    pallas_call x1, Pallas kernels, warp(): pl.pallas_call(warp_kernel, grid=(count + 1,), in_specs=[pl.BlockSpec((KN...  29.7 us
    all_to_all x1, blocking collectives, local(): depth_terms = lax.all_to_all(depth_terms, 'gy', 0, 0)  10.6 us
    ppermute x6, starting transfers between devices, swapped(): return lax.ppermute(part, axis, pairs + [(j, i) for i, j in pairs])  8.07 us
    all_to_all x1, starting transfers between devices, local(): depth_terms = lax.all_to_all(depth_terms, 'gy', 0, 0)  5.98 us
    ppermute x3, starting transfers between devices, local(): lax.ppermute(plane_terms, 'gz', [(i, i ^ hop) for i in range(n_gz)])  5.86 us
    ppermute x3, waiting for transfers between devices, local(): lax.ppermute(plane_terms, 'gz', [(i, i ^ hop) for i in range(n_gz)])  3.91 us
    pallas_call x1, Pallas kernels, ends(): pl.pallas_call(ends_kernel, in_specs=[pl.BlockSpec(memory_space=pl.ANY)],...  3.09 us
    pallas_call x1, Pallas kernels, squares(): pl.pallas_call(squares_kernel, out_shape=jax.ShapeDtypeStruct((width // L...  1.52 us
  transfers between devices with their start and end apart: 10, of which 2 were waited for; matrix products, arithmetic and copies ran while one was open for 0% of the time, Pallas kernels for 3%

profile of v27, /device:TPU:0, one launch (start us, length us, event | category | flops | bytes accessed | tf_op | source)
XLA Modules:
  0.0 71.4 jit_solution(6460011023984320618)
XLA Ops:
  0.6 3.1 %ends.1 = (bf16[64,128]{1,0:T(8,128)(2,1)}, bf16[64,128]{1,0:T(8,128)(2,1)}, bf16[64,512]{1,0:T(8,128)(2,1)}, bf16[64,512]{1,0:T(8,128)(2,1)}) custom-call(bf16[64,64,512]{2,1,0:T(8,128)(2,1)} %cells_ref.1), custom_call_target="tpu_custom_call" | custom-call | flops 2097152 | bytes 4194304 | tf_op jit(solution)/shard_map/ends/pallas_call | solution.py:78
  3.7 3.1 %collective-permute-start = (bf16[64,128]{1,0:T(8,128)(2,1)}, bf16[64,128]{1,0:T(8,128)(2,1)S(1)}, u32[]{:S(2)}, u32[]{:S(2)}) collective-permute-start(bf16[64,128]{1,0:T(8,128)(2,1)} %get-tuple-element.20), channel_id=1, source_target_pairs={{0,1},{2,3},{1,0},{3,2},{4,5},{6,7},{5,4},{7,6},{8,9},{10,11},{9,8... | collective-permute-start | bytes 49160 | tf_op jit(solution)/shard_map/ppermute | solution.py:124
  6.8 0.7 collective-permute-start.1
  7.5 0.7 collective-permute-start.2
  8.1 0.0 copy-start
  8.2 2.9 %collective-permute-start.3 = (bf16[64,512]{1,0:T(8,128)(2,1)}, bf16[64,512]{1,0:T(8,128)(2,1)S(1)}, u32[]{:S(2)}, u32[]{:S(2)}) collective-permute-start(bf16[64,512]{1,0:T(8,128)(2,1)} %get-tuple-element.25), channel_id=1, source_target_pairs={{0,4},{8,12},{16,20},{24,28},{4,0},{12,8},{20,16},{28,24},{1,5},{9... | collective-permute-start | bytes 196616 | tf_op jit(solution)/shard_map/ppermute | solution.py:124
  11.1 0.0 collective-permute-done.inner_ref
  11.1 0.0 collective-permute-done.1.outer_ref
  11.1 0.2 corners.1
  11.3 0.0 copy-start.1
  11.3 0.0 copy-start.2
  11.3 0.1 collective-permute-start.5
  11.4 0.7 collective-permute-start.4
  12.0 0.0 copy-done
  12.0 1.5 %squares.1.sums = f32[4,64,128]{2,1,0:T(8,128)S(1)} custom-call(bf16[64,64,512]{2,1,0:T(8,128)(2,1)S(1)} %copy-done, bf16[64,128]{1,0:T(8,128)(2,1)S(1)} %get-tuple-element.22.later_ref), custom_call_target="tpu_custom_call" | custom-call | flops 6291456 | bytes 4194304 | tf_op jit(solution)/shard_map/squares/pallas_call | solution.py:149
  13.6 0.0 copy-done.1
  13.6 0.0 copy-done.2
  13.6 0.7 terms.1
  14.3 0.0 collective-permute-done.5.inside_tile_ref
  14.3 0.0 collective-permute-done.4.across_tile_ref
  14.3 0.0 collective-permute-done.2.across_ref
  14.3 0.0 collective-permute-done.3.inside_ref
  14.3 29.7 %warp.1 = (bf16[64,64,512]{2,1,0:T(8,128)(2,1)}, f32[8,8,896]{2,1,0:T(8,128)}, f32[64,128]{1,0:T(8,128)S(1)}) custom-call(bf16[64,64,512]{2,1,0:T(8,128)(2,1)} %cells_ref.1, bf16[64,64,512]{2,1,0:T(8,128)(2,1)} %image_hbm.1, bf16[3,64,64,512]{3,2,1,0:T(8,128)(2,1)} %shift_hbm.1, bf16[64,64,128]{2,1,0:T(8,128)(2,1)S(1)} %get-tuple-element.23.beyond_ref, ...), custom_call_target="tpu_custom_call" | custom-call | flops 125829120 | bytes 25165824 | tf_op jit(solution)/shard_map/warp/pallas_call | solution.py:408
  44.1 6.0 %all-to-all-start = ((f32[8,8,896]{2,1,0:T(8,128)}), f32[8,8,896]{2,1,0:T(8,128)S(1)}, u32[]{:S(2)}, u32[]{:S(2)}) async-start(f32[8,8,896]{2,1,0:T(8,128)} %get-tuple-element.31), calls=%async_computation | async-start | bytes 458752 | tf_op jit(solution)/shard_map/all_to_all | solution.py:513
  50.0 2.5 %collective-permute-start.8 = (f32[64,128]{1,0:T(8,128)S(1)}, f32[64,128]{1,0:T(8,128)S(1)}, u32[]{:S(2)}, u32[]{:S(2)}) collective-permute-start(f32[64,128]{1,0:T(8,128)S(1)} %get-tuple-element.32.refs_0_), channel_id=1, source_target_pairs={{0,3},{1,2},{2,1},{3,0},{4,7},{5,6},{6,5},{7,4},{8,11},{9,10},{10,... | collective-permute-start | bytes 98312 | tf_op jit(solution)/shard_map/ppermute | solution.py:515
  52.5 3.4 %collective-permute-start.7 = (f32[64,128]{1,0:T(8,128)S(1)}, f32[64,128]{1,0:T(8,128)S(1)}, u32[]{:S(2)}, u32[]{:S(2)}) collective-permute-start(f32[64,128]{1,0:T(8,128)S(1)} %get-tuple-element.32.refs_0_), channel_id=1, source_target_pairs={{0,2},{1,3},{2,0},{3,1},{4,6},{5,7},{6,4},{7,5},{8,10},{9,11},{10,... | collective-permute-start | bytes 98312 | tf_op jit(solution)/shard_map/ppermute | solution.py:515
  55.9 0.0 collective-permute-start.6
  55.9 0.0 collective-permute-done.8.refs_3_
  55.9 3.2 %collective-permute-done.7.refs_2_ = f32[64,128]{1,0:T(8,128)S(1)} collective-permute-done((f32[64,128]{1,0:T(8,128)S(1)}, f32[64,128]{1,0:T(8,128)S(1)}, u32[]{:S(2)}, u32[]{:S(2)}) %collective-permute-start.7) | collective-permute-done | bytes 32800 | tf_op jit(solution)/shard_map/ppermute | solution.py:515
  59.1 0.7 %collective-permute-done.6.refs_1_ = f32[64,128]{1,0:T(8,128)S(1)} collective-permute-done((f32[64,128]{1,0:T(8,128)S(1)}, f32[64,128]{1,0:T(8,128)S(1)}, u32[]{:S(2)}, u32[]{:S(2)}) %collective-permute-start.6) | collective-permute-done | bytes 32800 | tf_op jit(solution)/shard_map/ppermute | solution.py:515
  59.8 0.0 all-to-all-done.depth_ref
  59.8 0.1 gather.1
  60.0 10.6 %all_to_all.10.depth_ref = f32[8,8,896]{2,1,0:T(8,128)S(1)} all-to-all(f32[8,8,896]{2,1,0:T(8,128)S(1)} %get-tuple-element.33), channel_id=1, replica_groups=mesh['gy'=8,'gz'=4] {'gy'}, dimensions={0} | all-to-all | bytes 458752 | tf_op jit(solution)/shard_map/all_to_all | solution.py:526
  70.5 0.8 %steps.1 = (f32[2,32,512]{2,1,0:T(8,128)}, f32[2,64,32]{2,1,0:T(8,128)}) custom-call(f32[8,8,896]{2,1,0:T(8,128)S(1)} %all_to_all.10.depth_ref, f32[64,128]{1,0:T(8,128)S(1)} %get-tuple-element.34.plane_ref), custom_call_target="tpu_custom_call" | custom-call | tf_op jit(solution)/shard_map/steps/pallas_call | solution.py:528
Async XLA Ops:
  3.7 7.3 %collective-permute-start = (bf16[64,128]{1,0:T(8,128)(2,1)}, bf16[64,128]{1,0:T(8,128)(2,1)S(1)}, u32[]{:S(2)}, u32[]{:S(2)}) collective-permute-start(bf16[64,128]{1,0:T(8,128)(2,1)} %get-tuple-element.20), channel_id=1, source_target_pairs={{0,1},{2,3},{1,0},{3,2},{4,5},{6,7},{5,4},{7,6},{8,9},{10,11},{9,8... | collective-permute-start | bytes 49160 | tf_op jit(solution)/shard_map/ppermute | solution.py:124
  6.8 4.3 %collective-permute-start.1 = (bf16[64,128]{1,0:T(8,128)(2,1)}, bf16[64,128]{1,0:T(8,128)(2,1)S(1)}, u32[]{:S(2)}, u32[]{:S(2)}) collective-permute-start(bf16[64,128]{1,0:T(8,128)(2,1)} %get-tuple-element.21), channel_id=1, source_target_pairs={{1,2},{2,1},{5,6},{6,5},{9,10},{10,9},{13,14},{14,13},{17,18},{18,... | collective-permute-start | bytes 49160 | tf_op jit(solution)/shard_map/ppermute | solution.py:124
  7.5 6.8 %collective-permute-start.2 = (bf16[64,512]{1,0:T(8,128)(2,1)}, bf16[64,512]{1,0:T(8,128)(2,1)S(1)}, u32[]{:S(2)}, u32[]{:S(2)}) collective-permute-start(bf16[64,512]{1,0:T(8,128)(2,1)} %get-tuple-element.24), channel_id=1, source_target_pairs={{4,8},{12,16},{20,24},{8,4},{16,12},{24,20},{5,9},{13,17},{21,25},... | collective-permute-start | bytes 196616 | tf_op jit(solution)/shard_map/ppermute | solution.py:124
  8.1 3.9 %copy-start = (bf16[64,64,512]{2,1,0:T(8,128)(2,1)S(1)}, bf16[64,64,512]{2,1,0:T(8,128)(2,1)}, u32[]{:S(2)}) copy-start(bf16[64,64,512]{2,1,0:T(8,128)(2,1)} %image_hbm.1) | copy-start | bytes 12582916
  8.2 6.2 %collective-permute-start.3 = (bf16[64,512]{1,0:T(8,128)(2,1)}, bf16[64,512]{1,0:T(8,128)(2,1)S(1)}, u32[]{:S(2)}, u32[]{:S(2)}) collective-permute-start(bf16[64,512]{1,0:T(8,128)(2,1)} %get-tuple-element.25), channel_id=1, source_target_pairs={{0,4},{8,12},{16,20},{24,28},{4,0},{12,8},{20,16},{28,24},{1,5},{9... | collective-permute-start | bytes 196616 | tf_op jit(solution)/shard_map/ppermute | solution.py:124
  11.3 2.3 %copy-start.1 = (f32[2,32,512]{2,1,0:T(8,128)S(1)}, f32[2,32,512]{2,1,0:T(8,128)}, u32[]{:S(2)}) copy-start(f32[2,32,512]{2,1,0:T(8,128)} %depth_ref.3) | copy-start | bytes 393220
  11.3 2.3 %copy-start.2 = (f32[2,32,8,8]{1,3,2,0:T(8,128)S(1)}, f32[2,32,8,8]{1,3,2,0:T(8,128)}, u32[]{:S(2)}) copy-start(f32[2,32,8,8]{1,3,2,0:T(8,128)} %param.8) | copy-start | bytes 49156
  11.3 3.0 %collective-permute-start.5 = (bf16[64,128]{1,0:T(8,128)(2,1)S(1)}, bf16[64,128]{1,0:T(8,128)(2,1)S(1)}, u32[]{:S(2)}, u32[]{:S(2)}) collective-permute-start(bf16[64,128]{1,0:T(8,128)(2,1)S(1)} %get-tuple-element.26), channel_id=1, source_target_pairs={{0,4},{8,12},{16,20},{24,28},{4,0},{12,8},{20,16},{28,24},{1,5},{9... | collective-permute-start | bytes 49160 | tf_op jit(solution)/shard_map/ppermute | solution.py:124
  11.4 2.9 %collective-permute-start.4 = (bf16[64,128]{1,0:T(8,128)(2,1)S(1)}, bf16[64,128]{1,0:T(8,128)(2,1)S(1)}, u32[]{:S(2)}, u32[]{:S(2)}) collective-permute-start(bf16[64,128]{1,0:T(8,128)(2,1)S(1)} %get-tuple-element.22.later_ref), channel_id=1, source_target_pairs={{4,8},{12,16},{20,24},{8,4},{16,12},{24,20},{5,9},{13,17},{21,25},... | collective-permute-start | bytes 49160 | tf_op jit(solution)/shard_map/ppermute | solution.py:124
  44.1 15.8 %all-to-all-start = ((f32[8,8,896]{2,1,0:T(8,128)}), f32[8,8,896]{2,1,0:T(8,128)S(1)}, u32[]{:S(2)}, u32[]{:S(2)}) async-start(f32[8,8,896]{2,1,0:T(8,128)} %get-tuple-element.31), calls=%async_computation | async-start | bytes 458752 | tf_op jit(solution)/shard_map/all_to_all | solution.py:513
  50.0 5.9 %collective-permute-start.8 = (f32[64,128]{1,0:T(8,128)S(1)}, f32[64,128]{1,0:T(8,128)S(1)}, u32[]{:S(2)}, u32[]{:S(2)}) collective-permute-start(f32[64,128]{1,0:T(8,128)S(1)} %get-tuple-element.32.refs_0_), channel_id=1, source_target_pairs={{0,3},{1,2},{2,1},{3,0},{4,7},{5,6},{6,5},{7,4},{8,11},{9,10},{10,... | collective-permute-start | bytes 98312 | tf_op jit(solution)/shard_map/ppermute | solution.py:515
  52.5 6.6 %collective-permute-start.7 = (f32[64,128]{1,0:T(8,128)S(1)}, f32[64,128]{1,0:T(8,128)S(1)}, u32[]{:S(2)}, u32[]{:S(2)}) collective-permute-start(f32[64,128]{1,0:T(8,128)S(1)} %get-tuple-element.32.refs_0_), channel_id=1, source_target_pairs={{0,2},{1,3},{2,0},{3,1},{4,6},{5,7},{6,4},{7,5},{8,10},{9,11},{10,... | collective-permute-start | bytes 98312 | tf_op jit(solution)/shard_map/ppermute | solution.py:515
  55.9 3.9 %collective-permute-start.6 = (f32[64,128]{1,0:T(8,128)S(1)}, f32[64,128]{1,0:T(8,128)S(1)}, u32[]{:S(2)}, u32[]{:S(2)}) collective-permute-start(f32[64,128]{1,0:T(8,128)S(1)} %get-tuple-element.32.refs_0_), channel_id=1, source_target_pairs={{0,1},{1,0},{2,3},{3,2},{4,5},{5,4},{6,7},{7,6},{8,9},{9,8},{10,11... | collective-permute-start | bytes 98312 | tf_op jit(solution)/shard_map/ppermute | solution.py:515

commit v28 on v27

--- a/solution.py
+++ b/solution.py
@@ -200,7 +200,7 @@
     across_tile_ref, inside_tile_ref, field, plane_ref, depth_ref,
     diag_depth_ref, diag_plane_ref,
     residual_hbm, depth_out, plane_out,
-    ahead_ref, here_ref, behind_ref, wide, bands, blocks, energy, held,
+    ahead_ref, here_ref, behind_ref, wide, bands, blocks, energy,
     image_ref, shift_ref, residual_ref, got, sent,
 ):
     step = pl.program_id(0)
@@ -317,33 +317,33 @@
             at = pl.multiple_of(tile * LANES, LANES)
             top = pl.multiple_of(pair * 16, 16)
             origins = [first + tile * pitch + top + TOP for first in first_rows]
-            for half in range(2):
-                node = (step - 1) * nodes + pair * 2 + half
-                mine = slice(8 * half, 8 * half + 8)
-
-                def taps(x):
-                    part = 0 if x == 0 else 2 if x == planes + 1 else 1
-                    plus = (x - 1) * plane_rows + 8 * half if part == 1 else 8 * half
-                    return [
-                        [window[c][pl.ds(origins[part] + (plus + b), 8), :] for c in range(3)] for b in (-1, 0, 1)
-                    ]
-
-                contrast = jnp.broadcast_to(field[0, tile, pl.ds(node, 1), :], (8, LANES))
-                brightness = jnp.broadcast_to(field[1, tile, pl.ds(node, 1), :], (8, LANES))
-                by_image = jnp.zeros((8, LANES), f32)
-                plain = jnp.zeros((8, LANES), f32)
-                here = taps(1)
-                for k in range(planes):
-                    before, after = taps(k), taps(k + 2)
-                    place = (k, pl.ds(top, 16), pl.ds(at, LANES))
-                    sx, sy, sz = (shift_ref[(here_slot, axis) + place].astype(f32)[mine] for axis in range(3))
-                    image = image_ref[(here_slot,) + place].astype(f32)[mine]
+            first_node = (step - 1) * nodes + pair * 2
+
+            def taps(x, half):
+                part = 0 if x == 0 else 2 if x == planes + 1 else 1
+                plus = (x - 1) * plane_rows + 8 * half if part == 1 else 8 * half
+                return [[window[c][pl.ds(origins[part] + (plus + b), 8), :] for c in range(3)] for b in (-1, 0, 1)]
+
+            def node_rows(k, half):
+                return jnp.broadcast_to(field[k, tile, pl.ds(first_node + half, 1), :], (8, LANES))
+
+            by_image = [jnp.zeros((8, LANES), f32) for _ in range(2)]
+            plain = [jnp.zeros((8, LANES), f32) for _ in range(2)]
+            here = [taps(1, half) for half in range(2)]
+            for k in range(planes):
+                place = (k, pl.ds(top, 16), pl.ds(at, LANES))
+                inputs = [shift_ref[(here_slot, axis) + place].astype(f32) for axis in range(3)]
+                inputs.append(image_ref[(here_slot,) + place].astype(f32))
+                results = []
+                for half in range(2):
+                    before, after = taps(k, half), taps(k + 2, half)
+                    sx, sy, sz, image = (v[8 * half : 8 * half + 8] for v in inputs)
                     px, py, pz = sx > 0, sy > 0, sz > 0
                     ax, ay = jnp.abs(sx), jnp.abs(sy)
 
                     def sides(c):
                         far = [jnp.where(px, after[b][c], before[b][c]) for b in range(3)]
-                        near = [here[b][c] for b in range(3)]
+                        near = [here[half][b][c] for b in range(3)]
                         return [(v[1], jnp.where(py, v[2], v[0])) for v in (near, far)]
 
                     ahead, middle, behind = sides(0), sides(1), sides(2)
@@ -352,17 +352,16 @@
                         near, far = (middle[v][b] + sz * jnp.where(pz, ahead[v][b], behind[v][b]) for v in range(2))
                         lines.append(near + ax * (far - near))
                     warped = lines[0] + ay * (lines[1] - lines[0])
-                    misfit = warped - contrast * image - brightness
-                    if half == 0:
-                        held[k] = misfit
-                    else:
-                        residual_ref[(here_slot,) + place] = jnp.concatenate([held[k], misfit], axis=0).astype(bf16)
-                    by_image = by_image + misfit * image
-                    plain = plain + misfit
+                    misfit = warped - node_rows(0, half) * image - node_rows(1, half)
+                    results.append(misfit)
+                    by_image[half] = by_image[half] + misfit * image
+                    plain[half] = plain[half] + misfit
                     total = total + misfit * misfit
-                    here = after
-                for k, value in ((0, by_image), (1, plain)):
-                    blocks[k, tile, pl.ds(node, 1), :] = jnp.sum(value, axis=0, keepdims=True)
+                    here[half] = after
+                residual_ref[(here_slot,) + place] = jnp.concatenate(results, axis=0).astype(bf16)
+            for half in range(2):
+                for k, value in ((0, by_image[half]), (1, plain[half])):
+                    blocks[k, tile, pl.ds(first_node + half, 1), :] = jnp.sum(value, axis=0, keepdims=True)
             return total
 
         energy[...] = lax.fori_loop(0, (rows // 16) * tiles, one, energy[...])
@@ -439,7 +438,6 @@
             pltpu.VMEM((2, 3 * LANES, 2 * LANES), bf16),
             pltpu.VMEM((2, tiles, nodes, LANES), f32),
             pltpu.VMEM((8, LANES), f32),
-            pltpu.VMEM((KNOT, 8, LANES), f32),
             pltpu.VMEM((2, KNOT, rows, width), bf16),
             pltpu.VMEM((2, 3, KNOT, rows, width), bf16),
             pltpu.VMEM((2, KNOT, rows, width), bf16),

time: 71.7 us -> 73.8 us (1.029)
  Pallas kernels: 36.1 us -> 38.3 us
    pallas_call x1, Pallas kernels: 29.7 us -> 31.9 us  [warp(): pl.pallas_call(warp_kernel, grid=(count + 1,), in_specs=[pl.BlockSpec((KN...]
where the time goes in v28:
time: 73.8 us; the launch traced here: 73.5 us
  Pallas kernels  38.3 us (52%)
  starting transfers between devices  19.9 us (27%)
  blocking collectives  10.6 us (14%)
  waiting for transfers between devices  3.93 us (5%)
  between operations  0.78 us (1%)
    pallas_call x1, Pallas kernels, warp(): pl.pallas_call(warp_kernel, grid=(count + 1,), in_specs=[pl.BlockSpec((KN...  31.9 us
    all_to_all x1, blocking collectives, local(): depth_terms = lax.all_to_all(depth_terms, 'gy', 0, 0)  10.6 us
    ppermute x6, starting transfers between devices, swapped(): return lax.ppermute(part, axis, pairs + [(j, i) for i, j in pairs])  8.07 us
    all_to_all x1, starting transfers between devices, local(): depth_terms = lax.all_to_all(depth_terms, 'gy', 0, 0)  5.98 us
    ppermute x3, starting transfers between devices, local(): lax.ppermute(plane_terms, 'gz', [(i, i ^ hop) for i in range(n_gz)])  5.86 us
    ppermute x3, waiting for transfers between devices, local(): lax.ppermute(plane_terms, 'gz', [(i, i ^ hop) for i in range(n_gz)])  3.91 us
    pallas_call x1, Pallas kernels, ends(): pl.pallas_call(ends_kernel, in_specs=[pl.BlockSpec(memory_space=pl.ANY)],...  3.09 us
    pallas_call x1, Pallas kernels, squares(): pl.pallas_call(squares_kernel, out_shape=jax.ShapeDtypeStruct((width // L...  1.52 us
  transfers between devices with their start and end apart: 10, of which 2 were waited for; matrix products, arithmetic and copies ran while one was open for 0% of the time, Pallas kernels for 3%

profile of v28, /device:TPU:0, one launch (start us, length us, event | category | flops | bytes accessed | tf_op | source)
XLA Modules:
  0.0 73.5 jit_solution(5115055186431559801)
XLA Ops:
  0.6 3.1 %ends.1 = (bf16[64,128]{1,0:T(8,128)(2,1)}, bf16[64,128]{1,0:T(8,128)(2,1)}, bf16[64,512]{1,0:T(8,128)(2,1)}, bf16[64,512]{1,0:T(8,128)(2,1)}) custom-call(bf16[64,64,512]{2,1,0:T(8,128)(2,1)} %cells_ref.1), custom_call_target="tpu_custom_call" | custom-call | flops 2097152 | bytes 4194304 | tf_op jit(solution)/shard_map/ends/pallas_call | solution.py:78
  3.7 3.1 %collective-permute-start = (bf16[64,128]{1,0:T(8,128)(2,1)}, bf16[64,128]{1,0:T(8,128)(2,1)S(1)}, u32[]{:S(2)}, u32[]{:S(2)}) collective-permute-start(bf16[64,128]{1,0:T(8,128)(2,1)} %get-tuple-element.20), channel_id=1, source_target_pairs={{0,1},{2,3},{1,0},{3,2},{4,5},{6,7},{5,4},{7,6},{8,9},{10,11},{9,8... | collective-permute-start | bytes 49160 | tf_op jit(solution)/shard_map/ppermute | solution.py:124
  6.8 0.7 collective-permute-start.1
  7.5 0.7 collective-permute-start.2
  8.1 0.0 copy-start
  8.2 2.9 %collective-permute-start.3 = (bf16[64,512]{1,0:T(8,128)(2,1)}, bf16[64,512]{1,0:T(8,128)(2,1)S(1)}, u32[]{:S(2)}, u32[]{:S(2)}) collective-permute-start(bf16[64,512]{1,0:T(8,128)(2,1)} %get-tuple-element.25), channel_id=1, source_target_pairs={{0,4},{8,12},{16,20},{24,28},{4,0},{12,8},{20,16},{28,24},{1,5},{9... | collective-permute-start | bytes 196616 | tf_op jit(solution)/shard_map/ppermute | solution.py:124
  11.1 0.0 collective-permute-done.inner_ref
  11.1 0.0 collective-permute-done.1.outer_ref
  11.1 0.2 corners.1
  11.3 0.0 copy-start.1
  11.3 0.0 copy-start.2
  11.3 0.1 collective-permute-start.5
  11.4 0.7 collective-permute-start.4
  12.0 0.0 copy-done
  12.0 1.5 %squares.1.sums = f32[4,64,128]{2,1,0:T(8,128)S(1)} custom-call(bf16[64,64,512]{2,1,0:T(8,128)(2,1)S(1)} %copy-done, bf16[64,128]{1,0:T(8,128)(2,1)S(1)} %get-tuple-element.22.later_ref), custom_call_target="tpu_custom_call" | custom-call | flops 6291456 | bytes 4194304 | tf_op jit(solution)/shard_map/squares/pallas_call | solution.py:149
  13.6 0.0 copy-done.1
  13.6 0.0 copy-done.2
  13.6 0.7 terms.1
  14.3 0.0 collective-permute-done.5.inside_tile_ref
  14.3 0.0 collective-permute-done.4.across_tile_ref
  14.3 0.0 collective-permute-done.2.across_ref
  14.3 0.0 collective-permute-done.3.inside_ref
  14.3 31.9 %warp.1 = (bf16[64,64,512]{2,1,0:T(8,128)(2,1)}, f32[8,8,896]{2,1,0:T(8,128)}, f32[64,128]{1,0:T(8,128)S(1)}) custom-call(bf16[64,64,512]{2,1,0:T(8,128)(2,1)} %cells_ref.1, bf16[64,64,512]{2,1,0:T(8,128)(2,1)} %image_hbm.1, bf16[3,64,64,512]{3,2,1,0:T(8,128)(2,1)} %shift_hbm.1, bf16[64,64,128]{2,1,0:T(8,128)(2,1)S(1)} %get-tuple-element.23.beyond_ref, ...), custom_call_target="tpu_custom_call" | custom-call | flops 125829120 | bytes 25165824 | tf_op jit(solution)/shard_map/warp/pallas_call | solution.py:407
  46.2 6.0 %all-to-all-start = ((f32[8,8,896]{2,1,0:T(8,128)}), f32[8,8,896]{2,1,0:T(8,128)S(1)}, u32[]{:S(2)}, u32[]{:S(2)}) async-start(f32[8,8,896]{2,1,0:T(8,128)} %get-tuple-element.31), calls=%async_computation | async-start | bytes 458752 | tf_op jit(solution)/shard_map/all_to_all | solution.py:511
  52.2 2.5 %collective-permute-start.8 = (f32[64,128]{1,0:T(8,128)S(1)}, f32[64,128]{1,0:T(8,128)S(1)}, u32[]{:S(2)}, u32[]{:S(2)}) collective-permute-start(f32[64,128]{1,0:T(8,128)S(1)} %get-tuple-element.32.refs_0_), channel_id=1, source_target_pairs={{0,3},{1,2},{2,1},{3,0},{4,7},{5,6},{6,5},{7,4},{8,11},{9,10},{10,... | collective-permute-start | bytes 98312 | tf_op jit(solution)/shard_map/ppermute | solution.py:513
  54.7 3.4 %collective-permute-start.7 = (f32[64,128]{1,0:T(8,128)S(1)}, f32[64,128]{1,0:T(8,128)S(1)}, u32[]{:S(2)}, u32[]{:S(2)}) collective-permute-start(f32[64,128]{1,0:T(8,128)S(1)} %get-tuple-element.32.refs_0_), channel_id=1, source_target_pairs={{0,2},{1,3},{2,0},{3,1},{4,6},{5,7},{6,4},{7,5},{8,10},{9,11},{10,... | collective-permute-start | bytes 98312 | tf_op jit(solution)/shard_map/ppermute | solution.py:513
  58.0 0.0 collective-permute-start.6
  58.0 0.0 collective-permute-done.8.refs_3_
  58.0 3.2 %collective-permute-done.7.refs_2_ = f32[64,128]{1,0:T(8,128)S(1)} collective-permute-done((f32[64,128]{1,0:T(8,128)S(1)}, f32[64,128]{1,0:T(8,128)S(1)}, u32[]{:S(2)}, u32[]{:S(2)}) %collective-permute-start.7) | collective-permute-done | bytes 32800 | tf_op jit(solution)/shard_map/ppermute | solution.py:513
  61.2 0.7 %collective-permute-done.6.refs_1_ = f32[64,128]{1,0:T(8,128)S(1)} collective-permute-done((f32[64,128]{1,0:T(8,128)S(1)}, f32[64,128]{1,0:T(8,128)S(1)}, u32[]{:S(2)}, u32[]{:S(2)}) %collective-permute-start.6) | collective-permute-done | bytes 32800 | tf_op jit(solution)/shard_map/ppermute | solution.py:513
  62.0 0.0 all-to-all-done.depth_ref
  62.0 0.1 gather.1
  62.1 10.6 %all_to_all.10.depth_ref = f32[8,8,896]{2,1,0:T(8,128)S(1)} all-to-all(f32[8,8,896]{2,1,0:T(8,128)S(1)} %get-tuple-element.33), channel_id=1, replica_groups=mesh['gy'=8,'gz'=4] {'gy'}, dimensions={0} | all-to-all | bytes 458752 | tf_op jit(solution)/shard_map/all_to_all | solution.py:524
  72.7 0.8 %steps.1 = (f32[2,32,512]{2,1,0:T(8,128)}, f32[2,64,32]{2,1,0:T(8,128)}) custom-call(f32[8,8,896]{2,1,0:T(8,128)S(1)} %all_to_all.10.depth_ref, f32[64,128]{1,0:T(8,128)S(1)} %get-tuple-element.34.plane_ref), custom_call_target="tpu_custom_call" | custom-call | tf_op jit(solution)/shard_map/steps/pallas_call | solution.py:526
Async XLA Ops:
  3.7 7.3 %collective-permute-start = (bf16[64,128]{1,0:T(8,128)(2,1)}, bf16[64,128]{1,0:T(8,128)(2,1)S(1)}, u32[]{:S(2)}, u32[]{:S(2)}) collective-permute-start(bf16[64,128]{1,0:T(8,128)(2,1)} %get-tuple-element.20), channel_id=1, source_target_pairs={{0,1},{2,3},{1,0},{3,2},{4,5},{6,7},{5,4},{7,6},{8,9},{10,11},{9,8... | collective-permute-start | bytes 49160 | tf_op jit(solution)/shard_map/ppermute | solution.py:124
  6.8 4.3 %collective-permute-start.1 = (bf16[64,128]{1,0:T(8,128)(2,1)}, bf16[64,128]{1,0:T(8,128)(2,1)S(1)}, u32[]{:S(2)}, u32[]{:S(2)}) collective-permute-start(bf16[64,128]{1,0:T(8,128)(2,1)} %get-tuple-element.21), channel_id=1, source_target_pairs={{1,2},{2,1},{5,6},{6,5},{9,10},{10,9},{13,14},{14,13},{17,18},{18,... | collective-permute-start | bytes 49160 | tf_op jit(solution)/shard_map/ppermute | solution.py:124
  7.5 6.8 %collective-permute-start.2 = (bf16[64,512]{1,0:T(8,128)(2,1)}, bf16[64,512]{1,0:T(8,128)(2,1)S(1)}, u32[]{:S(2)}, u32[]{:S(2)}) collective-permute-start(bf16[64,512]{1,0:T(8,128)(2,1)} %get-tuple-element.24), channel_id=1, source_target_pairs={{4,8},{12,16},{20,24},{8,4},{16,12},{24,20},{5,9},{13,17},{21,25},... | collective-permute-start | bytes 196616 | tf_op jit(solution)/shard_map/ppermute | solution.py:124
  8.1 3.9 %copy-start = (bf16[64,64,512]{2,1,0:T(8,128)(2,1)S(1)}, bf16[64,64,512]{2,1,0:T(8,128)(2,1)}, u32[]{:S(2)}) copy-start(bf16[64,64,512]{2,1,0:T(8,128)(2,1)} %image_hbm.1) | copy-start | bytes 12582916
  8.2 6.2 %collective-permute-start.3 = (bf16[64,512]{1,0:T(8,128)(2,1)}, bf16[64,512]{1,0:T(8,128)(2,1)S(1)}, u32[]{:S(2)}, u32[]{:S(2)}) collective-permute-start(bf16[64,512]{1,0:T(8,128)(2,1)} %get-tuple-element.25), channel_id=1, source_target_pairs={{0,4},{8,12},{16,20},{24,28},{4,0},{12,8},{20,16},{28,24},{1,5},{9... | collective-permute-start | bytes 196616 | tf_op jit(solution)/shard_map/ppermute | solution.py:124
  11.3 2.3 %copy-start.1 = (f32[2,32,512]{2,1,0:T(8,128)S(1)}, f32[2,32,512]{2,1,0:T(8,128)}, u32[]{:S(2)}) copy-start(f32[2,32,512]{2,1,0:T(8,128)} %depth_ref.3) | copy-start | bytes 393220
  11.3 2.3 %copy-start.2 = (f32[2,32,8,8]{1,3,2,0:T(8,128)S(1)}, f32[2,32,8,8]{1,3,2,0:T(8,128)}, u32[]{:S(2)}) copy-start(f32[2,32,8,8]{1,3,2,0:T(8,128)} %param.8) | copy-start | bytes 49156
  11.3 3.0 %collective-permute-start.5 = (bf16[64,128]{1,0:T(8,128)(2,1)S(1)}, bf16[64,128]{1,0:T(8,128)(2,1)S(1)}, u32[]{:S(2)}, u32[]{:S(2)}) collective-permute-start(bf16[64,128]{1,0:T(8,128)(2,1)S(1)} %get-tuple-element.26), channel_id=1, source_target_pairs={{0,4},{8,12},{16,20},{24,28},{4,0},{12,8},{20,16},{28,24},{1,5},{9... | collective-permute-start | bytes 49160 | tf_op jit(solution)/shard_map/ppermute | solution.py:124
  11.4 2.9 %collective-permute-start.4 = (bf16[64,128]{1,0:T(8,128)(2,1)S(1)}, bf16[64,128]{1,0:T(8,128)(2,1)S(1)}, u32[]{:S(2)}, u32[]{:S(2)}) collective-permute-start(bf16[64,128]{1,0:T(8,128)(2,1)S(1)} %get-tuple-element.22.later_ref), channel_id=1, source_target_pairs={{4,8},{12,16},{20,24},{8,4},{16,12},{24,20},{5,9},{13,17},{21,25},... | collective-permute-start | bytes 49160 | tf_op jit(solution)/shard_map/ppermute | solution.py:124
  46.2 15.8 %all-to-all-start = ((f32[8,8,896]{2,1,0:T(8,128)}), f32[8,8,896]{2,1,0:T(8,128)S(1)}, u32[]{:S(2)}, u32[]{:S(2)}) async-start(f32[8,8,896]{2,1,0:T(8,128)} %get-tuple-element.31), calls=%async_computation | async-start | bytes 458752 | tf_op jit(solution)/shard_map/all_to_all | solution.py:511
  52.2 5.9 %collective-permute-start.8 = (f32[64,128]{1,0:T(8,128)S(1)}, f32[64,128]{1,0:T(8,128)S(1)}, u32[]{:S(2)}, u32[]{:S(2)}) collective-permute-start(f32[64,128]{1,0:T(8,128)S(1)} %get-tuple-element.32.refs_0_), channel_id=1, source_target_pairs={{0,3},{1,2},{2,1},{3,0},{4,7},{5,6},{6,5},{7,4},{8,11},{9,10},{10,... | collective-permute-start | bytes 98312 | tf_op jit(solution)/shard_map/ppermute | solution.py:513
  54.7 6.6 %collective-permute-start.7 = (f32[64,128]{1,0:T(8,128)S(1)}, f32[64,128]{1,0:T(8,128)S(1)}, u32[]{:S(2)}, u32[]{:S(2)}) collective-permute-start(f32[64,128]{1,0:T(8,128)S(1)} %get-tuple-element.32.refs_0_), channel_id=1, source_target_pairs={{0,2},{1,3},{2,0},{3,1},{4,6},{5,7},{6,4},{7,5},{8,10},{9,11},{10,... | collective-permute-start | bytes 98312 | tf_op jit(solution)/shard_map/ppermute | solution.py:513
  58.0 3.9 %collective-permute-start.6 = (f32[64,128]{1,0:T(8,128)S(1)}, f32[64,128]{1,0:T(8,128)S(1)}, u32[]{:S(2)}, u32[]{:S(2)}) collective-permute-start(f32[64,128]{1,0:T(8,128)S(1)} %get-tuple-element.32.refs_0_), channel_id=1, source_target_pairs={{0,1},{1,0},{2,3},{3,2},{4,5},{5,4},{6,7},{7,6},{8,9},{9,8},{10,11... | collective-permute-start | bytes 98312 | tf_op jit(solution)/shard_map/ppermute | solution.py:513
